TPU v7x, 32 devices: a whole 2x2x4 slice. The times are simulated.
32 devices in a mesh: tok: 4 (over y, x), ffn: 8 (over z, core).
Axes of the slice: x: 2, y: 2, z: 4, core: 2. Of those that a mesh axis runs over, the one named last changes fastest.
Arguments:
- targets: bfloat16 [8192, 1024], P(('tok', 'ffn')), may hold values from -6 to 6
- memory: bfloat16 [64, 2048, 1024], P('tok', 'ffn'), may hold values from -6 to 6
- out_grad: bfloat16 [8192, 1024], P(('tok', 'ffn')), may hold values from -6 to 6
- target_lengths: int32 [64], P(('tok', 'ffn')), may hold values from 32 to 128
- memory_lengths: int32 [64], P(('tok', 'ffn')), may hold values from 512 to 2048, as said below
- buckets: int32 [128, 128], replicated, may hold values from 0 to 31
- rel_table: bfloat16 [512], P(('tok', 'ffn')), may hold values from -5 to 5
- gain_self: bfloat16 [1024], P(('tok', 'ffn')), may hold values from 0.25 to 1.75
- gain_cross: bfloat16 [1024], P(('tok', 'ffn')), may hold values from 0.25 to 1.75
- gain_ffn: bfloat16 [1024], P(('tok', 'ffn')), may hold values from 0.25 to 1.75
- self_query: bfloat16 [1024, 1024], P(('tok', 'ffn')), may hold values from -0.1875 to 0.1875
- self_key: bfloat16 [1024, 512], P(('tok', 'ffn')), may hold values from -0.1875 to 0.1875
- self_value: bfloat16 [1024, 512], P(('tok', 'ffn')), may hold values from -0.1875 to 0.1875
- self_output: bfloat16 [1024, 1024], P(('tok', 'ffn')), may hold values from -0.75 to 0.75
- cross_query: bfloat16 [1024, 1024], P(('tok', 'ffn')), may hold values from -0.1875 to 0.1875
- cross_key: bfloat16 [1024, 512], P(('tok', 'ffn')), may hold values from -0.1875 to 0.1875
- cross_value: bfloat16 [1024, 512], P(('tok', 'ffn')), may hold values from -0.1875 to 0.1875
- cross_output: bfloat16 [1024, 1024], P(('tok', 'ffn')), may hold values from -2 to 2
- ffn_gate: bfloat16 [1024, 2816], P(None, 'ffn'), may hold values from -0.1875 to 0.1875
- ffn_up: bfloat16 [1024, 2816], P(None, 'ffn'), may hold values from -0.1875 to 0.1875
- ffn_down: bfloat16 [2816, 1024], P('ffn'), may hold values from -0.109375 to 0.109375
Outputs:
- layer_out: bfloat16 [8192, 1024], P(('tok', 'ffn'))
- targets_grad: bfloat16 [8192, 1024], P(('tok', 'ffn'))
- memory_grad: bfloat16 [64, 2048, 1024], P('tok', 'ffn')
- rms_values: float32 [64, 4], P(('tok', 'ffn'))
- rel_table_grad: float32 [512], P(('tok', 'ffn'))
- gain_self_grad: float32 [1024], P(('tok', 'ffn'))
- gain_cross_grad: float32 [1024], P(('tok', 'ffn'))
- gain_ffn_grad: float32 [1024], P(('tok', 'ffn'))
- self_query_grad: float32 [1024, 1024], P(('tok', 'ffn'))
- self_key_grad: float32 [1024, 512], P(('tok', 'ffn'))
- self_value_grad: float32 [1024, 512], P(('tok', 'ffn'))
- self_output_grad: float32 [1024, 1024], P(('tok', 'ffn'))
- cross_query_grad: float32 [1024, 1024], P(('tok', 'ffn'))
- cross_key_grad: float32 [1024, 512], P(('tok', 'ffn'))
- cross_value_grad: float32 [1024, 512], P(('tok', 'ffn'))
- cross_output_grad: float32 [1024, 1024], P(('tok', 'ffn'))
- ffn_gate_grad: float32 [1024, 2816], P(None, 'ffn')
- ffn_up_grad: float32 [1024, 2816], P(None, 'ffn')
- ffn_down_grad: float32 [2816, 1024], P('ffn')
Inputs may be any that keep to these rules, and one draw needn't show every extreme that they name: `memory_lengths`: in every aligned run of 8 pairs one pair has all 2048 memory positions valid and another a quarter of them.
All inputs are finite; a program needn't handle non-finite values.
Results may differ from a plain program's by a relative error of at most 0.024.
Values may be sent and summed in bfloat16 or wider, within the bound.
No kernel may reach another device: no remote copies, remote signals or barrier semaphores. Data moves between devices by JAX's collectives and lax.ppermute only.
A program may use at most 320 MiB of HBM per device.

v0:
```python
import jax
import jax.numpy as jnp
from jax import lax
from jax.sharding import PartitionSpec as P

D = 1024
HEADS = 16
HEAD = 64
GROUPS = 8
BUCKETS = 32
TGT = 128
MEM = 2048


norm_epsilon = 1e-06
masked_value = -1e30


def matmul(left, right):
    return jnp.dot(left, right, preferred_element_type=jnp.float32)


def norm_rows(hidden, gain):
    scale = lax.rsqrt(jnp.mean(hidden * hidden, axis=-1, keepdims=True) + norm_epsilon)
    return hidden * scale * gain


def norm_back(hidden, gain, cotangent):
    unused, pullback = jax.vjp(norm_rows, hidden, gain)
    return pullback(cotangent)


def gated(gate_value, up_value):
    return jax.nn.gelu(gate_value, approximate=True) * up_value


def gated_back(gate_value, up_value, cotangent):
    unused, pullback = jax.vjp(gated, gate_value, up_value)
    gate_grad, up_grad = pullback(cotangent)
    return (gate_grad.astype(jnp.bfloat16), up_grad.astype(jnp.bfloat16))


def attention_scores(queries, keys, bias, mask):
    raw = jnp.einsum("pqgre,pkge->pgrqk", queries, keys, preferred_element_type=jnp.float32)
    return jnp.where(mask, raw * HEAD ** (-0.5) + bias, masked_value)


def attention_forward(queries, keys, values, bias, mask):
    scores = attention_scores(queries, keys, bias, mask)
    highest = jnp.max(scores, axis=-1, keepdims=True)
    weights = jnp.exp(scores - highest)
    totals = jnp.sum(weights, axis=-1, keepdims=True)
    probs = (weights / totals).astype(jnp.bfloat16)
    mixed = jnp.einsum("pgrqk,pkge->pqgre", probs, values, preferred_element_type=jnp.float32)
    return (mixed.astype(jnp.bfloat16), highest + jnp.log(totals))


def attention_backward(queries, keys, values, bias, mask, log_totals, mixed_grad):
    scores = attention_scores(queries, keys, bias, mask)
    probs = jnp.exp(scores - log_totals)
    prob_grad = jnp.einsum(
        "pqgre,pkge->pgrqk", mixed_grad, values, preferred_element_type=jnp.float32
    )
    values_grad = jnp.einsum(
        "pgrqk,pqgre->pkge",
        probs.astype(jnp.bfloat16),
        mixed_grad,
        preferred_element_type=jnp.float32,
    )
    inner = jnp.sum(probs * prob_grad, axis=-1, keepdims=True)
    score_grad = (probs * (prob_grad - inner)).astype(jnp.bfloat16)
    queries_grad = jnp.einsum(
        "pgrqk,pkge->pqgre", score_grad, keys, preferred_element_type=jnp.float32
    ) * HEAD ** (-0.5)
    keys_grad = jnp.einsum(
        "pgrqk,pqgre->pkge", score_grad, queries, preferred_element_type=jnp.float32
    ) * HEAD ** (-0.5)
    return (queries_grad, keys_grad, values_grad, score_grad)


def on_device(
    targets,
    memory,
    out_grad,
    target_lengths,
    memory_lengths,
    buckets,
    rel_table,
    gain_self,
    gain_cross,
    gain_ffn,
    self_query,
    self_key,
    self_value,
    self_output,
    cross_query,
    cross_key,
    cross_value,
    cross_output,
    ffn_gate,
    ffn_up,
    ffn_down,
):
    pair_count = target_lengths.shape[0]
    row_count = targets.shape[0]
    group_width = HEADS // GROUPS
    key_width = GROUPS * HEAD
    params = (
        rel_table,
        gain_self,
        gain_cross,
        gain_ffn,
        self_query,
        self_key,
        self_value,
        self_output,
        cross_query,
        cross_key,
        cross_value,
        cross_output,
    )
    gathered_params = (
        lax.all_gather(params[0], ("tok", "ffn"), axis=0, tiled=True),
        lax.all_gather(params[1], ("tok", "ffn"), axis=0, tiled=True),
        lax.all_gather(params[2], ("tok", "ffn"), axis=0, tiled=True),
        lax.all_gather(params[3], ("tok", "ffn"), axis=0, tiled=True),
        lax.all_gather(params[4], ("tok", "ffn"), axis=0, tiled=True),
        lax.all_gather(params[5], ("tok", "ffn"), axis=0, tiled=True),
        lax.all_gather(params[6], ("tok", "ffn"), axis=0, tiled=True),
        lax.all_gather(params[7], ("tok", "ffn"), axis=0, tiled=True),
        lax.all_gather(params[8], ("tok", "ffn"), axis=0, tiled=True),
        lax.all_gather(params[9], ("tok", "ffn"), axis=0, tiled=True),
        lax.all_gather(params[10], ("tok", "ffn"), axis=0, tiled=True),
        lax.all_gather(params[11], ("tok", "ffn"), axis=0, tiled=True),
    )
    (
        full_table,
        full_gain_self,
        full_gain_cross,
        full_gain_ffn,
        full_self_query,
        full_self_key,
        full_self_value,
        full_self_output,
        full_cross_query,
        full_cross_key,
        full_cross_value,
        full_cross_output,
    ) = gathered_params
    onehot = (buckets[:, :, None] == jnp.arange(BUCKETS)[None, None, :]).astype(jnp.bfloat16)
    position = jnp.arange(TGT)
    self_bias = jnp.einsum(
        "qkb,hb->hqk",
        onehot,
        full_table.reshape(HEADS, BUCKETS),
        preferred_element_type=jnp.float32,
    ).reshape(1, GROUPS, group_width, TGT, TGT)
    causal = position[None, :] <= position[:, None]
    self_mask = causal[None, None, None] & (
        position[None, None, None, None, :] < target_lengths[:, None, None, None, None]
    )
    cross_mask = (jnp.arange(MEM)[None, :] < memory_lengths[:, None])[:, None, None, None, :]
    inputs = targets.astype(jnp.float32)
    normed_one = norm_rows(inputs, full_gain_self.astype(jnp.float32)).astype(jnp.bfloat16)
    self_queries = (
        matmul(normed_one, full_self_query)
        .astype(jnp.bfloat16)
        .reshape(pair_count, TGT, GROUPS, group_width, HEAD)
    )
    self_keys = (
        matmul(normed_one, full_self_key)
        .astype(jnp.bfloat16)
        .reshape(pair_count, TGT, GROUPS, HEAD)
    )
    self_values = (
        matmul(normed_one, full_self_value)
        .astype(jnp.bfloat16)
        .reshape(pair_count, TGT, GROUPS, HEAD)
    )
    self_mixed, self_totals = attention_forward(
        self_queries, self_keys, self_values, self_bias, self_mask
    )
    self_flat = self_mixed.reshape(row_count, D)
    self_branch = matmul(self_flat, full_self_output)
    hidden_one = inputs + self_branch
    normed_two = norm_rows(hidden_one, full_gain_cross.astype(jnp.float32)).astype(jnp.bfloat16)
    cross_queries = (
        matmul(normed_two, full_cross_query)
        .astype(jnp.bfloat16)
        .reshape(pair_count, TGT, GROUPS, group_width, HEAD)
    )
    memory_flat = memory.reshape(-1, D)
    memory_keys = (
        matmul(memory_flat, full_cross_key)
        .astype(jnp.bfloat16)
        .reshape(memory.shape[0], memory.shape[1], key_width)
    )
    memory_values = (
        matmul(memory_flat, full_cross_value)
        .astype(jnp.bfloat16)
        .reshape(memory.shape[0], memory.shape[1], key_width)
    )
    pair_keys, pair_values = (
        lax.all_to_all(memory_keys, "ffn", split_axis=0, concat_axis=1, tiled=True),
        lax.all_to_all(memory_values, "ffn", split_axis=0, concat_axis=1, tiled=True),
    )
    pair_keys = pair_keys.reshape(pair_count, MEM, GROUPS, HEAD)
    pair_values = pair_values.reshape(pair_count, MEM, GROUPS, HEAD)
    cross_mixed, cross_totals = attention_forward(
        cross_queries, pair_keys, pair_values, 0.0, cross_mask
    )
    cross_flat = cross_mixed.reshape(row_count, D)
    cross_branch = matmul(cross_flat, full_cross_output)
    hidden_two = hidden_one + cross_branch
    normed_three = norm_rows(hidden_two, full_gain_ffn.astype(jnp.float32)).astype(jnp.bfloat16)
    all_rows = lax.all_gather(normed_three, "ffn", axis=0, tiled=True)
    gate_value = matmul(all_rows, ffn_gate)
    up_value = matmul(all_rows, ffn_up)
    hidden = gated(gate_value, up_value).astype(jnp.bfloat16)
    ffn_branch = lax.psum_scatter(
        matmul(hidden, ffn_down).astype(jnp.bfloat16), "ffn", scatter_dimension=0, tiled=True
    ).astype(jnp.float32)
    all_cotangent = lax.all_gather(out_grad, "ffn", axis=0, tiled=True)
    hidden_grad = matmul(all_cotangent, ffn_down.T)
    down_part = matmul(hidden.T, all_cotangent)
    gate_grad, up_grad = gated_back(gate_value, up_value, hidden_grad)
    gate_part = matmul(all_rows.T, gate_grad)
    up_part = matmul(all_rows.T, up_grad)
    normed_three_grad = lax.psum_scatter(
        matmul(gate_grad, ffn_gate.T) + matmul(up_grad, ffn_up.T),
        "ffn",
        scatter_dimension=0,
        tiled=True,
    )
    gate_weight_grad, up_weight_grad, down_weight_grad = (
        lax.psum(gate_part.astype(jnp.bfloat16), "tok").astype(jnp.float32),
        lax.psum(up_part.astype(jnp.bfloat16), "tok").astype(jnp.float32),
        lax.psum(down_part.astype(jnp.bfloat16), "tok").astype(jnp.float32),
    )
    hidden_three = hidden_two + ffn_branch
    layer_out = hidden_three.astype(jnp.bfloat16)
    valid = (position[None, :] < target_lengths[:, None])[:, :, None]
    counted = target_lengths.astype(jnp.float32) * D

    def root_mean(field):
        squares = field.reshape(pair_count, TGT, D)
        squares = jnp.where(valid, squares * squares, 0.0)
        return jnp.sqrt(jnp.sum(squares, axis=(1, 2)) / counted)

    rms_values = jnp.stack(
        [
            root_mean(hidden_three),
            root_mean(self_branch),
            root_mean(cross_branch),
            root_mean(ffn_branch),
        ],
        axis=1,
    )
    back_params = (
        lax.all_gather(params[0], ("tok", "ffn"), axis=0, tiled=True),
        lax.all_gather(params[1], ("tok", "ffn"), axis=0, tiled=True),
        lax.all_gather(params[2], ("tok", "ffn"), axis=0, tiled=True),
        lax.all_gather(params[3], ("tok", "ffn"), axis=0, tiled=True),
        lax.all_gather(params[4], ("tok", "ffn"), axis=0, tiled=True),
        lax.all_gather(params[5], ("tok", "ffn"), axis=0, tiled=True),
        lax.all_gather(params[6], ("tok", "ffn"), axis=0, tiled=True),
        lax.all_gather(params[7], ("tok", "ffn"), axis=0, tiled=True),
        lax.all_gather(params[8], ("tok", "ffn"), axis=0, tiled=True),
        lax.all_gather(params[9], ("tok", "ffn"), axis=0, tiled=True),
        lax.all_gather(params[10], ("tok", "ffn"), axis=0, tiled=True),
        lax.all_gather(params[11], ("tok", "ffn"), axis=0, tiled=True),
    )
    (
        unused_table,
        back_gain_self,
        back_gain_cross,
        back_gain_ffn,
        back_self_query,
        back_self_key,
        back_self_value,
        back_self_output,
        back_cross_query,
        back_cross_key,
        back_cross_value,
        back_cross_output,
    ) = back_params
    cotangent = out_grad.astype(jnp.float32)
    norm_three_back, gain_ffn_grad = norm_back(
        hidden_two, back_gain_ffn.astype(jnp.float32), normed_three_grad
    )
    hidden_two_grad = cotangent + norm_three_back
    cross_branch_low = hidden_two_grad.astype(jnp.bfloat16)
    cross_output_grad = matmul(cross_flat.T, cross_branch_low)
    cross_mixed_grad = (
        matmul(cross_branch_low, back_cross_output.T)
        .astype(jnp.bfloat16)
        .reshape(pair_count, TGT, GROUPS, group_width, HEAD)
    )
    cross_queries_grad, pair_keys_grad, pair_values_grad, unused_scores = attention_backward(
        cross_queries, pair_keys, pair_values, 0.0, cross_mask, cross_totals, cross_mixed_grad
    )
    cross_queries_low = cross_queries_grad.astype(jnp.bfloat16).reshape(row_count, D)
    keys_back, values_back = (
        lax.all_to_all(
            pair_keys_grad.astype(jnp.bfloat16).reshape(pair_count, MEM, key_width),
            "ffn",
            split_axis=1,
            concat_axis=0,
            tiled=True,
        ),
        lax.all_to_all(
            pair_values_grad.astype(jnp.bfloat16).reshape(pair_count, MEM, key_width),
            "ffn",
            split_axis=1,
            concat_axis=0,
            tiled=True,
        ),
    )
    keys_back = keys_back.reshape(-1, key_width)
    values_back = values_back.reshape(-1, key_width)
    cross_key_grad = matmul(memory_flat.T, keys_back)
    cross_value_grad = matmul(memory_flat.T, values_back)
    memory_grad = (
        (matmul(keys_back, back_cross_key.T) + matmul(values_back, back_cross_value.T))
        .astype(jnp.bfloat16)
        .reshape(memory.shape)
    )
    cross_query_grad = matmul(normed_two.T, cross_queries_low)
    normed_two_grad = matmul(cross_queries_low, back_cross_query.T)
    norm_two_back, gain_cross_grad = norm_back(
        hidden_one, back_gain_cross.astype(jnp.float32), normed_two_grad
    )
    hidden_one_grad = hidden_two_grad + norm_two_back
    self_branch_low = hidden_one_grad.astype(jnp.bfloat16)
    self_output_grad = matmul(self_flat.T, self_branch_low)
    self_mixed_grad = (
        matmul(self_branch_low, back_self_output.T)
        .astype(jnp.bfloat16)
        .reshape(pair_count, TGT, GROUPS, group_width, HEAD)
    )
    self_queries_grad, self_keys_grad, self_values_grad, self_score_grad = attention_backward(
        self_queries, self_keys, self_values, self_bias, self_mask, self_totals, self_mixed_grad
    )
    table_grad = jnp.einsum(
        "pgrqk,qkb->grb", self_score_grad, onehot, preferred_element_type=jnp.float32
    ).reshape(HEADS * BUCKETS)
    queries_low = self_queries_grad.astype(jnp.bfloat16).reshape(row_count, D)
    keys_low = self_keys_grad.astype(jnp.bfloat16).reshape(row_count, key_width)
    values_low = self_values_grad.astype(jnp.bfloat16).reshape(row_count, key_width)
    self_query_grad = matmul(normed_one.T, queries_low)
    self_key_grad = matmul(normed_one.T, keys_low)
    self_value_grad = matmul(normed_one.T, values_low)
    normed_one_grad = (
        matmul(queries_low, back_self_query.T)
        + matmul(keys_low, back_self_key.T)
        + matmul(values_low, back_self_value.T)
    )
    norm_one_back, gain_self_grad = norm_back(
        inputs, back_gain_self.astype(jnp.float32), normed_one_grad
    )
    targets_grad = (hidden_one_grad + norm_one_back).astype(jnp.bfloat16)
    (
        table_share,
        gain_self_share,
        gain_cross_share,
        gain_ffn_share,
        self_query_share,
        self_key_share,
        self_value_share,
        self_output_share,
        cross_query_share,
        cross_key_share,
        cross_value_share,
        cross_output_share,
    ) = (
        lax.psum_scatter(table_grad, ("tok", "ffn"), scatter_dimension=0, tiled=True),
        lax.psum_scatter(gain_self_grad, ("tok", "ffn"), scatter_dimension=0, tiled=True),
        lax.psum_scatter(gain_cross_grad, ("tok", "ffn"), scatter_dimension=0, tiled=True),
        lax.psum_scatter(gain_ffn_grad, ("tok", "ffn"), scatter_dimension=0, tiled=True),
        lax.psum_scatter(self_query_grad, ("tok", "ffn"), scatter_dimension=0, tiled=True),
        lax.psum_scatter(self_key_grad, ("tok", "ffn"), scatter_dimension=0, tiled=True),
        lax.psum_scatter(self_value_grad, ("tok", "ffn"), scatter_dimension=0, tiled=True),
        lax.psum_scatter(self_output_grad, ("tok", "ffn"), scatter_dimension=0, tiled=True),
        lax.psum_scatter(cross_query_grad, ("tok", "ffn"), scatter_dimension=0, tiled=True),
        lax.psum_scatter(cross_key_grad, ("tok", "ffn"), scatter_dimension=0, tiled=True),
        lax.psum_scatter(cross_value_grad, ("tok", "ffn"), scatter_dimension=0, tiled=True),
        lax.psum_scatter(cross_output_grad, ("tok", "ffn"), scatter_dimension=0, tiled=True),
    )
    return (
        layer_out,
        targets_grad,
        memory_grad,
        rms_values,
        table_share,
        gain_self_share,
        gain_cross_share,
        gain_ffn_share,
        self_query_share,
        self_key_share,
        self_value_share,
        self_output_share,
        cross_query_share,
        cross_key_share,
        cross_value_share,
        cross_output_share,
        gate_weight_grad,
        up_weight_grad,
        down_weight_grad,
    )


def solution(mesh):
    in_specs = (
        P(("tok", "ffn"), None),
        P("tok", "ffn", None),
        P(("tok", "ffn"), None),
        P(("tok", "ffn")),
        P(("tok", "ffn")),
        P(),
        P(("tok", "ffn")),
        P(("tok", "ffn")),
        P(("tok", "ffn")),
        P(("tok", "ffn")),
        P(("tok", "ffn"), None),
        P(("tok", "ffn"), None),
        P(("tok", "ffn"), None),
        P(("tok", "ffn"), None),
        P(("tok", "ffn"), None),
        P(("tok", "ffn"), None),
        P(("tok", "ffn"), None),
        P(("tok", "ffn"), None),
        P(None, "ffn"),
        P(None, "ffn"),
        P("ffn", None),
    )
    out_specs = (
        P(("tok", "ffn"), None),
        P(("tok", "ffn"), None),
        P("tok", "ffn", None),
        P(("tok", "ffn"), None),
        P(("tok", "ffn")),
        P(("tok", "ffn")),
        P(("tok", "ffn")),
        P(("tok", "ffn")),
        P(("tok", "ffn"), None),
        P(("tok", "ffn"), None),
        P(("tok", "ffn"), None),
        P(("tok", "ffn"), None),
        P(("tok", "ffn"), None),
        P(("tok", "ffn"), None),
        P(("tok", "ffn"), None),
        P(("tok", "ffn"), None),
        P(None, "ffn"),
        P(None, "ffn"),
        P("ffn", None),
    )
    return jax.shard_map(
        on_device, mesh=mesh, in_specs=in_specs, out_specs=out_specs, check_vma=False
    )
```

profile of v0, /device:TPU:0, one launch (start us, length us, event | category | flops | bytes accessed | tf_op | source)
XLA Modules:
  0.0 2029.5 jit_solution(336059380363038151)
XLA Ops:
  10.6 57.0 %all-gather.21.cloned.1.call-done = bf16[1024,512]{1,0:T(8,128)(2,1)} async-done(((bf16[32,512]{1,0:T(8,128)(2,1)}), bf16[1024,512]{1,0:T(8,128)(2,1)}) %all-gather.21.cloned.1.call-update) | async-done | bytes 1048592 | tf_op jit(solution)/shard_map/all_gather | solution.py:132
  67.6 10.2 convolution_convert_fusion
  77.7 4.6 all-to-all-start.1
  83.6 52.7 %all-gather.19.cloned.1.call-done = bf16[1024,512]{1,0:T(8,128)(2,1)} async-done(((bf16[32,512]{1,0:T(8,128)(2,1)}), bf16[1024,512]{1,0:T(8,128)(2,1)}) %all-gather.19.cloned.1.call-update) | async-done | bytes 1048592 | tf_op jit(solution)/shard_map/all_gather | solution.py:133
  136.3 10.2 convolution_convert_fusion.1
  146.5 36.3 %all-to-all-done.1 = bf16[16,256,512]{2,1,0:T(8,128)(2,1)} async-done(((bf16[16,256,512]{2,1,0:T(8,128)(2,1)}), bf16[16,256,512]{2,1,0:T(8,128)(2,1)}, u32[]{:S(2)}, u32[]{:S(2)}) %all-to-all-start.1) | async-done | bytes 4194336 | tf_op jit(solution)/shard_map/all_to_all | solution.py:204
  182.8 4.7 all-to-all-start
  189.3 119.8 %all-reduce.9 = (bf16[1024]{0:T(1024)(128)(2,1)S(1)}, bf16[512]{0:T(512)(128)(2,1)S(1)}, bf16[1024]{0:T(1024)(128)(2,1)S(1)}, bf16[1024]{0:T(1024)(128)(2,1)S(1)}) all-reduce(bf16[1024]{0:T(1024)(128)(2,1)S(1)} %dynamic-update-slice, bf16[512]{0:T(512)(128)(2,1)S(1)} %dynamic-update-slice.1, ...), channel_id=1, replica_groups=mesh['tok'=4,'ffn'=8] {'tok','ffn'}, use_global_device_ids=true, to_apply=%add | all-reduce | flops 3584 | bytes 14336
  319.1 29.0 %all-gather.15.cloned.1.call-done = bf16[1024,1024]{1,0:T(8,128)(2,1)} async-done(((bf16[32,1024]{1,0:T(8,128)(2,1)}), bf16[1024,1024]{1,0:T(8,128)(2,1)}) %all-gather.15.cloned.1.call-update) | async-done | bytes 2097168 | tf_op jit(solution)/shard_map/all_gather | solution.py:127
  356.1 50.2 %all-gather.17.cloned.1.call-done = bf16[1024,1024]{1,0:T(8,128)(2,1)} async-done(((bf16[32,1024]{1,0:T(8,128)(2,1)}), bf16[1024,1024]{1,0:T(8,128)(2,1)}) %all-gather.17.cloned.1.call-update) | async-done | bytes 2097168 | tf_op jit(solution)/shard_map/all_gather | solution.py:130
  406.3 3.4 multiply_reduce_fusion.5
  409.7 55.0 %all-gather.23.cloned.1.call-done = bf16[1024,1024]{1,0:T(8,128)(2,1)} async-done(((bf16[32,1024]{1,0:T(8,128)(2,1)}), bf16[1024,1024]{1,0:T(8,128)(2,1)}) %all-gather.23.cloned.1.call-update) | async-done | bytes 2097168 | tf_op jit(solution)/shard_map/all_gather | solution.py:131
  471.1 8.2 copy.214
  479.3 7.4 reshape.325
  486.7 8.0 copy.213
  494.8 7.4 reshape.326
  502.2 16.7 bitcast_reduce_fusion
  518.8 14.5 fusion.5
  533.3 15.9 fusion.54
  549.8 3.5 multiply_reduce_fusion.4
  555.2 45.5 %all-gather.27.cloned.1.call-done = bf16[2048,1024]{1,0:T(8,128)(2,1)} async-done(((bf16[256,1024]{1,0:T(8,128)(2,1)}), bf16[2048,1024]{1,0:T(8,128)(2,1)}) %all-gather.27.cloned.1.call-update) | async-done | bytes 4194320 | tf_op jit(solution)/shard_map/all_gather | solution.py:216
  600.7 5.8 fusion.138
  606.5 3.3 fusion.139
  609.8 38.3 %all-gather.29.cloned.1.call-done = bf16[2048,1024]{1,0:T(8,128)(2,1)} async-done(((bf16[256,1024]{1,0:T(8,128)(2,1)}), bf16[2048,1024]{1,0:T(8,128)(2,1)}) %all-gather.29.cloned.1.call-update) | async-done | bytes 4194320 | tf_op jit(solution)/shard_map/all_gather | solution.py:223
  648.1 8.8 multiply_convert_fusion
  658.0 4.4 convolution_convert_fusion.2
  663.5 3.9 fusion.140
  667.4 6.1 convolution_add_fusion
  674.3 5.4 convolution_convert_fusion.3
  679.7 2.5 convolution_convert_fusion.4
  682.5 2.6 convolution_convert_fusion.5
  685.2 26.1 %reduce-scatter.15.cloned.1.call-done = bf16[256,1024]{1,0:T(8,128)(2,1)} async-done(((bf16[2048,1024]{1,0:T(8,128)(2,1)}), bf16[256,1024]{1,0:T(8,128)(2,1)}) %reduce-scatter.15.cloned.1.call-update) | async-done | bytes 524304 | tf_op jit(solution)/shard_map/reduce_scatter | solution.py:220
  711.3 90.5 %reduce-scatter.17.cloned.1.call-done = f32[256,1024]{1,0:T(8,128)} async-done(((f32[2048,1024]{1,0:T(8,128)}), f32[256,1024]{1,0:T(8,128)}) %reduce-scatter.17.cloned.1.call-update) | async-done | bytes 1048592 | tf_op jit(solution)/shard_map/reduce_scatter | solution.py:229
  801.8 3.4 multiply_reduce_fusion
  811.8 26.6 %fusion = (f32[2,8,2,128]{3,2,1,0:T(2,128)S(1)}, f32[2,8,2048,128,2]{3,2,4,1,0:T(8,128)}) fusion(f32[2,8,2,128]{3,2,1,0:T(2,128)S(1)} %bitcast.336, f32[2,8,2048,128,2]{3,2,4,1,0:T(8,128)} %get-tuple-element.155, pred[2,2048]{1,0:T(4,128)(4,1)S(1)} %iota_compare_fusion.2, bf16[2,128,8,2,64]{1,4,3,2,0:T(8,128)(2,1)S(1)} %copy.220, ...), kind=kOutput, calls=%fused_computation.2 | convolution fusion | flops 1115680768 | bytes 71864320 | tf_op jit(solution)/shard_map/pqgre,pkge->pgrqk/dot_general | solution.py:61
  838.4 29.8 %fusion.2 = bf16[2,8,2,128,2048]{3,4,2,1,0:T(8,128)(2,1)} fusion(f32[2,8,2048,128,2]{3,2,4,1,0:T(8,128)} %get-tuple-element.158, f32[2,8,2,128]{3,2,1,0:T(2,128)S(1)} %get-tuple-element.157, f32[2,8,2,128]{3,2,1,0:T(2,128)S(1)} %bitcast.337, f32[2,8,2048,128,2]{3,2,4,1,0:T(8,128)} %get-tuple-element.155, pred[2,2048]{1,0:T(4,128)(4,1)S(1)} %iota_compare_fusion.2), kind=kLoop, calls=%fused_computation.4 | loop fusion | flops 50331648 | bytes 83922944 | tf_op jit(solution)/shard_map/convert_element_type | solution.py:71
  868.2 10.0 fusion.48
  897.5 4.1 fusion.82
  901.7 2.7 fusion.86
  905.4 2.7 fusion.90
  908.2 15.8 bitcast_convert_fusion
  924.0 11.1 copy.242
  935.2 4.7 all-to-all-start.3
  940.8 2.8 fusion.78
  943.7 10.0 fusion.11
  953.7 11.1 copy.237
  964.8 82.1 %all-to-all-done.3 = bf16[2,2048,512]{2,0,1:T(2,128)(2,1)} async-done(((bf16[2,2048,512]{2,0,1:T(2,128)(2,1)}), bf16[2,2048,512]{2,0,1:T(2,128)(2,1)}, u32[]{:S(2)}, u32[]{:S(2)}) %all-to-all-start.3) | async-done | bytes 4194336 | tf_op jit(solution)/shard_map/all_to_all | solution.py:311
  1046.9 4.8 all-to-all-start.2
  1051.7 3.0 copy.243
  1058.5 5.8 convolution_bitcast_fusion
  1064.4 2.9 copy.279
  1075.3 2.5 fusion.80
  1079.1 104.6 %all-reduce.8 = (f32[512]{0:T(512)S(1)}, f32[1024]{0:T(1024)S(1)}, f32[1024]{0:T(1024)S(1)}, f32[1024]{0:T(1024)S(1)}) all-reduce(f32[512]{0:T(512)S(1)} %reshape.313, f32[1024]{0:T(1024)S(1)} %get-tuple-element.118, f32[1024]{0:T(1024)S(1)} %get-tuple-element.116, ...), channel_id=4, replica_groups=mesh['tok'=4,'ffn'=8] {'tok','ffn'}, use_global_device_ids=true, to_apply=%region_23.24.clone | all-reduce | flops 3584 | bytes 28672
  1187.0 3.0 copy.238
  1193.8 5.9 convolution_bitcast_fusion.1
  1199.8 2.9 copy.277
  1203.8 13.0 fusion.141
  1216.8 10.3 add_convert_fusion
  1227.2 95.7 %reduce-scatter.27.cloned.1.call-done = f32[32,1024]{1,0:T(8,128)} async-done(((f32[1024,1024]{1,0:T(8,128)}), f32[32,1024]{1,0:T(8,128)}) %reduce-scatter.27.cloned.1.call-update) | async-done | bytes 131088 | tf_op jit(solution)/shard_map/reduce_scatter | solution.py:384
  1322.8 142.0 %reduce-scatter.29.cloned.1.call-done = f32[32,1024]{1,0:T(8,128)} async-done(((f32[1024,1024]{1,0:T(8,128)}), f32[32,1024]{1,0:T(8,128)}) %reduce-scatter.29.cloned.1.call-update) | async-done | bytes 131088 | tf_op jit(solution)/shard_map/reduce_scatter | solution.py:387
  1464.8 142.3 %reduce-scatter.25.cloned.1.call-done = f32[32,1024]{1,0:T(8,128)} async-done(((f32[1024,1024]{1,0:T(8,128)}), f32[32,1024]{1,0:T(8,128)}) %reduce-scatter.25.cloned.1.call-update) | async-done | bytes 131088 | tf_op jit(solution)/shard_map/reduce_scatter | solution.py:383
  1607.1 142.2 %reduce-scatter.19.cloned.1.call-done = f32[32,1024]{1,0:T(8,128)} async-done(((f32[1024,1024]{1,0:T(8,128)}), f32[32,1024]{1,0:T(8,128)}) %reduce-scatter.19.cloned.1.call-update) | async-done | bytes 131088 | tf_op jit(solution)/shard_map/reduce_scatter | solution.py:380
  1749.3 136.3 %reduce-scatter.33.cloned.1.call-done = f32[32,512]{1,0:T(8,128)} async-done(((f32[1024,512]{1,0:T(8,128)}), f32[32,512]{1,0:T(8,128)}) %reduce-scatter.33.cloned.1.call-update) | async-done | bytes 65552
  1885.6 136.6 %reduce-scatter.31.cloned.1.call-done = f32[32,512]{1,0:T(8,128)} async-done(((f32[1024,512]{1,0:T(8,128)}), f32[32,512]{1,0:T(8,128)}) %reduce-scatter.31.cloned.1.call-update) | async-done | bytes 65552
  (314 shorter events, 85.1 us)
Async XLA Ops:
  7.2 640.9 %copy-start = (bf16[352,1024]{1,0:T(8,128)(2,1)S(1)}, bf16[352,1024]{1,0:T(8,128)(2,1)}, u32[]{:S(2)}) copy-start(bf16[352,1024]{1,0:T(8,128)(2,1)} %param.41) | copy-start | bytes 2162692
  7.2 60.4 %all-gather.21.cloned.1.call-start = ((), (), s32[]{:S(2)}) async-start(), calls=%async_computation.19 | async-start | bytes 1081344 | tf_op jit(solution)/shard_map/all_gather | solution.py:132
  7.9 128.4 %all-gather.19.cloned.1.call-start = ((), (), s32[]{:S(2)}) async-start(), calls=%async_computation.18 | async-start | bytes 1081344 | tf_op jit(solution)/shard_map/all_gather | solution.py:133
  8.7 306.4 %all-gather.13.cloned.1.call-start = ((), (), s32[]{:S(2)}) async-start(), calls=%async_computation.15 | async-start | bytes 1081344 | tf_op jit(solution)/shard_map/all_gather | solution.py:128
  9.4 307.6 %all-gather.11.cloned.1.call-start = ((), (), s32[]{:S(2)}) async-start(), calls=%async_computation.14 | async-start | bytes 1081344 | tf_op jit(solution)/shard_map/all_gather | solution.py:129
  10.0 338.1 %all-gather.15.cloned.1.call-start = ((), (), s32[]{:S(2)}) async-start(), calls=%async_computation.16 | async-start | bytes 2162688 | tf_op jit(solution)/shard_map/all_gather | solution.py:127
  77.7 105.0 %all-to-all-start.1 = ((bf16[16,256,512]{2,1,0:T(8,128)(2,1)}), bf16[16,256,512]{2,1,0:T(8,128)(2,1)}, u32[]{:S(2)}, u32[]{:S(2)}) async-start(bf16[16,256,512]{2,1,0:T(8,128)(2,1)} %bitcast.318), calls=%async_computation.1 | async-start | bytes 8388608 | tf_op jit(solution)/shard_map/all_to_all | solution.py:204
  82.3 324.0 %all-gather.17.cloned.1.call-start = ((), (), s32[]{:S(2)}) async-start(), calls=%async_computation.17 | async-start | bytes 2162688 | tf_op jit(solution)/shard_map/all_gather | solution.py:130
  82.9 381.8 %all-gather.23.cloned.1.call-start = ((), (), s32[]{:S(2)}) async-start(), calls=%async_computation.20 | async-start | bytes 2162688 | tf_op jit(solution)/shard_map/all_gather | solution.py:131
  182.8 5.6 copy-start.77
  182.8 5.8 copy-start.78
  182.8 6.1 copy-start.79
  182.8 6.3 copy-start.80
  182.8 126.5 %copy-start.60 = (s32[128,128]{1,0:T(8,128)S(1)}, s32[128,128]{1,0:T(8,128)}, u32[]{:S(2)}) copy-start(s32[128,128]{1,0:T(8,128)} %param.26) | copy-start | bytes 196612
  182.8 304.0 %all-to-all-start = ((bf16[16,256,512]{2,1,0:T(8,128)(2,1)}), bf16[16,256,512]{2,1,0:T(8,128)(2,1)}, u32[]{:S(2)}, u32[]{:S(2)}) async-start(bf16[16,256,512]{2,1,0:T(8,128)(2,1)} %bitcast.317), calls=%async_computation | async-start | bytes 8388608 | tf_op jit(solution)/shard_map/all_to_all | solution.py:205
  187.5 126.6 %copy-start.6 = (bf16[256,1024]{1,0:T(8,128)(2,1)S(1)}, bf16[256,1024]{1,0:T(8,128)(2,1)}, u32[]{:S(2)}) copy-start(bf16[256,1024]{1,0:T(8,128)(2,1)} %param.21) | copy-start | bytes 1572868
  187.5 126.8 %copy-start.71 = (s32[2]{0:T(128)S(1)}, s32[2]{0:T(128)}, u32[]{:S(2)}) copy-start(s32[2]{0:T(128)} %param.24) | copy-start | bytes 28
  187.5 127.5 %copy-start.70 = (s32[2]{0:T(128)S(1)}, s32[2]{0:T(128)}, u32[]{:S(2)}) copy-start(s32[2]{0:T(128)} %param.25) | copy-start | bytes 28
  187.5 362.3 %all-gather.25.cloned.1.call-start = ((), (), s32[]{:S(2)}) async-start(), calls=%async_computation.21 | async-start | bytes 2162688 | tf_op jit(solution)/shard_map/all_gather | solution.py:134
  188.3 412.4 %all-gather.27.cloned.1.call-start = ((), (), s32[]{:S(2)}) async-start(), calls=%async_computation.22 | async-start | bytes 4718592 | tf_op jit(solution)/shard_map/all_gather | solution.py:216
  309.1 38.9 %copy-start.52 = (f32[1024]{0:T(1024)}, f32[1024]{0:T(1024)S(1)}, u32[]{:S(2)}) copy-start(f32[1024]{0:T(1024)S(1)} %convert_element_type.173) | copy-start | bytes 12292
  314.1 150.6 %copy-start.56 = (f32[1024]{0:T(1024)}, f32[1024]{0:T(1024)S(1)}, u32[]{:S(2)}) copy-start(f32[1024]{0:T(1024)S(1)} %convert_element_type.183) | copy-start | bytes 12292
  314.3 33.8 %copy-start.65 = (f32[256]{0:T(256)}, f32[256]{0:T(256)S(1)}, u32[]{:S(2)}) copy-start(f32[256]{0:T(256)S(1)} %fusion.73) | copy-start | bytes 3076
  314.9 33.2 %copy-start.63 = (f32[256]{0:T(256)}, f32[256]{0:T(256)S(1)}, u32[]{:S(2)}) copy-start(f32[256]{0:T(256)S(1)} %fusion.121) | copy-start | bytes 3076
  317.0 35.0 %copy-start.33 = (bf16[2,128,8,64]{1,0,3,2:T(2,128)(2,1)}, bf16[2,128,8,64]{1,0,3,2:T(2,128)(2,1)S(1)}, u32[]{:S(2)}) copy-start(bf16[2,128,8,64]{1,0,3,2:T(2,128)(2,1)S(1)} %reshape.291) | copy-start | bytes 786436
  319.1 35.4 %copy-start.44 = (bf16[2,128,8,64]{1,0,3,2:T(2,128)(2,1)}, bf16[2,128,8,64]{1,0,3,2:T(2,128)(2,1)S(1)}, u32[]{:S(2)}) copy-start(bf16[2,128,8,64]{1,0,3,2:T(2,128)(2,1)S(1)} %reshape.290) | copy-start | bytes 786436
  356.1 110.9 %copy-start.24 = (bf16[2,128,8,2,64]{1,0,4,3,2:T(2,128)(2,1)}, bf16[2,128,8,2,64]{1,0,4,3,2:T(2,128)(2,1)S(1)}, u32[]{:S(2)}) copy-start(bf16[2,128,8,2,64]{1,0,4,3,2:T(2,128)(2,1)S(1)} %copy.212) | copy-start | bytes 1572868
  409.7 69.7 %copy-start.67 = (f32[256]{0:T(256)}, f32[256]{0:T(256)S(1)}, u32[]{:S(2)}) copy-start(f32[256]{0:T(256)S(1)} %get-tuple-element.139) | copy-start | bytes 3076
  409.7 470.2 %copy-start.4 = (f32[256,1024]{1,0:T(8,128)}, f32[256,1024]{1,0:T(8,128)S(1)}, u32[]{:S(2)}) copy-start(f32[256,1024]{1,0:T(8,128)S(1)} %get-tuple-element.140) | copy-start | bytes 3145732
  409.7 69.7 %copy-start.61 = (f32[256]{0:T(256)}, f32[256]{0:T(256)S(1)}, u32[]{:S(2)}) copy-start(f32[256]{0:T(256)S(1)} %fusion.122) | copy-start | bytes 3076
  471.1 31.0 %copy-start.15 = (bf16[2,128,8,2,64]{1,4,3,2,0:T(8,128)(2,1)}, bf16[2,128,8,2,64]{1,4,3,2,0:T(8,128)(2,1)S(1)}, u32[]{:S(2)}) copy-start(bf16[2,128,8,2,64]{1,4,3,2,0:T(8,128)(2,1)S(1)} %copy.216) | copy-start | bytes 1572868
  553.3 248.6 %copy-start.12 = (f32[256,1024]{1,0:T(8,128)}, f32[256,1024]{1,0:T(8,128)S(1)}, u32[]{:S(2)}) copy-start(f32[256,1024]{1,0:T(8,128)S(1)} %get-tuple-element.138) | copy-start | bytes 3145732
  554.4 93.7 %all-gather.29.cloned.1.call-start = ((), (), s32[]{:S(2)}) async-start(), calls=%async_computation.24 | async-start | bytes 4718592 | tf_op jit(solution)/shard_map/all_gather | solution.py:223
  555.0 156.3 %reduce-scatter.15.cloned.1.call-start = ((), (), s32[]{:S(2)}) async-start(), calls=%async_computation.23 | async-start | bytes 4718592 | tf_op jit(solution)/shard_map/reduce_scatter | solution.py:220
  600.7 5.8 copy-start.48
  600.7 5.8 copy-start.73
  662.4 139.4 %reduce-scatter.17.cloned.1.call-start = ((), (), s32[]{:S(2)}) async-start(), calls=%async_computation.25 | async-start | bytes 9437184 | tf_op jit(solution)/shard_map/reduce_scatter | solution.py:229
  673.5 393.9 %all-reduce.13.cloned.1.call-start = ((), (), s32[]{:S(2)}) async-start(), calls=%async_computation.34 | async-start | bytes 4325376 | tf_op jit(solution)/shard_map/psum | solution.py:236
  682.5 119.3 %copy-start.69 = (pred[256]{0:T(512)(128)(4,1)S(1)}, pred[256]{0:T(512)(128)(4,1)}, u32[]{:S(2)}) copy-start(pred[256]{0:T(512)(128)(4,1)} %get-tuple-element.149) | copy-start | bytes 772
  685.1 120.2 %copy-start.40 = (bf16[256,1024]{1,0:T(8,128)(2,1)S(1)}, bf16[256,1024]{1,0:T(8,128)(2,1)}, u32[]{:S(2)}) copy-start(bf16[256,1024]{1,0:T(8,128)(2,1)} %param.23) | copy-start | bytes 1572868
  685.1 542.0 %reduce-scatter.23.cloned.1.call-start = ((), (), s32[]{:S(2)}) async-start(), calls=%async_computation.28 | async-start | bytes 2162688 | tf_op jit(solution)/shard_map/reduce_scatter | solution.py:382
  806.9 73.0 %copy-start.10 = (f32[256,1024]{1,0:T(8,128)}, f32[256,1024]{1,0:T(8,128)S(1)}, u32[]{:S(2)}) copy-start(f32[256,1024]{1,0:T(8,128)S(1)} %fusion.68) | copy-start | bytes 3145732
  811.8 26.7 %copy-start.37 = (bf16[2,128,8,2,64]{1,4,3,2,0:T(8,128)(2,1)}, bf16[2,128,8,2,64]{1,4,3,2,0:T(8,128)(2,1)S(1)}, u32[]{:S(2)}) copy-start(bf16[2,128,8,2,64]{1,4,3,2,0:T(8,128)(2,1)S(1)} %copy.220) | copy-start | bytes 1572868
  868.2 10.6 copy-start.39
  868.2 10.6 copy-start.57
  868.2 10.6 copy-start.62
  881.9 5.7 copy-start.7
  881.9 5.6 copy-start.53
  881.9 5.6 copy-start.64
  889.6 337.6 %reduce-scatter.21.cloned.1.call-start = ((), (), s32[]{:S(2)}) async-start(), calls=%async_computation.27 | async-start | bytes 2162688 | tf_op jit(solution)/shard_map/reduce_scatter | solution.py:381
  897.5 425.3 %reduce-scatter.27.cloned.1.call-start = ((), (), s32[]{:S(2)}) async-start(), calls=%async_computation.30 | async-start | bytes 4325376 | tf_op jit(solution)/shard_map/reduce_scatter | solution.py:384
  901.6 563.2 %reduce-scatter.29.cloned.1.call-start = ((), (), s32[]{:S(2)}) async-start(), calls=%async_computation.31 | async-start | bytes 4325376 | tf_op jit(solution)/shard_map/reduce_scatter | solution.py:387
  904.4 702.7 %reduce-scatter.25.cloned.1.call-start = ((), (), s32[]{:S(2)}) async-start(), calls=%async_computation.29 | async-start | bytes 4325376 | tf_op jit(solution)/shard_map/reduce_scatter | solution.py:383
  935.2 111.7 %all-to-all-start.3 = ((bf16[2,2048,512]{2,0,1:T(2,128)(2,1)}), bf16[2,2048,512]{2,0,1:T(2,128)(2,1)}, u32[]{:S(2)}, u32[]{:S(2)}) async-start(bf16[2,2048,512]{2,0,1:T(2,128)(2,1)} %copy.242), calls=%async_computation.5 | async-start | bytes 8388608 | tf_op jit(solution)/shard_map/all_to_all | solution.py:311
  939.9 809.4 %reduce-scatter.19.cloned.1.call-start = ((), (), s32[]{:S(2)}) async-start(), calls=%async_computation.26 | async-start | bytes 4325376 | tf_op jit(solution)/shard_map/reduce_scatter | solution.py:380
  1046.9 140.1 %all-to-all-start.2 = ((bf16[2,2048,512]{2,0,1:T(2,128)(2,1)}), bf16[2,2048,512]{2,0,1:T(2,128)(2,1)}, u32[]{:S(2)}, u32[]{:S(2)}) async-start(bf16[2,2048,512]{2,0,1:T(2,128)(2,1)} %copy.237), calls=%async_computation.4 | async-start | bytes 8388608 | tf_op jit(solution)/shard_map/all_to_all | solution.py:304
  1051.6 833.9 %reduce-scatter.33.cloned.1.call-start = ((), (), s32[]{:S(2)}) async-start(), calls=%async_computation.33 | async-start | bytes 2162688
  1067.3 6.2 copy-start.51
  1067.3 954.9 %reduce-scatter.31.cloned.1.call-start = ((), (), s32[]{:S(2)}) async-start(), calls=%async_computation.32 | async-start | bytes 2162688
  1069.9 8.0 copy-start.36
  1077.8 107.9 %copy-start.72 = (s32[2]{0:T(128)S(1)}, s32[2]{0:T(128)}, u32[]{:S(2)}) copy-start(s32[2]{0:T(128)} %param.24) | copy-start | bytes 28
  1203.8 13.0 copy-start.28
  1203.8 13.0 copy-start.76
  1216.8 805.4 %copy-start.1 = (bf16[352,1024]{1,0:T(8,128)(2,1)S(1)}, bf16[352,1024]{1,0:T(8,128)(2,1)}, u32[]{:S(2)}) copy-start(bf16[352,1024]{1,0:T(8,128)(2,1)} %param.41) | copy-start | bytes 2162692
  (48 other events, 144.1 us)
Sparse Core Ops, SparseCore 0:
  11.0 56.4 all-gather.20
  70.6 65.7 all-gather.18
  139.3 69.3 all-gather.12
  211.6 78.2 all-gather.10
  292.7 55.3 all-gather.14
  350.9 55.3 all-gather.16
  409.3 55.3 all-gather.22
  467.6 55.3 all-gather.24
  554.5 46.1 all-gather.26
  602.2 45.8 all-gather.28
  662.6 48.7 reduce-scatter.14
  714.0 87.7 reduce-scatter.16
  805.2 69.5 all-reduce.12
  889.7 140.8 reduce-scatter.22
  1033.3 146.2 reduce-scatter.20
  1182.4 140.4 reduce-scatter.26
  1325.5 139.2 reduce-scatter.28
  1467.5 139.5 reduce-scatter.24
  1610.0 139.2 reduce-scatter.18
  1752.0 133.5 reduce-scatter.32
  1888.5 133.6 reduce-scatter.30
where the time goes:
time: 2040 us; the launch traced here: 2030 us
  waiting for transfers between devices  1360 us (67%)
  matrix products  238 us (12%)
  blocking collectives  224 us (11%)
  local copies, waits for them, and re-layouts  106 us (5%)
  other arithmetic  61.4 us (3%)
    unnamed x23, waiting for transfers between devices  279 us
    unnamed x2, blocking collectives  224 us
    reduce_scatter x1, waiting for transfers between devices, on_device(): lax.psum_scatter(self_output_grad, ('tok', 'ffn'), scatter_dimension=0, t...  142 us
    reduce_scatter x1, waiting for transfers between devices, on_device(): lax.psum_scatter(self_query_grad, ('tok', 'ffn'), scatter_dimension=0, ti...  142 us
    reduce_scatter x1, waiting for transfers between devices, on_device(): lax.psum_scatter(cross_output_grad, ('tok', 'ffn'), scatter_dimension=0,...  142 us
    dot_general x33, matrix products, matmul(): return jnp.dot(left, right, preferred_element_type=jnp.float32)  136 us
    reduce_scatter x1, waiting for transfers between devices, on_device(): lax.psum_scatter(cross_query_grad, ('tok', 'ffn'), scatter_dimension=0, t...  95.7 us
    reduce_scatter x1, waiting for transfers between devices, on_device(): lax.psum_scatter(matmul(gate_grad, ffn_gate.T) + matmul(up_grad, ffn_up.T...  90.5 us
  transfers between devices with their start and end apart: 25, of which 17 were waited for; matrix products, arithmetic and copies ran while one was open for 18% of the time, Pallas kernels for 0%

commit v1 on v0

v1 whole, which is shorter than its diff:
```python
import functools

import jax
import jax.numpy as jnp
from jax import lax
from jax.experimental import pallas as pl
from jax.experimental.pallas import tpu as pltpu
from jax.sharding import PartitionSpec as P

D = 1024
HEADS = 16
HEAD = 64
GROUPS = 8
BUCKETS = 32
TGT = 128
KEYS = GROUPS * HEAD
SMALL = 128

norm_epsilon = 1e-06
masked_value = -1e30
bf16 = jnp.bfloat16
f32 = jnp.float32


def matmul(left, right):
    return jnp.dot(left, right, preferred_element_type=jnp.float32)


def contract(left, right, left_dim, right_dim):
    return lax.dot_general(
        left, right, (((left_dim,), (right_dim,)), ((), ())), preferred_element_type=jnp.float32
    )


def norm_rows(hidden, gain):
    scale = lax.rsqrt(jnp.mean(hidden * hidden, axis=-1, keepdims=True) + norm_epsilon)
    return hidden * scale * gain


def norm_back(hidden, gain, cotangent):
    unused, pullback = jax.vjp(norm_rows, hidden, gain)
    return pullback(cotangent)


def gated(gate_value, up_value):
    return jax.nn.gelu(gate_value, approximate=True) * up_value


def gated_back(gate_value, up_value, cotangent):
    unused, pullback = jax.vjp(gated, gate_value, up_value)
    gate_grad, up_grad = pullback(cotangent)
    return (gate_grad.astype(jnp.bfloat16), up_grad.astype(jnp.bfloat16))


def attention_scores(queries, keys, bias, mask):
    raw = jnp.einsum("pqgre,pkge->pgrqk", queries, keys, preferred_element_type=jnp.float32)
    return jnp.where(mask, raw * HEAD ** (-0.5) + bias, masked_value)


def attention_forward(queries, keys, values, bias, mask):
    scores = attention_scores(queries, keys, bias, mask)
    highest = jnp.max(scores, axis=-1, keepdims=True)
    weights = jnp.exp(scores - highest)
    totals = jnp.sum(weights, axis=-1, keepdims=True)
    probs = (weights / totals).astype(jnp.bfloat16)
    mixed = jnp.einsum("pgrqk,pkge->pqgre", probs, values, preferred_element_type=jnp.float32)
    return (mixed.astype(jnp.bfloat16), highest + jnp.log(totals))


def attention_backward(queries, keys, values, bias, mask, log_totals, mixed_grad):
    scores = attention_scores(queries, keys, bias, mask)
    probs = jnp.exp(scores - log_totals)
    prob_grad = jnp.einsum(
        "pqgre,pkge->pgrqk", mixed_grad, values, preferred_element_type=jnp.float32
    )
    values_grad = jnp.einsum(
        "pgrqk,pqgre->pkge",
        probs.astype(jnp.bfloat16),
        mixed_grad,
        preferred_element_type=jnp.float32,
    )
    inner = jnp.sum(probs * prob_grad, axis=-1, keepdims=True)
    score_grad = (probs * (prob_grad - inner)).astype(jnp.bfloat16)
    queries_grad = jnp.einsum(
        "pgrqk,pkge->pqgre", score_grad, keys, preferred_element_type=jnp.float32
    ) * HEAD ** (-0.5)
    keys_grad = jnp.einsum(
        "pgrqk,pqgre->pkge", score_grad, queries, preferred_element_type=jnp.float32
    ) * HEAD ** (-0.5)
    return (queries_grad, keys_grad, values_grad, score_grad)


def split_terms(value):
    high = value.astype(bf16)
    rest = value - high.astype(f32)
    middle = rest.astype(bf16)
    low = (rest - middle.astype(f32)).astype(bf16)
    return [high, middle, low]


def join_terms(block):
    return (
        block[:HEADS].astype(f32)
        + block[HEADS : 2 * HEADS].astype(f32)
        + block[2 * HEADS : 3 * HEADS].astype(f32)
    )


def both_heads(ref, group):
    start = group * 2 * HEAD
    return jnp.concatenate(
        [ref[start : start + HEAD, :], ref[start + HEAD : start + 2 * HEAD, :]], axis=1
    )


def both_rows(stat, group):
    return jnp.concatenate([stat[2 * group : 2 * group + 1], stat[2 * group + 1 : 2 * group + 2]], axis=1)


def cross_forward_kernel(chunk, info_ref, query_ref, memory_ref, mix_ref, stat_ref):
    pair = pl.program_id(0)
    left = info_ref[chunk, 2 + pair] - info_ref[chunk, 1]
    mask = lax.broadcasted_iota(jnp.int32, (memory_ref.shape[1], 2 * TGT), 0) < left
    for group in range(GROUPS):
        keys = memory_ref[0, :, group * HEAD : (group + 1) * HEAD]
        values = memory_ref[0, :, KEYS + group * HEAD : KEYS + (group + 1) * HEAD]
        scores = jnp.where(mask, matmul(keys, both_heads(query_ref, group)), masked_value)
        highest = jnp.max(scores, axis=0, keepdims=True)
        weights = jnp.exp(scores - highest)
        totals = jnp.sum(weights, axis=0, keepdims=True)
        mixed = contract(weights.astype(bf16), values, 0, 0).T * (1.0 / totals)
        mixed = mixed.astype(bf16)
        start = group * 2 * HEAD
        mix_ref[start : start + HEAD, :] = mixed[:, :TGT]
        mix_ref[start + HEAD : start + 2 * HEAD, :] = mixed[:, TGT:]
        logsum = highest + jnp.log(totals)
        stat_ref[2 * group : 2 * group + 1, :] = logsum[:, :TGT]
        stat_ref[2 * group + 1 : 2 * group + 2, :] = logsum[:, TGT:]
    for place, term in enumerate(split_terms(stat_ref[...])):
        mix_ref[D + place * HEADS : D + (place + 1) * HEADS, :] = term


def cross_forward(chunk, info, queries, memory_parts):
    held, wide = memory_parts.shape[1], memory_parts.shape[2]
    rows = queries.shape[1]
    return pl.pallas_call(
        functools.partial(cross_forward_kernel, chunk),
        grid_spec=pltpu.PrefetchScalarGridSpec(
            num_scalar_prefetch=1,
            grid=(rows // TGT,),
            in_specs=[
                pl.BlockSpec((D, TGT), lambda pair, info: (0, pair)),
                pl.BlockSpec((1, held, wide), lambda pair, info: (info[chunk, 0] + pair, 0, 0)),
            ],
            out_specs=pl.BlockSpec((D + 3 * HEADS, TGT), lambda pair, info: (0, pair)),
            scratch_shapes=[pltpu.VMEM((HEADS, TGT), f32)],
        ),
        out_shape=jax.ShapeDtypeStruct((D + 3 * HEADS, rows), bf16),
        compiler_params=pltpu.CompilerParams(vmem_limit_bytes=32 * 1024 * 1024),
        cost_estimate=pl.CostEstimate(flops=4000000000, bytes_accessed=3000000, transcendentals=0),
        name="cross_forward",
    )(info, queries, memory_parts)


def cross_backward_kernel(
    chunk, info_ref, query_ref, grad_ref, memory_ref, unused_ref, query_grad_ref, memory_grad_ref
):
    pair = pl.program_id(0)
    left = info_ref[chunk, 2 + pair] - info_ref[chunk, 1]
    mask = lax.broadcasted_iota(jnp.int32, (memory_ref.shape[1], 2 * TGT), 0) < left
    logsum = join_terms(grad_ref[D : D + 3 * HEADS, :])
    inner = join_terms(grad_ref[D + 3 * HEADS : D + 6 * HEADS, :])
    for tile in range(GROUPS // 2):
        key_parts, value_parts = [], []
        for group in (2 * tile, 2 * tile + 1):
            keys = memory_ref[0, :, group * HEAD : (group + 1) * HEAD]
            values = memory_ref[0, :, KEYS + group * HEAD : KEYS + (group + 1) * HEAD]
            queries = both_heads(query_ref, group)
            mixed_grad = both_heads(grad_ref, group)
            scores = matmul(keys, queries) - both_rows(logsum, group)
            probs = jnp.exp(jnp.where(mask, scores, masked_value))
            prob_grad = matmul(values, mixed_grad) - both_rows(inner, group)
            score_grad = (probs * prob_grad).astype(bf16)
            value_parts.append(contract(probs.astype(bf16), mixed_grad, 1, 1).astype(bf16))
            key_parts.append(contract(score_grad, queries, 1, 1).astype(bf16))
            query_grad = (contract(keys, score_grad, 0, 0) * HEAD ** (-0.5)).astype(bf16)
            start = group * 2 * HEAD
            query_grad_ref[start : start + HEAD, :] = query_grad[:, :TGT]
            query_grad_ref[start + HEAD : start + 2 * HEAD, :] = query_grad[:, TGT:]
        columns = 2 * HEAD * tile
        memory_grad_ref[0, :, columns : columns + 2 * HEAD] = jnp.concatenate(key_parts, axis=1)
        memory_grad_ref[0, :, KEYS + columns : KEYS + columns + 2 * HEAD] = jnp.concatenate(
            value_parts, axis=1
        )


def cross_backward(chunk, info, queries, grads, memory_parts, memory_grads):
    held, wide = memory_parts.shape[1], memory_parts.shape[2]
    rows = queries.shape[1]
    place = pl.BlockSpec((1, held, wide), lambda pair, info: (info[chunk, 0] + pair, 0, 0))
    return pl.pallas_call(
        functools.partial(cross_backward_kernel, chunk),
        grid_spec=pltpu.PrefetchScalarGridSpec(
            num_scalar_prefetch=1,
            grid=(rows // TGT,),
            in_specs=[
                pl.BlockSpec((D, TGT), lambda pair, info: (0, pair)),
                pl.BlockSpec((D + 6 * HEADS, TGT), lambda pair, info: (0, pair)),
                place,
                pl.BlockSpec(memory_space=pl.ANY),
            ],
            out_specs=[pl.BlockSpec((D, TGT), lambda pair, info: (0, pair)), place],
        ),
        out_shape=[
            jax.ShapeDtypeStruct((D, rows), bf16),
            jax.ShapeDtypeStruct(memory_parts.shape, bf16),
        ],
        input_output_aliases={4: 1},
        compiler_params=pltpu.CompilerParams(vmem_limit_bytes=32 * 1024 * 1024),
        cost_estimate=pl.CostEstimate(flops=6000000000, bytes_accessed=5000000, transcendentals=0),
        name="cross_backward",
    )(info, queries, grads, memory_parts, memory_grads)


def exchange(value, axis, size, mask):
    return lax.ppermute(value, axis, [(place, place ^ mask) for place in range(size)])


def gather_chunks(value, size):
    chunks = [value, exchange(value, "ffn", size, 1)]
    far = [exchange(value, "ffn", size, 2 * step) for step in range(1, size // 2)]
    for one in far:
        chunks += [one, exchange(one, "ffn", size, 1)]
    return chunks


def scatter_chunks(parts, size, join):
    joined = []
    for step in range(size // 2):
        other = exchange(parts[2 * step + 1], "ffn", size, 1)
        joined.append(join([parts[2 * step], other], step == -1))
    arrived = [joined[0]] + [
        exchange(joined[step], "ffn", size, 2 * step) for step in range(1, size // 2)
    ]
    return join(arrived, True)


def join_sums(parts, last):
    total = parts[0].astype(f32)
    for part in parts[1:]:
        total = total + part.astype(f32)
    return total if last else total.astype(bf16)


def join_mixes(parts, last):
    logs = [join_terms(part[D:]) for part in parts]
    highest = functools.reduce(jnp.maximum, logs)
    weights = [jnp.exp(log - highest) for log in logs]
    totals = functools.reduce(jnp.add, weights)
    rows = parts[0].shape[1]
    mixed = functools.reduce(
        jnp.add,
        [
            part[:D].astype(f32).reshape(HEADS, HEAD, rows) * (weight / totals)[:, None, :]
            for part, weight in zip(parts, weights, strict=True)
        ],
    ).reshape(D, rows)
    logsum = highest + jnp.log(totals)
    if last:
        return mixed, logsum
    return jnp.concatenate([mixed.astype(bf16)] + split_terms(logsum), axis=0)


def reduce_blocks(grads, tok_size, ffn_size):
    columns = grads.shape[1]
    me_ffn, me_tok = lax.axis_index("ffn"), lax.axis_index("tok")

    def halves(value, dim, bit):
        first = lax.index_in_dim(value, 0, dim, keepdims=False)
        second = lax.index_in_dim(value, 1, dim, keepdims=False)
        return jnp.where(bit == 0, first, second), jnp.where(bit == 0, second, first)

    rows = grads.shape[0] // (tok_size * ffn_size)
    value = grads.reshape(tok_size, ffn_size // 2, 2, rows, columns)
    kept, sent = halves(value, 2, me_ffn & 1)
    value = kept.astype(f32) + exchange(sent.astype(bf16), "ffn", ffn_size, 1).astype(f32)

    bits = tok_size.bit_length() - 1
    value = value.reshape((2,) * bits + (ffn_size // 2, rows, columns))
    half = columns // 2 // 128 * 128
    sides = []
    for part, order in (
        (value[..., :half], list(range(bits))),
        (value[..., half:], list(range(bits))[::-1]),
    ):
        left = list(range(bits))
        for bit in order:
            dim = left.index(bit)
            left.remove(bit)
            weight = 1 << (bits - 1 - bit)
            kept, sent = halves(part, dim, (me_tok // weight) & 1)
            part = kept.astype(f32) + exchange(sent.astype(bf16), "tok", tok_size, weight).astype(f32)
        sides.append(part)
    value = jnp.concatenate(sides, axis=-1)
    line = me_ffn // 2
    total = lax.dynamic_index_in_dim(value, line, 0, keepdims=False)
    low = value.astype(bf16)
    for step in range(1, ffn_size // 2):
        part = lax.dynamic_index_in_dim(low, line ^ step, 0, keepdims=False)
        total = total + exchange(part, "ffn", ffn_size, 2 * step).astype(f32)
    return total


def on_device(
    tok_size,
    ffn_size,
    targets,
    memory,
    out_grad,
    target_lengths,
    memory_lengths,
    buckets,
    rel_table,
    gain_self,
    gain_cross,
    gain_ffn,
    self_query,
    self_key,
    self_value,
    self_output,
    cross_query,
    cross_key,
    cross_value,
    cross_output,
    ffn_gate,
    ffn_up,
    ffn_down,
):
    pair_count = target_lengths.shape[0]
    row_count = targets.shape[0]
    group_width = HEADS // GROUPS
    held = memory.shape[1]
    devices = tok_size * ffn_size
    me_tok, me_ffn = lax.axis_index("tok"), lax.axis_index("ffn")
    share = self_query.shape[0]
    table_share, gain_share = rel_table.shape[0], gain_self.shape[0]

    small = jnp.concatenate(
        [
            rel_table,
            gain_self,
            gain_cross,
            gain_ffn,
            (memory_lengths // 64).astype(bf16),
            (memory_lengths % 64).astype(bf16),
        ]
    )
    small = jnp.pad(small[None, :], ((0, share - 1), (0, SMALL - small.shape[0])))
    self_pack = jnp.concatenate([self_query, self_key, self_value, self_output, small], axis=1)
    cross_pack = jnp.concatenate([cross_query, cross_key, cross_value, cross_output], axis=1)
    full_self = lax.all_gather(self_pack, ("tok", "ffn"), axis=0, tiled=True)
    full_cross = lax.all_gather(cross_pack, ("tok", "ffn"), axis=0, tiled=True)
    full_self_query = full_self[:, :D]
    full_self_key = full_self[:, D : D + KEYS]
    full_self_value = full_self[:, D + KEYS : D + 2 * KEYS]
    full_self_output = full_self[:, D + 2 * KEYS : 2 * D + 2 * KEYS]
    full_small = full_self[:, 2 * D + 2 * KEYS :].reshape(devices, share, SMALL)[:, 0]
    full_cross_query = full_cross[:, :D]
    full_memory_weight = full_cross[:, D : D + 2 * KEYS]
    full_cross_output = full_cross[:, D + 2 * KEYS :]
    full_table = full_small[:, :table_share].reshape(-1)
    at = table_share
    full_gains = []
    for unused in range(3):
        full_gains.append(full_small[:, at : at + gain_share].reshape(-1).astype(f32))
        at += gain_share
    full_gain_self, full_gain_cross, full_gain_ffn = full_gains
    lengths = full_small[:, at : at + 2 * pair_count].astype(jnp.int32)
    lengths = lengths[:, :pair_count] * 64 + lengths[:, pair_count:]
    lengths = lax.dynamic_index_in_dim(
        lengths.reshape(tok_size, ffn_size, pair_count), me_tok, 0, keepdims=False
    )
    owner = me_ffn ^ jnp.arange(ffn_size)
    info = jnp.concatenate(
        [
            (owner * pair_count)[:, None],
            jnp.broadcast_to(me_ffn * held, (ffn_size, 1)),
            jnp.take(lengths, owner, axis=0),
        ],
        axis=1,
    ).astype(jnp.int32)

    all_cotangent = jnp.concatenate(gather_chunks(out_grad, ffn_size), axis=0)
    memory_flat = memory.reshape(-1, D)

    onehot = (buckets[:, :, None] == jnp.arange(BUCKETS)[None, None, :]).astype(jnp.bfloat16)
    position = jnp.arange(TGT)
    self_bias = jnp.einsum(
        "qkb,hb->hqk",
        onehot,
        full_table.reshape(HEADS, BUCKETS),
        preferred_element_type=jnp.float32,
    ).reshape(1, GROUPS, group_width, TGT, TGT)
    causal = position[None, :] <= position[:, None]
    self_mask = causal[None, None, None] & (
        position[None, None, None, None, :] < target_lengths[:, None, None, None, None]
    )
    inputs = targets.astype(jnp.float32)
    normed_one = norm_rows(inputs, full_gain_self).astype(jnp.bfloat16)
    self_queries = (
        matmul(normed_one, full_self_query)
        .astype(jnp.bfloat16)
        .reshape(pair_count, TGT, GROUPS, group_width, HEAD)
    )
    self_keys = (
        matmul(normed_one, full_self_key)
        .astype(jnp.bfloat16)
        .reshape(pair_count, TGT, GROUPS, HEAD)
    )
    self_values = (
        matmul(normed_one, full_self_value)
        .astype(jnp.bfloat16)
        .reshape(pair_count, TGT, GROUPS, HEAD)
    )
    self_mixed, self_totals = attention_forward(
        self_queries, self_keys, self_values, self_bias, self_mask
    )
    self_flat = self_mixed.reshape(row_count, D)
    self_branch = matmul(self_flat, full_self_output)
    hidden_one = inputs + self_branch
    normed_two = norm_rows(hidden_one, full_gain_cross).astype(jnp.bfloat16)

    cross_queries = (contract(full_cross_query, normed_two, 0, 1).astype(bf16)) * bf16(HEAD ** (-0.5))
    memory_parts = matmul(memory_flat, full_memory_weight).astype(bf16).reshape(-1, held, 2 * KEYS)
    query_chunks = gather_chunks(cross_queries, ffn_size)
    mixed_parts = [
        cross_forward(chunk, info, query_chunks[chunk], memory_parts) for chunk in range(ffn_size)
    ]
    cross_mixed, cross_totals = scatter_chunks(mixed_parts, ffn_size, join_mixes)
    cross_flat = cross_mixed.astype(bf16)
    cross_branch = contract(cross_flat, full_cross_output, 0, 0)
    hidden_two = hidden_one + cross_branch
    normed_three = norm_rows(hidden_two, full_gain_ffn).astype(jnp.bfloat16)

    all_rows = jnp.concatenate(gather_chunks(normed_three, ffn_size), axis=0)
    gate_value = matmul(all_rows, ffn_gate)
    up_value = matmul(all_rows, ffn_up)
    hidden = gated(gate_value, up_value).astype(jnp.bfloat16)
    hidden_grad = matmul(all_cotangent, ffn_down.T)
    gate_grad, up_grad = gated_back(gate_value, up_value, hidden_grad)
    rows_grad = (matmul(gate_grad, ffn_gate.T) + matmul(up_grad, ffn_up.T)).astype(bf16)
    normed_three_grad = scatter_chunks(jnp.split(rows_grad, ffn_size), ffn_size, join_sums)
    branch_part = matmul(hidden, ffn_down).astype(bf16)
    ffn_branch = scatter_chunks(jnp.split(branch_part, ffn_size), ffn_size, join_sums)
    down_part = matmul(hidden.T, all_cotangent)
    gate_part = matmul(all_rows.T, gate_grad)
    up_part = matmul(all_rows.T, up_grad)
    gate_weight_grad, up_weight_grad, down_weight_grad = (
        lax.psum(gate_part.astype(jnp.bfloat16), "tok").astype(jnp.float32),
        lax.psum(up_part.astype(jnp.bfloat16), "tok").astype(jnp.float32),
        lax.psum(down_part.astype(jnp.bfloat16), "tok").astype(jnp.float32),
    )
    hidden_three = hidden_two + ffn_branch
    layer_out = hidden_three.astype(jnp.bfloat16)
    valid = (position[None, :] < target_lengths[:, None])[:, :, None]
    counted = target_lengths.astype(jnp.float32) * D

    def root_mean(field):
        squares = field.reshape(pair_count, TGT, D)
        squares = jnp.where(valid, squares * squares, 0.0)
        return jnp.sqrt(jnp.sum(squares, axis=(1, 2)) / counted)

    rms_values = jnp.stack(
        [
            root_mean(hidden_three),
            root_mean(self_branch),
            root_mean(cross_branch),
            root_mean(ffn_branch),
        ],
        axis=1,
    )

    cotangent = out_grad.astype(jnp.float32)
    norm_three_back, gain_ffn_grad = norm_back(hidden_two, full_gain_ffn, normed_three_grad)
    hidden_two_grad = cotangent + norm_three_back
    cross_branch_low = hidden_two_grad.astype(jnp.bfloat16)
    cross_output_grad = matmul(cross_flat, cross_branch_low)
    cross_mixed_grad = contract(full_cross_output, cross_branch_low, 1, 1).astype(bf16)
    inner = jnp.sum(
        (cross_mixed_grad.astype(f32) * cross_mixed).reshape(HEADS, HEAD, row_count), axis=1
    )
    grad_pack = jnp.concatenate(
        [cross_mixed_grad] + split_terms(cross_totals) + split_terms(inner), axis=0
    )
    grad_chunks = gather_chunks(grad_pack, ffn_size)
    memory_grads = jnp.zeros(memory_parts.shape, bf16)
    query_parts = []
    for chunk in range(ffn_size):
        part, memory_grads = cross_backward(
            chunk, info, query_chunks[chunk], grad_chunks[chunk], memory_parts, memory_grads
        )
        query_parts.append(part)
    cross_queries_low = scatter_chunks(query_parts, ffn_size, join_sums).astype(bf16)
    cross_query_grad = contract(normed_two, cross_queries_low, 0, 1)
    normed_two_grad = contract(cross_queries_low, full_cross_query, 0, 1)
    memory_grads = memory_grads.reshape(-1, 2 * KEYS)
    memory_weight_grad = matmul(memory_flat.T, memory_grads)
    memory_grad = (
        contract(memory_grads, full_memory_weight, 1, 1).astype(jnp.bfloat16).reshape(memory.shape)
    )
    norm_two_back, gain_cross_grad = norm_back(hidden_one, full_gain_cross, normed_two_grad)
    hidden_one_grad = hidden_two_grad + norm_two_back
    self_branch_low = hidden_one_grad.astype(jnp.bfloat16)
    self_output_grad = matmul(self_flat.T, self_branch_low)
    self_mixed_grad = (
        matmul(self_branch_low, full_self_output.T)
        .astype(jnp.bfloat16)
        .reshape(pair_count, TGT, GROUPS, group_width, HEAD)
    )
    self_queries_grad, self_keys_grad, self_values_grad, self_score_grad = attention_backward(
        self_queries, self_keys, self_values, self_bias, self_mask, self_totals, self_mixed_grad
    )
    table_grad = jnp.einsum(
        "pgrqk,qkb->grb", self_score_grad, onehot, preferred_element_type=jnp.float32
    ).reshape(HEADS * BUCKETS)
    queries_low = self_queries_grad.astype(jnp.bfloat16).reshape(row_count, D)
    keys_low = self_keys_grad.astype(jnp.bfloat16).reshape(row_count, KEYS)
    values_low = self_values_grad.astype(jnp.bfloat16).reshape(row_count, KEYS)
    self_query_grad = matmul(normed_one.T, queries_low)
    self_key_grad = matmul(normed_one.T, keys_low)
    self_value_grad = matmul(normed_one.T, values_low)
    normed_one_grad = (
        matmul(queries_low, full_self_query.T)
        + matmul(keys_low, full_self_key.T)
        + matmul(values_low, full_self_value.T)
    )
    norm_one_back, gain_self_grad = norm_back(inputs, full_gain_self, normed_one_grad)
    targets_grad = (hidden_one_grad + norm_one_back).astype(jnp.bfloat16)

    cross_sum = reduce_blocks(
        jnp.concatenate([cross_query_grad, memory_weight_grad, cross_output_grad], axis=1),
        tok_size,
        ffn_size,
    )
    small_grads = jnp.concatenate(
        [
            table_grad.reshape(devices, table_share),
            gain_self_grad.reshape(devices, gain_share),
            gain_cross_grad.reshape(devices, gain_share),
            gain_ffn_grad.reshape(devices, gain_share),
        ],
        axis=1,
    )
    small_grads = jnp.pad(
        small_grads[:, None, :], ((0, 0), (0, share - 1), (0, SMALL - small_grads.shape[1]))
    ).reshape(devices * share, SMALL)
    self_sum = reduce_blocks(
        jnp.concatenate(
            [self_query_grad, self_key_grad, self_value_grad, self_output_grad, small_grads], axis=1
        ),
        tok_size,
        ffn_size,
    )
    small_sum = self_sum[0, 2 * D + 2 * KEYS :]
    gains_at = [table_share + place * gain_share for place in range(4)]
    return (
        layer_out,
        targets_grad,
        memory_grad,
        rms_values,
        small_sum[:table_share],
        small_sum[gains_at[0] : gains_at[1]],
        small_sum[gains_at[1] : gains_at[2]],
        small_sum[gains_at[2] : gains_at[3]],
        self_sum[:, :D],
        self_sum[:, D : D + KEYS],
        self_sum[:, D + KEYS : D + 2 * KEYS],
        self_sum[:, D + 2 * KEYS : 2 * D + 2 * KEYS],
        cross_sum[:, :D],
        cross_sum[:, D : D + KEYS],
        cross_sum[:, D + KEYS : D + 2 * KEYS],
        cross_sum[:, D + 2 * KEYS :],
        gate_weight_grad,
        up_weight_grad,
        down_weight_grad,
    )


def solution(mesh):
    rows = P(("tok", "ffn"), None)
    flat = P(("tok", "ffn"))
    memory = P("tok", "ffn", None)
    columns, inner = P(None, "ffn"), P("ffn", None)
    in_specs = (
        (rows, memory, rows, flat, flat, P()) + (flat,) * 4 + (rows,) * 8 + (columns, columns, inner)
    )
    out_specs = (
        (rows, rows, memory, rows) + (flat,) * 4 + (rows,) * 8 + (columns, columns, inner)
    )
    return jax.shard_map(
        functools.partial(on_device, mesh.shape["tok"], mesh.shape["ffn"]),
        mesh=mesh,
        in_specs=in_specs,
        out_specs=out_specs,
        check_vma=False,
    )
```

time: 2040 us -> 857 us (0.42)
  waiting for transfers between devices: 1360 us -> 367 us
  blocking collectives: 224 us -> 0 us
  matrix products: 238 us -> 117 us
  starting transfers between devices: 20.3 us -> 110 us
  Pallas kernels: 0 us -> 68.9 us
    reduce_scatter x8 -> x0, waiting for transfers between devices: 639 us -> none  [the longest x1 142 us: on_device(): lax.psum_scatter(self_output_grad, ('tok', 'ffn'), scatter_dimension=0, t...]
    unnamed x23 -> x3, waiting for transfers between devices: 279 us -> 0.05 us
    ppermute x0 -> x72, waiting for transfers between devices: none -> 257 us  [exchange(): lax.ppermute(value, axis, [(place, place ^ mask) for place in range(size)])]
    unnamed x2 -> x0, blocking collectives: 224 us -> none
    all_gather x10 -> x2, waiting for transfers between devices: 328 us -> 110 us  [the longest x1 63.9 us: on_device(): full_cross = lax.all_gather(cross_pack, ('tok', 'ffn'), axis=0, tiled=True)]
    all_to_all x4 -> x0, waiting for transfers between devices: 118 us -> none  [the longest x1 82.1 us: on_device(): lax.all_to_all(pair_values_grad.astype(jnp.bfloat16).reshape(pair_count,...]
    ppermute x0 -> x72, starting transfers between devices: none -> 110 us  [exchange(): lax.ppermute(value, axis, [(place, place ^ mask) for place in range(size)])]
    pallas_call x0 -> x16, Pallas kernels: none -> 68.9 us  [the longest x8 43.3 us: cross_backward(): pl.pallas_call(functools.partial(cross_backward_kernel, chunk), grid_spec...]
  transfers between devices with their start and end apart: 25 -> 75, of which waited for: 17 -> 28; matrix products, arithmetic and copies ran while one was open for 18% -> 23% of each run, Pallas kernels for 0% -> 8%
where the time goes in v1:
time: 857 us; the launch traced here: 849 us
  waiting for transfers between devices  367 us (43%)
  matrix products  117 us (14%)
  starting transfers between devices  110 us (13%)
  local copies, waits for them, and re-layouts  96.5 us (11%)
  other arithmetic  74.4 us (9%)
  Pallas kernels  68.9 us (8%)
  between operations  16.1 us (2%)
    ppermute x72, waiting for transfers between devices, exchange(): lax.ppermute(value, axis, [(place, place ^ mask) for place in range(size)])  257 us
    ppermute x72, starting transfers between devices, exchange(): lax.ppermute(value, axis, [(place, place ^ mask) for place in range(size)])  110 us
    dot_general x24, matrix products, matmul(): return jnp.dot(left, right, preferred_element_type=jnp.float32)  83.7 us
    all_gather x1, waiting for transfers between devices, on_device(): full_cross = lax.all_gather(cross_pack, ('tok', 'ffn'), axis=0, tiled=True)  63.9 us
    unnamed x207, local copies, waits for them, and re-layouts  47.1 us
    all_gather x1, waiting for transfers between devices, on_device(): full_self = lax.all_gather(self_pack, ('tok', 'ffn'), axis=0, tiled=True)  45.8 us
    pallas_call x8, Pallas kernels, cross_backward(): pl.pallas_call(functools.partial(cross_backward_kernel, chunk), grid_spec...  43.3 us
    dot_general x6, matrix products, contract(): lax.dot_general(left, right, (((left_dim,), (right_dim,)), ((), ())), pre...  28.3 us
  transfers between devices with their start and end apart: 75, of which 28 were waited for; matrix products, arithmetic and copies ran while one was open for 23% of the time, Pallas kernels for 8%

profile of v1, /device:TPU:0, one launch (start us, length us, event | category | flops | bytes accessed | tf_op | source)
XLA Modules:
  0.0 849.2 jit_solution(1373756415127887975)
XLA Ops:
  28.1 17.8 %collective-permute-done.29 = bf16[256,1024]{1,0:T(8,128)(2,1)S(1)} collective-permute-done((bf16[256,1024]{1,0:T(8,128)(2,1)}, bf16[256,1024]{1,0:T(8,128)(2,1)S(1)}, u32[]{:S(2)}, u32[]{:S(2)}) %collective-permute-start.29) | collective-permute-done | bytes 524320 | tf_op jit(solution)/shard_map/ppermute | solution.py:226
  46.8 63.9 %all-gather.5.cloned.1.call-done = bf16[1024,3072]{1,0:T(8,128)(2,1)} async-done(((bf16[32,3072]{1,0:T(8,128)(2,1)}), bf16[1024,3072]{1,0:T(8,128)(2,1)}) %all-gather.5.cloned.1.call-update) | async-done | bytes 6291472 | tf_op jit(solution)/shard_map/all_gather | solution.py:362
  110.7 14.9 %convert_bitcast_fusion = bf16[4096,1024]{0,1:T(8,128)(2,1)} fusion(bf16[4096,1024]{1,0:T(8,128)(2,1)} %bitcast.447, bf16[1024,3072]{1,0:T(8,128)(2,1)} %all-gather.5.cloned.1.call-done), kind=kOutput, calls=%fused_computation.3 | convolution fusion | flops 8594128896 | bytes 18874368 | tf_op jit(solution)/shard_map/dot_general | solution.py:26
  125.6 12.0 %copy.305 = bf16[4096,1024]{1,0:T(8,128)(2,1)} copy(bf16[4096,1024]{0,1:T(8,128)(2,1)} %convert_bitcast_fusion) | data formatting | bytes 16777216 | tf_op jit(solution)/shard_map/convert_element_type | solution.py:434
  137.6 45.8 %all-gather.3.cloned.1.call-done = bf16[1024,3200]{1,0:T(8,128)(2,1)} async-done(((bf16[32,3200]{1,0:T(8,128)(2,1)}), bf16[1024,3200]{1,0:T(8,128)(2,1)}) %all-gather.3.cloned.1.call-update) | async-done | bytes 6553616 | tf_op jit(solution)/shard_map/all_gather | solution.py:361
  196.3 3.3 multiply_reduce_fusion.5
  208.3 3.4 copy-done.2
  214.9 12.4 %collective-permute-done.2.query_ref = bf16[1024,256]{1,0:T(8,128)(2,1)S(1)} collective-permute-done((bf16[1024,256]{1,0:T(8,128)(2,1)S(1)}, bf16[1024,256]{1,0:T(8,128)(2,1)S(1)}, u32[]{:S(2)}, u32[]{:S(2)}) %collective-permute-start.2) | collective-permute-done | bytes 524320 | tf_op jit(solution)/shard_map/ppermute | solution.py:226
  230.5 12.0 %collective-permute-done.6.query_ref = bf16[1024,256]{1,0:T(8,128)(2,1)S(1)} collective-permute-done((bf16[1024,256]{1,0:T(8,128)(2,1)S(1)}, bf16[1024,256]{1,0:T(8,128)(2,1)S(1)}, u32[]{:S(2)}, u32[]{:S(2)}) %collective-permute-start.6) | collective-permute-done | bytes 524320 | tf_op jit(solution)/shard_map/ppermute | solution.py:226
  249.6 3.6 cross_forward.11
  261.1 7.2 collective-permute-start.5
  276.3 15.6 %collective-permute-done.5 = bf16[1072,256]{1,0:T(8,128)(2,1)S(1)} collective-permute-done((bf16[1072,256]{1,0:T(8,128)(2,1)S(1)}, bf16[1072,256]{1,0:T(8,128)(2,1)S(1)}, u32[]{:S(2)}, u32[]{:S(2)}) %collective-permute-start.5) | collective-permute-done | bytes 548896 | tf_op jit(solution)/shard_map/ppermute | solution.py:226
  291.9 16.5 %collective-permute-done.9 = bf16[1072,256]{1,0:T(8,128)(2,1)S(1)} collective-permute-done((bf16[1072,256]{1,0:T(8,128)(2,1)S(1)}, bf16[1072,256]{1,0:T(8,128)(2,1)S(1)}, u32[]{:S(2)}, u32[]{:S(2)}) %collective-permute-start.9) | collective-permute-done | bytes 548896 | tf_op jit(solution)/shard_map/ppermute | solution.py:226
  309.0 3.7 multiply_reduce_fusion.4
  312.9 11.6 %collective-permute-start.15 = (bf16[256,1024]{1,0:T(8,128)(2,1)S(1)}, bf16[256,1024]{1,0:T(8,128)(2,1)S(1)}, u32[]{:S(2)}, u32[]{:S(2)}) collective-permute-start(bf16[256,1024]{1,0:T(8,128)(2,1)S(1)} %get-tuple-element.185), channel_id=1, source_target_pairs={{0,2},{1,3},{2,0},{3,1},{4,6},{5,7},{6,4},{7,5},{8,10},{9,11},{10,... | collective-permute-start | bytes 1572872 | tf_op jit(solution)/shard_map/ppermute | solution.py:226
  333.3 12.6 %collective-permute-done.15 = bf16[256,1024]{1,0:T(8,128)(2,1)S(1)} collective-permute-done((bf16[256,1024]{1,0:T(8,128)(2,1)S(1)}, bf16[256,1024]{1,0:T(8,128)(2,1)S(1)}, u32[]{:S(2)}, u32[]{:S(2)}) %collective-permute-start.15) | collective-permute-done | bytes 524320 | tf_op jit(solution)/shard_map/ppermute | solution.py:226
  345.9 16.9 %collective-permute-done.17 = bf16[256,1024]{1,0:T(8,128)(2,1)S(1)} collective-permute-done((bf16[256,1024]{1,0:T(8,128)(2,1)S(1)}, bf16[256,1024]{1,0:T(8,128)(2,1)S(1)}, u32[]{:S(2)}, u32[]{:S(2)}) %collective-permute-start.17) | collective-permute-done | bytes 524320 | tf_op jit(solution)/shard_map/ppermute | solution.py:226
  362.8 3.9 fusion.179
  371.7 4.1 multiply_convert_fusion.1
  387.5 5.0 collective-permute-start.23
  402.1 10.8 %collective-permute-done.23 = bf16[256,1024]{1,0:T(8,128)(2,1)S(1)} collective-permute-done((bf16[256,1024]{1,0:T(8,128)(2,1)S(1)}, bf16[256,1024]{1,0:T(8,128)(2,1)S(1)}, u32[]{:S(2)}, u32[]{:S(2)}) %collective-permute-start.23) | collective-permute-done | bytes 524320 | tf_op jit(solution)/shard_map/ppermute | solution.py:226
  417.5 4.9 convolution_convert_fusion.4
  422.5 11.1 %collective-permute-done.25 = bf16[256,1024]{1,0:T(8,128)(2,1)} collective-permute-done((bf16[256,1024]{1,0:T(8,128)(2,1)}, bf16[256,1024]{1,0:T(8,128)(2,1)}, u32[]{:S(2)}, u32[]{:S(2)}) %collective-permute-start.25) | collective-permute-done | bytes 524320 | tf_op jit(solution)/shard_map/ppermute | solution.py:226
  433.6 5.1 collective-permute-done.37
  438.7 39.9 %collective-permute-done.39 = bf16[256,1024]{1,0:T(8,128)(2,1)} collective-permute-done((bf16[256,1024]{1,0:T(8,128)(2,1)}, bf16[256,1024]{1,0:T(8,128)(2,1)}, u32[]{:S(2)}, u32[]{:S(2)}) %collective-permute-start.39) | collective-permute-done | bytes 524320 | tf_op jit(solution)/shard_map/ppermute | solution.py:226
  478.6 4.9 multiply_reduce_fusion
  484.7 3.6 constant_dynamic-update-slice_fusion.27
  492.1 10.3 %collective-permute-start.44 = (bf16[1120,256]{1,0:T(8,128)(2,1)}, bf16[1120,256]{1,0:T(8,128)(2,1)S(1)}, u32[]{:S(2)}, u32[]{:S(2)}) collective-permute-start(bf16[1120,256]{1,0:T(8,128)(2,1)} %constant_dynamic-update-slice_fusion.21.grad_ref), channel_id=1, source_target_pairs={{0,2},{1,3},{2,0},{3,1},{4,6},{5,7},{6,4},{7,5},{8,10},{9,11},{10,... | collective-permute-start | bytes 1720328 | tf_op jit(solution)/shard_map/ppermute | solution.py:226
  504.8 4.5 broadcast_in_dim.111.unused_ref
  509.3 3.4 copy-done.5
  512.7 5.7 cross_backward.8
  518.4 3.4 copy-done.6
  527.7 3.4 copy-done.3
  531.1 3.4 copy-done.7
  534.5 5.5 cross_backward.9
  540.6 3.4 collective-permute-done.48.grad_ref
  544.4 4.9 cross_backward.10
  549.4 3.4 copy-done.8
  558.9 3.4 copy-done.4
  562.3 3.4 copy-done.9
  565.7 6.1 cross_backward.11
  572.0 5.0 cross_backward.12
  577.0 6.1 cross_backward.13
  583.6 5.0 cross_backward.14
  588.6 5.0 cross_backward.15
  593.8 12.2 %collective-permute-start.47 = (bf16[1024,256]{1,0:T(8,128)(2,1)S(1)}, bf16[1024,256]{1,0:T(8,128)(2,1)S(1)}, u32[]{:S(2)}, u32[]{:S(2)}) collective-permute-start(bf16[1024,256]{1,0:T(8,128)(2,1)S(1)} %add_convert_fusion.4), channel_id=1, source_target_pairs={{0,2},{1,3},{2,0},{3,1},{4,6},{5,7},{6,4},{7,5},{8,10},{9,11},{10,... | collective-permute-start | bytes 1572872 | tf_op jit(solution)/shard_map/ppermute | solution.py:226
  608.9 10.7 %convolution_bitcast_fusion = f32[1024,1024]{0,1:T(8,128)} fusion(bf16[16,256,1024]{2,1,0:T(8,128)(2,1)S(1)} %get-tuple-element.50, bf16[16,256,1024]{2,1,0:T(8,128)(2,1)S(1)} %bitcast.449), kind=kOutput, calls=%fused_computation.28 | convolution fusion | flops 8589934592 | bytes 20971520 | tf_op jit(solution)/shard_map/dot_general | solution.py:26
  619.6 8.7 %collective-permute-done.47 = bf16[1024,256]{1,0:T(8,128)(2,1)S(1)} collective-permute-done((bf16[1024,256]{1,0:T(8,128)(2,1)S(1)}, bf16[1024,256]{1,0:T(8,128)(2,1)S(1)}, u32[]{:S(2)}, u32[]{:S(2)}) %collective-permute-start.47) | collective-permute-done | bytes 524320 | tf_op jit(solution)/shard_map/ppermute | solution.py:226
  628.3 16.2 %collective-permute-done.51 = bf16[1024,256]{1,0:T(8,128)(2,1)S(1)} collective-permute-done((bf16[1024,256]{1,0:T(8,128)(2,1)S(1)}, bf16[1024,256]{1,0:T(8,128)(2,1)S(1)}, u32[]{:S(2)}, u32[]{:S(2)}) %collective-permute-start.51) | collective-permute-done | bytes 524320 | tf_op jit(solution)/shard_map/ppermute | solution.py:226
  665.8 5.6 pad_maximum_fusion
  671.4 12.9 %copy.335 = f32[1024,3072]{1,0:T(8,128)} copy(f32[1024,3072]{0,1:T(8,128)} %pad_maximum_fusion) | data formatting | bytes 25165824 | tf_op jit(solution)/shard_map/concatenate | solution.py:541
  684.3 7.0 fusion.3
  713.4 7.3 fusion.2
  721.2 12.9 %convolution_convert_fusion = bf16[4096,1024]{1,0:T(8,128)(2,1)} fusion(bf16[4096,1024]{1,0:T(8,128)(2,1)S(1)} %bitcast.407, bf16[1024,3072]{1,0:T(8,128)(2,1)} %all-gather.5.cloned.1.call-done), kind=kOutput, calls=%fused_computation.4 | convolution fusion | flops 8594128896 | bytes 18874368 | tf_op jit(solution)/shard_map/dot_general | solution.py:30
  734.1 7.8 bitcast_add_fusion
  746.3 6.0 fusion.1
  755.0 8.7 %collective-permute-done.65 = bf16[2,4,32,1536]{3,2,1,0:T(8,128)(2,1)S(1)} collective-permute-done((bf16[2,4,32,1536]{3,2,1,0:T(8,128)(2,1)}, bf16[2,4,32,1536]{3,2,1,0:T(8,128)(2,1)S(1)}, u32[]{:S(2)}, u32[]{:S(2)}) %collective-permute-start.65) | collective-permute-done | bytes 786464 | tf_op jit(solution)/shard_map/ppermute | solution.py:226
  766.4 3.9 fusion.45
  772.4 8.2 collective-permute-done.57
  785.8 3.3 collective-permute-done.68
  789.2 3.8 collective-permute-done.66
  793.3 10.7 %collective-permute-start.69 = (bf16[32,3072]{1,0:T(8,128)(2,1)S(1)}, bf16[32,3072]{1,0:T(8,128)(2,1)S(1)}, u32[]{:S(2)}, u32[]{:S(2)}) collective-permute-start(bf16[32,3072]{1,0:T(8,128)(2,1)S(1)} %get-tuple-element.238), channel_id=1, source_target_pairs={{0,2},{1,3},{2,0},{3,1},{4,6},{5,7},{6,4},{7,5},{8,10},{9,11},{10,... | collective-permute-start | bytes 589832 | tf_op jit(solution)/shard_map/ppermute | solution.py:226
  809.3 10.0 %collective-permute-done.70 = bf16[32,3072]{1,0:T(8,128)(2,1)S(1)} collective-permute-done((bf16[32,3072]{1,0:T(8,128)(2,1)S(1)}, bf16[32,3072]{1,0:T(8,128)(2,1)S(1)}, u32[]{:S(2)}, u32[]{:S(2)}) %collective-permute-start.70) | collective-permute-done | bytes 196640 | tf_op jit(solution)/shard_map/ppermute | solution.py:226
  829.5 10.1 %collective-permute-done.62 = bf16[32,3200]{1,0:T(8,128)(2,1)S(1)} collective-permute-done((bf16[32,3200]{1,0:T(8,128)(2,1)S(1)}, bf16[32,3200]{1,0:T(8,128)(2,1)S(1)}, u32[]{:S(2)}, u32[]{:S(2)}) %collective-permute-start.62) | collective-permute-done | bytes 204832 | tf_op jit(solution)/shard_map/ppermute | solution.py:226
  (499 shorter events, 215.8 us)
Async XLA Ops:
  7.2 103.5 %all-gather.5.cloned.1.call-start = ((), (), s32[]{:S(2)}) async-start(), calls=%async_computation.1 | async-start | bytes 6488064 | tf_op jit(solution)/shard_map/all_gather | solution.py:362
  8.9 174.5 %all-gather.3.cloned.1.call-start = ((), (), s32[]{:S(2)}) async-start(), calls=%async_computation | async-start | bytes 6758400 | tf_op jit(solution)/shard_map/all_gather | solution.py:361
  16.3 536.5 %all-reduce.5.cloned.1.call-start = ((), (), s32[]{:S(2)}) async-start(), calls=%async_computation.2 | async-start | bytes 4325376 | tf_op jit(solution)/shard_map/psum | solution.py:459
  16.4 29.5 %collective-permute-start.29 = (bf16[256,1024]{1,0:T(8,128)(2,1)}, bf16[256,1024]{1,0:T(8,128)(2,1)S(1)}, u32[]{:S(2)}, u32[]{:S(2)}) collective-permute-start(bf16[256,1024]{1,0:T(8,128)(2,1)} %param.23), channel_id=1, source_target_pairs={{0,2},{1,3},{2,0},{3,1},{4,6},{5,7},{6,4},{7,5},{8,10},{9,11},{10,... | collective-permute-start | bytes 1572872 | tf_op jit(solution)/shard_map/ppermute | solution.py:226
  19.5 7.8 collective-permute-start.28
  19.5 256.2 %collective-permute-start.31 = (bf16[256,1024]{1,0:T(8,128)(2,1)}, bf16[256,1024]{1,0:T(8,128)(2,1)}, u32[]{:S(2)}, u32[]{:S(2)}) collective-permute-start(bf16[256,1024]{1,0:T(8,128)(2,1)} %param.23), channel_id=1, source_target_pairs={{0,4},{1,5},{2,6},{3,7},{4,0},{5,1},{6,2},{7,3},{8,12},{9,13},{10,... | collective-permute-start | bytes 1572872 | tf_op jit(solution)/shard_map/ppermute | solution.py:226
  22.1 253.7 %collective-permute-start.33 = (bf16[256,1024]{1,0:T(8,128)(2,1)}, bf16[256,1024]{1,0:T(8,128)(2,1)}, u32[]{:S(2)}, u32[]{:S(2)}) collective-permute-start(bf16[256,1024]{1,0:T(8,128)(2,1)} %param.23), channel_id=1, source_target_pairs={{0,6},{1,7},{2,4},{3,5},{4,2},{5,3},{6,0},{7,1},{8,14},{9,15},{10,... | collective-permute-start | bytes 1572872 | tf_op jit(solution)/shard_map/ppermute | solution.py:226
  202.8 24.4 %collective-permute-start.2 = (bf16[1024,256]{1,0:T(8,128)(2,1)S(1)}, bf16[1024,256]{1,0:T(8,128)(2,1)S(1)}, u32[]{:S(2)}, u32[]{:S(2)}) collective-permute-start(bf16[1024,256]{1,0:T(8,128)(2,1)S(1)} %fusion.64.query_ref), channel_id=1, source_target_pairs={{0,2},{1,3},{2,0},{3,1},{4,6},{5,7},{6,4},{7,5},{8,10},{9,11},{10,... | collective-permute-start | bytes 1572872 | tf_op jit(solution)/shard_map/ppermute | solution.py:226
  204.3 38.2 %collective-permute-start.6 = (bf16[1024,256]{1,0:T(8,128)(2,1)S(1)}, bf16[1024,256]{1,0:T(8,128)(2,1)S(1)}, u32[]{:S(2)}, u32[]{:S(2)}) collective-permute-start(bf16[1024,256]{1,0:T(8,128)(2,1)S(1)} %fusion.64.query_ref), channel_id=1, source_target_pairs={{0,4},{1,5},{2,6},{3,7},{4,0},{5,1},{6,2},{7,3},{8,12},{9,13},{10,... | collective-permute-start | bytes 1572872 | tf_op jit(solution)/shard_map/ppermute | solution.py:226
  206.3 39.4 %collective-permute-start.10 = (bf16[1024,256]{1,0:T(8,128)(2,1)S(1)}, bf16[1024,256]{1,0:T(8,128)(2,1)S(1)}, u32[]{:S(2)}, u32[]{:S(2)}) collective-permute-start(bf16[1024,256]{1,0:T(8,128)(2,1)S(1)} %fusion.64.query_ref), channel_id=1, source_target_pairs={{0,6},{1,7},{2,4},{3,5},{4,2},{5,3},{6,0},{7,1},{8,14},{9,15},{10,... | collective-permute-start | bytes 1572872 | tf_op jit(solution)/shard_map/ppermute | solution.py:226
  227.3 43.1 %collective-permute-start.1 = (bf16[1072,256]{1,0:T(8,128)(2,1)S(1)}, bf16[1072,256]{1,0:T(8,128)(2,1)S(1)}, u32[]{:S(2)}, u32[]{:S(2)}) collective-permute-start(bf16[1072,256]{1,0:T(8,128)(2,1)S(1)} %cross_forward.9), channel_id=1, source_target_pairs={{0,1},{1,0},{2,3},{3,2},{4,5},{5,4},{6,7},{7,6},{8,9},{9,8},{10,11... | collective-permute-start | bytes 1646600 | tf_op jit(solution)/shard_map/ppermute | solution.py:226
  245.7 7.5 collective-permute-start.7
  260.2 8.4 collective-permute-start.12
  261.1 30.8 %collective-permute-start.5 = (bf16[1072,256]{1,0:T(8,128)(2,1)S(1)}, bf16[1072,256]{1,0:T(8,128)(2,1)S(1)}, u32[]{:S(2)}, u32[]{:S(2)}) collective-permute-start(bf16[1072,256]{1,0:T(8,128)(2,1)S(1)} %pad_maximum_fusion.3), channel_id=1, source_target_pairs={{0,2},{1,3},{2,0},{3,1},{4,6},{5,7},{6,4},{7,5},{8,10},{9,11},{10,... | collective-permute-start | bytes 1646600 | tf_op jit(solution)/shard_map/ppermute | solution.py:226
  268.6 39.8 %collective-permute-start.9 = (bf16[1072,256]{1,0:T(8,128)(2,1)S(1)}, bf16[1072,256]{1,0:T(8,128)(2,1)S(1)}, u32[]{:S(2)}, u32[]{:S(2)}) collective-permute-start(bf16[1072,256]{1,0:T(8,128)(2,1)S(1)} %pad_maximum_fusion.4), channel_id=1, source_target_pairs={{0,4},{1,5},{2,6},{3,7},{4,0},{5,1},{6,2},{7,3},{8,12},{9,13},{10,... | collective-permute-start | bytes 1646600 | tf_op jit(solution)/shard_map/ppermute | solution.py:226
  270.4 38.0 %collective-permute-start.13 = (bf16[1072,256]{1,0:T(8,128)(2,1)S(1)}, bf16[1072,256]{1,0:T(8,128)(2,1)S(1)}, u32[]{:S(2)}, u32[]{:S(2)}) collective-permute-start(bf16[1072,256]{1,0:T(8,128)(2,1)S(1)} %pad_maximum_fusion.5), channel_id=1, source_target_pairs={{0,6},{1,7},{2,4},{3,5},{4,2},{5,3},{6,0},{7,1},{8,14},{9,15},{10,... | collective-permute-start | bytes 1646600 | tf_op jit(solution)/shard_map/ppermute | solution.py:226
  275.7 49.2 %collective-permute-start.30 = (bf16[256,1024]{1,0:T(8,128)(2,1)S(1)}, bf16[256,1024]{1,0:T(8,128)(2,1)S(1)}, u32[]{:S(2)}, u32[]{:S(2)}) collective-permute-start(bf16[256,1024]{1,0:T(8,128)(2,1)S(1)} %copy-done.62), channel_id=1, source_target_pairs={{0,1},{1,0},{2,3},{3,2},{4,5},{5,4},{6,7},{7,6},{8,9},{9,8},{10,11... | collective-permute-start | bytes 1572872 | tf_op jit(solution)/shard_map/ppermute | solution.py:226
  275.8 51.9 %collective-permute-start.32 = (bf16[256,1024]{1,0:T(8,128)(2,1)}, bf16[256,1024]{1,0:T(8,128)(2,1)S(1)}, u32[]{:S(2)}, u32[]{:S(2)}) collective-permute-start(bf16[256,1024]{1,0:T(8,128)(2,1)} %collective-permute-done.31), channel_id=1, source_target_pairs={{0,1},{1,0},{2,3},{3,2},{4,5},{5,4},{6,7},{7,6},{8,9},{9,8},{10,11... | collective-permute-start | bytes 1572872 | tf_op jit(solution)/shard_map/ppermute | solution.py:226
  291.9 40.6 %collective-permute-start.34 = (bf16[256,1024]{1,0:T(8,128)(2,1)}, bf16[256,1024]{1,0:T(8,128)(2,1)S(1)}, u32[]{:S(2)}, u32[]{:S(2)}) collective-permute-start(bf16[256,1024]{1,0:T(8,128)(2,1)} %collective-permute-done.33), channel_id=1, source_target_pairs={{0,1},{1,0},{2,3},{3,2},{4,5},{5,4},{6,7},{7,6},{8,9},{9,8},{10,11... | collective-permute-start | bytes 1572872 | tf_op jit(solution)/shard_map/ppermute | solution.py:226
  312.9 33.0 %collective-permute-start.15 = (bf16[256,1024]{1,0:T(8,128)(2,1)S(1)}, bf16[256,1024]{1,0:T(8,128)(2,1)S(1)}, u32[]{:S(2)}, u32[]{:S(2)}) collective-permute-start(bf16[256,1024]{1,0:T(8,128)(2,1)S(1)} %get-tuple-element.185), channel_id=1, source_target_pairs={{0,2},{1,3},{2,0},{3,1},{4,6},{5,7},{6,4},{7,5},{8,10},{9,11},{10,... | collective-permute-start | bytes 1572872 | tf_op jit(solution)/shard_map/ppermute | solution.py:226
  324.6 38.2 %collective-permute-start.17 = (bf16[256,1024]{1,0:T(8,128)(2,1)S(1)}, bf16[256,1024]{1,0:T(8,128)(2,1)S(1)}, u32[]{:S(2)}, u32[]{:S(2)}) collective-permute-start(bf16[256,1024]{1,0:T(8,128)(2,1)S(1)} %get-tuple-element.185), channel_id=1, source_target_pairs={{0,4},{1,5},{2,6},{3,7},{4,0},{5,1},{6,2},{7,3},{8,12},{9,13},{10,... | collective-permute-start | bytes 1572872 | tf_op jit(solution)/shard_map/ppermute | solution.py:226
  330.4 37.7 %collective-permute-start.14 = (bf16[256,1024]{1,0:T(8,128)(2,1)S(1)}, bf16[256,1024]{1,0:T(8,128)(2,1)S(1)}, u32[]{:S(2)}, u32[]{:S(2)}) collective-permute-start(bf16[256,1024]{1,0:T(8,128)(2,1)S(1)} %get-tuple-element.185), channel_id=1, source_target_pairs={{0,1},{1,0},{2,3},{3,2},{4,5},{5,4},{6,7},{7,6},{8,9},{9,8},{10,11... | collective-permute-start | bytes 1572872 | tf_op jit(solution)/shard_map/ppermute | solution.py:226
  330.4 37.2 %collective-permute-start.19 = (bf16[256,1024]{1,0:T(8,128)(2,1)S(1)}, bf16[256,1024]{1,0:T(8,128)(2,1)S(1)}, u32[]{:S(2)}, u32[]{:S(2)}) collective-permute-start(bf16[256,1024]{1,0:T(8,128)(2,1)S(1)} %get-tuple-element.185), channel_id=1, source_target_pairs={{0,6},{1,7},{2,4},{3,5},{4,2},{5,3},{6,0},{7,1},{8,14},{9,15},{10,... | collective-permute-start | bytes 1572872 | tf_op jit(solution)/shard_map/ppermute | solution.py:226
  345.9 22.3 %collective-permute-start.16 = (bf16[256,1024]{1,0:T(8,128)(2,1)S(1)}, bf16[256,1024]{1,0:T(8,128)(2,1)S(1)}, u32[]{:S(2)}, u32[]{:S(2)}) collective-permute-start(bf16[256,1024]{1,0:T(8,128)(2,1)S(1)} %collective-permute-done.15), channel_id=1, source_target_pairs={{0,1},{1,0},{2,3},{3,2},{4,5},{5,4},{6,7},{7,6},{8,9},{9,8},{10,11... | collective-permute-start | bytes 1572872 | tf_op jit(solution)/shard_map/ppermute | solution.py:226
  384.7 10.4 %collective-permute-start.38 = (bf16[256,1024]{1,0:T(8,128)(2,1)S(1)}, bf16[256,1024]{1,0:T(8,128)(2,1)S(1)}, u32[]{:S(2)}, u32[]{:S(2)}) collective-permute-start(bf16[256,1024]{1,0:T(8,128)(2,1)S(1)} %get-tuple-element.213), channel_id=1, source_target_pairs={{0,1},{1,0},{2,3},{3,2},{4,5},{5,4},{6,7},{7,6},{8,9},{9,8},{10,11... | collective-permute-start | bytes 1572872 | tf_op jit(solution)/shard_map/ppermute | solution.py:226
  385.2 10.9 %collective-permute-start.40 = (bf16[256,1024]{1,0:T(8,128)(2,1)S(1)}, bf16[256,1024]{1,0:T(8,128)(2,1)S(1)}, u32[]{:S(2)}, u32[]{:S(2)}) collective-permute-start(bf16[256,1024]{1,0:T(8,128)(2,1)S(1)} %get-tuple-element.212), channel_id=1, source_target_pairs={{0,1},{1,0},{2,3},{3,2},{4,5},{5,4},{6,7},{7,6},{8,9},{9,8},{10,11... | collective-permute-start | bytes 1572872 | tf_op jit(solution)/shard_map/ppermute | solution.py:226
  385.3 14.5 %collective-permute-start.35 = (bf16[256,1024]{1,0:T(8,128)(2,1)S(1)}, bf16[256,1024]{1,0:T(8,128)(2,1)S(1)}, u32[]{:S(2)}, u32[]{:S(2)}) collective-permute-start(bf16[256,1024]{1,0:T(8,128)(2,1)S(1)} %get-tuple-element.211), channel_id=1, source_target_pairs={{0,1},{1,0},{2,3},{3,2},{4,5},{5,4},{6,7},{7,6},{8,9},{9,8},{10,11... | collective-permute-start | bytes 1572872 | tf_op jit(solution)/shard_map/ppermute | solution.py:226
  385.7 14.5 %collective-permute-start.21 = (bf16[256,1024]{1,0:T(8,128)(2,1)S(1)}, bf16[256,1024]{1,0:T(8,128)(2,1)S(1)}, u32[]{:S(2)}, u32[]{:S(2)}) collective-permute-start(bf16[256,1024]{1,0:T(8,128)(2,1)S(1)} %get-tuple-element.204), channel_id=1, source_target_pairs={{0,1},{1,0},{2,3},{3,2},{4,5},{5,4},{6,7},{7,6},{8,9},{9,8},{10,11... | collective-permute-start | bytes 1572872 | tf_op jit(solution)/shard_map/ppermute | solution.py:226
  387.5 25.4 %collective-permute-start.23 = (bf16[256,1024]{1,0:T(8,128)(2,1)S(1)}, bf16[256,1024]{1,0:T(8,128)(2,1)S(1)}, u32[]{:S(2)}, u32[]{:S(2)}) collective-permute-start(bf16[256,1024]{1,0:T(8,128)(2,1)S(1)} %get-tuple-element.208), channel_id=1, source_target_pairs={{0,2},{1,3},{2,0},{3,1},{4,6},{5,7},{6,4},{7,5},{8,10},{9,11},{10,... | collective-permute-start | bytes 1572872 | tf_op jit(solution)/shard_map/ppermute | solution.py:226
  395.1 38.5 %collective-permute-start.25 = (bf16[256,1024]{1,0:T(8,128)(2,1)}, bf16[256,1024]{1,0:T(8,128)(2,1)}, u32[]{:S(2)}, u32[]{:S(2)}) collective-permute-start(bf16[256,1024]{1,0:T(8,128)(2,1)} %get-tuple-element.210), channel_id=1, source_target_pairs={{0,4},{1,5},{2,6},{3,7},{4,0},{5,1},{6,2},{7,3},{8,12},{9,13},{10,... | collective-permute-start | bytes 1572872 | tf_op jit(solution)/shard_map/ppermute | solution.py:226
  396.1 37.6 %collective-permute-start.27 = (bf16[256,1024]{1,0:T(8,128)(2,1)}, bf16[256,1024]{1,0:T(8,128)(2,1)}, u32[]{:S(2)}, u32[]{:S(2)}) collective-permute-start(bf16[256,1024]{1,0:T(8,128)(2,1)} %get-tuple-element.209), channel_id=1, source_target_pairs={{0,6},{1,7},{2,4},{3,5},{4,2},{5,3},{6,0},{7,1},{8,14},{9,15},{10,... | collective-permute-start | bytes 1572872 | tf_op jit(solution)/shard_map/ppermute | solution.py:226
  399.8 38.9 %collective-permute-start.37 = (bf16[256,1024]{1,0:T(8,128)(2,1)}, bf16[256,1024]{1,0:T(8,128)(2,1)}, u32[]{:S(2)}, u32[]{:S(2)}) collective-permute-start(bf16[256,1024]{1,0:T(8,128)(2,1)} %get-tuple-element.215), channel_id=1, source_target_pairs={{0,2},{1,3},{2,0},{3,1},{4,6},{5,7},{6,4},{7,5},{8,10},{9,11},{10,... | collective-permute-start | bytes 1572872 | tf_op jit(solution)/shard_map/ppermute | solution.py:226
  400.2 78.3 %collective-permute-start.39 = (bf16[256,1024]{1,0:T(8,128)(2,1)}, bf16[256,1024]{1,0:T(8,128)(2,1)}, u32[]{:S(2)}, u32[]{:S(2)}) collective-permute-start(bf16[256,1024]{1,0:T(8,128)(2,1)} %get-tuple-element.217), channel_id=1, source_target_pairs={{0,4},{1,5},{2,6},{3,7},{4,0},{5,1},{6,2},{7,3},{8,12},{9,13},{10,... | collective-permute-start | bytes 1572872 | tf_op jit(solution)/shard_map/ppermute | solution.py:226
  412.9 65.7 %collective-permute-start.41 = (bf16[256,1024]{1,0:T(8,128)(2,1)}, bf16[256,1024]{1,0:T(8,128)(2,1)}, u32[]{:S(2)}, u32[]{:S(2)}) collective-permute-start(bf16[256,1024]{1,0:T(8,128)(2,1)} %get-tuple-element.216), channel_id=1, source_target_pairs={{0,6},{1,7},{2,4},{3,5},{4,2},{5,3},{6,0},{7,1},{8,14},{9,15},{10,... | collective-permute-start | bytes 1572872 | tf_op jit(solution)/shard_map/ppermute | solution.py:226
  492.1 35.7 %collective-permute-start.42 = (bf16[1120,256]{1,0:T(8,128)(2,1)}, bf16[1120,256]{1,0:T(8,128)(2,1)S(1)}, u32[]{:S(2)}, u32[]{:S(2)}) collective-permute-start(bf16[1120,256]{1,0:T(8,128)(2,1)} %constant_dynamic-update-slice_fusion.21.grad_ref), channel_id=1, source_target_pairs={{0,1},{1,0},{2,3},{3,2},{4,5},{5,4},{6,7},{7,6},{8,9},{9,8},{10,11... | collective-permute-start | bytes 1720328 | tf_op jit(solution)/shard_map/ppermute | solution.py:226
  492.1 35.6 %collective-permute-start.44 = (bf16[1120,256]{1,0:T(8,128)(2,1)}, bf16[1120,256]{1,0:T(8,128)(2,1)S(1)}, u32[]{:S(2)}, u32[]{:S(2)}) collective-permute-start(bf16[1120,256]{1,0:T(8,128)(2,1)} %constant_dynamic-update-slice_fusion.21.grad_ref), channel_id=1, source_target_pairs={{0,2},{1,3},{2,0},{3,1},{4,6},{5,7},{6,4},{7,5},{8,10},{9,11},{10,... | collective-permute-start | bytes 1720328 | tf_op jit(solution)/shard_map/ppermute | solution.py:226
  502.4 41.5 %collective-permute-start.48 = (bf16[1120,256]{1,0:T(8,128)(2,1)}, bf16[1120,256]{1,0:T(8,128)(2,1)S(1)}, u32[]{:S(2)}, u32[]{:S(2)}) collective-permute-start(bf16[1120,256]{1,0:T(8,128)(2,1)} %constant_dynamic-update-slice_fusion.21.grad_ref), channel_id=1, source_target_pairs={{0,4},{1,5},{2,6},{3,7},{4,0},{5,1},{6,2},{7,3},{8,12},{9,13},{10,... | collective-permute-start | bytes 1720328 | tf_op jit(solution)/shard_map/ppermute | solution.py:226
  502.8 41.2 %collective-permute-start.52 = (bf16[1120,256]{1,0:T(8,128)(2,1)}, bf16[1120,256]{1,0:T(8,128)(2,1)S(1)}, u32[]{:S(2)}, u32[]{:S(2)}) collective-permute-start(bf16[1120,256]{1,0:T(8,128)(2,1)} %constant_dynamic-update-slice_fusion.21.grad_ref), channel_id=1, source_target_pairs={{0,6},{1,7},{2,4},{3,5},{4,2},{5,3},{6,0},{7,1},{8,14},{9,15},{10,... | collective-permute-start | bytes 1720328 | tf_op jit(solution)/shard_map/ppermute | solution.py:226
  527.7 31.2 %collective-permute-start.45 = (bf16[1120,256]{1,0:T(8,128)(2,1)S(1)}, bf16[1120,256]{1,0:T(8,128)(2,1)}, u32[]{:S(2)}, u32[]{:S(2)}) collective-permute-start(bf16[1120,256]{1,0:T(8,128)(2,1)S(1)} %collective-permute-done.44.grad_ref), channel_id=1, source_target_pairs={{0,1},{1,0},{2,3},{3,2},{4,5},{5,4},{6,7},{7,6},{8,9},{9,8},{10,11... | collective-permute-start | bytes 1720328 | tf_op jit(solution)/shard_map/ppermute | solution.py:226
  540.0 79.5 %collective-permute-start.43 = (bf16[1024,256]{1,0:T(8,128)(2,1)}, bf16[1024,256]{1,0:T(8,128)(2,1)}, u32[]{:S(2)}, u32[]{:S(2)}) collective-permute-start(bf16[1024,256]{1,0:T(8,128)(2,1)} %get-tuple-element.37), channel_id=1, source_target_pairs={{0,1},{1,0},{2,3},{3,2},{4,5},{5,4},{6,7},{7,6},{8,9},{9,8},{10,11... | collective-permute-start | bytes 1572872 | tf_op jit(solution)/shard_map/ppermute | solution.py:226
  543.9 33.0 %collective-permute-start.49 = (bf16[1120,256]{1,0:T(8,128)(2,1)S(1)}, bf16[1120,256]{1,0:T(8,128)(2,1)}, u32[]{:S(2)}, u32[]{:S(2)}) collective-permute-start(bf16[1120,256]{1,0:T(8,128)(2,1)S(1)} %collective-permute-done.48.grad_ref), channel_id=1, source_target_pairs={{0,1},{1,0},{2,3},{3,2},{4,5},{5,4},{6,7},{7,6},{8,9},{9,8},{10,11... | collective-permute-start | bytes 1720328 | tf_op jit(solution)/shard_map/ppermute | solution.py:226
  543.9 44.6 %collective-permute-start.53 = (bf16[1120,256]{1,0:T(8,128)(2,1)S(1)}, bf16[1120,256]{1,0:T(8,128)(2,1)S(1)}, u32[]{:S(2)}, u32[]{:S(2)}) collective-permute-start(bf16[1120,256]{1,0:T(8,128)(2,1)S(1)} %collective-permute-done.52.grad_ref), channel_id=1, source_target_pairs={{0,1},{1,0},{2,3},{3,2},{4,5},{5,4},{6,7},{7,6},{8,9},{9,8},{10,11... | collective-permute-start | bytes 1720328 | tf_op jit(solution)/shard_map/ppermute | solution.py:226
  571.8 21.8 %collective-permute-start.46 = (bf16[1024,256]{1,0:T(8,128)(2,1)S(1)}, bf16[1024,256]{1,0:T(8,128)(2,1)S(1)}, u32[]{:S(2)}, u32[]{:S(2)}) collective-permute-start(bf16[1024,256]{1,0:T(8,128)(2,1)S(1)} %get-tuple-element.41), channel_id=1, source_target_pairs={{0,1},{1,0},{2,3},{3,2},{4,5},{5,4},{6,7},{7,6},{8,9},{9,8},{10,11... | collective-permute-start | bytes 1572872 | tf_op jit(solution)/shard_map/ppermute | solution.py:226
  583.0 23.0 %collective-permute-start.50 = (bf16[1024,256]{1,0:T(8,128)(2,1)S(1)}, bf16[1024,256]{1,0:T(8,128)(2,1)S(1)}, u32[]{:S(2)}, u32[]{:S(2)}) collective-permute-start(bf16[1024,256]{1,0:T(8,128)(2,1)S(1)} %get-tuple-element.45), channel_id=1, source_target_pairs={{0,1},{1,0},{2,3},{3,2},{4,5},{5,4},{6,7},{7,6},{8,9},{9,8},{10,11... | collective-permute-start | bytes 1572872 | tf_op jit(solution)/shard_map/ppermute | solution.py:226
  593.6 13.0 %collective-permute-start.54 = (bf16[1024,256]{1,0:T(8,128)(2,1)S(1)}, bf16[1024,256]{1,0:T(8,128)(2,1)S(1)}, u32[]{:S(2)}, u32[]{:S(2)}) collective-permute-start(bf16[1024,256]{1,0:T(8,128)(2,1)S(1)} %get-tuple-element.49), channel_id=1, source_target_pairs={{0,1},{1,0},{2,3},{3,2},{4,5},{5,4},{6,7},{7,6},{8,9},{9,8},{10,11... | collective-permute-start | bytes 1572872 | tf_op jit(solution)/shard_map/ppermute | solution.py:226
  593.8 34.4 %collective-permute-start.47 = (bf16[1024,256]{1,0:T(8,128)(2,1)S(1)}, bf16[1024,256]{1,0:T(8,128)(2,1)S(1)}, u32[]{:S(2)}, u32[]{:S(2)}) collective-permute-start(bf16[1024,256]{1,0:T(8,128)(2,1)S(1)} %add_convert_fusion.4), channel_id=1, source_target_pairs={{0,2},{1,3},{2,0},{3,1},{4,6},{5,7},{6,4},{7,5},{8,10},{9,11},{10,... | collective-permute-start | bytes 1572872 | tf_op jit(solution)/shard_map/ppermute | solution.py:226
  606.2 38.3 %collective-permute-start.51 = (bf16[1024,256]{1,0:T(8,128)(2,1)S(1)}, bf16[1024,256]{1,0:T(8,128)(2,1)S(1)}, u32[]{:S(2)}, u32[]{:S(2)}) collective-permute-start(bf16[1024,256]{1,0:T(8,128)(2,1)S(1)} %add_convert_fusion.3), channel_id=1, source_target_pairs={{0,4},{1,5},{2,6},{3,7},{4,0},{5,1},{6,2},{7,3},{8,12},{9,13},{10,... | collective-permute-start | bytes 1572872 | tf_op jit(solution)/shard_map/ppermute | solution.py:226
  606.8 37.7 %collective-permute-start.55 = (bf16[1024,256]{1,0:T(8,128)(2,1)S(1)}, bf16[1024,256]{1,0:T(8,128)(2,1)S(1)}, u32[]{:S(2)}, u32[]{:S(2)}) collective-permute-start(bf16[1024,256]{1,0:T(8,128)(2,1)S(1)} %add_convert_fusion.2), channel_id=1, source_target_pairs={{0,6},{1,7},{2,4},{3,5},{4,2},{5,3},{6,0},{7,1},{8,14},{9,15},{10,... | collective-permute-start | bytes 1572872 | tf_op jit(solution)/shard_map/ppermute | solution.py:226
  691.3 42.9 %collective-permute-start.64 = (bf16[4,4,32,3072]{3,2,1,0:T(8,128)(2,1)}, bf16[4,4,32,3072]{3,2,1,0:T(8,128)(2,1)}, u32[]{:S(2)}, u32[]{:S(2)}) collective-permute-start(bf16[4,4,32,3072]{3,2,1,0:T(8,128)(2,1)} %fusion.3), channel_id=1, source_target_pairs={{0,1},{1,0},{2,3},{3,2},{4,5},{5,4},{6,7},{7,6},{8,9},{9,8},{10,11... | collective-permute-start | bytes 9437192 | tf_op jit(solution)/shard_map/ppermute | solution.py:226
  720.7 25.6 %collective-permute-start.56 = (bf16[4,4,32,3200]{3,2,1,0:T(8,128)(2,1)}, bf16[4,4,32,3200]{3,2,1,0:T(8,128)(2,1)S(1)}, u32[]{:S(2)}, u32[]{:S(2)}) collective-permute-start(bf16[4,4,32,3200]{3,2,1,0:T(8,128)(2,1)} %fusion.2), channel_id=1, source_target_pairs={{0,1},{1,0},{2,3},{3,2},{4,5},{5,4},{6,7},{7,6},{8,9},{9,8},{10,11... | collective-permute-start | bytes 9830408 | tf_op jit(solution)/shard_map/ppermute | solution.py:226
  743.1 20.6 %collective-permute-start.65 = (bf16[2,4,32,1536]{3,2,1,0:T(8,128)(2,1)}, bf16[2,4,32,1536]{3,2,1,0:T(8,128)(2,1)S(1)}, u32[]{:S(2)}, u32[]{:S(2)}) collective-permute-start(bf16[2,4,32,1536]{3,2,1,0:T(8,128)(2,1)} %fusion.104), channel_id=1, source_target_pairs={{0,16},{8,24},{16,0},{24,8},{1,17},{9,25},{17,1},{25,9},{2,18},{10... | collective-permute-start | bytes 2359304 | tf_op jit(solution)/shard_map/ppermute | solution.py:226
  745.7 20.8 %collective-permute-start.67 = (bf16[2,4,32,1536]{3,2,1,0:T(8,128)(2,1)}, bf16[2,4,32,1536]{3,2,1,0:T(8,128)(2,1)}, u32[]{:S(2)}, u32[]{:S(2)}) collective-permute-start(bf16[2,4,32,1536]{3,2,1,0:T(8,128)(2,1)} %fusion.105), channel_id=1, source_target_pairs={{0,8},{8,0},{16,24},{24,16},{1,9},{9,1},{17,25},{25,17},{2,10},{10... | collective-permute-start | bytes 2359304 | tf_op jit(solution)/shard_map/ppermute | solution.py:226
  752.5 28.1 %collective-permute-start.57 = (bf16[2,4,32,1536]{3,2,1,0:T(8,128)(2,1)S(1)}, bf16[2,4,32,1536]{3,2,1,0:T(8,128)(2,1)S(1)}, u32[]{:S(2)}, u32[]{:S(2)}) collective-permute-start(bf16[2,4,32,1536]{3,2,1,0:T(8,128)(2,1)S(1)} %fusion.103), channel_id=1, source_target_pairs={{0,16},{8,24},{16,0},{24,8},{1,17},{9,25},{17,1},{25,9},{2,18},{10... | collective-permute-start | bytes 2359304 | tf_op jit(solution)/shard_map/ppermute | solution.py:226
  753.9 30.7 %collective-permute-start.59 = (bf16[2,4,32,1664]{3,2,1,0:T(8,128)(2,1)S(1)}, bf16[2,4,32,1664]{3,2,1,0:T(8,128)(2,1)S(1)}, u32[]{:S(2)}, u32[]{:S(2)}) collective-permute-start(bf16[2,4,32,1664]{3,2,1,0:T(8,128)(2,1)S(1)} %fusion.102), channel_id=1, source_target_pairs={{0,8},{8,0},{16,24},{24,16},{1,9},{9,1},{17,25},{25,17},{2,10},{10... | collective-permute-start | bytes 2555912 | tf_op jit(solution)/shard_map/ppermute | solution.py:226
  770.4 18.6 %collective-permute-start.68 = (bf16[4,32,1536]{2,1,0:T(8,128)(2,1)S(1)}, bf16[4,32,1536]{2,1,0:T(8,128)(2,1)S(1)}, u32[]{:S(2)}, u32[]{:S(2)}) collective-permute-start(bf16[4,32,1536]{2,1,0:T(8,128)(2,1)S(1)} %fusion.118), channel_id=1, source_target_pairs={{0,16},{8,24},{16,0},{24,8},{1,17},{9,25},{17,1},{25,9},{2,18},{10... | collective-permute-start | bytes 1179656 | tf_op jit(solution)/shard_map/ppermute | solution.py:226
  771.4 21.6 %collective-permute-start.66 = (bf16[4,32,1536]{2,1,0:T(8,128)(2,1)S(1)}, bf16[4,32,1536]{2,1,0:T(8,128)(2,1)S(1)}, u32[]{:S(2)}, u32[]{:S(2)}) collective-permute-start(bf16[4,32,1536]{2,1,0:T(8,128)(2,1)S(1)} %fusion.117), channel_id=1, source_target_pairs={{0,8},{8,0},{16,24},{24,16},{1,9},{9,1},{17,25},{25,17},{2,10},{10... | collective-permute-start | bytes 1179656 | tf_op jit(solution)/shard_map/ppermute | solution.py:226
  780.9 25.5 %collective-permute-start.58 = (bf16[4,32,1536]{2,1,0:T(8,128)(2,1)S(1)}, bf16[4,32,1536]{2,1,0:T(8,128)(2,1)S(1)}, u32[]{:S(2)}, u32[]{:S(2)}) collective-permute-start(bf16[4,32,1536]{2,1,0:T(8,128)(2,1)S(1)} %fusion.116), channel_id=1, source_target_pairs={{0,8},{8,0},{16,24},{24,16},{1,9},{9,1},{17,25},{25,17},{2,10},{10... | collective-permute-start | bytes 1179656 | tf_op jit(solution)/shard_map/ppermute | solution.py:226
  784.9 35.2 %collective-permute-start.60 = (bf16[4,32,1664]{2,1,0:T(8,128)(2,1)S(1)}, bf16[4,32,1664]{2,1,0:T(8,128)(2,1)S(1)}, u32[]{:S(2)}, u32[]{:S(2)}) collective-permute-start(bf16[4,32,1664]{2,1,0:T(8,128)(2,1)S(1)} %fusion.110), channel_id=1, source_target_pairs={{0,16},{8,24},{16,0},{24,8},{1,17},{9,25},{17,1},{25,9},{2,18},{10... | collective-permute-start | bytes 1277960 | tf_op jit(solution)/shard_map/ppermute | solution.py:226
  793.3 16.0 %collective-permute-start.69 = (bf16[32,3072]{1,0:T(8,128)(2,1)S(1)}, bf16[32,3072]{1,0:T(8,128)(2,1)S(1)}, u32[]{:S(2)}, u32[]{:S(2)}) collective-permute-start(bf16[32,3072]{1,0:T(8,128)(2,1)S(1)} %get-tuple-element.238), channel_id=1, source_target_pairs={{0,2},{1,3},{2,0},{3,1},{4,6},{5,7},{6,4},{7,5},{8,10},{9,11},{10,... | collective-permute-start | bytes 589832 | tf_op jit(solution)/shard_map/ppermute | solution.py:226
  804.0 15.3 %collective-permute-start.70 = (bf16[32,3072]{1,0:T(8,128)(2,1)S(1)}, bf16[32,3072]{1,0:T(8,128)(2,1)S(1)}, u32[]{:S(2)}, u32[]{:S(2)}) collective-permute-start(bf16[32,3072]{1,0:T(8,128)(2,1)S(1)} %get-tuple-element.240), channel_id=1, source_target_pairs={{0,4},{1,5},{2,6},{3,7},{4,0},{5,1},{6,2},{7,3},{8,12},{9,13},{10,... | collective-permute-start | bytes 589832 | tf_op jit(solution)/shard_map/ppermute | solution.py:226
  804.3 14.9 %collective-permute-start.71 = (bf16[32,3072]{1,0:T(8,128)(2,1)S(1)}, bf16[32,3072]{1,0:T(8,128)(2,1)S(1)}, u32[]{:S(2)}, u32[]{:S(2)}) collective-permute-start(bf16[32,3072]{1,0:T(8,128)(2,1)S(1)} %get-tuple-element.239), channel_id=1, source_target_pairs={{0,6},{1,7},{2,4},{3,5},{4,2},{5,3},{6,0},{7,1},{8,14},{9,15},{10,... | collective-permute-start | bytes 589832 | tf_op jit(solution)/shard_map/ppermute | solution.py:226
  820.4 9.2 %collective-permute-start.61 = (bf16[32,3200]{1,0:T(8,128)(2,1)S(1)}, bf16[32,3200]{1,0:T(8,128)(2,1)S(1)}, u32[]{:S(2)}, u32[]{:S(2)}) collective-permute-start(bf16[32,3200]{1,0:T(8,128)(2,1)S(1)} %get-tuple-element.235), channel_id=1, source_target_pairs={{0,2},{1,3},{2,0},{3,1},{4,6},{5,7},{6,4},{7,5},{8,10},{9,11},{10,... | collective-permute-start | bytes 614408 | tf_op jit(solution)/shard_map/ppermute | solution.py:226
  823.3 16.4 %collective-permute-start.62 = (bf16[32,3200]{1,0:T(8,128)(2,1)S(1)}, bf16[32,3200]{1,0:T(8,128)(2,1)S(1)}, u32[]{:S(2)}, u32[]{:S(2)}) collective-permute-start(bf16[32,3200]{1,0:T(8,128)(2,1)S(1)} %get-tuple-element.237), channel_id=1, source_target_pairs={{0,4},{1,5},{2,6},{3,7},{4,0},{5,1},{6,2},{7,3},{8,12},{9,13},{10,... | collective-permute-start | bytes 614408 | tf_op jit(solution)/shard_map/ppermute | solution.py:226
  823.7 16.0 %collective-permute-start.63 = (bf16[32,3200]{1,0:T(8,128)(2,1)S(1)}, bf16[32,3200]{1,0:T(8,128)(2,1)S(1)}, u32[]{:S(2)}, u32[]{:S(2)}) collective-permute-start(bf16[32,3200]{1,0:T(8,128)(2,1)S(1)} %get-tuple-element.236), channel_id=1, source_target_pairs={{0,6},{1,7},{2,4},{3,5},{4,2},{5,3},{6,0},{7,1},{8,14},{9,15},{10,... | collective-permute-start | bytes 614408 | tf_op jit(solution)/shard_map/ppermute | solution.py:226
  (104 other events, 1972.7 us)
Sparse Core Ops, SparseCore 0:
  11.6 99.0 all-gather.4
  114.1 69.2 all-gather.2
  422.6 69.6 all-reduce.4

commit v2 on v1

v2 whole, which is shorter than its diff:
```python
import functools

import jax
import jax.numpy as jnp
from jax import lax
from jax.experimental import pallas as pl
from jax.experimental.pallas import tpu as pltpu
from jax.sharding import PartitionSpec as P

D = 1024
HEADS = 16
HEAD = 64
GROUPS = 8
BUCKETS = 32
TGT = 128
KEYS = GROUPS * HEAD
SMALL = 128
VMEM = 56 * 1024 * 1024

norm_epsilon = 1e-06
masked_value = -1e30
bf16 = jnp.bfloat16
f32 = jnp.float32


def matmul(left, right):
    return jnp.dot(left, right, preferred_element_type=jnp.float32)


def contract(left, right, left_dim, right_dim):
    return lax.dot_general(
        left, right, (((left_dim,), (right_dim,)), ((), ())), preferred_element_type=jnp.float32
    )


def vmem_call(body, outs, operands, scalars=(), scratch=(), name=None, flops=1000000000):
    return pl.pallas_call(
        body,
        in_specs=[pl.BlockSpec(memory_space=pltpu.SMEM)] * len(scalars)
        + [pl.BlockSpec(memory_space=pltpu.VMEM)] * len(operands),
        out_specs=[pl.BlockSpec(memory_space=pltpu.VMEM)] * len(outs),
        out_shape=[jax.ShapeDtypeStruct(shape, dtype) for shape, dtype in outs],
        scratch_shapes=list(scratch),
        compiler_params=pltpu.CompilerParams(vmem_limit_bytes=VMEM),
        cost_estimate=pl.CostEstimate(flops=flops, bytes_accessed=8000000, transcendentals=0),
        name=name,
    )(*scalars, *operands)


def inverse_root(hidden):
    return lax.rsqrt(jnp.mean(hidden * hidden, axis=-1, keepdims=True) + norm_epsilon)


def norm_pull(hidden, gain, cotangent):
    scale = inverse_root(hidden)
    weighted = cotangent * gain
    inner = jnp.mean(hidden * weighted, axis=-1, keepdims=True)
    hidden_grad = scale * weighted - hidden * (scale * scale * scale * inner)
    return hidden_grad, jnp.sum(cotangent * hidden * scale, axis=0, keepdims=True)


def self_pieces(pair, group, wide_ref):
    rows = slice(pair * TGT, (pair + 1) * TGT)
    start = group * 2 * HEAD
    queries = jnp.concatenate(
        [wide_ref[rows, start : start + HEAD], wide_ref[rows, start + HEAD : start + 2 * HEAD]],
        axis=0,
    )
    start = D + group * HEAD
    return (
        queries,
        wide_ref[rows, start : start + HEAD],
        wide_ref[rows, start + KEYS : start + KEYS + HEAD],
    )


def self_scores(queries, keys, bias, length):
    raw = contract(keys, queries, 1, 1) * HEAD ** (-0.5) + bias
    key = lax.broadcasted_iota(jnp.int32, (TGT, 2 * TGT), 0)
    query = lax.broadcasted_iota(jnp.int32, (TGT, 2 * TGT), 1) % TGT
    return jnp.where((key <= query) & (key < length), raw, masked_value)


def self_bias(table_ref, bucket_ref, group):
    buckets = bucket_ref[...]
    return jnp.concatenate(
        [
            jnp.take_along_axis(
                jnp.broadcast_to(table_ref[head : head + 1, :], (TGT, TGT)), buckets, axis=1
            )
            for head in (2 * group, 2 * group + 1)
        ],
        axis=1,
    )


def self_forward_kernel(
    length_ref, row_ref, weight_ref, gain_ref, table_ref, bucket_ref, norm_ref, wide_ref, mix_ref, stat_ref
):
    inputs = row_ref[...].astype(f32)
    normed = (inputs * inverse_root(inputs) * gain_ref[0:1, :]).astype(bf16)
    norm_ref[...] = normed
    wide_ref[...] = matmul(normed, weight_ref[:, : D + 2 * KEYS]).astype(bf16)
    for group in range(GROUPS):
        bias = self_bias(table_ref, bucket_ref, group)
        for pair in range(row_ref.shape[0] // TGT):
            queries, keys, values = self_pieces(pair, group, wide_ref)
            scores = self_scores(queries, keys, bias, length_ref[pair])
            highest = jnp.max(scores, axis=0, keepdims=True)
            weights = jnp.exp(scores - highest)
            totals = jnp.sum(weights, axis=0, keepdims=True)
            probs = (weights * (1.0 / totals)).astype(bf16)
            mixed = contract(probs, values, 0, 0).astype(bf16)
            start = group * 2 * HEAD
            mix_ref[pair * TGT : (pair + 1) * TGT, start : start + 2 * HEAD] = jnp.concatenate(
                [mixed[:TGT], mixed[TGT:]], axis=1
            )
            logsum = highest + jnp.log(totals)
            at = pair * HEADS + 2 * group
            stat_ref[at : at + 1, :] = logsum[:, :TGT]
            stat_ref[at + 1 : at + 2, :] = logsum[:, TGT:]


def self_forward(lengths, rows, weights, gains, table, buckets):
    count = rows.shape[0]
    return vmem_call(
        self_forward_kernel,
        [
            ((count, D), bf16),
            ((count, D + 2 * KEYS), bf16),
            ((count, D), bf16),
            ((count // TGT * HEADS, TGT), f32),
        ],
        [rows, weights, gains, table, buckets],
        [lengths],
        name="self_forward",
    )


def self_output_kernel(row_ref, mix_ref, weight_ref, gain_ref, hidden_ref, norm_ref, query_ref, square_ref):
    branch = matmul(mix_ref[...], weight_ref[:, :D])
    square_ref[...] = jnp.sum(branch * branch, axis=1, keepdims=True)
    hidden = row_ref[...].astype(f32) + branch
    hidden_ref[...] = hidden
    normed = (hidden * inverse_root(hidden) * gain_ref[1:2, :]).astype(bf16)
    norm_ref[...] = normed
    queries = matmul(normed, weight_ref[:, D:]).astype(bf16) * bf16(HEAD ** (-0.5))
    query_ref[...] = queries.T


def self_output_part(rows, mixed, weights, gains):
    count = rows.shape[0]
    return vmem_call(
        self_output_kernel,
        [((count, D), f32), ((count, D), bf16), ((D, count), bf16), ((count, 1), f32)],
        [rows, mixed, weights, gains],
        name="self_output",
    )


def cross_join_kernel(
    hidden_ref, gain_ref, weight_ref, *refs
):
    parts, (mix_ref, stat_ref, out_ref, norm_ref, square_ref) = refs[:-5], refs[-5:]
    logs = [join_terms(part[D : D + 3 * HEADS, :]) for part in parts]
    highest = functools.reduce(jnp.maximum, logs)
    weights = [jnp.exp(log - highest) for log in logs]
    totals = functools.reduce(jnp.add, weights)
    stat_ref[...] = highest + jnp.log(totals)
    weights = [weight * (1.0 / totals) for weight in weights]
    for head in range(HEADS):
        at = slice(head * HEAD, (head + 1) * HEAD)
        mix_ref[at, :] = functools.reduce(
            jnp.add,
            [
                part[at, :].astype(f32) * weight[head : head + 1, :]
                for part, weight in zip(parts, weights, strict=True)
            ],
        )
    branch = contract(mix_ref[...].astype(bf16), weight_ref[...], 0, 0)
    square_ref[...] = jnp.sum(branch * branch, axis=1, keepdims=True)
    hidden = hidden_ref[...] + branch
    out_ref[...] = hidden
    norm_ref[...] = (hidden * inverse_root(hidden) * gain_ref[2:3, :]).astype(bf16)


def cross_join(hidden, gains, weights, parts):
    count = hidden.shape[0]
    return vmem_call(
        cross_join_kernel,
        [
            ((D, count), f32),
            ((HEADS, count), f32),
            ((count, D), f32),
            ((count, D), bf16),
            ((count, 1), f32),
        ],
        [hidden, gains, weights, *parts],
        name="cross_join",
    )


def ffn_join_kernel(cotangent_ref, hidden_ref, gain_ref, weight_ref, mix_ref, stat_ref, *refs):
    parts, (grad_ref, low_ref, pack_ref, gain_grad_ref) = refs[:-4], refs[-4:]
    norm_grad = functools.reduce(jnp.add, [part[...].astype(f32) for part in parts])
    back, gain_grad_ref[...] = norm_pull(hidden_ref[...], gain_ref[2:3, :], norm_grad)
    grad = cotangent_ref[...].astype(f32) + back
    grad_ref[...] = grad
    low = grad.astype(bf16)
    low_ref[...] = low
    mixed_grad = contract(weight_ref[...], low, 1, 1).astype(bf16)
    pack_ref[:D, :] = mixed_grad
    product = mixed_grad.astype(f32) * mix_ref[...]
    inner = jnp.concatenate(
        [
            jnp.sum(product[head * HEAD : (head + 1) * HEAD], axis=0, keepdims=True)
            for head in range(HEADS)
        ],
        axis=0,
    )
    for place, term in enumerate(split_terms(stat_ref[...]) + split_terms(inner)):
        pack_ref[D + place * HEADS : D + (place + 1) * HEADS, :] = term


def ffn_join(cotangent, hidden, gains, weights, mixed, stats, parts):
    count = hidden.shape[0]
    return vmem_call(
        ffn_join_kernel,
        [((count, D), f32), ((count, D), bf16), ((D + 6 * HEADS, count), bf16), ((1, D), f32)],
        [cotangent, hidden, gains, weights, mixed, stats, *parts],
        name="ffn_join",
    )


def query_join_kernel(grad_ref, hidden_ref, gain_ref, weight_ref, *refs):
    parts, (sum_ref, out_ref, low_ref, mix_grad_ref, gain_grad_ref) = refs[:-5], refs[-5:]
    queries = functools.reduce(jnp.add, [part[...].astype(f32) for part in parts]).astype(bf16)
    sum_ref[...] = queries
    norm_grad = contract(queries, weight_ref[:, D:], 0, 1)
    back, gain_grad_ref[...] = norm_pull(hidden_ref[...], gain_ref[1:2, :], norm_grad)
    grad = grad_ref[...] + back
    out_ref[...] = grad
    low = grad.astype(bf16)
    low_ref[...] = low
    mix_grad_ref[...] = contract(low, weight_ref[:, :D], 1, 1).astype(bf16)


def query_join(grad, hidden, gains, weights, parts):
    count = hidden.shape[0]
    return vmem_call(
        query_join_kernel,
        [
            ((D, count), bf16),
            ((count, D), f32),
            ((count, D), bf16),
            ((count, D), bf16),
            ((1, D), f32),
        ],
        [grad, hidden, gains, weights, *parts],
        name="query_join",
    )


def self_backward_kernel(
    length_ref,
    mix_grad_ref,
    wide_ref,
    stat_ref,
    table_ref,
    bucket_ref,
    wide_grad_ref,
    table_grad_ref,
    score_ref,
):
    pairs = mix_grad_ref.shape[0] // TGT
    for group in range(GROUPS):
        bias = self_bias(table_ref, bucket_ref, group)
        score_total = None
        for pair in range(pairs):
            queries, keys, values = self_pieces(pair, group, wide_ref)
            rows = slice(pair * TGT, (pair + 1) * TGT)
            start = group * 2 * HEAD
            mixed_grad = jnp.concatenate(
                [
                    mix_grad_ref[rows, start : start + HEAD],
                    mix_grad_ref[rows, start + HEAD : start + 2 * HEAD],
                ],
                axis=0,
            )
            at = pair * HEADS + 2 * group
            logsum = jnp.concatenate([stat_ref[at : at + 1, :], stat_ref[at + 1 : at + 2, :]], axis=1)
            scores = self_scores(queries, keys, bias, length_ref[pair])
            probs = jnp.exp(scores - logsum)
            prob_grad = contract(values, mixed_grad, 1, 1)
            inner = jnp.sum(probs * prob_grad, axis=0, keepdims=True)
            score_grad = (probs * (prob_grad - inner)).astype(bf16)
            value_grad = matmul(probs.astype(bf16), mixed_grad).astype(bf16)
            key_grad = (matmul(score_grad, queries) * HEAD ** (-0.5)).astype(bf16)
            query_grad = (contract(score_grad, keys, 0, 0) * HEAD ** (-0.5)).astype(bf16)
            wide_grad_ref[rows, start : start + 2 * HEAD] = jnp.concatenate(
                [query_grad[:TGT], query_grad[TGT:]], axis=1
            )
            start = D + group * HEAD
            wide_grad_ref[rows, start : start + HEAD] = key_grad
            wide_grad_ref[rows, start + KEYS : start + KEYS + HEAD] = value_grad
            wide = score_grad.astype(f32)
            score_total = wide if score_total is None else score_total + wide
        score_ref[2 * group] = score_total[:, :TGT]
        score_ref[2 * group + 1] = score_total[:, TGT:]
    buckets = bucket_ref[...]
    lane = lax.broadcasted_iota(jnp.int32, (HEADS, TGT), 1)

    def one_bucket(bucket, table_grad):
        inside = buckets == bucket
        sums = jnp.concatenate(
            [
                jnp.sum(jnp.where(inside, score_ref[head], 0.0), axis=0, keepdims=True)
                for head in range(HEADS)
            ],
            axis=0,
        )
        return jnp.where(lane == bucket, jnp.sum(sums, axis=1, keepdims=True), table_grad)

    table_grad_ref[...] = lax.fori_loop(0, BUCKETS, one_bucket, jnp.zeros((HEADS, TGT), f32))


def self_backward(lengths, mix_grad, wide, stats, table, buckets):
    return vmem_call(
        self_backward_kernel,
        [(wide.shape, bf16), ((HEADS, TGT), f32)],
        [mix_grad, wide, stats, table, buckets],
        [lengths],
        [pltpu.VMEM((HEADS, TGT, TGT), f32)],
        name="self_backward",
        flops=8000000000,
    )


def input_grads_kernel(wide_grad_ref, weight_ref, gain_ref, row_ref, grad_ref, out_ref, gain_grad_ref):
    norm_grad = contract(wide_grad_ref[...], weight_ref[:, : D + 2 * KEYS], 1, 1)
    back, gain_grad_ref[...] = norm_pull(row_ref[...].astype(f32), gain_ref[0:1, :], norm_grad)
    out_ref[...] = (grad_ref[...] + back).astype(bf16)


def input_grads(wide_grad, weights, gains, rows, grad):
    return vmem_call(
        input_grads_kernel,
        [(rows.shape, bf16), ((1, D), f32)],
        [wide_grad, weights, gains, rows, grad],
        name="input_grads",
    )


def split_terms(value):
    high = value.astype(bf16)
    rest = value - high.astype(f32)
    middle = rest.astype(bf16)
    low = (rest - middle.astype(f32)).astype(bf16)
    return [high, middle, low]


def join_terms(block):
    return (
        block[:HEADS].astype(f32)
        + block[HEADS : 2 * HEADS].astype(f32)
        + block[2 * HEADS : 3 * HEADS].astype(f32)
    )


def both_heads(ref, group):
    start = group * 2 * HEAD
    return jnp.concatenate(
        [ref[start : start + HEAD, :], ref[start + HEAD : start + 2 * HEAD, :]], axis=1
    )


def both_rows(stat, group):
    return jnp.concatenate([stat[2 * group : 2 * group + 1], stat[2 * group + 1 : 2 * group + 2]], axis=1)


def valid_positions(info_ref, chunk, pair, positions):
    held = positions // 2
    length = info_ref[chunk, 3 + pair]
    place = lax.broadcasted_iota(jnp.int32, (positions, 2 * TGT), 0)
    limit = jnp.where(
        place < held, length - info_ref[chunk, 1], held + length - info_ref[chunk, 2]
    )
    return place < limit


def cross_forward_kernel(chunk, info_ref, query_ref, memory_ref, mix_ref, stat_ref):
    pair = pl.program_id(0)
    mask = valid_positions(info_ref, chunk, pair, memory_ref.shape[1])
    for group in range(GROUPS):
        keys = memory_ref[0, :, group * HEAD : (group + 1) * HEAD]
        values = memory_ref[0, :, KEYS + group * HEAD : KEYS + (group + 1) * HEAD]
        scores = jnp.where(mask, matmul(keys, both_heads(query_ref, group)), masked_value)
        highest = jnp.max(scores, axis=0, keepdims=True)
        weights = jnp.exp(scores - highest)
        totals = jnp.sum(weights, axis=0, keepdims=True)
        mixed = contract(weights.astype(bf16), values, 0, 0).T * (1.0 / totals)
        mixed = mixed.astype(bf16)
        start = group * 2 * HEAD
        mix_ref[start : start + HEAD, :] = mixed[:, :TGT]
        mix_ref[start + HEAD : start + 2 * HEAD, :] = mixed[:, TGT:]
        logsum = highest + jnp.log(totals)
        stat_ref[2 * group : 2 * group + 1, :] = logsum[:, :TGT]
        stat_ref[2 * group + 1 : 2 * group + 2, :] = logsum[:, TGT:]
    for place, term in enumerate(split_terms(stat_ref[...])):
        mix_ref[D + place * HEADS : D + (place + 1) * HEADS, :] = term


def cross_forward(chunk, info, queries, memory_parts):
    positions, wide = memory_parts.shape[1], memory_parts.shape[2]
    rows = queries.shape[1]
    return pl.pallas_call(
        functools.partial(cross_forward_kernel, chunk),
        grid_spec=pltpu.PrefetchScalarGridSpec(
            num_scalar_prefetch=1,
            grid=(rows // TGT,),
            in_specs=[
                pl.BlockSpec((D, TGT), lambda pair, info: (0, pair)),
                pl.BlockSpec((1, positions, wide), lambda pair, info: (info[chunk, 0] + pair, 0, 0)),
            ],
            out_specs=pl.BlockSpec((D + 3 * HEADS, TGT), lambda pair, info: (0, pair)),
            scratch_shapes=[pltpu.VMEM((HEADS, TGT), f32)],
        ),
        out_shape=jax.ShapeDtypeStruct((D + 3 * HEADS, rows), bf16),
        compiler_params=pltpu.CompilerParams(vmem_limit_bytes=VMEM),
        cost_estimate=pl.CostEstimate(flops=6000000000, bytes_accessed=4000000, transcendentals=0),
        name="cross_forward",
    )(info, queries, memory_parts)


def cross_backward_kernel(chunk, info_ref, query_ref, grad_ref, memory_ref, *rest):
    query_grad_ref, memory_grad_ref = rest[-2:]
    pair = pl.program_id(0)
    mask = valid_positions(info_ref, chunk, pair, memory_ref.shape[1])
    logsum = join_terms(grad_ref[D : D + 3 * HEADS, :])
    inner = join_terms(grad_ref[D + 3 * HEADS : D + 6 * HEADS, :])
    for tile in range(GROUPS // 2):
        key_parts, value_parts = [], []
        for group in (2 * tile, 2 * tile + 1):
            keys = memory_ref[0, :, group * HEAD : (group + 1) * HEAD]
            values = memory_ref[0, :, KEYS + group * HEAD : KEYS + (group + 1) * HEAD]
            queries = both_heads(query_ref, group)
            mixed_grad = both_heads(grad_ref, group)
            scores = matmul(keys, queries) - both_rows(logsum, group)
            probs = jnp.exp(jnp.where(mask, scores, masked_value))
            prob_grad = matmul(values, mixed_grad) - both_rows(inner, group)
            score_grad = (probs * prob_grad).astype(bf16)
            value_parts.append(contract(probs.astype(bf16), mixed_grad, 1, 1).astype(bf16))
            key_parts.append(contract(score_grad, queries, 1, 1).astype(bf16))
            query_grad = (contract(keys, score_grad, 0, 0) * HEAD ** (-0.5)).astype(bf16)
            start = group * 2 * HEAD
            query_grad_ref[start : start + HEAD, :] = query_grad[:, :TGT]
            query_grad_ref[start + HEAD : start + 2 * HEAD, :] = query_grad[:, TGT:]
        columns = 2 * HEAD * tile
        memory_grad_ref[0, :, columns : columns + 2 * HEAD] = jnp.concatenate(key_parts, axis=1)
        memory_grad_ref[0, :, KEYS + columns : KEYS + columns + 2 * HEAD] = jnp.concatenate(
            value_parts, axis=1
        )


def cross_backward(chunk, info, queries, grads, memory_parts, *earlier):
    positions, wide = memory_parts.shape[1], memory_parts.shape[2]
    rows = queries.shape[1]
    place = pl.BlockSpec((1, positions, wide), lambda pair, info: (info[chunk, 0] + pair, 0, 0))
    return pl.pallas_call(
        functools.partial(cross_backward_kernel, chunk),
        grid_spec=pltpu.PrefetchScalarGridSpec(
            num_scalar_prefetch=1,
            grid=(rows // TGT,),
            in_specs=[
                pl.BlockSpec((D, TGT), lambda pair, info: (0, pair)),
                pl.BlockSpec((D + 6 * HEADS, TGT), lambda pair, info: (0, pair)),
                place,
            ]
            + [pl.BlockSpec(memory_space=pl.ANY)] * len(earlier),
            out_specs=[pl.BlockSpec((D, TGT), lambda pair, info: (0, pair)), place],
        ),
        out_shape=[
            jax.ShapeDtypeStruct((D, rows), bf16),
            jax.ShapeDtypeStruct(memory_parts.shape, bf16),
        ],
        input_output_aliases={4: 1} if earlier else {},
        compiler_params=pltpu.CompilerParams(vmem_limit_bytes=VMEM),
        cost_estimate=pl.CostEstimate(flops=10000000000, bytes_accessed=8000000, transcendentals=0),
        name="cross_backward",
    )(info, queries, grads, memory_parts, *earlier)


def ffn_kernel(row_ref, cotangent_ref, gate_ref, up_ref, down_ref, *rest):
    row_grad_ref, branch_ref, rows_ref, hidden_ref, gate_grad_ref, up_grad_ref = rest[-6:]
    rows = row_ref[...]
    rows_ref[0] = rows
    gate = matmul(rows, gate_ref[...])
    up = matmul(rows, up_ref[...])
    hidden_grad = contract(cotangent_ref[...], down_ref[...], 1, 1)
    square = gate * gate
    slope = 0.7978845608028654
    bend = jnp.tanh(slope * gate * (1.0 + 0.044715 * square))
    half = 0.5 * (1.0 + bend)
    value = gate * half
    derivative = half + 0.5 * gate * (1.0 - bend * bend) * slope * (1.0 + 3 * 0.044715 * square)
    hidden = (value * up).astype(bf16)
    gate_grad = (hidden_grad * up * derivative).astype(bf16)
    up_grad = (hidden_grad * value).astype(bf16)
    row_grad = contract(gate_grad, gate_ref[...], 1, 1) + contract(up_grad, up_ref[...], 1, 1)
    row_grad_ref[...] = row_grad.astype(bf16)
    branch_ref[...] = matmul(hidden, down_ref[...]).astype(bf16)
    hidden_ref[0] = hidden
    gate_grad_ref[0] = gate_grad
    up_grad_ref[0] = up_grad


def ffn_chunk(chunk, chunks, rows, cotangent, gate, up, down, *earlier):
    count, width = rows.shape
    wide = gate.shape[1]
    kept = [width, wide, wide, wide]
    return pl.pallas_call(
        ffn_kernel,
        grid=(1,),
        in_specs=[
            pl.BlockSpec((count, width), lambda step: (0, 0)),
            pl.BlockSpec((count, width), lambda step: (0, 0)),
            pl.BlockSpec(gate.shape, lambda step: (0, 0)),
            pl.BlockSpec(up.shape, lambda step: (0, 0)),
            pl.BlockSpec(down.shape, lambda step: (0, 0)),
        ]
        + [pl.BlockSpec(memory_space=pl.ANY)] * len(earlier),
        out_specs=[pl.BlockSpec((count, width), lambda step: (0, 0))] * 2
        + [pl.BlockSpec((1, count, size), lambda step: (chunk, 0, 0)) for size in kept],
        out_shape=[jax.ShapeDtypeStruct((count, width), bf16)] * 2
        + [jax.ShapeDtypeStruct((chunks, count, size), bf16) for size in kept],
        input_output_aliases={5 + place: 2 + place for place in range(len(earlier))},
        compiler_params=pltpu.CompilerParams(vmem_limit_bytes=VMEM),
        cost_estimate=pl.CostEstimate(flops=3000000000, bytes_accessed=8000000, transcendentals=0),
        name="ffn_chunk",
    )(rows, cotangent, gate, up, down, *earlier)


def exchange(value, axis, size, mask):
    return lax.ppermute(value, axis, [(place, place ^ mask) for place in range(size)])


def gather_chunks(value, size):
    lines = size // 2
    if lines != 4:
        return [value] + [exchange(value, "ffn", size, 2 * step) for step in range(1, lines)]

    def by_lines(array, pairs):
        pairs = [(2 * old + core, 2 * new + core) for old, new in pairs for core in range(2)]
        return lax.ppermute(array, "ffn", pairs)

    across = exchange(value, "ffn", size, 4)
    beside = exchange(value, "ffn", size, 2)
    middle = by_lines(value, [(1, 2), (2, 1)])
    onward = by_lines(across, [(2, 3), (1, 0)])
    line = lax.axis_index("ffn") // 2
    return [value, beside, across, jnp.where((line == 0) | (line == 3), onward, middle)]


def return_chunks(parts, size):
    return [parts[0]] + [
        exchange(parts[step], "ffn", size, 2 * step) for step in range(1, size // 2)
    ]


def join_sums(parts):
    return functools.reduce(jnp.add, [part.astype(f32) for part in parts])


def reduce_rows(grads, tok_size, ffn_size):
    columns = grads.shape[1]
    me_ffn, me_tok = lax.axis_index("ffn"), lax.axis_index("tok")

    def halves(value, dim, bit):
        first = lax.index_in_dim(value, 0, dim, keepdims=False)
        second = lax.index_in_dim(value, 1, dim, keepdims=False)
        return jnp.where(bit == 0, first, second), jnp.where(bit == 0, second, first)

    rows = grads.shape[0] // (tok_size * ffn_size)
    value = grads.reshape(tok_size, ffn_size // 2, 2, rows, columns)
    kept, sent = halves(value, 2, me_ffn & 1)
    value = kept.astype(f32) + exchange(sent.astype(bf16), "ffn", ffn_size, 1).astype(f32)

    bits = tok_size.bit_length() - 1
    value = value.reshape((2,) * bits + (ffn_size // 2, rows, columns))
    half = columns // 2 // 128 * 128
    sides = []
    for part, order in (
        (value[..., :half], list(range(bits))),
        (value[..., half:], list(range(bits))[::-1]),
    ):
        left = list(range(bits))
        for bit in order:
            dim = left.index(bit)
            left.remove(bit)
            weight = 1 << (bits - 1 - bit)
            kept, sent = halves(part, dim, (me_tok // weight) & 1)
            part = kept.astype(f32) + exchange(sent.astype(bf16), "tok", tok_size, weight).astype(f32)
        sides.append(part)
    value = jnp.concatenate(sides, axis=-1)
    line = me_ffn // 2
    total = lax.dynamic_index_in_dim(value, line, 0, keepdims=False)
    low = value.astype(bf16)
    for step in range(1, ffn_size // 2):
        part = lax.dynamic_index_in_dim(low, line ^ step, 0, keepdims=False)
        total = total + exchange(part, "ffn", ffn_size, 2 * step).astype(f32)
    return total


def memory_forward_kernel(own_ref, other_ref, weight_ref, out_ref):
    pairs, held, width = own_ref.shape
    for place, ref in enumerate((own_ref, other_ref)):
        part = matmul(ref[...].reshape(pairs * held, width), weight_ref[...]).astype(bf16)
        out_ref[:, place] = part.reshape(pairs, held, part.shape[1])


def memory_forward(own, other, weights, column):
    pairs, held, width = own.shape
    step = 4 if pairs % 4 == 0 else 1
    block = pl.BlockSpec((step, held, width), lambda pair: (pair, 0, 0))
    return pl.pallas_call(
        memory_forward_kernel,
        grid=(pairs // step,),
        in_specs=[
            block,
            block,
            pl.BlockSpec((width, 2 * KEYS), lambda pair: (0, column // (2 * KEYS))),
        ],
        out_specs=pl.BlockSpec((step, 2, held, 2 * KEYS), lambda pair: (pair, 0, 0, 0)),
        out_shape=jax.ShapeDtypeStruct((pairs, 2, held, 2 * KEYS), bf16),
        compiler_params=pltpu.CompilerParams(vmem_limit_bytes=VMEM),
        cost_estimate=pl.CostEstimate(flops=8600000000, bytes_accessed=18000000, transcendentals=0),
        name="memory_forward",
    )(own, other, weights)


def memory_backward_kernel(sizes, me_ref, own_ref, other_ref, grad_ref, weight_ref, *rest):
    own_grad_ref, other_grad_ref, sum_ref, total = rest
    step = pl.program_id(0)
    pairs, held, width = own_ref.shape
    for place, (ref, out_ref) in enumerate(((own_ref, own_grad_ref), (other_ref, other_grad_ref))):
        grads = grad_ref[:, place].reshape(pairs * held, grad_ref.shape[3])
        out = contract(grads, weight_ref[...], 1, 1).astype(bf16)
        out_ref[...] = out.reshape(out_ref.shape)
        part = contract(ref[...].reshape(pairs * held, width), grads, 0, 0)
        if place == 0:
            total[...] = jnp.where(step == 0, part, total[...] + part)
        else:
            total[...] += part

    @pl.when(step == pl.num_programs(0) - 1)
    def last():
        store_blocks(sizes, me_ref, sum_ref, 0, total[...])


def memory_backward(sizes, me, own, other, grads, weights, column):
    lines = sizes[1] // 2
    pairs, held, width = own.shape
    step = pairs // lines
    block = pl.BlockSpec((step, held, width), lambda line, me: (line, 0, 0))
    shape = blocks_shape(sizes, 2 * KEYS)
    return pl.pallas_call(
        functools.partial(memory_backward_kernel, sizes),
        grid_spec=pltpu.PrefetchScalarGridSpec(
            num_scalar_prefetch=1,
            grid=(lines,),
            in_specs=[
                block,
                block,
                pl.BlockSpec((step, 2, held, 2 * KEYS), lambda line, me: (line, 0, 0, 0)),
                pl.BlockSpec((width, 2 * KEYS), lambda line, me: (0, column // (2 * KEYS))),
            ],
            out_specs=[
                pl.BlockSpec((1, 1, step, held, width), lambda line, me: (line, me[2], 0, 0, 0)),
                block,
                pl.BlockSpec(shape, lambda line, me: (0,) * len(shape)),
            ],
            scratch_shapes=[pltpu.VMEM((width, 2 * KEYS), f32)],
        ),
        out_shape=[
            jax.ShapeDtypeStruct((lines, 2, step, held, width), bf16),
            jax.ShapeDtypeStruct(own.shape, bf16),
            jax.ShapeDtypeStruct(shape, bf16),
        ],
        compiler_params=pltpu.CompilerParams(vmem_limit_bytes=VMEM),
        cost_estimate=pl.CostEstimate(flops=17200000000, bytes_accessed=28000000, transcendentals=0),
        name="memory_backward",
    )(me, own, other, grads, weights)


def place_pairs_kernel(me_ref, pair_ref, unused_ref, out_ref):
    out_ref[0, 0] = pair_ref[...]


def place_pairs(me, whole, pairs):
    lines, unused, step, held, width = whole.shape
    return pl.pallas_call(
        place_pairs_kernel,
        grid_spec=pltpu.PrefetchScalarGridSpec(
            num_scalar_prefetch=1,
            grid=(lines,),
            in_specs=[
                pl.BlockSpec((step, held, width), lambda line, me: (line, 0, 0)),
                pl.BlockSpec(memory_space=pl.ANY),
            ],
            out_specs=pl.BlockSpec(
                (1, 1, step, held, width), lambda line, me: (line, 1 - me[2], 0, 0, 0)
            ),
        ),
        out_shape=jax.ShapeDtypeStruct(whole.shape, bf16),
        input_output_aliases={2: 0},
        compiler_params=pltpu.CompilerParams(vmem_limit_bytes=VMEM),
        name="place_pairs",
    )(me, pairs, whole)


def blocks_shape(sizes, columns):
    tok_size, ffn_size = sizes
    return (2, tok_size * ffn_size // 2, D // (tok_size * ffn_size), columns)


def store_blocks(sizes, me_ref, out_ref, column, value):
    tok_size, ffn_size = sizes
    rows = D // (tok_size * ffn_size)
    low = value.astype(bf16)
    for block in range(tok_size * ffn_size):
        tok, line, core = block // ffn_size, block % ffn_size // 2, block % 2
        place = (tok ^ me_ref[0]) * (ffn_size // 2) + (line ^ me_ref[1])
        out_ref[core ^ me_ref[2], place, :, column : column + value.shape[1]] = low[
            block * rows : (block + 1) * rows
        ]


def grad_blocks_kernel(sizes, dims, me_ref, *refs):
    out_ref = refs[-1]
    column = 0
    for place, (left_dim, right_dim) in enumerate(dims):
        left, right = refs[2 * place], refs[2 * place + 1]
        for start in range(0, right.shape[1 - right_dim], 512):
            if right_dim == 0:
                part = right[:, start : start + 512]
            else:
                part = right[start : start + 512, :]
            store_blocks(
                sizes, me_ref, out_ref, column, contract(left[...], part, left_dim, right_dim)
            )
            column += 512
    for ref in refs[2 * len(dims) : -1]:
        if len(ref.shape) == 4:
            out_ref[:, :, :, column : column + ref.shape[3]] = ref[...]
            column += ref.shape[3]
        else:
            filled = jnp.concatenate(
                [ref[...], jnp.zeros((SMALL - ref.shape[0], ref.shape[1]), f32)], axis=0
            )
            store_blocks(sizes, me_ref, out_ref, column, filled.T)
            column += SMALL


def grad_blocks(sizes, me, products, *extra):
    operands = [array for left, right, unused, also in products for array in (left, right)]
    columns = sum(right.shape[1 - dim] for unused, right, also, dim in products)
    for array in extra:
        operands.append(array)
        columns += array.shape[3] if array.ndim == 4 else SMALL
    return pl.pallas_call(
        functools.partial(grad_blocks_kernel, sizes, [(one[2], one[3]) for one in products]),
        in_specs=[pl.BlockSpec(memory_space=pltpu.SMEM)]
        + [pl.BlockSpec(memory_space=pltpu.VMEM)] * len(operands),
        out_specs=pl.BlockSpec(memory_space=pltpu.VMEM),
        out_shape=jax.ShapeDtypeStruct(blocks_shape(sizes, columns), bf16),
        compiler_params=pltpu.CompilerParams(vmem_limit_bytes=VMEM),
        name="grad_blocks",
    )(me, *operands)


def plus(*parts):
    return functools.reduce(jnp.add, [part.astype(f32) for part in parts]).astype(bf16)


def reduce_core(sizes, blocks):
    lines = sizes[1] // 2
    other = exchange(blocks[1], "ffn", sizes[1], 1)
    return [
        plus(blocks[0, tok * lines : (tok + 1) * lines], other[tok * lines : (tok + 1) * lines])
        for tok in range(4)
    ]


def reduce_corner(sizes, parts):
    own, by_x, by_y, across = parts
    half = sizes[1] // 4
    top = exchange(across[:half], "tok", sizes[0], 1)
    bottom = exchange(across[half:], "tok", sizes[0], 2)
    by_x = jnp.concatenate([by_x[:half], plus(by_x[half:], bottom)], axis=0)
    by_y = jnp.concatenate([plus(by_y[:half], top), by_y[half:]], axis=0)
    return [own, by_x, by_y]


def reduce_sides(sizes, parts):
    own, by_x, by_y = parts
    return plus(own, exchange(by_x, "tok", sizes[0], 1), exchange(by_y, "tok", sizes[0], 2))


def reduce_line(sizes, total):
    parts = [total[0]] + [
        exchange(total[step], "ffn", sizes[1], 2 * step) for step in range(1, sizes[1] // 2)
    ]
    return functools.reduce(jnp.add, [part.astype(f32) for part in parts])


def place_rows_kernel(sizes, share, me_ref, *refs):
    tok_size, ffn_size = sizes
    lines = ffn_size // 2
    half = lines // 2
    out_ref, sems = refs[-2:]
    copies = []
    for core in range(2):
        line_ref, x_ref, y_ref, top_ref, bottom_ref = refs[5 * core : 5 * core + 5]
        for tok in range(4):
            for line in range(lines):
                if tok < 3:
                    source = (line_ref, x_ref, y_ref)[tok].at[line]
                else:
                    source = top_ref.at[line] if line < half else bottom_ref.at[line - half]
                block = ((tok ^ me_ref[0]) * lines + (line ^ me_ref[1])) * 2 + (core ^ me_ref[2])
                target = out_ref.at[pl.ds(pl.multiple_of(block * share, share), share), :]
                copies.append(pltpu.make_async_copy(source, target, sems.at[len(copies)]))
    for copy in copies:
        copy.start()
    for copy in copies:
        copy.wait()


def place_rows(sizes, me, held, share, columns):
    count = sizes[0] * sizes[1]
    return pl.pallas_call(
        functools.partial(place_rows_kernel, sizes, share),
        in_specs=[pl.BlockSpec(memory_space=pltpu.SMEM)]
        + [pl.BlockSpec(memory_space=pl.ANY)] * len(held),
        out_specs=pl.BlockSpec(memory_space=pltpu.VMEM),
        out_shape=jax.ShapeDtypeStruct((count * share, columns), bf16),
        scratch_shapes=[pltpu.SemaphoreType.DMA((count,))],
        compiler_params=pltpu.CompilerParams(vmem_limit_bytes=VMEM),
        name="place_rows",
    )(me, *held)


def after(values, earlier):
    return lax.optimization_barrier((values, earlier))[0]


def gather_blocks(sizes, me, packs, between):
    tok_size, ffn_size = sizes
    lines = ffn_size // 2
    half = lines // 2
    stages = [(), (), (), ()]
    for place, pack in enumerate(packs):
        share, columns = pack.shape
        pack = after(pack, stages[0])
        line = [pack] + [exchange(pack, "ffn", ffn_size, 2 * step) for step in range(1, lines)]
        stages[0] = line
        line = jnp.stack(after(line, stages[1]))
        by_x = exchange(line, "tok", tok_size, 1)
        by_y = exchange(line, "tok", tok_size, 2)
        stages[1] = [by_x, by_y]
        by_x, by_y = after([by_x, by_y], stages[2])
        top = exchange(by_y[:half], "tok", tok_size, 1)
        bottom = exchange(by_x[half:], "tok", tok_size, 2)
        stages[2] = [top, bottom]
        held = after([line, by_x, by_y, top, bottom], stages[3])
        held = held + [exchange(one, "ffn", ffn_size, 1) for one in held]
        stages[3] = between(place, place_rows(sizes, me, held, share, columns), stages[0])


def on_device(
    tok_size,
    ffn_size,
    targets,
    memory,
    out_grad,
    target_lengths,
    memory_lengths,
    buckets,
    rel_table,
    gain_self,
    gain_cross,
    gain_ffn,
    self_query,
    self_key,
    self_value,
    self_output,
    cross_query,
    cross_key,
    cross_value,
    cross_output,
    ffn_gate,
    ffn_up,
    ffn_down,
):
    pair_count = target_lengths.shape[0]
    row_count = targets.shape[0]
    held = memory.shape[1]
    devices = tok_size * ffn_size
    me_tok, me_ffn = lax.axis_index("tok"), lax.axis_index("ffn")
    share = self_query.shape[0]
    table_share = rel_table.shape[0]

    sizes = (tok_size, ffn_size)
    direct = tok_size == 4 and share % 16 == 0
    me = jnp.stack([me_tok, me_ffn // 2, me_ffn % 2]).astype(jnp.int32)
    per_row = [
        jnp.pad(part.astype(bf16), (0, share - part.shape[0]))
        for part in (gain_self, gain_cross, gain_ffn, rel_table, memory_lengths // 64, memory_lengths % 64)
    ]
    small = jnp.pad(jnp.stack(per_row, axis=1), ((0, 0), (0, SMALL - len(per_row))))

    core = me_ffn % 2
    lines = ffn_size // 2

    def by_parity(array, parity):
        array = array.reshape((lines, 2, pair_count) + array.shape[1:])
        array = lax.dynamic_index_in_dim(array, parity, 1, keepdims=False)
        return array.reshape((lines * pair_count,) + array.shape[2:])

    memory_own = by_parity(memory, core)
    memory_other = exchange(by_parity(memory, 1 - core), "ffn", ffn_size, 1)
    both_gate = jnp.concatenate([ffn_gate, exchange(ffn_gate, "ffn", ffn_size, 1)], axis=1)
    both_up = jnp.concatenate([ffn_up, exchange(ffn_up, "ffn", ffn_size, 1)], axis=1)
    both_down = jnp.concatenate([ffn_down, exchange(ffn_down, "ffn", ffn_size, 1)], axis=0)

    packs = [
        jnp.concatenate(parts, axis=1)
        for parts in (
            [self_query, self_key, self_value, small],
            [self_output, cross_query],
            [cross_key, cross_value, cross_output],
        )
    ]
    buckets = buckets.T
    kept = {}

    def begin(place, pack, begun):
        if place == 0:
            full_small = pack[:, D + 2 * KEYS : D + 2 * KEYS + len(per_row)].T.astype(f32)
            table = full_small[3].reshape(devices, share)[:, :table_share].reshape(HEADS, BUCKETS)
            kept["table"] = jnp.pad(table, ((0, 0), (0, TGT - BUCKETS)))
            lengths = (full_small[4] * 64 + full_small[5]).astype(jnp.int32)
            kept["lengths"] = lengths.reshape(devices, share)[:, :pair_count]
            kept["gains"] = full_small[:3]
            kept["self"] = self_forward(
                target_lengths,
                after(targets, (both_gate, both_up, both_down, memory_other, memory_own)),
                pack,
                kept["gains"],
                kept["table"],
                buckets,
            )
            result = kept["self"][2]
        elif place == 1:
            kept["output"] = self_output_part(targets, kept["self"][2], pack, kept["gains"])
            result = kept["output"][2]
        else:
            kept["cotangents"] = gather_chunks(after(out_grad, begun), ffn_size)
            kept["memory"] = memory_forward(memory_own, memory_other, pack, 0)
            result = kept["memory"]
        kept[place] = pack
        return result

    if direct:
        gather_blocks(sizes, me, packs, begin)
    else:
        for place, pack in enumerate(packs):
            begin(place, lax.all_gather(pack, ("tok", "ffn"), axis=0, tiled=True), pack)
    full_first, full_second, full_third = kept[0], kept[1], kept[2]
    gains, table, lengths = kept["gains"], kept["table"], kept["lengths"]
    cotangent_chunks = kept["cotangents"]
    normed_one, self_wide, self_mixed, self_stats = kept["self"]
    hidden_one, normed_two, cross_queries, self_squares = kept["output"]
    memory_parts = kept["memory"].reshape(-1, 2 * held, 2 * KEYS)
    cross_weight = full_third[:, 2 * KEYS :]
    lengths = lax.dynamic_index_in_dim(
        lengths.reshape(tok_size, ffn_size, pair_count), me_tok, 0, keepdims=False
    )
    owner = me_ffn ^ (2 * jnp.arange(lines))
    info = jnp.concatenate(
        [
            (owner // 2 * pair_count)[:, None],
            jnp.broadcast_to(me_ffn * held, (lines, 1)),
            jnp.broadcast_to((me_ffn ^ 1) * held, (lines, 1)),
            jnp.take(lengths, owner, axis=0),
        ],
        axis=1,
    ).astype(jnp.int32)


    position = jnp.arange(TGT)

    cross_queries = after(cross_queries, cotangent_chunks)
    query_chunks = gather_chunks(cross_queries, ffn_size)
    mixed_parts = []
    for chunk in range(lines):
        chunk_queries = query_chunks[chunk]
        if chunk:
            chunk_queries = after(chunk_queries, mixed_parts[-1])
        mixed_parts.append(cross_forward(chunk, info, chunk_queries, memory_parts))
    cross_mixed, cross_stats, hidden_two, normed_three, cross_squares = cross_join(
        hidden_one, gains, cross_weight, return_chunks(mixed_parts, ffn_size)
    )

    row_chunks = gather_chunks(normed_three, ffn_size)
    earlier, row_parts, branch_parts = [], [], []
    for chunk in range(lines):
        row_part, branch_part, *earlier = ffn_chunk(
            chunk,
            lines,
            row_chunks[chunk],
            cotangent_chunks[chunk],
            both_gate,
            both_up,
            both_down,
            *earlier,
        )
        row_parts.append(row_part)
        branch_parts.append(branch_part)
    row_parts = return_chunks(row_parts, ffn_size)
    all_rows, hidden, gate_grad, up_grad = [
        array.reshape(lines * row_count, array.shape[2]) for array in earlier
    ]
    all_cotangent = jnp.concatenate(cotangent_chunks, axis=0)
    units = ffn_gate.shape[1]
    weight_grads = []
    for part, dim in (
        (contract(all_rows, gate_grad, 0, 0), 1),
        (contract(all_rows, up_grad, 0, 0), 1),
        (contract(hidden, all_cotangent, 0, 0), 0),
    ):
        kept = lax.slice_in_dim(part, 0, units, axis=dim)
        sent = lax.slice_in_dim(part, units, 2 * units, axis=dim).astype(bf16)
        weight_grads.append((kept + exchange(sent, "ffn", ffn_size, 1).astype(f32)).astype(bf16))
    weight_sums = [lax.psum(part, "tok") for part in weight_grads]
    gate_weight_grad, up_weight_grad, down_weight_grad = [part.astype(f32) for part in weight_sums]

    row_parts = row_parts[:2] + after(row_parts[2:], weight_grads)
    hidden_two_grad, cross_low, grad_pack, gain_ffn_grad = ffn_join(
        out_grad, hidden_two, gains, cross_weight, cross_mixed, cross_stats, row_parts
    )
    output_product = (cross_mixed.astype(bf16), cross_low, 1, 0)
    stage = [grad_blocks(sizes, me, [output_product])] if direct else [()]
    grad_chunks = gather_chunks(grad_pack, ffn_size)
    earlier = []
    query_parts = []
    reductions = [reduce_core, reduce_corner, reduce_sides, reduce_line]
    for chunk in range(lines):
        part, memory_grads = cross_backward(
            chunk,
            info,
            after(query_chunks[chunk], stage[-1]),
            grad_chunks[chunk],
            memory_parts,
            *earlier,
        )
        earlier = [memory_grads]
        query_parts.append(part)
        if direct and chunk < 4:
            stage.append(reductions[chunk](sizes, stage[-1]))
    for reduction in reductions[lines:] if direct else ():
        stage.append(reduction(sizes, stage[-1]))
    output_sum = stage[-1]
    query_parts = return_chunks(query_parts, ffn_size)
    memory_grad, other_grad, memory_sum = memory_backward(
        sizes,
        me,
        memory_own,
        memory_other,
        after(memory_grads, query_parts[1]).reshape(-1, 2, held, 2 * KEYS),
        full_third,
        0,
    )
    query_parts = query_parts[:2] + after(query_parts[2:], (memory_sum, output_sum, weight_sums))
    query_grads, hidden_one_grad, self_low, mix_grad, gain_cross_grad = query_join(
        hidden_two_grad, hidden_one, gains, full_second, query_parts
    )
    other_grad = exchange(other_grad, "ffn", ffn_size, 1)
    memory_grad = place_pairs(me, memory_grad, other_grad).reshape(memory.shape)
    products = [(normed_two, query_grads, 0, 1), (self_mixed, self_low, 0, 0)]
    middle = ()
    if direct:
        middle = grad_blocks(sizes, me, products, memory_sum)
        mix_grad = after(mix_grad, (middle, other_grad))
        middle = reduce_core(sizes, middle)
    wide_grad, table_grad = self_backward(
        target_lengths, mix_grad, self_wide, self_stats, table, buckets
    )
    wide_grad = after(wide_grad, middle)
    targets_grad, gain_self_grad = input_grads(wide_grad, full_first, gains, targets, hidden_one_grad)

    branch_parts = after(branch_parts, query_grads)
    ffn_branch = join_sums(return_chunks(branch_parts, ffn_size))
    hidden_three = hidden_two + ffn_branch
    layer_out = hidden_three.astype(jnp.bfloat16)
    valid = position[None, :] < target_lengths[:, None]
    counted = target_lengths.astype(jnp.float32) * D
    squares = [
        jnp.sum(hidden_three * hidden_three, axis=1),
        self_squares[:, 0],
        cross_squares[:, 0],
        jnp.sum(ffn_branch * ffn_branch, axis=1),
    ]
    squares = jnp.stack([part.reshape(pair_count, TGT) for part in squares], axis=1)
    squares = jnp.sum(jnp.where(valid[:, None, :], squares, 0.0), axis=2)
    rms_values = jnp.sqrt(squares / counted[:, None])

    table_grad = jnp.pad(
        table_grad[:, :BUCKETS].reshape(devices, table_share), ((0, 0), (0, share - table_share))
    )
    small_rows = jnp.concatenate(
        [gain_self_grad, gain_cross_grad, gain_ffn_grad, table_grad.reshape(1, D), jnp.zeros((4, D), f32)]
    )
    last_product = (normed_one, wide_grad, 0, 0)
    if direct:
        middle = reduce_corner(sizes, middle)
        first = grad_blocks(sizes, me, [last_product], after(small_rows, middle))
        first = reduce_core(sizes, first)
        middle = reduce_sides(sizes, middle)
        first = reduce_corner(sizes, first)
        first = reduce_sides(sizes, first)
        middle_sum = reduce_line(sizes, middle)
        first_sum = reduce_line(sizes, first)
    else:
        order = [(block // ffn_size, block % ffn_size // 2, block % 2) for block in range(devices)]
        memory_rows = jnp.concatenate(
            [
                memory_sum[core ^ me[2], (tok ^ me[0]) * (ffn_size // 2) + (line ^ me[1])]
                for tok, line, core in order
            ]
        )
        output_sum, middle_sum, first_sum = [
            reduce_rows(jnp.concatenate(parts, axis=1), tok_size, ffn_size)
            for parts in (
                [contract(*output_product)],
                [contract(*one) for one in products] + [memory_rows],
                [contract(*last_product), jnp.pad(small_rows.T, ((0, 0), (0, SMALL - 8)))],
            )
        ]
    small_sum = first_sum[:, D + 2 * KEYS :]
    return (
        layer_out,
        targets_grad,
        memory_grad,
        rms_values,
        small_sum[:table_share, 3],
        small_sum[:, 0],
        small_sum[:, 1],
        small_sum[:, 2],
        first_sum[:, :D],
        first_sum[:, D : D + KEYS],
        first_sum[:, D + KEYS : D + 2 * KEYS],
        middle_sum[:, D : 2 * D],
        middle_sum[:, :D],
        middle_sum[:, 2 * D : 2 * D + KEYS],
        middle_sum[:, 2 * D + KEYS :],
        output_sum,
        gate_weight_grad,
        up_weight_grad,
        down_weight_grad,
    )


def solution(mesh):
    rows = P(("tok", "ffn"), None)
    flat = P(("tok", "ffn"))
    memory = P("tok", "ffn", None)
    columns, inner = P(None, "ffn"), P("ffn", None)
    in_specs = (
        (rows, memory, rows, flat, flat, P()) + (flat,) * 4 + (rows,) * 8 + (columns, columns, inner)
    )
    out_specs = (
        (rows, rows, memory, rows) + (flat,) * 4 + (rows,) * 8 + (columns, columns, inner)
    )
    return jax.shard_map(
        functools.partial(on_device, mesh.shape["tok"], mesh.shape["ffn"]),
        mesh=mesh,
        in_specs=in_specs,
        out_specs=out_specs,
        check_vma=False,
    )
```

time: 857 us -> 701 us (0.82)
  Pallas kernels: 68.9 us -> 211 us
  waiting for transfers between devices: 367 us -> 234 us
  matrix products: 117 us -> 7.42 us
  local copies, waits for them, and re-layouts: 96.5 us -> 48.9 us
  other arithmetic: 74.4 us -> 34.1 us
  starting transfers between devices: 110 us -> 143 us
    pallas_call x0 -> x20, Pallas kernels: none -> 146 us  [the longest x7 44.5 us: vmem_call(): pl.pallas_call(body, in_specs=[pl.BlockSpec(memory_space=pltpu.SMEM)] * l...]
    all_gather x2 -> x0, waiting for transfers between devices: 110 us -> none  [the longest x1 63.9 us: on_device(): full_cross = lax.all_gather(cross_pack, ('tok', 'ffn'), axis=0, tiled=True)]
    dot_general x32 -> x0, matrix products: 88.4 us -> none  [the longest x24 83.7 us: matmul(): return jnp.dot(left, right, preferred_element_type=jnp.float32)]
    ppermute x72 -> x88, waiting for transfers between devices: 257 us -> 205 us  [exchange(): lax.ppermute(value, axis, [(place, place ^ mask) for place in range(size)])]
    unnamed x207 -> x177, local copies, waits for them, and re-layouts: 47.1 us -> 14 us
    ppermute x0 -> x8, waiting for transfers between devices: none -> 29.1 us  [by_lines(): return lax.ppermute(array, 'ffn', pairs)]
    ppermute x72 -> x88, starting transfers between devices: 110 us -> 133 us  [exchange(): lax.ppermute(value, axis, [(place, place ^ mask) for place in range(size)])]
    dot_general x6 -> x3, matrix products: 28.3 us -> 7.42 us  [contract(): lax.dot_general(left, right, (((left_dim,), (right_dim,)), ((), ())), pre...]
  transfers between devices with their start and end apart: 75 -> 97, of which waited for: 28 -> 35; matrix products, arithmetic and copies ran while one was open for 23% -> 7% of each run, Pallas kernels for 8% -> 24%
where the time goes in v2:
time: 701 us; the launch traced here: 695 us
  waiting for transfers between devices  234 us (33%)
  Pallas kernels  211 us (30%)
  starting transfers between devices  143 us (20%)
  local copies, waits for them, and re-layouts  48.9 us (7%)
  other arithmetic  34.1 us (5%)
  between operations  15.9 us (2%)
  matrix products  7.42 us (1%)
    ppermute x88, waiting for transfers between devices, exchange(): lax.ppermute(value, axis, [(place, place ^ mask) for place in range(size)])  205 us
    ppermute x88, starting transfers between devices, exchange(): lax.ppermute(value, axis, [(place, place ^ mask) for place in range(size)])  133 us
    pallas_call x7, Pallas kernels, vmem_call(): pl.pallas_call(body, in_specs=[pl.BlockSpec(memory_space=pltpu.SMEM)] * l...  44.5 us
    pallas_call x4, Pallas kernels, cross_backward(): pl.pallas_call(functools.partial(cross_backward_kernel, chunk), grid_spec...  34.8 us
    pallas_call x4, Pallas kernels, cross_forward(): pl.pallas_call(functools.partial(cross_forward_kernel, chunk), grid_spec=...  29.9 us
    ppermute x8, waiting for transfers between devices, by_lines(): return lax.ppermute(array, 'ffn', pairs)  29.1 us
    pallas_call x4, Pallas kernels, ffn_chunk(): pl.pallas_call(ffn_kernel, grid=(1,), in_specs=[pl.BlockSpec((count, widt...  26.9 us
    pallas_call x1, Pallas kernels, memory_backward(): pl.pallas_call(functools.partial(memory_backward_kernel, sizes), grid_spe...  24.6 us
  transfers between devices with their start and end apart: 97, of which 35 were waited for; matrix products, arithmetic and copies ran while one was open for 7% of the time, Pallas kernels for 24%

profile of v2, /device:TPU:0, one launch (start us, length us, event | category | flops | bytes accessed | tf_op | source)
XLA Modules:
  0.0 694.6 jit_solution(3719482466319480346)
XLA Ops:
  7.4 8.4 %constant_dynamic-slice_fusion.1 = (bf16[4,1,2,256,1024]{4,3,2,1,0:T(8,128)(2,1)}, bf16[4,1,2,256,1024]{4,3,2,1,0:T(8,128)(2,1)}) fusion(bf16[4,2,2,256,1024]{4,3,2,1,0:T(8,128)(2,1)} %bitcast.162, s32[]{:T(128)S(6)} %select_n.104, s32[]{:T(128)S(6)} %select_n.103), kind=kLoop, calls=%fused_computation.153 | loop fusion | bytes 16777224 | tf_op jit(solution)/shard_map/jit(dynamic_index_in_dim)/dynamic_slice | solution.py:927
  21.7 4.2 collective-permute-done.4
  26.0 6.6 collective-permute-done.5
  39.8 8.1 %collective-permute-done.17 = bf16[32,2048]{1,0:T(8,128)(2,1)S(1)} collective-permute-done((bf16[32,2048]{1,0:T(8,128)(2,1)S(1)}, bf16[32,2048]{1,0:T(8,128)(2,1)S(1)}, u32[]{:S(2)}, u32[]{:S(2)}) %collective-permute-start.17) | collective-permute-done | bytes 131104 | tf_op jit(solution)/shard_map/ppermute | solution.py:544
  50.8 3.4 collective-permute-done.28
  58.4 7.5 %collective-permute-done.8.refs_2_ = bf16[4,32,2176]{2,1,0:T(8,128)(2,1)S(1)} collective-permute-done((bf16[4,32,2176]{2,1,0:T(8,128)(2,1)S(1)}, bf16[4,32,2176]{2,1,0:T(8,128)(2,1)S(1)}, u32[]{:S(2)}, u32[]{:S(2)}) %collective-permute-start.8) | collective-permute-done | bytes 557088 | tf_op jit(solution)/shard_map/ppermute | solution.py:544
  68.4 4.5 collective-permute-done.30
  76.0 7.9 %collective-permute-start.41 = (bf16[256,1024]{1,0:T(8,128)(2,1)}, bf16[256,1024]{1,0:T(8,128)(2,1)}, u32[]{:S(2)}, u32[]{:S(2)}) collective-permute-start(bf16[256,1024]{1,0:T(8,128)(2,1)} %cotangent_ref.2), channel_id=1, source_target_pairs={{0,4},{1,5},{2,6},{3,7},{4,0},{5,1},{6,2},{7,3},{8,12},{9,13},{10,... | collective-permute-start | bytes 1572872 | tf_op jit(solution)/shard_map/ppermute | solution.py:544
  93.1 3.9 collective-permute-done.41.cotangent_ref
  113.3 5.4 place_rows.3.weight_ref
  123.3 6.2 self_forward.1
  129.5 9.4 %collective-permute-done.22.refs_4_ = bf16[2,32,2048]{2,1,0:T(8,128)(2,1)S(1)} collective-permute-done((bf16[2,32,2048]{2,1,0:T(8,128)(2,1)}, bf16[2,32,2048]{2,1,0:T(8,128)(2,1)S(1)}, u32[]{:S(2)}, u32[]{:S(2)}) %collective-permute-start.22) | collective-permute-done | bytes 262176 | tf_op jit(solution)/shard_map/ppermute | solution.py:544
  143.3 3.8 collective-permute-start.40
  149.3 5.3 place_rows.4.weight_ref
  154.6 4.9 self_output.1
  166.0 3.6 collective-permute-start.44
  170.4 5.2 place_rows.5.weight_ref
  175.6 13.9 %memory_forward.1 = bf16[8,2,256,1024]{3,2,1,0:T(8,128)(2,1)} custom-call(bf16[8,256,1024]{2,1,0:T(8,128)(2,1)} %bitcast.164, bf16[8,256,1024]{2,1,0:T(8,128)(2,1)} %collective-permute-done.3.other_ref, bf16[1024,2048]{1,0:T(8,128)(2,1)} %place_rows.5.weight_ref), custom_call_target="tpu_custom_call" | custom-call | flops 8600000512 | bytes 18000000 | tf_op jit(solution)/shard_map/memory_forward/pallas_call | solution.py:625
  189.5 7.4 %cross_forward.4.refs_0_ = bf16[1072,256]{1,0:T(8,128)(2,1)} custom-call(s32[4,5]{1,0:T(4,128)} %pad_add_fusion.info_ref, bf16[1024,256]{1,0:T(8,128)(2,1)} %get-tuple-element.213.query_ref, bf16[8,512,1024]{2,1,0:T(8,128)(2,1)} %bitcast.189), custom_call_target="tpu_custom_call" | custom-call | flops 6000000000 | bytes 4000000 | tf_op jit(solution)/shard_map/cross_forward/pallas_call | solution.py:416
  197.7 7.3 %cross_forward.5 = bf16[1072,256]{1,0:T(8,128)(2,1)} custom-call(s32[4,5]{1,0:T(4,128)} %pad_add_fusion.info_ref, bf16[1024,256]{1,0:T(8,128)(2,1)} %copy-done.76, bf16[8,512,1024]{2,1,0:T(8,128)(2,1)} %bitcast.190), custom_call_target="tpu_custom_call" | custom-call | flops 6000000000 | bytes 4000000 | tf_op jit(solution)/shard_map/cross_forward/pallas_call | solution.py:416
  206.6 7.3 %cross_forward.6 = bf16[1072,256]{1,0:T(8,128)(2,1)} custom-call(s32[4,5]{1,0:T(4,128)} %pad_add_fusion.info_ref, bf16[1024,256]{1,0:T(8,128)(2,1)} %copy-done.75, bf16[8,512,1024]{2,1,0:T(8,128)(2,1)} %bitcast.191), custom_call_target="tpu_custom_call" | custom-call | flops 6000000000 | bytes 4000000 | tf_op jit(solution)/shard_map/cross_forward/pallas_call | solution.py:416
  214.0 3.8 collective-permute-start.47
  217.8 24.1 %collective-permute-done.48 = bf16[1024,256]{1,0:T(8,128)(2,1)S(1)} collective-permute-done((bf16[1024,256]{1,0:T(8,128)(2,1)S(1)}, bf16[1024,256]{1,0:T(8,128)(2,1)S(1)}, u32[]{:S(2)}, u32[]{:S(2)}) %collective-permute-start.48) | collective-permute-done | bytes 524320 | tf_op jit(solution)/shard_map/ppermute | solution.py:554
  242.8 7.9 %cross_forward.7 = bf16[1072,256]{1,0:T(8,128)(2,1)} custom-call(s32[4,5]{1,0:T(4,128)} %pad_add_fusion.info_ref, bf16[1024,256]{1,0:T(8,128)(2,1)} %broadcast_select_fusion.1.query_ref, bf16[8,512,1024]{2,1,0:T(8,128)(2,1)} %bitcast.192), custom_call_target="tpu_custom_call" | custom-call | flops 6000000000 | bytes 4000000 | tf_op jit(solution)/shard_map/cross_forward/pallas_call | solution.py:416
  254.9 7.3 %collective-permute-done.50.refs_3_ = bf16[1072,256]{1,0:T(8,128)(2,1)S(1)} collective-permute-done((bf16[1072,256]{1,0:T(8,128)(2,1)}, bf16[1072,256]{1,0:T(8,128)(2,1)S(1)}, u32[]{:S(2)}, u32[]{:S(2)}) %collective-permute-start.50) | collective-permute-done | bytes 548896 | tf_op jit(solution)/shard_map/ppermute | solution.py:544
  263.0 4.9 cross_join.1
  268.0 13.2 %collective-permute-start.52 = (bf16[256,1024]{1,0:T(8,128)(2,1)}, bf16[256,1024]{1,0:T(8,128)(2,1)S(1)}, u32[]{:S(2)}, u32[]{:S(2)}) collective-permute-start(bf16[256,1024]{1,0:T(8,128)(2,1)} %get-tuple-element.182.row_ref), channel_id=1, source_target_pairs={{0,4},{1,5},{2,6},{3,7},{4,0},{5,1},{6,2},{7,3},{8,12},{9,13},{10,... | collective-permute-start | bytes 1572872 | tf_op jit(solution)/shard_map/ppermute | solution.py:544
  281.9 6.6 ffn_chunk.4
  288.5 5.8 collective-permute-done.52.row_ref
  298.4 6.8 ffn_chunk.5
  305.1 6.7 ffn_chunk.6
  312.7 6.8 ffn_chunk.7
  319.6 3.5 fusion
  337.8 19.7 %collective-permute-done.56.refs_2_ = bf16[256,1024]{1,0:T(8,128)(2,1)S(1)} collective-permute-done((bf16[256,1024]{1,0:T(8,128)(2,1)S(1)}, bf16[256,1024]{1,0:T(8,128)(2,1)S(1)}, u32[]{:S(2)}, u32[]{:S(2)}) %collective-permute-start.56) | collective-permute-done | bytes 524320 | tf_op jit(solution)/shard_map/ppermute | solution.py:544
  357.4 10.4 %collective-permute-done.57.refs_3_ = bf16[256,1024]{1,0:T(8,128)(2,1)S(1)} collective-permute-done((bf16[256,1024]{1,0:T(8,128)(2,1)S(1)}, bf16[256,1024]{1,0:T(8,128)(2,1)S(1)}, u32[]{:S(2)}, u32[]{:S(2)}) %collective-permute-start.57) | collective-permute-done | bytes 524320 | tf_op jit(solution)/shard_map/ppermute | solution.py:544
  368.8 5.2 ffn_join.1
  374.0 3.3 grad_blocks.3
  379.7 12.0 %collective-permute-start.66 = (bf16[1120,256]{1,0:T(8,128)(2,1)}, bf16[1120,256]{1,0:T(8,128)(2,1)S(1)}, u32[]{:S(2)}, u32[]{:S(2)}) collective-permute-start(bf16[1120,256]{1,0:T(8,128)(2,1)} %get-tuple-element.214.grad_ref), channel_id=1, source_target_pairs={{0,4},{1,5},{2,6},{3,7},{4,0},{5,1},{6,2},{7,3},{8,12},{9,13},{10,... | collective-permute-start | bytes 1720328 | tf_op jit(solution)/shard_map/ppermute | solution.py:544
  395.5 8.7 %cross_backward.4 = (bf16[1024,256]{1,0:T(8,128)(2,1)}, bf16[8,512,1024]{2,1,0:T(8,128)(2,1)}) custom-call(s32[4,5]{1,0:T(4,128)} %pad_add_fusion.info_ref, bf16[1024,256]{1,0:T(8,128)(2,1)} %get-tuple-element.213.query_ref, bf16[1120,256]{1,0:T(8,128)(2,1)} %get-tuple-element.214.grad_ref, bf16[8,512,1024]{2,1,0:T(8,128)(2,1)} %bitcast.193), custom_call_target="tpu_custom_call" | custom-call | flops 10000000000 | bytes 8000000 | tf_op jit(solution)/shard_map/cross_backward/pallas_call | solution.py:469
  404.2 13.9 %collective-permute-done.66.grad_ref = bf16[1120,256]{1,0:T(8,128)(2,1)S(1)} collective-permute-done((bf16[1120,256]{1,0:T(8,128)(2,1)}, bf16[1120,256]{1,0:T(8,128)(2,1)S(1)}, u32[]{:S(2)}, u32[]{:S(2)}) %collective-permute-start.66) | collective-permute-done | bytes 573472 | tf_op jit(solution)/shard_map/ppermute | solution.py:544
  421.9 6.2 collective-permute-done.65
  429.6 5.0 collective-permute-done.70
  441.1 8.6 %cross_backward.5 = (bf16[1024,256]{1,0:T(8,128)(2,1)}, bf16[8,512,1024]{2,1,0:T(8,128)(2,1)}) custom-call(s32[4,5]{1,0:T(4,128)} %pad_add_fusion.info_ref, bf16[1024,256]{1,0:T(8,128)(2,1)} %copy-done.76, bf16[1120,256]{1,0:T(8,128)(2,1)} %copy-done.74, bf16[8,512,1024]{2,1,0:T(8,128)(2,1)} %bitcast.194, ...), custom_call_target="tpu_custom_call", output_to_operand_aliasing={{1}: (4, {})} | custom-call | flops 10000000000 | bytes 8000000 | tf_op jit(solution)/shard_map/cross_backward/pallas_call | solution.py:469
  450.3 8.7 %cross_backward.6 = (bf16[1024,256]{1,0:T(8,128)(2,1)}, bf16[8,512,1024]{2,1,0:T(8,128)(2,1)}) custom-call(s32[4,5]{1,0:T(4,128)} %pad_add_fusion.info_ref, bf16[1024,256]{1,0:T(8,128)(2,1)} %copy-done.75, bf16[1120,256]{1,0:T(8,128)(2,1)} %copy-done.73, bf16[8,512,1024]{2,1,0:T(8,128)(2,1)} %bitcast.195, ...), custom_call_target="tpu_custom_call", output_to_operand_aliasing={{1}: (4, {})} | custom-call | flops 10000000000 | bytes 8000000 | tf_op jit(solution)/shard_map/cross_backward/pallas_call | solution.py:469
  459.0 8.8 %cross_backward.7 = (bf16[1024,256]{1,0:T(8,128)(2,1)}, bf16[8,512,1024]{2,1,0:T(8,128)(2,1)}) custom-call(s32[4,5]{1,0:T(4,128)} %pad_add_fusion.info_ref, bf16[1024,256]{1,0:T(8,128)(2,1)} %broadcast_select_fusion.1.query_ref, bf16[1120,256]{1,0:T(8,128)(2,1)} %broadcast_select_fusion.grad_ref, ...), custom_call_target="tpu_custom_call", output_to_operand_aliasing={{1}: (4, {})} | custom-call | flops 10000000000 | bytes 8000000 | tf_op jit(solution)/shard_map/cross_backward/pallas_call | solution.py:469
  471.4 24.6 %memory_backward.1 = (bf16[4,2,2,256,1024]{4,3,2,1,0:T(8,128)(2,1)}, bf16[8,256,1024]{2,1,0:T(8,128)(2,1)}, bf16[2,16,32,1024]{3,2,1,0:T(8,128)(2,1)}) custom-call(s32[3]{0:T(128)} %pad_add_fusion.1.me_ref, bf16[8,256,1024]{2,1,0:T(8,128)(2,1)} %bitcast.165, bf16[8,256,1024]{2,1,0:T(8,128)(2,1)} %collective-permute-done.3.other_ref, ...), custom_call_target="tpu_custom_call" | custom-call | flops 17200001024 | bytes 28000000 | tf_op jit(solution)/shard_map/memory_backward/pallas_call | solution.py:666
  496.0 17.8 %collective-permute-done.67.refs_2_ = bf16[1024,256]{1,0:T(8,128)(2,1)S(1)} collective-permute-done((bf16[1024,256]{1,0:T(8,128)(2,1)S(1)}, bf16[1024,256]{1,0:T(8,128)(2,1)S(1)}, u32[]{:S(2)}, u32[]{:S(2)}) %collective-permute-start.67) | collective-permute-done | bytes 524320 | tf_op jit(solution)/shard_map/ppermute | solution.py:544
  514.7 6.0 query_join.1
  520.7 6.4 grad_blocks.4
  530.2 4.9 collective-permute-done.80
  540.1 8.8 %collective-permute-done.81 = bf16[2,32,3072]{2,1,0:T(8,128)(2,1)S(1)} collective-permute-done((bf16[2,32,3072]{2,1,0:T(8,128)(2,1)S(1)}, bf16[2,32,3072]{2,1,0:T(8,128)(2,1)S(1)}, u32[]{:S(2)}, u32[]{:S(2)}) %collective-permute-start.81) | collective-permute-done | bytes 393248 | tf_op jit(solution)/shard_map/ppermute | solution.py:544
  553.2 12.1 %self_backward.1 = (bf16[256,2048]{1,0:T(8,128)(2,1)}, f32[16,128]{1,0:T(8,128)}) custom-call(s32[2]{0:T(128)} %length_ref.3, bf16[256,1024]{1,0:T(8,128)(2,1)} %get-tuple-element.239.mix_grad_ref, bf16[256,2048]{1,0:T(8,128)(2,1)} %get-tuple-element.240.wide_ref, f32[32,128]{1,0:T(8,128)} %get-tuple-element.241.stat_ref, f32[16,128]{1,0:T(8,128)} %pad.27.table_ref, ...), custom_call_target="tpu_custom_call" | custom-call | flops 8000000000 | bytes 8000000 | tf_op jit(solution)/shard_map/self_backward/pallas_call | solution.py:37
  571.2 3.0 add_convert_fusion
  574.3 5.3 input_grads.1
  581.0 4.8 grad_blocks.5
  585.7 3.3 slice_bitcast_fusion.1
  598.7 15.5 %collective-permute-done.76 = bf16[256,1024]{1,0:T(8,128)(2,1)} collective-permute-done((bf16[256,1024]{1,0:T(8,128)(2,1)}, bf16[256,1024]{1,0:T(8,128)(2,1)}, u32[]{:S(2)}, u32[]{:S(2)}) %collective-permute-start.76) | collective-permute-done | bytes 524320 | tf_op jit(solution)/shard_map/ppermute | solution.py:544
  614.2 13.4 %collective-permute-done.77 = bf16[256,1024]{1,0:T(8,128)(2,1)} collective-permute-done((bf16[256,1024]{1,0:T(8,128)(2,1)}, bf16[256,1024]{1,0:T(8,128)(2,1)}, u32[]{:S(2)}, u32[]{:S(2)}) %collective-permute-start.77) | collective-permute-done | bytes 524320 | tf_op jit(solution)/shard_map/ppermute | solution.py:544
  630.9 5.9 place_pairs.1
  638.2 11.4 %collective-permute-start.93 = (bf16[32,3072]{1,0:T(8,128)(2,1)S(1)}, bf16[32,3072]{1,0:T(8,128)(2,1)S(1)}, u32[]{:S(2)}, u32[]{:S(2)}) collective-permute-start(bf16[32,3072]{1,0:T(8,128)(2,1)S(1)} %get-tuple-element.298), channel_id=1, source_target_pairs={{0,2},{1,3},{2,0},{3,1},{4,6},{5,7},{6,4},{7,5},{8,10},{9,11},{10,... | collective-permute-start | bytes 589832 | tf_op jit(solution)/shard_map/ppermute | solution.py:544
  654.4 7.3 %collective-permute-done.86 = bf16[2,32,2176]{2,1,0:T(8,128)(2,1)S(1)} collective-permute-done((bf16[2,32,2176]{2,1,0:T(8,128)(2,1)S(1)}, bf16[2,32,2176]{2,1,0:T(8,128)(2,1)S(1)}, u32[]{:S(2)}, u32[]{:S(2)}) %collective-permute-start.86) | collective-permute-done | bytes 278560 | tf_op jit(solution)/shard_map/ppermute | solution.py:544
  663.2 3.6 collective-permute-done.94
  667.6 3.9 collective-permute-done.85
  680.4 4.1 collective-permute-done.89
  (454 shorter events, 174.7 us)
Async XLA Ops:
  7.2 506.7 %all-reduce.9.cloned.1.call-start = ((), (), s32[]{:S(2)}) async-start(), calls=%async_computation | async-start | bytes 4325376 | tf_op jit(solution)/shard_map/psum | solution.py:1045
  15.8 105.0 %collective-permute-start.3 = (bf16[8,256,1024]{2,1,0:T(8,128)(2,1)}, bf16[8,256,1024]{2,1,0:T(8,128)(2,1)}, u32[]{:S(2)}, u32[]{:S(2)}) collective-permute-start(bf16[8,256,1024]{2,1,0:T(8,128)(2,1)} %bitcast.1), channel_id=1, source_target_pairs={{0,1},{1,0},{2,3},{3,2},{4,5},{5,4},{6,7},{7,6},{8,9},{9,8},{10,11... | collective-permute-start | bytes 12582920 | tf_op jit(solution)/shard_map/ppermute | solution.py:544
  19.1 13.4 %collective-permute-start.5 = (bf16[32,2176]{1,0:T(8,128)(2,1)S(1)}, bf16[32,2176]{1,0:T(8,128)(2,1)S(1)}, u32[]{:S(2)}, u32[]{:S(2)}) collective-permute-start(bf16[32,2176]{1,0:T(8,128)(2,1)S(1)} %fusion.28), channel_id=1, source_target_pairs={{0,4},{1,5},{2,6},{3,7},{4,0},{5,1},{6,2},{7,3},{8,12},{9,13},{10,... | collective-permute-start | bytes 417800 | tf_op jit(solution)/shard_map/ppermute | solution.py:544
  35.4 12.5 %collective-permute-start.17 = (bf16[32,2048]{1,0:T(8,128)(2,1)S(1)}, bf16[32,2048]{1,0:T(8,128)(2,1)S(1)}, u32[]{:S(2)}, u32[]{:S(2)}) collective-permute-start(bf16[32,2048]{1,0:T(8,128)(2,1)S(1)} %pad_maximum_fusion.11), channel_id=1, source_target_pairs={{0,4},{1,5},{2,6},{3,7},{4,0},{5,1},{6,2},{7,3},{8,12},{9,13},{10,... | collective-permute-start | bytes 393224 | tf_op jit(solution)/shard_map/ppermute | solution.py:544
  38.0 19.9 %collective-permute-start.7 = (bf16[4,32,2176]{2,1,0:T(8,128)(2,1)S(1)}, bf16[4,32,2176]{2,1,0:T(8,128)(2,1)S(1)}, u32[]{:S(2)}, u32[]{:S(2)}) collective-permute-start(bf16[4,32,2176]{2,1,0:T(8,128)(2,1)S(1)} %pad_maximum_fusion.4.refs_0_), channel_id=1, source_target_pairs={{0,8},{8,0},{16,24},{24,16},{1,9},{9,1},{17,25},{25,17},{2,10},{10... | collective-permute-start | bytes 1671176 | tf_op jit(solution)/shard_map/ppermute | solution.py:544
  50.8 23.6 %collective-permute-start = (bf16[1024,352]{0,1:T(8,128)(2,1)S(1)}, bf16[1024,352]{0,1:T(8,128)(2,1)S(1)}, u32[]{:S(2)}, u32[]{:S(2)}) collective-permute-start(bf16[1024,352]{0,1:T(8,128)(2,1)S(1)} %copy-done.17), channel_id=1, source_target_pairs={{0,1},{1,0},{2,3},{3,2},{4,5},{5,4},{6,7},{7,6},{8,9},{9,8},{10,11... | collective-permute-start | bytes 2162696 | tf_op jit(solution)/shard_map/ppermute | solution.py:544
  54.3 11.7 %collective-permute-start.8 = (bf16[4,32,2176]{2,1,0:T(8,128)(2,1)S(1)}, bf16[4,32,2176]{2,1,0:T(8,128)(2,1)S(1)}, u32[]{:S(2)}, u32[]{:S(2)}) collective-permute-start(bf16[4,32,2176]{2,1,0:T(8,128)(2,1)S(1)} %pad_maximum_fusion.4.refs_0_), channel_id=1, source_target_pairs={{0,16},{8,24},{16,0},{24,8},{1,17},{9,25},{17,1},{25,9},{2,18},{10... | collective-permute-start | bytes 1671176 | tf_op jit(solution)/shard_map/ppermute | solution.py:544
  57.9 18.2 %collective-permute-start.1 = (bf16[1024,352]{0,1:T(8,128)(2,1)S(1)}, bf16[1024,352]{0,1:T(8,128)(2,1)S(1)}, u32[]{:S(2)}, u32[]{:S(2)}) collective-permute-start(bf16[1024,352]{0,1:T(8,128)(2,1)S(1)} %copy-done.18), channel_id=1, source_target_pairs={{0,1},{1,0},{2,3},{3,2},{4,5},{5,4},{6,7},{7,6},{8,9},{9,8},{10,11... | collective-permute-start | bytes 2162696 | tf_op jit(solution)/shard_map/ppermute | solution.py:544
  57.9 28.0 %collective-permute-start.2 = (bf16[352,1024]{1,0:T(8,128)(2,1)S(1)}, bf16[352,1024]{1,0:T(8,128)(2,1)S(1)}, u32[]{:S(2)}, u32[]{:S(2)}) collective-permute-start(bf16[352,1024]{1,0:T(8,128)(2,1)S(1)} %copy-done.19), channel_id=1, source_target_pairs={{0,1},{1,0},{2,3},{3,2},{4,5},{5,4},{6,7},{7,6},{8,9},{9,8},{10,11... | collective-permute-start | bytes 2162696 | tf_op jit(solution)/shard_map/ppermute | solution.py:544
  76.0 21.0 %collective-permute-start.41 = (bf16[256,1024]{1,0:T(8,128)(2,1)}, bf16[256,1024]{1,0:T(8,128)(2,1)}, u32[]{:S(2)}, u32[]{:S(2)}) collective-permute-start(bf16[256,1024]{1,0:T(8,128)(2,1)} %cotangent_ref.2), channel_id=1, source_target_pairs={{0,4},{1,5},{2,6},{3,7},{4,0},{5,1},{6,2},{7,3},{8,12},{9,13},{10,... | collective-permute-start | bytes 1572872 | tf_op jit(solution)/shard_map/ppermute | solution.py:544
  84.0 13.0 %collective-permute-start.19 = (bf16[4,32,2048]{2,1,0:T(8,128)(2,1)S(1)}, bf16[4,32,2048]{2,1,0:T(8,128)(2,1)}, u32[]{:S(2)}, u32[]{:S(2)}) collective-permute-start(bf16[4,32,2048]{2,1,0:T(8,128)(2,1)S(1)} %pad_maximum_fusion.7.refs_0_), channel_id=1, source_target_pairs={{0,8},{8,0},{16,24},{24,16},{1,9},{9,1},{17,25},{25,17},{2,10},{10... | collective-permute-start | bytes 1572872 | tf_op jit(solution)/shard_map/ppermute | solution.py:544
  85.5 12.0 %collective-permute-start.20 = (bf16[4,32,2048]{2,1,0:T(8,128)(2,1)S(1)}, bf16[4,32,2048]{2,1,0:T(8,128)(2,1)}, u32[]{:S(2)}, u32[]{:S(2)}) collective-permute-start(bf16[4,32,2048]{2,1,0:T(8,128)(2,1)S(1)} %pad_maximum_fusion.7.refs_0_), channel_id=1, source_target_pairs={{0,16},{8,24},{16,0},{24,8},{1,17},{9,25},{17,1},{25,9},{2,18},{10... | collective-permute-start | bytes 1572872 | tf_op jit(solution)/shard_map/ppermute | solution.py:544
  85.9 11.6 %collective-permute-start.14 = (bf16[2,32,2176]{2,1,0:T(8,128)(2,1)}, bf16[2,32,2176]{2,1,0:T(8,128)(2,1)}, u32[]{:S(2)}, u32[]{:S(2)}) collective-permute-start(bf16[2,32,2176]{2,1,0:T(8,128)(2,1)} %copy-done.46), channel_id=1, source_target_pairs={{0,1},{1,0},{2,3},{3,2},{4,5},{5,4},{6,7},{7,6},{8,9},{9,8},{10,11... | collective-permute-start | bytes 835592 | tf_op jit(solution)/shard_map/ppermute | solution.py:544
  97.0 12.0 %collective-permute-start.11 = (bf16[4,32,2176]{2,1,0:T(8,128)(2,1)}, bf16[4,32,2176]{2,1,0:T(8,128)(2,1)}, u32[]{:S(2)}, u32[]{:S(2)}) collective-permute-start(bf16[4,32,2176]{2,1,0:T(8,128)(2,1)} %copy-done.9), channel_id=1, source_target_pairs={{0,1},{1,0},{2,3},{3,2},{4,5},{5,4},{6,7},{7,6},{8,9},{9,8},{10,11... | collective-permute-start | bytes 1671176 | tf_op jit(solution)/shard_map/ppermute | solution.py:544
  97.0 13.5 %collective-permute-start.12 = (bf16[4,32,2176]{2,1,0:T(8,128)(2,1)}, bf16[4,32,2176]{2,1,0:T(8,128)(2,1)}, u32[]{:S(2)}, u32[]{:S(2)}) collective-permute-start(bf16[4,32,2176]{2,1,0:T(8,128)(2,1)} %copy-done.13), channel_id=1, source_target_pairs={{0,1},{1,0},{2,3},{3,2},{4,5},{5,4},{6,7},{7,6},{8,9},{9,8},{10,11... | collective-permute-start | bytes 1671176 | tf_op jit(solution)/shard_map/ppermute | solution.py:544
  97.5 14.5 %collective-permute-start.13 = (bf16[4,32,2176]{2,1,0:T(8,128)(2,1)}, bf16[4,32,2176]{2,1,0:T(8,128)(2,1)}, u32[]{:S(2)}, u32[]{:S(2)}) collective-permute-start(bf16[4,32,2176]{2,1,0:T(8,128)(2,1)} %copy-done.14), channel_id=1, source_target_pairs={{0,1},{1,0},{2,3},{3,2},{4,5},{5,4},{6,7},{7,6},{8,9},{9,8},{10,11... | collective-permute-start | bytes 1671176 | tf_op jit(solution)/shard_map/ppermute | solution.py:544
  105.2 14.7 %collective-permute-start.21 = (bf16[2,32,2048]{2,1,0:T(8,128)(2,1)S(1)}, bf16[2,32,2048]{2,1,0:T(8,128)(2,1)}, u32[]{:S(2)}, u32[]{:S(2)}) collective-permute-start(bf16[2,32,2048]{2,1,0:T(8,128)(2,1)S(1)} %slice.281), channel_id=1, source_target_pairs={{0,8},{8,0},{16,24},{24,16},{1,9},{9,1},{17,25},{25,17},{2,10},{10... | collective-permute-start | bytes 786440 | tf_op jit(solution)/shard_map/ppermute | solution.py:544
  109.0 30.2 %collective-permute-start.43 = (bf16[256,1024]{1,0:T(8,128)(2,1)}, bf16[256,1024]{1,0:T(8,128)(2,1)}, u32[]{:S(2)}, u32[]{:S(2)}) collective-permute-start(bf16[256,1024]{1,0:T(8,128)(2,1)} %cotangent_ref.2), channel_id=1, source_target_pairs={{2,4},{3,5},{4,2},{5,3},{10,12},{11,13},{12,10},{13,11},{18,20},{1... | collective-permute-start | bytes 1572872 | tf_op jit(solution)/shard_map/ppermute | solution.py:554
  110.5 29.3 %collective-permute-start.42 = (bf16[256,1024]{1,0:T(8,128)(2,1)}, bf16[256,1024]{1,0:T(8,128)(2,1)}, u32[]{:S(2)}, u32[]{:S(2)}) collective-permute-start(bf16[256,1024]{1,0:T(8,128)(2,1)} %collective-permute-done.41.cotangent_ref), channel_id=1, source_target_pairs={{4,6},{5,7},{2,0},{3,1},{12,14},{13,15},{10,8},{11,9},{20,22},{21,... | collective-permute-start | bytes 1572872 | tf_op jit(solution)/shard_map/ppermute | solution.py:554
  112.0 27.8 %collective-permute-start.31 = (bf16[4,32,2048]{2,1,0:T(8,128)(2,1)S(1)}, bf16[4,32,2048]{2,1,0:T(8,128)(2,1)S(1)}, u32[]{:S(2)}, u32[]{:S(2)}) collective-permute-start(bf16[4,32,2048]{2,1,0:T(8,128)(2,1)S(1)} %pad_maximum_fusion.8.refs_0_), channel_id=1, source_target_pairs={{0,8},{8,0},{16,24},{24,16},{1,9},{9,1},{17,25},{25,17},{2,10},{10... | collective-permute-start | bytes 1572872 | tf_op jit(solution)/shard_map/ppermute | solution.py:544
  119.8 20.4 %collective-permute-start.32 = (bf16[4,32,2048]{2,1,0:T(8,128)(2,1)S(1)}, bf16[4,32,2048]{2,1,0:T(8,128)(2,1)S(1)}, u32[]{:S(2)}, u32[]{:S(2)}) collective-permute-start(bf16[4,32,2048]{2,1,0:T(8,128)(2,1)S(1)} %pad_maximum_fusion.8.refs_0_), channel_id=1, source_target_pairs={{0,16},{8,24},{16,0},{24,8},{1,17},{9,25},{17,1},{25,9},{2,18},{10... | collective-permute-start | bytes 1572872 | tf_op jit(solution)/shard_map/ppermute | solution.py:544
  120.8 18.1 %collective-permute-start.22 = (bf16[2,32,2048]{2,1,0:T(8,128)(2,1)}, bf16[2,32,2048]{2,1,0:T(8,128)(2,1)S(1)}, u32[]{:S(2)}, u32[]{:S(2)}) collective-permute-start(bf16[2,32,2048]{2,1,0:T(8,128)(2,1)} %slice.282), channel_id=1, source_target_pairs={{0,16},{8,24},{16,0},{24,8},{1,17},{9,25},{17,1},{25,9},{2,18},{10... | collective-permute-start | bytes 786440 | tf_op jit(solution)/shard_map/ppermute | solution.py:544
  143.3 18.0 %collective-permute-start.40 = (bf16[256,1024]{1,0:T(8,128)(2,1)}, bf16[256,1024]{1,0:T(8,128)(2,1)S(1)}, u32[]{:S(2)}, u32[]{:S(2)}) collective-permute-start(bf16[256,1024]{1,0:T(8,128)(2,1)} %cotangent_ref.2), channel_id=1, source_target_pairs={{0,2},{1,3},{2,0},{3,1},{4,6},{5,7},{6,4},{7,5},{8,10},{9,11},{10,... | collective-permute-start | bytes 1572872 | tf_op jit(solution)/shard_map/ppermute | solution.py:544
  147.3 12.2 %collective-permute-start.33 = (bf16[2,32,2048]{2,1,0:T(8,128)(2,1)S(1)}, bf16[2,32,2048]{2,1,0:T(8,128)(2,1)S(1)}, u32[]{:S(2)}, u32[]{:S(2)}) collective-permute-start(bf16[2,32,2048]{2,1,0:T(8,128)(2,1)S(1)} %slice.283), channel_id=1, source_target_pairs={{0,8},{8,0},{16,24},{24,16},{1,9},{9,1},{17,25},{25,17},{2,10},{10... | collective-permute-start | bytes 786440 | tf_op jit(solution)/shard_map/ppermute | solution.py:544
  163.6 41.6 %collective-permute-start.46 = (bf16[1024,256]{1,0:T(8,128)(2,1)}, bf16[1024,256]{1,0:T(8,128)(2,1)S(1)}, u32[]{:S(2)}, u32[]{:S(2)}) collective-permute-start(bf16[1024,256]{1,0:T(8,128)(2,1)} %get-tuple-element.213.query_ref), channel_id=1, source_target_pairs={{0,4},{1,5},{2,6},{3,7},{4,0},{5,1},{6,2},{7,3},{8,12},{9,13},{10,... | collective-permute-start | bytes 1572872 | tf_op jit(solution)/shard_map/ppermute | solution.py:544
  164.7 53.1 %collective-permute-start.49 = (bf16[1024,256]{1,0:T(8,128)(2,1)}, bf16[1024,256]{1,0:T(8,128)(2,1)S(1)}, u32[]{:S(2)}, u32[]{:S(2)}) collective-permute-start(bf16[1024,256]{1,0:T(8,128)(2,1)} %get-tuple-element.213.query_ref), channel_id=1, source_target_pairs={{2,4},{3,5},{4,2},{5,3},{10,12},{11,13},{12,10},{13,11},{18,20},{1... | collective-permute-start | bytes 1572872 | tf_op jit(solution)/shard_map/ppermute | solution.py:554
  166.0 30.9 %collective-permute-start.44 = (bf16[1024,256]{1,0:T(8,128)(2,1)}, bf16[1024,256]{1,0:T(8,128)(2,1)S(1)}, u32[]{:S(2)}, u32[]{:S(2)}) collective-permute-start(bf16[1024,256]{1,0:T(8,128)(2,1)} %get-tuple-element.213.query_ref), channel_id=1, source_target_pairs={{0,2},{1,3},{2,0},{3,1},{4,6},{5,7},{6,4},{7,5},{8,10},{9,11},{10,... | collective-permute-start | bytes 1572872 | tf_op jit(solution)/shard_map/ppermute | solution.py:544
  205.1 49.9 %collective-permute-start.45 = (bf16[1072,256]{1,0:T(8,128)(2,1)}, bf16[1072,256]{1,0:T(8,128)(2,1)S(1)}, u32[]{:S(2)}, u32[]{:S(2)}) collective-permute-start(bf16[1072,256]{1,0:T(8,128)(2,1)} %cross_forward.5), channel_id=1, source_target_pairs={{0,2},{1,3},{2,0},{3,1},{4,6},{5,7},{6,4},{7,5},{8,10},{9,11},{10,... | collective-permute-start | bytes 1646600 | tf_op jit(solution)/shard_map/ppermute | solution.py:544
  205.1 36.8 %collective-permute-start.48 = (bf16[1024,256]{1,0:T(8,128)(2,1)S(1)}, bf16[1024,256]{1,0:T(8,128)(2,1)S(1)}, u32[]{:S(2)}, u32[]{:S(2)}) collective-permute-start(bf16[1024,256]{1,0:T(8,128)(2,1)S(1)} %collective-permute-done.46.query_ref), channel_id=1, source_target_pairs={{4,6},{5,7},{2,0},{3,1},{12,14},{13,15},{10,8},{11,9},{20,22},{21,... | collective-permute-start | bytes 1572872 | tf_op jit(solution)/shard_map/ppermute | solution.py:554
  214.0 41.0 %collective-permute-start.47 = (bf16[1072,256]{1,0:T(8,128)(2,1)}, bf16[1072,256]{1,0:T(8,128)(2,1)S(1)}, u32[]{:S(2)}, u32[]{:S(2)}) collective-permute-start(bf16[1072,256]{1,0:T(8,128)(2,1)} %cross_forward.6), channel_id=1, source_target_pairs={{0,4},{1,5},{2,6},{3,7},{4,0},{5,1},{6,2},{7,3},{8,12},{9,13},{10,... | collective-permute-start | bytes 1646600 | tf_op jit(solution)/shard_map/ppermute | solution.py:544
  250.7 11.6 %collective-permute-start.50 = (bf16[1072,256]{1,0:T(8,128)(2,1)}, bf16[1072,256]{1,0:T(8,128)(2,1)S(1)}, u32[]{:S(2)}, u32[]{:S(2)}) collective-permute-start(bf16[1072,256]{1,0:T(8,128)(2,1)} %cross_forward.7), channel_id=1, source_target_pairs={{0,6},{1,7},{2,4},{3,5},{4,2},{5,3},{6,0},{7,1},{8,14},{9,15},{10,... | collective-permute-start | bytes 1646600 | tf_op jit(solution)/shard_map/ppermute | solution.py:544
  268.0 26.3 %collective-permute-start.52 = (bf16[256,1024]{1,0:T(8,128)(2,1)}, bf16[256,1024]{1,0:T(8,128)(2,1)S(1)}, u32[]{:S(2)}, u32[]{:S(2)}) collective-permute-start(bf16[256,1024]{1,0:T(8,128)(2,1)} %get-tuple-element.182.row_ref), channel_id=1, source_target_pairs={{0,4},{1,5},{2,6},{3,7},{4,0},{5,1},{6,2},{7,3},{8,12},{9,13},{10,... | collective-permute-start | bytes 1572872 | tf_op jit(solution)/shard_map/ppermute | solution.py:544
  281.2 16.3 %collective-permute-start.51 = (bf16[256,1024]{1,0:T(8,128)(2,1)}, bf16[256,1024]{1,0:T(8,128)(2,1)S(1)}, u32[]{:S(2)}, u32[]{:S(2)}) collective-permute-start(bf16[256,1024]{1,0:T(8,128)(2,1)} %get-tuple-element.182.row_ref), channel_id=1, source_target_pairs={{0,2},{1,3},{2,0},{3,1},{4,6},{5,7},{6,4},{7,5},{8,10},{9,11},{10,... | collective-permute-start | bytes 1572872 | tf_op jit(solution)/shard_map/ppermute | solution.py:544
  281.2 30.6 %collective-permute-start.54 = (bf16[256,1024]{1,0:T(8,128)(2,1)}, bf16[256,1024]{1,0:T(8,128)(2,1)S(1)}, u32[]{:S(2)}, u32[]{:S(2)}) collective-permute-start(bf16[256,1024]{1,0:T(8,128)(2,1)} %get-tuple-element.182.row_ref), channel_id=1, source_target_pairs={{2,4},{3,5},{4,2},{5,3},{10,12},{11,13},{12,10},{13,11},{18,20},{1... | collective-permute-start | bytes 1572872 | tf_op jit(solution)/shard_map/ppermute | solution.py:554
  294.3 17.5 %collective-permute-start.53 = (bf16[256,1024]{1,0:T(8,128)(2,1)S(1)}, bf16[256,1024]{1,0:T(8,128)(2,1)S(1)}, u32[]{:S(2)}, u32[]{:S(2)}) collective-permute-start(bf16[256,1024]{1,0:T(8,128)(2,1)S(1)} %collective-permute-done.52.row_ref), channel_id=1, source_target_pairs={{4,6},{5,7},{2,0},{3,1},{12,14},{13,15},{10,8},{11,9},{20,22},{21,... | collective-permute-start | bytes 1572872 | tf_op jit(solution)/shard_map/ppermute | solution.py:554
  330.0 27.4 %collective-permute-start.56 = (bf16[256,1024]{1,0:T(8,128)(2,1)S(1)}, bf16[256,1024]{1,0:T(8,128)(2,1)S(1)}, u32[]{:S(2)}, u32[]{:S(2)}) collective-permute-start(bf16[256,1024]{1,0:T(8,128)(2,1)S(1)} %copy-done.78), channel_id=1, source_target_pairs={{0,4},{1,5},{2,6},{3,7},{4,0},{5,1},{6,2},{7,3},{8,12},{9,13},{10,... | collective-permute-start | bytes 1572872 | tf_op jit(solution)/shard_map/ppermute | solution.py:544
  331.3 36.6 %collective-permute-start.55 = (bf16[256,1024]{1,0:T(8,128)(2,1)S(1)}, bf16[256,1024]{1,0:T(8,128)(2,1)S(1)}, u32[]{:S(2)}, u32[]{:S(2)}) collective-permute-start(bf16[256,1024]{1,0:T(8,128)(2,1)S(1)} %copy-done.77), channel_id=1, source_target_pairs={{0,2},{1,3},{2,0},{3,1},{4,6},{5,7},{6,4},{7,5},{8,10},{9,11},{10,... | collective-permute-start | bytes 1572872 | tf_op jit(solution)/shard_map/ppermute | solution.py:544
  333.3 34.5 %collective-permute-start.57 = (bf16[256,1024]{1,0:T(8,128)(2,1)S(1)}, bf16[256,1024]{1,0:T(8,128)(2,1)S(1)}, u32[]{:S(2)}, u32[]{:S(2)}) collective-permute-start(bf16[256,1024]{1,0:T(8,128)(2,1)S(1)} %copy-done.79), channel_id=1, source_target_pairs={{0,6},{1,7},{2,4},{3,5},{4,2},{5,3},{6,0},{7,1},{8,14},{9,15},{10,... | collective-permute-start | bytes 1572872 | tf_op jit(solution)/shard_map/ppermute | solution.py:544
  379.7 14.6 %collective-permute-start.61 = (bf16[16,32,1024]{2,1,0:T(8,128)(2,1)}, bf16[16,32,1024]{2,1,0:T(8,128)(2,1)S(1)}, u32[]{:S(2)}, u32[]{:S(2)}) collective-permute-start(bf16[16,32,1024]{2,1,0:T(8,128)(2,1)} %slice_bitcast_fusion.2), channel_id=1, source_target_pairs={{0,1},{1,0},{2,3},{3,2},{4,5},{5,4},{6,7},{7,6},{8,9},{9,8},{10,11... | collective-permute-start | bytes 3145736 | tf_op jit(solution)/shard_map/ppermute | solution.py:544
  379.7 38.4 %collective-permute-start.66 = (bf16[1120,256]{1,0:T(8,128)(2,1)}, bf16[1120,256]{1,0:T(8,128)(2,1)S(1)}, u32[]{:S(2)}, u32[]{:S(2)}) collective-permute-start(bf16[1120,256]{1,0:T(8,128)(2,1)} %get-tuple-element.214.grad_ref), channel_id=1, source_target_pairs={{0,4},{1,5},{2,6},{3,7},{4,0},{5,1},{6,2},{7,3},{8,12},{9,13},{10,... | collective-permute-start | bytes 1720328 | tf_op jit(solution)/shard_map/ppermute | solution.py:544
  391.8 37.8 %collective-permute-start.71 = (bf16[1120,256]{1,0:T(8,128)(2,1)}, bf16[1120,256]{1,0:T(8,128)(2,1)S(1)}, u32[]{:S(2)}, u32[]{:S(2)}) collective-permute-start(bf16[1120,256]{1,0:T(8,128)(2,1)} %get-tuple-element.214.grad_ref), channel_id=1, source_target_pairs={{2,4},{3,5},{4,2},{5,3},{10,12},{11,13},{12,10},{13,11},{18,20},{1... | collective-permute-start | bytes 1720328 | tf_op jit(solution)/shard_map/ppermute | solution.py:554
  392.4 47.8 %collective-permute-start.62 = (bf16[1120,256]{1,0:T(8,128)(2,1)}, bf16[1120,256]{1,0:T(8,128)(2,1)S(1)}, u32[]{:S(2)}, u32[]{:S(2)}) collective-permute-start(bf16[1120,256]{1,0:T(8,128)(2,1)} %get-tuple-element.214.grad_ref), channel_id=1, source_target_pairs={{0,2},{1,3},{2,0},{3,1},{4,6},{5,7},{6,4},{7,5},{8,10},{9,11},{10,... | collective-permute-start | bytes 1720328 | tf_op jit(solution)/shard_map/ppermute | solution.py:544
  394.7 26.4 %collective-permute-start.64 = (bf16[2,32,1024]{2,1,0:T(8,128)(2,1)S(1)}, bf16[2,32,1024]{2,1,0:T(8,128)(2,1)S(1)}, u32[]{:S(2)}, u32[]{:S(2)}) collective-permute-start(bf16[2,32,1024]{2,1,0:T(8,128)(2,1)S(1)} %get-tuple-element.317), channel_id=1, source_target_pairs={{0,16},{8,24},{16,0},{24,8},{1,17},{9,25},{17,1},{25,9},{2,18},{10... | collective-permute-start | bytes 393224 | tf_op jit(solution)/shard_map/ppermute | solution.py:544
  418.1 16.5 %collective-permute-start.70 = (bf16[1120,256]{1,0:T(8,128)(2,1)S(1)}, bf16[1120,256]{1,0:T(8,128)(2,1)S(1)}, u32[]{:S(2)}, u32[]{:S(2)}) collective-permute-start(bf16[1120,256]{1,0:T(8,128)(2,1)S(1)} %collective-permute-done.66.grad_ref), channel_id=1, source_target_pairs={{4,6},{5,7},{2,0},{3,1},{12,14},{13,15},{10,8},{11,9},{20,22},{21,... | collective-permute-start | bytes 1720328 | tf_op jit(solution)/shard_map/ppermute | solution.py:554
  421.1 14.3 %collective-permute-start.68 = (bf16[4,32,1024]{2,1,0:T(8,128)(2,1)S(1)}, bf16[4,32,1024]{2,1,0:T(8,128)(2,1)S(1)}, u32[]{:S(2)}, u32[]{:S(2)}) collective-permute-start(bf16[4,32,1024]{2,1,0:T(8,128)(2,1)S(1)} %pad_maximum_fusion.9), channel_id=1, source_target_pairs={{0,8},{8,0},{16,24},{24,16},{1,9},{9,1},{17,25},{25,17},{2,10},{10... | collective-permute-start | bytes 786440 | tf_op jit(solution)/shard_map/ppermute | solution.py:544
  435.8 34.3 %collective-permute-start.73 = (bf16[32,1024]{1,0:T(8,128)(2,1)S(1)}, bf16[32,1024]{1,0:T(8,128)(2,1)S(1)}, u32[]{:S(2)}, u32[]{:S(2)}) collective-permute-start(bf16[32,1024]{1,0:T(8,128)(2,1)S(1)} %get-tuple-element.314), channel_id=1, source_target_pairs={{0,2},{1,3},{2,0},{3,1},{4,6},{5,7},{6,4},{7,5},{8,10},{9,11},{10,... | collective-permute-start | bytes 196616 | tf_op jit(solution)/shard_map/ppermute | solution.py:544
  437.3 33.3 %collective-permute-start.74 = (bf16[32,1024]{1,0:T(8,128)(2,1)S(1)}, bf16[32,1024]{1,0:T(8,128)(2,1)S(1)}, u32[]{:S(2)}, u32[]{:S(2)}) collective-permute-start(bf16[32,1024]{1,0:T(8,128)(2,1)S(1)} %get-tuple-element.316), channel_id=1, source_target_pairs={{0,4},{1,5},{2,6},{3,7},{4,0},{5,1},{6,2},{7,3},{8,12},{9,13},{10,... | collective-permute-start | bytes 196616 | tf_op jit(solution)/shard_map/ppermute | solution.py:544
  438.4 32.2 %collective-permute-start.75 = (bf16[32,1024]{1,0:T(8,128)(2,1)S(1)}, bf16[32,1024]{1,0:T(8,128)(2,1)S(1)}, u32[]{:S(2)}, u32[]{:S(2)}) collective-permute-start(bf16[32,1024]{1,0:T(8,128)(2,1)S(1)} %get-tuple-element.315), channel_id=1, source_target_pairs={{0,6},{1,7},{2,4},{3,5},{4,2},{5,3},{6,0},{7,1},{8,14},{9,15},{10,... | collective-permute-start | bytes 196616 | tf_op jit(solution)/shard_map/ppermute | solution.py:544
  449.7 21.6 %collective-permute-start.63 = (bf16[1024,256]{1,0:T(8,128)(2,1)}, bf16[1024,256]{1,0:T(8,128)(2,1)S(1)}, u32[]{:S(2)}, u32[]{:S(2)}) collective-permute-start(bf16[1024,256]{1,0:T(8,128)(2,1)} %get-tuple-element.218), channel_id=1, source_target_pairs={{0,2},{1,3},{2,0},{3,1},{4,6},{5,7},{6,4},{7,5},{8,10},{9,11},{10,... | collective-permute-start | bytes 1572872 | tf_op jit(solution)/shard_map/ppermute | solution.py:544
  467.8 28.3 %collective-permute-start.72 = (bf16[1024,256]{1,0:T(8,128)(2,1)}, bf16[1024,256]{1,0:T(8,128)(2,1)S(1)}, u32[]{:S(2)}, u32[]{:S(2)}) collective-permute-start(bf16[1024,256]{1,0:T(8,128)(2,1)} %get-tuple-element.224), channel_id=1, source_target_pairs={{0,6},{1,7},{2,4},{3,5},{4,2},{5,3},{6,0},{7,1},{8,14},{9,15},{10,... | collective-permute-start | bytes 1572872 | tf_op jit(solution)/shard_map/ppermute | solution.py:544
  470.1 43.7 %collective-permute-start.67 = (bf16[1024,256]{1,0:T(8,128)(2,1)S(1)}, bf16[1024,256]{1,0:T(8,128)(2,1)S(1)}, u32[]{:S(2)}, u32[]{:S(2)}) collective-permute-start(bf16[1024,256]{1,0:T(8,128)(2,1)S(1)} %copy-done.80), channel_id=1, source_target_pairs={{0,4},{1,5},{2,6},{3,7},{4,0},{5,1},{6,2},{7,3},{8,12},{9,13},{10,... | collective-permute-start | bytes 1572872 | tf_op jit(solution)/shard_map/ppermute | solution.py:544
  530.2 23.0 %collective-permute-start.79 = (bf16[8,256,1024]{2,1,0:T(8,128)(2,1)S(1)}, bf16[8,256,1024]{2,1,0:T(8,128)(2,1)}, u32[]{:S(2)}, u32[]{:S(2)}) collective-permute-start(bf16[8,256,1024]{2,1,0:T(8,128)(2,1)S(1)} %copy-done.72), channel_id=1, source_target_pairs={{0,1},{1,0},{2,3},{3,2},{4,5},{5,4},{6,7},{7,6},{8,9},{9,8},{10,11... | collective-permute-start | bytes 12582920 | tf_op jit(solution)/shard_map/ppermute | solution.py:544
  538.7 12.7 %collective-permute-start.82 = (bf16[2,32,3072]{2,1,0:T(8,128)(2,1)S(1)}, bf16[2,32,3072]{2,1,0:T(8,128)(2,1)S(1)}, u32[]{:S(2)}, u32[]{:S(2)}) collective-permute-start(bf16[2,32,3072]{2,1,0:T(8,128)(2,1)S(1)} %get-tuple-element.302), channel_id=1, source_target_pairs={{0,8},{8,0},{16,24},{24,16},{1,9},{9,1},{17,25},{25,17},{2,10},{10... | collective-permute-start | bytes 1179656 | tf_op jit(solution)/shard_map/ppermute | solution.py:544
  550.0 19.1 %collective-permute-start.91 = (bf16[4,32,3072]{2,1,0:T(8,128)(2,1)}, bf16[4,32,3072]{2,1,0:T(8,128)(2,1)}, u32[]{:S(2)}, u32[]{:S(2)}) collective-permute-start(bf16[4,32,3072]{2,1,0:T(8,128)(2,1)} %pad_maximum_fusion.2), channel_id=1, source_target_pairs={{0,8},{8,0},{16,24},{24,16},{1,9},{9,1},{17,25},{25,17},{2,10},{10... | collective-permute-start | bytes 2359304 | tf_op jit(solution)/shard_map/ppermute | solution.py:544
  552.5 18.8 %collective-permute-start.92 = (bf16[4,32,3072]{2,1,0:T(8,128)(2,1)}, bf16[4,32,3072]{2,1,0:T(8,128)(2,1)}, u32[]{:S(2)}, u32[]{:S(2)}) collective-permute-start(bf16[4,32,3072]{2,1,0:T(8,128)(2,1)} %pad_maximum_fusion.3), channel_id=1, source_target_pairs={{0,16},{8,24},{16,0},{24,8},{1,17},{9,25},{17,1},{25,9},{2,18},{10... | collective-permute-start | bytes 2359304 | tf_op jit(solution)/shard_map/ppermute | solution.py:544
  589.0 47.8 %collective-permute-start.83 = (bf16[16,32,2176]{2,1,0:T(8,128)(2,1)}, bf16[16,32,2176]{2,1,0:T(8,128)(2,1)S(1)}, u32[]{:S(2)}, u32[]{:S(2)}) collective-permute-start(bf16[16,32,2176]{2,1,0:T(8,128)(2,1)} %slice_bitcast_fusion.1), channel_id=1, source_target_pairs={{0,1},{1,0},{2,3},{3,2},{4,5},{5,4},{6,7},{7,6},{8,9},{9,8},{10,11... | collective-permute-start | bytes 6684680 | tf_op jit(solution)/shard_map/ppermute | solution.py:544
  589.0 25.1 %collective-permute-start.76 = (bf16[256,1024]{1,0:T(8,128)(2,1)}, bf16[256,1024]{1,0:T(8,128)(2,1)}, u32[]{:S(2)}, u32[]{:S(2)}) collective-permute-start(bf16[256,1024]{1,0:T(8,128)(2,1)} %get-tuple-element.232), channel_id=1, source_target_pairs={{0,2},{1,3},{2,0},{3,1},{4,6},{5,7},{6,4},{7,5},{8,10},{9,11},{10,... | collective-permute-start | bytes 1572872 | tf_op jit(solution)/shard_map/ppermute | solution.py:544
  589.0 38.5 %collective-permute-start.77 = (bf16[256,1024]{1,0:T(8,128)(2,1)}, bf16[256,1024]{1,0:T(8,128)(2,1)}, u32[]{:S(2)}, u32[]{:S(2)}) collective-permute-start(bf16[256,1024]{1,0:T(8,128)(2,1)} %get-tuple-element.233), channel_id=1, source_target_pairs={{0,4},{1,5},{2,6},{3,7},{4,0},{5,1},{6,2},{7,3},{8,12},{9,13},{10,... | collective-permute-start | bytes 1572872 | tf_op jit(solution)/shard_map/ppermute | solution.py:544
  591.4 36.1 %collective-permute-start.78 = (bf16[256,1024]{1,0:T(8,128)(2,1)}, bf16[256,1024]{1,0:T(8,128)(2,1)}, u32[]{:S(2)}, u32[]{:S(2)}) collective-permute-start(bf16[256,1024]{1,0:T(8,128)(2,1)} %get-tuple-element.234), channel_id=1, source_target_pairs={{0,6},{1,7},{2,4},{3,5},{4,2},{5,3},{6,0},{7,1},{8,14},{9,15},{10,... | collective-permute-start | bytes 1572872 | tf_op jit(solution)/shard_map/ppermute | solution.py:544
  637.3 15.8 %collective-permute-start.84 = (bf16[2,32,2176]{2,1,0:T(8,128)(2,1)S(1)}, bf16[2,32,2176]{2,1,0:T(8,128)(2,1)S(1)}, u32[]{:S(2)}, u32[]{:S(2)}) collective-permute-start(bf16[2,32,2176]{2,1,0:T(8,128)(2,1)S(1)} %get-tuple-element.306), channel_id=1, source_target_pairs={{0,16},{8,24},{16,0},{24,8},{1,17},{9,25},{17,1},{25,9},{2,18},{10... | collective-permute-start | bytes 835592 | tf_op jit(solution)/shard_map/ppermute | solution.py:544
  638.2 25.0 %collective-permute-start.93 = (bf16[32,3072]{1,0:T(8,128)(2,1)S(1)}, bf16[32,3072]{1,0:T(8,128)(2,1)S(1)}, u32[]{:S(2)}, u32[]{:S(2)}) collective-permute-start(bf16[32,3072]{1,0:T(8,128)(2,1)S(1)} %get-tuple-element.298), channel_id=1, source_target_pairs={{0,2},{1,3},{2,0},{3,1},{4,6},{5,7},{6,4},{7,5},{8,10},{9,11},{10,... | collective-permute-start | bytes 589832 | tf_op jit(solution)/shard_map/ppermute | solution.py:544
  649.6 17.2 %collective-permute-start.94 = (bf16[32,3072]{1,0:T(8,128)(2,1)S(1)}, bf16[32,3072]{1,0:T(8,128)(2,1)S(1)}, u32[]{:S(2)}, u32[]{:S(2)}) collective-permute-start(bf16[32,3072]{1,0:T(8,128)(2,1)S(1)} %get-tuple-element.300), channel_id=1, source_target_pairs={{0,4},{1,5},{2,6},{3,7},{4,0},{5,1},{6,2},{7,3},{8,12},{9,13},{10,... | collective-permute-start | bytes 589832 | tf_op jit(solution)/shard_map/ppermute | solution.py:544
  650.2 16.6 %collective-permute-start.95 = (bf16[32,3072]{1,0:T(8,128)(2,1)S(1)}, bf16[32,3072]{1,0:T(8,128)(2,1)S(1)}, u32[]{:S(2)}, u32[]{:S(2)}) collective-permute-start(bf16[32,3072]{1,0:T(8,128)(2,1)S(1)} %get-tuple-element.299), channel_id=1, source_target_pairs={{0,6},{1,7},{2,4},{3,5},{4,2},{5,3},{6,0},{7,1},{8,14},{9,15},{10,... | collective-permute-start | bytes 589832 | tf_op jit(solution)/shard_map/ppermute | solution.py:544
  653.3 18.2 %collective-permute-start.85 = (bf16[4,32,2176]{2,1,0:T(8,128)(2,1)S(1)}, bf16[4,32,2176]{2,1,0:T(8,128)(2,1)S(1)}, u32[]{:S(2)}, u32[]{:S(2)}) collective-permute-start(bf16[4,32,2176]{2,1,0:T(8,128)(2,1)S(1)} %pad_maximum_fusion.5), channel_id=1, source_target_pairs={{0,8},{8,0},{16,24},{24,16},{1,9},{9,1},{17,25},{25,17},{2,10},{10... | collective-permute-start | bytes 1671176 | tf_op jit(solution)/shard_map/ppermute | solution.py:544
  (118 other events, 1302.5 us)
Sparse Core Ops, SparseCore 0:
  379.9 87.4 all-reduce.8

commit v3 on v2

--- a/solution.py
+++ b/solution.py
@@ -34,10 +34,13 @@
 
 
 def vmem_call(body, outs, operands, scalars=(), scratch=(), name=None, flops=1000000000):
+    specs = [
+        one[1] if isinstance(one, tuple) else pl.BlockSpec(memory_space=pltpu.VMEM) for one in operands
+    ]
+    operands = [one[0] if isinstance(one, tuple) else one for one in operands]
     return pl.pallas_call(
         body,
-        in_specs=[pl.BlockSpec(memory_space=pltpu.SMEM)] * len(scalars)
-        + [pl.BlockSpec(memory_space=pltpu.VMEM)] * len(operands),
+        in_specs=[pl.BlockSpec(memory_space=pltpu.SMEM)] * len(scalars) + specs,
         out_specs=[pl.BlockSpec(memory_space=pltpu.VMEM)] * len(outs),
         out_shape=[jax.ShapeDtypeStruct(shape, dtype) for shape, dtype in outs],
         scratch_shapes=list(scratch),
@@ -81,28 +84,26 @@
     return jnp.where((key <= query) & (key < length), raw, masked_value)
 
 
-def self_bias(table_ref, bucket_ref, group):
-    buckets = bucket_ref[...]
+def self_bias(small_ref, lane_ref, group):
+    lanes = lane_ref[...]
+    source = jnp.broadcast_to(small_ref[3:4, group * TGT : (group + 1) * TGT], (TGT, TGT))
     return jnp.concatenate(
-        [
-            jnp.take_along_axis(
-                jnp.broadcast_to(table_ref[head : head + 1, :], (TGT, TGT)), buckets, axis=1
-            )
-            for head in (2 * group, 2 * group + 1)
-        ],
-        axis=1,
-    )
-
-
-def self_forward_kernel(
-    length_ref, row_ref, weight_ref, gain_ref, table_ref, bucket_ref, norm_ref, wide_ref, mix_ref, stat_ref
-):
+        [jnp.take_along_axis(source, lanes + head * HEAD, axis=1) for head in range(2)], axis=1
+    )
+
+
+def self_forward_kernel(sizes, share, me_ref, length_ref, row_ref, lane_ref, *refs):
+    pieces, refs = refs[:-7], refs[-7:]
+    norm_ref, wide_ref, mix_ref, stat_ref, small_ref, weight_ref, sems = refs
     inputs = row_ref[...].astype(f32)
-    normed = (inputs * inverse_root(inputs) * gain_ref[0:1, :]).astype(bf16)
+    place_pieces(sizes, share, me_ref, pieces, 0, weight_ref, sems)
+    small = weight_ref[:, D + 2 * KEYS :].astype(f32).T
+    small_ref[...] = small[:8]
+    normed = (inputs * inverse_root(inputs) * small[0:1, :]).astype(bf16)
     norm_ref[...] = normed
     wide_ref[...] = matmul(normed, weight_ref[:, : D + 2 * KEYS]).astype(bf16)
     for group in range(GROUPS):
-        bias = self_bias(table_ref, bucket_ref, group)
+        bias = self_bias(small_ref, lane_ref, group)
         for pair in range(row_ref.shape[0] // TGT):
             queries, keys, values = self_pieces(pair, group, wide_ref)
             scores = self_scores(queries, keys, bias, length_ref[pair])
@@ -121,39 +122,49 @@
             stat_ref[at + 1 : at + 2, :] = logsum[:, TGT:]
 
 
-def self_forward(lengths, rows, weights, gains, table, buckets):
+ANYWHERE = pl.BlockSpec(memory_space=pl.ANY)
+
+
+def self_forward(sizes, share, me, lengths, rows, lanes, pieces):
     count = rows.shape[0]
     return vmem_call(
-        self_forward_kernel,
+        functools.partial(self_forward_kernel, sizes, share),
         [
             ((count, D), bf16),
             ((count, D + 2 * KEYS), bf16),
             ((count, D), bf16),
             ((count // TGT * HEADS, TGT), f32),
+            ((8, D), f32),
         ],
-        [rows, weights, gains, table, buckets],
-        [lengths],
+        [rows, lanes] + [(piece, ANYWHERE) for piece in pieces],
+        [me, lengths],
+        [pltpu.VMEM((D, D + 2 * KEYS + SMALL), bf16), pltpu.SemaphoreType.DMA((sizes[0] * sizes[1],))],
         name="self_forward",
     )
 
 
-def self_output_kernel(row_ref, mix_ref, weight_ref, gain_ref, hidden_ref, norm_ref, query_ref, square_ref):
+def self_output_kernel(sizes, share, me_ref, row_ref, mix_ref, small_ref, *refs):
+    pieces, refs = refs[:-6], refs[-6:]
+    hidden_ref, norm_ref, query_ref, square_ref, weight_ref, sems = refs
+    place_pieces(sizes, share, me_ref, pieces, D + 2 * KEYS + SMALL, weight_ref, sems)
     branch = matmul(mix_ref[...], weight_ref[:, :D])
     square_ref[...] = jnp.sum(branch * branch, axis=1, keepdims=True)
     hidden = row_ref[...].astype(f32) + branch
     hidden_ref[...] = hidden
-    normed = (hidden * inverse_root(hidden) * gain_ref[1:2, :]).astype(bf16)
+    normed = (hidden * inverse_root(hidden) * small_ref[1:2, :]).astype(bf16)
     norm_ref[...] = normed
     queries = matmul(normed, weight_ref[:, D:]).astype(bf16) * bf16(HEAD ** (-0.5))
     query_ref[...] = queries.T
 
 
-def self_output_part(rows, mixed, weights, gains):
+def self_output_part(sizes, share, me, rows, mixed, small, pieces):
     count = rows.shape[0]
     return vmem_call(
-        self_output_kernel,
+        functools.partial(self_output_kernel, sizes, share),
         [((count, D), f32), ((count, D), bf16), ((D, count), bf16), ((count, 1), f32)],
-        [rows, mixed, weights, gains],
+        [rows, mixed, small] + [(piece, ANYWHERE) for piece in pieces],
+        [me],
+        [pltpu.VMEM((D, 2 * D), bf16), pltpu.SemaphoreType.DMA((sizes[0] * sizes[1],))],
         name="self_output",
     )
 
@@ -266,7 +277,8 @@
     mix_grad_ref,
     wide_ref,
     stat_ref,
-    table_ref,
+    small_ref,
+    lane_ref,
     bucket_ref,
     wide_grad_ref,
     table_grad_ref,
@@ -274,7 +286,7 @@
 ):
     pairs = mix_grad_ref.shape[0] // TGT
     for group in range(GROUPS):
-        bias = self_bias(table_ref, bucket_ref, group)
+        bias = self_bias(small_ref, lane_ref, group)
         score_total = None
         for pair in range(pairs):
             queries, keys, values = self_pieces(pair, group, wide_ref)
@@ -324,11 +336,11 @@
     table_grad_ref[...] = lax.fori_loop(0, BUCKETS, one_bucket, jnp.zeros((HEADS, TGT), f32))
 
 
-def self_backward(lengths, mix_grad, wide, stats, table, buckets):
+def self_backward(lengths, mix_grad, wide, stats, small, lanes, buckets):
     return vmem_call(
         self_backward_kernel,
         [(wide.shape, bf16), ((HEADS, TGT), f32)],
-        [mix_grad, wide, stats, table, buckets],
+        [mix_grad, wide, stats, small, lanes, buckets],
         [lengths],
         [pltpu.VMEM((HEADS, TGT, TGT), f32)],
         name="self_backward",
@@ -337,7 +349,7 @@
 
 
 def input_grads_kernel(wide_grad_ref, weight_ref, gain_ref, row_ref, grad_ref, out_ref, gain_grad_ref):
-    norm_grad = contract(wide_grad_ref[...], weight_ref[:, : D + 2 * KEYS], 1, 1)
+    norm_grad = contract(wide_grad_ref[...], weight_ref[...], 1, 1)
     back, gain_grad_ref[...] = norm_pull(row_ref[...].astype(f32), gain_ref[0:1, :], norm_grad)
     out_ref[...] = (grad_ref[...] + back).astype(bf16)
 
@@ -490,13 +502,17 @@
     )(info, queries, grads, memory_parts, *earlier)
 
 
-def ffn_kernel(row_ref, cotangent_ref, gate_ref, up_ref, down_ref, *rest):
-    row_grad_ref, branch_ref, rows_ref, hidden_ref, gate_grad_ref, up_grad_ref = rest[-6:]
+def ffn_kernel(me_ref, row_ref, cotangent_ref, gate_ref, up_ref, down_ref, *rest):
+    row_grad_ref, branch_ref, rows_ref, kept_cotangent_ref, hidden_ref, gate_grad_ref, up_grad_ref = rest[
+        -7:
+    ]
     rows = row_ref[...]
     rows_ref[0] = rows
     gate = matmul(rows, gate_ref[...])
     up = matmul(rows, up_ref[...])
-    hidden_grad = contract(cotangent_ref[...], down_ref[...], 1, 1)
+    cotangent = cotangent_ref[0]
+    kept_cotangent_ref[0] = cotangent
+    hidden_grad = contract(cotangent, down_ref[...], 1, 1)
     square = gate * gate
     slope = 0.7978845608028654
     bend = jnp.tanh(slope * gate * (1.0 + 0.044715 * square))
@@ -508,67 +524,72 @@
     up_grad = (hidden_grad * value).astype(bf16)
     row_grad = contract(gate_grad, gate_ref[...], 1, 1) + contract(up_grad, up_ref[...], 1, 1)
     row_grad_ref[...] = row_grad.astype(bf16)
-    branch_ref[...] = matmul(hidden, down_ref[...]).astype(bf16)
+    branch_ref[0] = matmul(hidden, down_ref[...]).astype(bf16)
     hidden_ref[0] = hidden
     gate_grad_ref[0] = gate_grad
     up_grad_ref[0] = up_grad
 
 
-def ffn_chunk(chunk, chunks, rows, cotangent, gate, up, down, *earlier):
+def ffn_chunk(chunk, chunks, me, rows, cotangent, gate, up, down, *earlier):
     count, width = rows.shape
     wide = gate.shape[1]
-    kept = [width, wide, wide, wide]
+    kept = [width, width, width, wide, wide, wide]
+    by_line = pl.BlockSpec((1, count, width), lambda step, me: (me[1] ^ chunk, 0, 0))
+
+    def whole(array):
+        return pl.BlockSpec(array.shape, lambda step, me: (0, 0))
+
     return pl.pallas_call(
         ffn_kernel,
-        grid=(1,),
-        in_specs=[
-            pl.BlockSpec((count, width), lambda step: (0, 0)),
-            pl.BlockSpec((count, width), lambda step: (0, 0)),
-            pl.BlockSpec(gate.shape, lambda step: (0, 0)),
-            pl.BlockSpec(up.shape, lambda step: (0, 0)),
-            pl.BlockSpec(down.shape, lambda step: (0, 0)),
-        ]
-        + [pl.BlockSpec(memory_space=pl.ANY)] * len(earlier),
-        out_specs=[pl.BlockSpec((count, width), lambda step: (0, 0))] * 2
-        + [pl.BlockSpec((1, count, size), lambda step: (chunk, 0, 0)) for size in kept],
-        out_shape=[jax.ShapeDtypeStruct((count, width), bf16)] * 2
+        grid_spec=pltpu.PrefetchScalarGridSpec(
+            num_scalar_prefetch=1,
+            grid=(1,),
+            in_specs=[whole(rows), by_line]
+            + [whole(array) for array in (gate, up, down)]
+            + [ANYWHERE] * len(earlier),
+            out_specs=[whole(rows), by_line]
+            + [pl.BlockSpec((1, count, size), lambda step, me: (chunk, 0, 0)) for size in kept[1:]],
+        ),
+        out_shape=[jax.ShapeDtypeStruct((count, width), bf16)]
         + [jax.ShapeDtypeStruct((chunks, count, size), bf16) for size in kept],
-        input_output_aliases={5 + place: 2 + place for place in range(len(earlier))},
+        input_output_aliases={6 + place: 1 + place for place in range(len(earlier))},
         compiler_params=pltpu.CompilerParams(vmem_limit_bytes=VMEM),
         cost_estimate=pl.CostEstimate(flops=3000000000, bytes_accessed=8000000, transcendentals=0),
         name="ffn_chunk",
-    )(rows, cotangent, gate, up, down, *earlier)
+    )(me, rows, cotangent, gate, up, down, *earlier)
 
 
 def exchange(value, axis, size, mask):
     return lax.ppermute(value, axis, [(place, place ^ mask) for place in range(size)])
 
 
-def gather_chunks(value, size):
+def visit_chunks(value, size, work):
     lines = size // 2
-    if lines != 4:
-        return [value] + [exchange(value, "ffn", size, 2 * step) for step in range(1, lines)]
 
     def by_lines(array, pairs):
         pairs = [(2 * old + core, 2 * new + core) for old, new in pairs for core in range(2)]
         return lax.ppermute(array, "ffn", pairs)
 
+    if lines != 4:
+        chunks = [value] + [exchange(value, "ffn", size, 2 * step) for step in range(1, lines)]
+        return [work(chunk, one) for chunk, one in enumerate(chunks)]
     across = exchange(value, "ffn", size, 4)
     beside = exchange(value, "ffn", size, 2)
     middle = by_lines(value, [(1, 2), (2, 1)])
+    results = [work(0, value)]
+    across = after(across, results[0])
     onward = by_lines(across, [(2, 3), (1, 0)])
+    results.append(work(1, after(beside, across)))
+    results.append(work(2, across))
     line = lax.axis_index("ffn") // 2
-    return [value, beside, across, jnp.where((line == 0) | (line == 3), onward, middle)]
+    results.append(work(3, jnp.where((line == 0) | (line == 3), onward, middle)))
+    return results
 
 
 def return_chunks(parts, size):
     return [parts[0]] + [
         exchange(parts[step], "ffn", size, 2 * step) for step in range(1, size // 2)
     ]
-
-
-def join_sums(parts):
-    return functools.reduce(jnp.add, [part.astype(f32) for part in parts])
 
 
 def reduce_rows(grads, tok_size, ffn_size):
@@ -611,85 +632,103 @@
     return total
 
 
-def memory_forward_kernel(own_ref, other_ref, weight_ref, out_ref):
-    pairs, held, width = own_ref.shape
-    for place, ref in enumerate((own_ref, other_ref)):
-        part = matmul(ref[...].reshape(pairs * held, width), weight_ref[...]).astype(bf16)
+def memory_forward_kernel(me_ref, own_ref, other_ref, weight_ref, out_ref):
+    pairs, held, width = other_ref.shape
+    for place, rows in enumerate((own_ref[0, 0], other_ref[...])):
+        part = matmul(rows.reshape(pairs * held, width), weight_ref[...]).astype(bf16)
         out_ref[:, place] = part.reshape(pairs, held, part.shape[1])
 
 
-def memory_forward(own, other, weights, column):
-    pairs, held, width = own.shape
-    step = 4 if pairs % 4 == 0 else 1
-    block = pl.BlockSpec((step, held, width), lambda pair: (pair, 0, 0))
+def own_pairs(memory):
+    unused, also, step, held, width = memory.shape
+    return pl.BlockSpec((1, 1, step, held, width), lambda line, me: (line, me[2], 0, 0, 0))
+
+
+def memory_forward(me, memory, other, weights):
+    lines, unused, step, held, width = memory.shape
     return pl.pallas_call(
         memory_forward_kernel,
-        grid=(pairs // step,),
-        in_specs=[
-            block,
-            block,
-            pl.BlockSpec((width, 2 * KEYS), lambda pair: (0, column // (2 * KEYS))),
-        ],
-        out_specs=pl.BlockSpec((step, 2, held, 2 * KEYS), lambda pair: (pair, 0, 0, 0)),
-        out_shape=jax.ShapeDtypeStruct((pairs, 2, held, 2 * KEYS), bf16),
+        grid_spec=pltpu.PrefetchScalarGridSpec(
+            num_scalar_prefetch=1,
+            grid=(lines,),
+            in_specs=[
+                own_pairs(memory),
+                pl.BlockSpec((step, held, width), lambda line, me: (line, 0, 0)),
+                pl.BlockSpec((width, 2 * KEYS), lambda line, me: (0, 0)),
+            ],
+            out_specs=pl.BlockSpec((step, 2, held, 2 * KEYS), lambda line, me: (line, 0, 0, 0)),
+        ),
+        out_shape=jax.ShapeDtypeStruct((lines * step, 2, held, 2 * KEYS), bf16),
         compiler_params=pltpu.CompilerParams(vmem_limit_bytes=VMEM),
         cost_estimate=pl.CostEstimate(flops=8600000000, bytes_accessed=18000000, transcendentals=0),
         name="memory_forward",
-    )(own, other, weights)
-
-
-def memory_backward_kernel(sizes, me_ref, own_ref, other_ref, grad_ref, weight_ref, *rest):
-    own_grad_ref, other_grad_ref, sum_ref, total = rest
+    )(me, memory, other, weights)
+
+
+def memory_backward_kernel(
+    sizes, me_ref, own_ref, other_ref, grad_ref, weight_ref, mix_ref, low_ref, *rest
+):
+    own_grad_ref, other_grad_ref, kept_ref, sent_ref, total = rest
     step = pl.program_id(0)
-    pairs, held, width = own_ref.shape
-    for place, (ref, out_ref) in enumerate(((own_ref, own_grad_ref), (other_ref, other_grad_ref))):
+    pairs, held, width = other_ref.shape
+    for place, (rows, out_ref) in enumerate(
+        ((own_ref[0, 0], own_grad_ref), (other_ref[...], other_grad_ref))
+    ):
         grads = grad_ref[:, place].reshape(pairs * held, grad_ref.shape[3])
         out = contract(grads, weight_ref[...], 1, 1).astype(bf16)
         out_ref[...] = out.reshape(out_ref.shape)
-        part = contract(ref[...].reshape(pairs * held, width), grads, 0, 0)
+        part = contract(rows.reshape(pairs * held, width), grads, 0, 0)
         if place == 0:
             total[...] = jnp.where(step == 0, part, total[...] + part)
         else:
             total[...] += part
 
+    @pl.when(step == 0)
+    def first():
+        low = low_ref[...]
+        for start in range(0, low.shape[1], 512):
+            part = matmul(mix_ref[...].astype(bf16), low[:, start : start + 512])
+            store_blocks(sizes, me_ref, kept_ref, sent_ref, 2 * KEYS + start, part)
+
     @pl.when(step == pl.num_programs(0) - 1)
     def last():
-        store_blocks(sizes, me_ref, sum_ref, 0, total[...])
-
-
-def memory_backward(sizes, me, own, other, grads, weights, column):
-    lines = sizes[1] // 2
-    pairs, held, width = own.shape
-    step = pairs // lines
+        store_blocks(sizes, me_ref, kept_ref, sent_ref, 0, total[...])
+
+
+def memory_backward(sizes, me, memory, other, grads, weights, mixed, low):
+    lines, unused, step, held, width = memory.shape
     block = pl.BlockSpec((step, held, width), lambda line, me: (line, 0, 0))
-    shape = blocks_shape(sizes, 2 * KEYS)
+    shape = blocks_shape(sizes, 2 * KEYS + low.shape[1])
     return pl.pallas_call(
         functools.partial(memory_backward_kernel, sizes),
         grid_spec=pltpu.PrefetchScalarGridSpec(
             num_scalar_prefetch=1,
             grid=(lines,),
             in_specs=[
-                block,
+                own_pairs(memory),
                 block,
                 pl.BlockSpec((step, 2, held, 2 * KEYS), lambda line, me: (line, 0, 0, 0)),
-                pl.BlockSpec((width, 2 * KEYS), lambda line, me: (0, column // (2 * KEYS))),
+                pl.BlockSpec((width, 2 * KEYS), lambda line, me: (0, 0)),
+                pl.BlockSpec(mixed.shape, lambda line, me: (0, 0)),
+                pl.BlockSpec(low.shape, lambda line, me: (0, 0)),
             ],
             out_specs=[
-                pl.BlockSpec((1, 1, step, held, width), lambda line, me: (line, me[2], 0, 0, 0)),
+                own_pairs(memory),
                 block,
-                pl.BlockSpec(shape, lambda line, me: (0,) * len(shape)),
-            ],
+            ]
+            + [pl.BlockSpec(shape, lambda line, me: (0,) * len(shape))] * 2,
             scratch_shapes=[pltpu.VMEM((width, 2 * KEYS), f32)],
         ),
         out_shape=[
-            jax.ShapeDtypeStruct((lines, 2, step, held, width), bf16),
-            jax.ShapeDtypeStruct(own.shape, bf16),
+            jax.ShapeDtypeStruct(memory.shape, bf16),
+            jax.ShapeDtypeStruct(other.shape, bf16),
+            jax.ShapeDtypeStruct(shape, bf16),
             jax.ShapeDtypeStruct(shape, bf16),
         ],
         compiler_params=pltpu.CompilerParams(vmem_limit_bytes=VMEM),
         cost_estimate=pl.CostEstimate(flops=17200000000, bytes_accessed=28000000, transcendentals=0),
         name="memory_backward",
-    )(me, own, other, grads, weights)
+    )(me, memory, other, grads, weights, mixed, low)
 
 
 def place_pairs_kernel(me_ref, pair_ref, unused_ref, out_ref):
@@ -720,23 +759,25 @@
 
 def blocks_shape(sizes, columns):
     tok_size, ffn_size = sizes
-    return (2, tok_size * ffn_size // 2, D // (tok_size * ffn_size), columns)
-
-
-def store_blocks(sizes, me_ref, out_ref, column, value):
+    return (tok_size * ffn_size // 2, D // (tok_size * ffn_size), columns)
+
+
+def store_blocks(sizes, me_ref, kept_ref, sent_ref, column, value):
     tok_size, ffn_size = sizes
     rows = D // (tok_size * ffn_size)
     low = value.astype(bf16)
-    for block in range(tok_size * ffn_size):
-        tok, line, core = block // ffn_size, block % ffn_size // 2, block % 2
+    columns = slice(column, column + value.shape[1])
+    for block in range(0, tok_size * ffn_size, 2):
+        tok, line = block // ffn_size, block % ffn_size // 2
         place = (tok ^ me_ref[0]) * (ffn_size // 2) + (line ^ me_ref[1])
-        out_ref[core ^ me_ref[2], place, :, column : column + value.shape[1]] = low[
-            block * rows : (block + 1) * rows
-        ]
+        first = low[block * rows : (block + 1) * rows]
+        second = low[(block + 1) * rows : (block + 2) * rows]
+        kept_ref[place, :, columns] = jnp.where(me_ref[2] == 0, first, second)
+        sent_ref[place, :, columns] = jnp.where(me_ref[2] == 0, second, first)
 
 
 def grad_blocks_kernel(sizes, dims, me_ref, *refs):
-    out_ref = refs[-1]
+    kept_ref, sent_ref = refs[-2:]
     column = 0
     for place, (left_dim, right_dim) in enumerate(dims):
         left, right = refs[2 * place], refs[2 * place + 1]
@@ -745,34 +786,31 @@
                 part = right[:, start : start + 512]
             else:
                 part = right[start : start + 512, :]
-            store_blocks(
-                sizes, me_ref, out_ref, column, contract(left[...], part, left_dim, right_dim)
-            )
+            product = contract(left[...], part, left_dim, right_dim)
+            store_blocks(sizes, me_ref, kept_ref, sent_ref, column, product)
             column += 512
-    for ref in refs[2 * len(dims) : -1]:
-        if len(ref.shape) == 4:
-            out_ref[:, :, :, column : column + ref.shape[3]] = ref[...]
-            column += ref.shape[3]
-        else:
-            filled = jnp.concatenate(
-                [ref[...], jnp.zeros((SMALL - ref.shape[0], ref.shape[1]), f32)], axis=0
-            )
-            store_blocks(sizes, me_ref, out_ref, column, filled.T)
-            column += SMALL
+    extra = refs[2 * len(dims) : -2]
+    if len(extra) == 2:
+        kept_ref[:, :, column:] = extra[0][...]
+        sent_ref[:, :, column:] = extra[1][...]
+    elif extra:
+        rows = extra[0][...]
+        filled = jnp.concatenate([rows, jnp.zeros((SMALL - rows.shape[0], D), f32)], axis=0)
+        store_blocks(sizes, me_ref, kept_ref, sent_ref, column, filled.T)
 
 
 def grad_blocks(sizes, me, products, *extra):
     operands = [array for left, right, unused, also in products for array in (left, right)]
     columns = sum(right.shape[1 - dim] for unused, right, also, dim in products)
-    for array in extra:
-        operands.append(array)
-        columns += array.shape[3] if array.ndim == 4 else SMALL
+    operands += extra
+    if extra:
+        columns += extra[0].shape[2] if extra[0].ndim == 3 else SMALL
     return pl.pallas_call(
         functools.partial(grad_blocks_kernel, sizes, [(one[2], one[3]) for one in products]),
         in_specs=[pl.BlockSpec(memory_space=pltpu.SMEM)]
         + [pl.BlockSpec(memory_space=pltpu.VMEM)] * len(operands),
-        out_specs=pl.BlockSpec(memory_space=pltpu.VMEM),
-        out_shape=jax.ShapeDtypeStruct(blocks_shape(sizes, columns), bf16),
+        out_specs=[pl.BlockSpec(memory_space=pltpu.VMEM)] * 2,
+        out_shape=[jax.ShapeDtypeStruct(blocks_shape(sizes, columns), bf16)] * 2,
         compiler_params=pltpu.CompilerParams(vmem_limit_bytes=VMEM),
         name="grad_blocks",
     )(me, *operands)
@@ -782,99 +820,103 @@
     return functools.reduce(jnp.add, [part.astype(f32) for part in parts]).astype(bf16)
 
 
-def reduce_core(sizes, blocks):
+def reduce_core(sizes, blocks, earlier=()):
     lines = sizes[1] // 2
-    other = exchange(blocks[1], "ffn", sizes[1], 1)
+    kept, sent = blocks
+    other = after(exchange(sent, "ffn", sizes[1], 1), earlier)
     return [
-        plus(blocks[0, tok * lines : (tok + 1) * lines], other[tok * lines : (tok + 1) * lines])
+        plus(kept[tok * lines : (tok + 1) * lines], other[tok * lines : (tok + 1) * lines])
         for tok in range(4)
     ]
 
 
-def reduce_corner(sizes, parts):
+def reduce_corner(sizes, parts, earlier=()):
     own, by_x, by_y, across = parts
     half = sizes[1] // 4
     top = exchange(across[:half], "tok", sizes[0], 1)
     bottom = exchange(across[half:], "tok", sizes[0], 2)
+    top, bottom = after([top, bottom], earlier)
     by_x = jnp.concatenate([by_x[:half], plus(by_x[half:], bottom)], axis=0)
     by_y = jnp.concatenate([plus(by_y[:half], top), by_y[half:]], axis=0)
     return [own, by_x, by_y]
 
 
-def reduce_sides(sizes, parts):
+def reduce_sides(sizes, parts, earlier=()):
     own, by_x, by_y = parts
-    return plus(own, exchange(by_x, "tok", sizes[0], 1), exchange(by_y, "tok", sizes[0], 2))
-
-
-def reduce_line(sizes, total):
+    arrived = [exchange(by_x, "tok", sizes[0], 1), exchange(by_y, "tok", sizes[0], 2)]
+    return plus(own, *after(arrived, earlier))
+
+
+def reduce_line(sizes, total, earlier=()):
     parts = [total[0]] + [
         exchange(total[step], "ffn", sizes[1], 2 * step) for step in range(1, sizes[1] // 2)
     ]
+    parts = after(parts, earlier)
     return functools.reduce(jnp.add, [part.astype(f32) for part in parts])
 
 
-def place_rows_kernel(sizes, share, me_ref, *refs):
-    tok_size, ffn_size = sizes
-    lines = ffn_size // 2
-    half = lines // 2
-    out_ref, sems = refs[-2:]
+def place_pieces(sizes, share, me_ref, pieces, column, target_ref, sems):
+    columns = pl.ds(column, target_ref.shape[1])
     copies = []
-    for core in range(2):
-        line_ref, x_ref, y_ref, top_ref, bottom_ref = refs[5 * core : 5 * core + 5]
-        for tok in range(4):
-            for line in range(lines):
-                if tok < 3:
-                    source = (line_ref, x_ref, y_ref)[tok].at[line]
-                else:
-                    source = top_ref.at[line] if line < half else bottom_ref.at[line - half]
-                block = ((tok ^ me_ref[0]) * lines + (line ^ me_ref[1])) * 2 + (core ^ me_ref[2])
-                target = out_ref.at[pl.ds(pl.multiple_of(block * share, share), share), :]
-                copies.append(pltpu.make_async_copy(source, target, sems.at[len(copies)]))
+    if len(pieces) == 1:
+        copies.append(pltpu.make_async_copy(pieces[0].at[:, columns], target_ref, sems.at[0]))
+    else:
+        lines = sizes[1] // 2
+        half = lines // 2
+        for core in range(2):
+            line_ref, x_ref, y_ref, top_ref, bottom_ref = pieces[5 * core : 5 * core + 5]
+            for tok in range(4):
+                for line in range(lines):
+                    if tok < 3:
+                        source = (line_ref, x_ref, y_ref)[tok].at[line]
+                    else:
+                        source = top_ref.at[line] if line < half else bottom_ref.at[line - half]
+                    block = ((tok ^ me_ref[0]) * lines + (line ^ me_ref[1])) * 2 + (core ^ me_ref[2])
+                    target = target_ref.at[pl.ds(pl.multiple_of(block * share, share), share), :]
+                    copies.append(
+                        pltpu.make_async_copy(source.at[:, columns], target, sems.at[len(copies)])
+                    )
     for copy in copies:
         copy.start()
     for copy in copies:
         copy.wait()
 
 
-def place_rows(sizes, me, held, share, columns):
-    count = sizes[0] * sizes[1]
-    return pl.pallas_call(
-        functools.partial(place_rows_kernel, sizes, share),
-        in_specs=[pl.BlockSpec(memory_space=pltpu.SMEM)]
-        + [pl.BlockSpec(memory_space=pl.ANY)] * len(held),
-        out_specs=pl.BlockSpec(memory_space=pltpu.VMEM),
-        out_shape=jax.ShapeDtypeStruct((count * share, columns), bf16),
-        scratch_shapes=[pltpu.SemaphoreType.DMA((count,))],
-        compiler_params=pltpu.CompilerParams(vmem_limit_bytes=VMEM),
+def place_rows_kernel(sizes, share, starts, me_ref, *refs):
+    pieces, outs, sems = refs[: -len(starts) - 1], refs[-len(starts) - 1 : -1], refs[-1]
+    for column, out_ref in zip(starts, outs, strict=True):
+        place_pieces(sizes, share, me_ref, pieces, column, out_ref, sems)
+
+
+def place_rows(sizes, share, me, pieces, starts, columns):
+    return vmem_call(
+        functools.partial(place_rows_kernel, sizes, share, starts),
+        [((sizes[0] * sizes[1] * share, columns), bf16) for unused in starts],
+        [(piece, ANYWHERE) for piece in pieces],
+        [me],
+        [pltpu.SemaphoreType.DMA((sizes[0] * sizes[1],))],
         name="place_rows",
-    )(me, *held)
+    )
 
 
 def after(values, earlier):
     return lax.optimization_barrier((values, earlier))[0]
 
 
-def gather_blocks(sizes, me, packs, between):
+def gather_pieces(sizes, pack, beside):
     tok_size, ffn_size = sizes
     lines = ffn_size // 2
     half = lines // 2
-    stages = [(), (), (), ()]
-    for place, pack in enumerate(packs):
-        share, columns = pack.shape
-        pack = after(pack, stages[0])
-        line = [pack] + [exchange(pack, "ffn", ffn_size, 2 * step) for step in range(1, lines)]
-        stages[0] = line
-        line = jnp.stack(after(line, stages[1]))
-        by_x = exchange(line, "tok", tok_size, 1)
-        by_y = exchange(line, "tok", tok_size, 2)
-        stages[1] = [by_x, by_y]
-        by_x, by_y = after([by_x, by_y], stages[2])
-        top = exchange(by_y[:half], "tok", tok_size, 1)
-        bottom = exchange(by_x[half:], "tok", tok_size, 2)
-        stages[2] = [top, bottom]
-        held = after([line, by_x, by_y, top, bottom], stages[3])
-        held = held + [exchange(one, "ffn", ffn_size, 1) for one in held]
-        stages[3] = between(place, place_rows(sizes, me, held, share, columns), stages[0])
+    line = [pack] + [exchange(pack, "ffn", ffn_size, 2 * step) for step in range(1, lines)]
+    line, extra = lax.optimization_barrier((line, beside(())))
+    begun = line
+    line = jnp.stack(line)
+    by_x = exchange(line, "tok", tok_size, 1)
+    by_y = exchange(line, "tok", tok_size, 2)
+    top = exchange(by_y[:half], "tok", tok_size, 1)
+    bottom = exchange(by_x[half:], "tok", tok_size, 2)
+    held = [line, by_x, by_y, top, bottom]
+    return held + [exchange(one, "ffn", ffn_size, 1) for one in held], extra, begun
 
 
 def on_device(
@@ -921,68 +963,49 @@
 
     core = me_ffn % 2
     lines = ffn_size // 2
-
-    def by_parity(array, parity):
-        array = array.reshape((lines, 2, pair_count) + array.shape[1:])
-        array = lax.dynamic_index_in_dim(array, parity, 1, keepdims=False)
-        return array.reshape((lines * pair_count,) + array.shape[2:])
-
-    memory_own = by_parity(memory, core)
-    memory_other = exchange(by_parity(memory, 1 - core), "ffn", ffn_size, 1)
-    both_gate = jnp.concatenate([ffn_gate, exchange(ffn_gate, "ffn", ffn_size, 1)], axis=1)
-    both_up = jnp.concatenate([ffn_up, exchange(ffn_up, "ffn", ffn_size, 1)], axis=1)
-    both_down = jnp.concatenate([ffn_down, exchange(ffn_down, "ffn", ffn_size, 1)], axis=0)
-
-    packs = [
-        jnp.concatenate(parts, axis=1)
-        for parts in (
-            [self_query, self_key, self_value, small],
-            [self_output, cross_query],
-            [cross_key, cross_value, cross_output],
-        )
-    ]
+    both = ("tok", "ffn")
+    pack = jnp.concatenate(
+        [self_query, self_key, self_value, small, self_output, cross_query, cross_key, cross_value],
+        axis=1,
+    )
+    same_core = [[2 * line + one for line in range(lines)] for one in range(2)]
+    memory_lines = memory.reshape(lines, 2, pair_count, held, D)
+
+    def swap_memory(begun):
+        sent = lax.dynamic_index_in_dim(after(memory_lines, begun), 1 - core, 1, keepdims=False)
+        return exchange(sent.reshape(lines * pair_count, held, D), "ffn", ffn_size, 1)
+
+    if direct:
+        pieces, memory_other, begun = gather_pieces(sizes, pack, swap_memory)
+    else:
+        pieces = [lax.all_gather(pack, both, axis=0, tiled=True)]
+        memory_other = swap_memory(pieces)
+        begun = pieces
+    cotangents = lax.all_gather(
+        after(out_grad, begun),
+        "ffn",
+        axis=0,
+        tiled=False,
+        axis_index_groups=same_core,
+    )
+
+    per_table = BUCKETS * HEADS // devices
     buckets = buckets.T
-    kept = {}
-
-    def begin(place, pack, begun):
-        if place == 0:
-            full_small = pack[:, D + 2 * KEYS : D + 2 * KEYS + len(per_row)].T.astype(f32)
-            table = full_small[3].reshape(devices, share)[:, :table_share].reshape(HEADS, BUCKETS)
-            kept["table"] = jnp.pad(table, ((0, 0), (0, TGT - BUCKETS)))
-            lengths = (full_small[4] * 64 + full_small[5]).astype(jnp.int32)
-            kept["lengths"] = lengths.reshape(devices, share)[:, :pair_count]
-            kept["gains"] = full_small[:3]
-            kept["self"] = self_forward(
-                target_lengths,
-                after(targets, (both_gate, both_up, both_down, memory_other, memory_own)),
-                pack,
-                kept["gains"],
-                kept["table"],
-                buckets,
-            )
-            result = kept["self"][2]
-        elif place == 1:
-            kept["output"] = self_output_part(targets, kept["self"][2], pack, kept["gains"])
-            result = kept["output"][2]
-        else:
-            kept["cotangents"] = gather_chunks(after(out_grad, begun), ffn_size)
-            kept["memory"] = memory_forward(memory_own, memory_other, pack, 0)
-            result = kept["memory"]
-        kept[place] = pack
-        return result
-
-    if direct:
-        gather_blocks(sizes, me, packs, begin)
-    else:
-        for place, pack in enumerate(packs):
-            begin(place, lax.all_gather(pack, ("tok", "ffn"), axis=0, tiled=True), pack)
-    full_first, full_second, full_third = kept[0], kept[1], kept[2]
-    gains, table, lengths = kept["gains"], kept["table"], kept["lengths"]
-    cotangent_chunks = kept["cotangents"]
-    normed_one, self_wide, self_mixed, self_stats = kept["self"]
-    hidden_one, normed_two, cross_queries, self_squares = kept["output"]
-    memory_parts = kept["memory"].reshape(-1, 2 * held, 2 * KEYS)
-    cross_weight = full_third[:, 2 * KEYS :]
+    lanes_of = buckets // per_table * (2 * per_table) + buckets % per_table
+    normed_one, self_wide, self_mixed, self_stats, small_rows = self_forward(
+        sizes, share, me, target_lengths, targets, lanes_of, pieces
+    )
+    hidden_one, normed_two, cross_queries, self_squares = self_output_part(
+        sizes, share, me, targets, self_mixed, small_rows, pieces
+    )
+    gains = small_rows[:3]
+    lengths = (small_rows[4] * 64 + small_rows[5]).astype(jnp.int32)
+    lengths = lengths.reshape(devices, share)[:, :pair_count]
+    (memory_weights,) = place_rows(
+        sizes, share, me, after(pieces, cross_queries), (3 * D + 2 * KEYS + SMALL,), 2 * KEYS
+    )
+    memory_parts = memory_forward(me, memory_lines, memory_other, memory_weights)
+    memory_parts = memory_parts.reshape(-1, 2 * held, 2 * KEYS)
     lengths = lax.dynamic_index_in_dim(
         lengths.reshape(tok_size, ffn_size, pair_count), me_tok, 0, keepdims=False
     )
@@ -1000,38 +1023,51 @@
 
     position = jnp.arange(TGT)
 
-    cross_queries = after(cross_queries, cotangent_chunks)
-    query_chunks = gather_chunks(cross_queries, ffn_size)
-    mixed_parts = []
-    for chunk in range(lines):
-        chunk_queries = query_chunks[chunk]
+    query_chunks, mixed_parts, kept = [], [], {}
+    kept["output"] = lax.all_gather(
+        after(cross_output, (self_mixed, cotangents)), both, axis=0, tiled=True
+    )
+
+    def visit_forward(chunk, chunk_queries):
+        query_chunks.append(chunk_queries)
         if chunk:
             chunk_queries = after(chunk_queries, mixed_parts[-1])
+        if chunk == lines - 1:
+            chunk_queries = after(chunk_queries, (kept["placed"], kept["units"]))
         mixed_parts.append(cross_forward(chunk, info, chunk_queries, memory_parts))
+        if chunk == 1:
+            held_pieces, units = after((pieces, (ffn_gate, ffn_up, ffn_down)), mixed_parts[1])
+            kept["placed"] = place_rows(
+                sizes, share, me, held_pieces, (0, D + 2 * KEYS + SMALL), 2 * D
+            )
+            kept["units"] = [
+                jnp.concatenate([array, exchange(array, "ffn", ffn_size, 1)], axis=dim)
+                for array, dim in zip(units, (1, 1, 0), strict=True)
+            ]
+        return mixed_parts[-1]
+
+    visit_chunks(cross_queries, ffn_size, visit_forward)
+    output_weights = kept["output"]
+    full_first, full_second = kept["placed"]
+    both_gate, both_up, both_down = kept["units"]
     cross_mixed, cross_stats, hidden_two, normed_three, cross_squares = cross_join(
-        hidden_one, gains, cross_weight, return_chunks(mixed_parts, ffn_size)
-    )
-
-    row_chunks = gather_chunks(normed_three, ffn_size)
-    earlier, row_parts, branch_parts = [], [], []
-    for chunk in range(lines):
-        row_part, branch_part, *earlier = ffn_chunk(
-            chunk,
-            lines,
-            row_chunks[chunk],
-            cotangent_chunks[chunk],
-            both_gate,
-            both_up,
-            both_down,
-            *earlier,
+        hidden_one, gains, output_weights, return_chunks(mixed_parts, ffn_size)
+    )
+
+    earlier, row_parts = [], []
+
+    def visit_ffn(chunk, rows):
+        row_part, *earlier[:] = ffn_chunk(
+            chunk, lines, me, rows, cotangents, both_gate, both_up, both_down, *earlier
         )
         row_parts.append(row_part)
-        branch_parts.append(branch_part)
+        return row_part
+
+    visit_chunks(normed_three, ffn_size, visit_ffn)
     row_parts = return_chunks(row_parts, ffn_size)
-    all_rows, hidden, gate_grad, up_grad = [
-        array.reshape(lines * row_count, array.shape[2]) for array in earlier
+    branch_part, all_rows, all_cotangent, hidden, gate_grad, up_grad = [
+        array.reshape(lines * row_count, array.shape[2]) for array in after(earlier, row_parts[1])
     ]
-    all_cotangent = jnp.concatenate(cotangent_chunks, axis=0)
     units = ffn_gate.shape[1]
     weight_grads = []
     for part, dim in (
@@ -1047,60 +1083,94 @@
 
     row_parts = row_parts[:2] + after(row_parts[2:], weight_grads)
     hidden_two_grad, cross_low, grad_pack, gain_ffn_grad = ffn_join(
-        out_grad, hidden_two, gains, cross_weight, cross_mixed, cross_stats, row_parts
-    )
-    output_product = (cross_mixed.astype(bf16), cross_low, 1, 0)
-    stage = [grad_blocks(sizes, me, [output_product])] if direct else [()]
-    grad_chunks = gather_chunks(grad_pack, ffn_size)
-    earlier = []
-    query_parts = []
-    reductions = [reduce_core, reduce_corner, reduce_sides, reduce_line]
-    for chunk in range(lines):
-        part, memory_grads = cross_backward(
-            chunk,
-            info,
-            after(query_chunks[chunk], stage[-1]),
-            grad_chunks[chunk],
-            memory_parts,
-            *earlier,
+        out_grad, hidden_two, gains, output_weights, cross_mixed, cross_stats, row_parts
+    )
+    earlier, query_parts = [], []
+
+    def visit_backward(chunk, grads):
+        part, *earlier[:] = cross_backward(
+            chunk, info, query_chunks[chunk], grads, memory_parts, *earlier
         )
-        earlier = [memory_grads]
         query_parts.append(part)
-        if direct and chunk < 4:
-            stage.append(reductions[chunk](sizes, stage[-1]))
-    for reduction in reductions[lines:] if direct else ():
-        stage.append(reduction(sizes, stage[-1]))
-    output_sum = stage[-1]
+        return part
+
+    visit_chunks(grad_pack, ffn_size, visit_backward)
+    memory_grads = earlier[0]
     query_parts = return_chunks(query_parts, ffn_size)
-    memory_grad, other_grad, memory_sum = memory_backward(
+    memory_grad, other_grad, *memory_sum = memory_backward(
         sizes,
         me,
-        memory_own,
+        memory_lines,
         memory_other,
         after(memory_grads, query_parts[1]).reshape(-1, 2, held, 2 * KEYS),
-        full_third,
-        0,
-    )
-    query_parts = query_parts[:2] + after(query_parts[2:], (memory_sum, output_sum, weight_sums))
+        memory_weights,
+        cross_mixed,
+        cross_low,
+    )
+    query_parts = query_parts[:2] + after(query_parts[2:], (memory_sum, weight_sums))
     query_grads, hidden_one_grad, self_low, mix_grad, gain_cross_grad = query_join(
         hidden_two_grad, hidden_one, gains, full_second, query_parts
     )
     other_grad = exchange(other_grad, "ffn", ffn_size, 1)
     memory_grad = place_pairs(me, memory_grad, other_grad).reshape(memory.shape)
     products = [(normed_two, query_grads, 0, 1), (self_mixed, self_low, 0, 0)]
-    middle = ()
+    outer = middle = memory_sum
     if direct:
-        middle = grad_blocks(sizes, me, products, memory_sum)
-        mix_grad = after(mix_grad, (middle, other_grad))
-        middle = reduce_core(sizes, middle)
+        middle = grad_blocks(sizes, me, products)
+        outer = reduce_core(sizes, after(memory_sum, query_grads), middle)
+        mix_grad = after(mix_grad, (middle, outer))
     wide_grad, table_grad = self_backward(
-        target_lengths, mix_grad, self_wide, self_stats, table, buckets
-    )
-    wide_grad = after(wide_grad, middle)
+        target_lengths, mix_grad, self_wide, self_stats, small_rows, lanes_of, buckets
+    )
+    if direct:
+        outer = reduce_corner(sizes, outer, wide_grad)
+        middle = reduce_core(sizes, middle, wide_grad)
+        wide_grad = after(wide_grad, (outer, middle))
     targets_grad, gain_self_grad = input_grads(wide_grad, full_first, gains, targets, hidden_one_grad)
 
-    branch_parts = after(branch_parts, query_grads)
-    ffn_branch = join_sums(return_chunks(branch_parts, ffn_size))
+    branch_sum = lax.psum_scatter(
+        after(branch_part, query_grads),
+        "ffn",
+        scatter_dimension=0,
+        tiled=True,
+        axis_index_groups=same_core,
+    )
+    table_grad = jnp.pad(
+        table_grad[:, :BUCKETS].reshape(devices, table_share), ((0, 0), (0, share - table_share))
+    )
+    small_grads = jnp.concatenate(
+        [gain_self_grad, gain_cross_grad, gain_ffn_grad, table_grad.reshape(1, D), jnp.zeros((4, D), f32)]
+    )
+    last_product = (normed_one, wide_grad, 0, 0)
+    if direct:
+        first = grad_blocks(sizes, me, [last_product], small_grads)
+        outer = reduce_sides(sizes, outer, first)
+        middle = reduce_corner(sizes, middle, first)
+        first = reduce_core(sizes, first, memory_grad)
+        outer_sum = reduce_line(sizes, outer, first)
+        middle = reduce_sides(sizes, middle, first)
+        first = reduce_corner(sizes, first, middle)
+        first = reduce_sides(sizes, first)
+        middle_sum = reduce_line(sizes, middle, (first, branch_sum))
+        first_sum = reduce_line(sizes, first)
+        branch_sum = after(branch_sum, first)
+    else:
+        order = [(block // ffn_size, block % ffn_size // 2, block % 2) for block in range(devices)]
+        memory_rows = jnp.concatenate(
+            [
+                jnp.stack(memory_sum)[core ^ me[2], (tok ^ me[0]) * lines + (line ^ me[1])]
+                for tok, line, core in order
+            ]
+        )
+        outer_sum, middle_sum, first_sum = [
+            reduce_rows(jnp.concatenate(parts, axis=1), tok_size, ffn_size)
+            for parts in (
+                [memory_rows],
+                [contract(*one) for one in products],
+                [contract(*last_product), jnp.pad(small_grads.T, ((0, 0), (0, SMALL - 8)))],
+            )
+        ]
+    ffn_branch = branch_sum.astype(f32)
     hidden_three = hidden_two + ffn_branch
     layer_out = hidden_three.astype(jnp.bfloat16)
     valid = position[None, :] < target_lengths[:, None]
@@ -1115,38 +1185,6 @@
     squares = jnp.sum(jnp.where(valid[:, None, :], squares, 0.0), axis=2)
     rms_values = jnp.sqrt(squares / counted[:, None])
 
-    table_grad = jnp.pad(
-        table_grad[:, :BUCKETS].reshape(devices, table_share), ((0, 0), (0, share - table_share))
-    )
-    small_rows = jnp.concatenate(
-        [gain_self_grad, gain_cross_grad, gain_ffn_grad, table_grad.reshape(1, D), jnp.zeros((4, D), f32)]
-    )
-    last_product = (normed_one, wide_grad, 0, 0)
-    if direct:
-        middle = reduce_corner(sizes, middle)
-        first = grad_blocks(sizes, me, [last_product], after(small_rows, middle))
-        first = reduce_core(sizes, first)
-        middle = reduce_sides(sizes, middle)
-        first = reduce_corner(sizes, first)
-        first = reduce_sides(sizes, first)
-        middle_sum = reduce_line(sizes, middle)
-        first_sum = reduce_line(sizes, first)
-    else:
-        order = [(block // ffn_size, block % ffn_size // 2, block % 2) for block in range(devices)]
-        memory_rows = jnp.concatenate(
-            [
-                memory_sum[core ^ me[2], (tok ^ me[0]) * (ffn_size // 2) + (line ^ me[1])]
-                for tok, line, core in order
-            ]
-        )
-        output_sum, middle_sum, first_sum = [
-            reduce_rows(jnp.concatenate(parts, axis=1), tok_size, ffn_size)
-            for parts in (
-                [contract(*output_product)],
-                [contract(*one) for one in products] + [memory_rows],
-                [contract(*last_product), jnp.pad(small_rows.T, ((0, 0), (0, SMALL - 8)))],
-            )
-        ]
     small_sum = first_sum[:, D + 2 * KEYS :]
     return (
         layer_out,
@@ -1162,9 +1200,9 @@
         first_sum[:, D + KEYS : D + 2 * KEYS],
         middle_sum[:, D : 2 * D],
         middle_sum[:, :D],
-        middle_sum[:, 2 * D : 2 * D + KEYS],
-        middle_sum[:, 2 * D + KEYS :],
-        output_sum,
+        outer_sum[:, :KEYS],
+        outer_sum[:, KEYS : 2 * KEYS],
+        outer_sum[:, 2 * KEYS :],
         gate_weight_grad,
         up_weight_grad,
         down_weight_grad,

time: 701 us -> 613 us (0.87)
  starting transfers between devices: 143 us -> 107 us
  waiting for transfers between devices: 234 us -> 202 us
  local copies, waits for them, and re-layouts: 48.9 us -> 37.9 us
    ppermute x88 -> x59, starting transfers between devices: 133 us -> 91.7 us  [exchange(): lax.ppermute(value, axis, [(place, place ^ mask) for place in range(size)])]
    ppermute x8 -> x6, waiting for transfers between devices: 29.1 us -> 0.02 us  [by_lines(): return lax.ppermute(array, 'ffn', pairs)]
    pallas_call x7 -> x9, Pallas kernels: 44.5 us -> 59.8 us  [vmem_call(): pl.pallas_call(body, in_specs=[pl.BlockSpec(memory_space=pltpu.SMEM)] * l...]
    pallas_call x8 -> x5, Pallas kernels: 56.7 us -> 43.1 us  [the longest x4 29.4 us: ffn_chunk(): pl.pallas_call(ffn_kernel, grid_spec=pltpu.PrefetchScalarGridSpec(num_sca...]
    squeeze x3 -> x0, local copies, waits for them, and re-layouts: 8.04 us -> none  [reduce_core(): other = exchange(blocks[1], 'ffn', sizes[1], 1)]
    ppermute x8 -> x6, starting transfers between devices: 9.99 us -> 15.3 us  [by_lines(): return lax.ppermute(array, 'ffn', pairs)]
    pallas_call x3 -> x2, Pallas kernels: 14.5 us -> 9.66 us  [grad_blocks(): pl.pallas_call(functools.partial(grad_blocks_kernel, sizes, [(one[2], one...]
    ppermute x88 -> x59, waiting for transfers between devices: 205 us -> 202 us  [exchange(): lax.ppermute(value, axis, [(place, place ^ mask) for place in range(size)])]
  transfers between devices with their start and end apart: 97 -> 69, of which waited for: 35 -> 22; matrix products, arithmetic and copies ran while one was open for 7% -> 9% of each run, Pallas kernels for 24% -> 32%
where the time goes in v3:
time: 613 us; the launch traced here: 608 us
  Pallas kernels  208 us (34%)
  waiting for transfers between devices  202 us (33%)
  starting transfers between devices  107 us (17%)
  local copies, waits for them, and re-layouts  37.9 us (6%)
  other arithmetic  29.4 us (5%)
  between operations  15.2 us (2%)
  matrix products  7.64 us (1%)
    ppermute x59, waiting for transfers between devices, exchange(): lax.ppermute(value, axis, [(place, place ^ mask) for place in range(size)])  202 us
    ppermute x59, starting transfers between devices, exchange(): lax.ppermute(value, axis, [(place, place ^ mask) for place in range(size)])  91.7 us
    pallas_call x9, Pallas kernels, vmem_call(): pl.pallas_call(body, in_specs=[pl.BlockSpec(memory_space=pltpu.SMEM)] * l...  59.8 us
    pallas_call x4, Pallas kernels, cross_backward(): pl.pallas_call(functools.partial(cross_backward_kernel, chunk), grid_spec...  34.4 us
    pallas_call x4, Pallas kernels, cross_forward(): pl.pallas_call(functools.partial(cross_forward_kernel, chunk), grid_spec=...  29.5 us
    pallas_call x4, Pallas kernels, ffn_chunk(): pl.pallas_call(ffn_kernel, grid_spec=pltpu.PrefetchScalarGridSpec(num_sca...  29.4 us
    pallas_call x1, Pallas kernels, memory_backward(): pl.pallas_call(functools.partial(memory_backward_kernel, sizes), grid_spe...  26.4 us
    ppermute x6, starting transfers between devices, by_lines(): return lax.ppermute(array, 'ffn', pairs)  15.3 us
  transfers between devices with their start and end apart: 69, of which 22 were waited for; matrix products, arithmetic and copies ran while one was open for 9% of the time, Pallas kernels for 32%

profile of v3, /device:TPU:0, one launch (start us, length us, event | category | flops | bytes accessed | tf_op | source)
XLA Modules:
  0.0 607.6 jit_solution(1814791963417298588)
XLA Ops:
  7.4 4.8 constant_dynamic-slice_fusion.1
  13.0 4.7 collective-permute-start.2
  18.3 8.2 %collective-permute-done.2 = bf16[32,5248]{1,0:T(8,128)(2,1)S(1)} collective-permute-done((bf16[32,5248]{1,0:T(8,128)(2,1)S(1)}, bf16[32,5248]{1,0:T(8,128)(2,1)S(1)}, u32[]{:S(2)}, u32[]{:S(2)}) %collective-permute-start.2) | collective-permute-done | bytes 335904 | tf_op jit(solution)/shard_map/ppermute | solution.py:563
  26.5 20.4 %collective-permute-done.1 = bf16[32,5248]{1,0:T(8,128)(2,1)S(1)} collective-permute-done((bf16[32,5248]{1,0:T(8,128)(2,1)S(1)}, bf16[32,5248]{1,0:T(8,128)(2,1)S(1)}, u32[]{:S(2)}, u32[]{:S(2)}) %collective-permute-start.1) | collective-permute-done | bytes 335904 | tf_op jit(solution)/shard_map/ppermute | solution.py:563
  50.3 28.0 %collective-permute-done.5.refs_2_ = bf16[4,32,5248]{2,1,0:T(8,128)(2,1)S(1)} collective-permute-done((bf16[4,32,5248]{2,1,0:T(8,128)(2,1)S(1)}, bf16[4,32,5248]{2,1,0:T(8,128)(2,1)S(1)}, u32[]{:S(2)}, u32[]{:S(2)}) %collective-permute-start.5) | collective-permute-done | bytes 1343520 | tf_op jit(solution)/shard_map/ppermute | solution.py:563
  85.2 10.2 %collective-permute-done.6.refs_3_ = bf16[2,32,5248]{2,1,0:T(8,128)(2,1)S(1)} collective-permute-done((bf16[2,32,5248]{2,1,0:T(8,128)(2,1)}, bf16[2,32,5248]{2,1,0:T(8,128)(2,1)S(1)}, u32[]{:S(2)}, u32[]{:S(2)}) %collective-permute-start.6) | collective-permute-done | bytes 671776 | tf_op jit(solution)/shard_map/ppermute | solution.py:563
  95.4 3.3 collective-permute-done.7.refs_4_
  101.9 7.4 %self_forward.1 = (bf16[256,1024]{1,0:T(8,128)(2,1)}, bf16[256,2048]{1,0:T(8,128)(2,1)}, bf16[256,1024]{1,0:T(8,128)(2,1)}, f32[32,128]{1,0:T(8,128)}, f32[8,1024]{1,0:T(8,128)}) custom-call(s32[3]{0:T(128)} %pad_add_fusion.1.me_ref, s32[2]{0:T(128)} %length_ref.3, bf16[256,1024]{1,0:T(8,128)(2,1)} %row_ref.5, s32[128,128]{1,0:T(8,128)} %fusion.6.lane_ref, ...), custom_call_target="tpu_custom_call" | custom-call | flops 1000000000 | bytes 8000000 | tf_op jit(solution)/shard_map/self_forward/pallas_call | solution.py:41
  109.3 6.2 %self_output.1 = (f32[256,1024]{1,0:T(8,128)}, bf16[256,1024]{1,0:T(8,128)(2,1)}, bf16[1024,256]{1,0:T(8,128)(2,1)}, f32[256,1]{1,0:T(8,128)}) custom-call(s32[3]{0:T(128)} %pad_add_fusion.1.me_ref, bf16[256,1024]{1,0:T(8,128)(2,1)} %row_ref.5, bf16[256,1024]{1,0:T(8,128)(2,1)} %get-tuple-element.180.mix_ref.refs_2_, ...), custom_call_target="tpu_custom_call" | custom-call | flops 1000000000 | bytes 8000000 | tf_op jit(solution)/shard_map/self_output/pallas_call | solution.py:41
  116.2 2.4 collective-permute-start.14
  120.9 3.9 place_rows.2.weight_ref
  124.8 13.7 %memory_forward.1 = bf16[8,2,256,1024]{3,2,1,0:T(8,128)(2,1)} custom-call(s32[3]{0:T(128)} %pad_add_fusion.1.me_ref, bf16[4,2,2,256,1024]{4,3,2,1,0:T(8,128)(2,1)} %bitcast.78, bf16[8,256,1024]{2,1,0:T(8,128)(2,1)} %collective-permute-done.3.other_ref, bf16[1024,1024]{1,0:T(8,128)(2,1)} %place_rows.2.weight_ref), custom_call_target="tpu_custom_call" | custom-call | flops 8600000512 | bytes 18000000 | tf_op jit(solution)/shard_map/memory_forward/pallas_call | solution.py:649
  139.3 7.3 %cross_forward.4.refs_0_ = bf16[1072,256]{1,0:T(8,128)(2,1)} custom-call(s32[4,5]{1,0:T(4,128)} %pad_add_fusion.info_ref, bf16[1024,256]{1,0:T(8,128)(2,1)} %get-tuple-element.185.query_ref, bf16[8,512,1024]{2,1,0:T(8,128)(2,1)} %bitcast.94), custom_call_target="tpu_custom_call" | custom-call | flops 6000000000 | bytes 4000000 | tf_op jit(solution)/shard_map/cross_forward/pallas_call | solution.py:428
  146.6 7.5 %collective-permute-done.14.query_ref = bf16[1024,256]{1,0:T(8,128)(2,1)} collective-permute-done((bf16[1024,256]{1,0:T(8,128)(2,1)}, bf16[1024,256]{1,0:T(8,128)(2,1)}, u32[]{:S(2)}, u32[]{:S(2)}) %collective-permute-start.14) | collective-permute-done | bytes 524320 | tf_op jit(solution)/shard_map/ppermute | solution.py:563
  156.4 7.3 %cross_forward.5 = bf16[1072,256]{1,0:T(8,128)(2,1)} custom-call(s32[4,5]{1,0:T(4,128)} %pad_add_fusion.info_ref, bf16[1024,256]{1,0:T(8,128)(2,1)} %copy-done.55, bf16[8,512,1024]{2,1,0:T(8,128)(2,1)} %bitcast.95), custom_call_target="tpu_custom_call" | custom-call | flops 6000000000 | bytes 4000000 | tf_op jit(solution)/shard_map/cross_forward/pallas_call | solution.py:428
  167.4 8.7 %place_rows.3 = (bf16[1024,2048]{1,0:T(8,128)(2,1)}, bf16[1024,2048]{1,0:T(8,128)(2,1)}) custom-call(s32[3]{0:T(128)} %pad_add_fusion.1.me_ref, bf16[4,32,5248]{2,1,0:T(8,128)(2,1)} %copy-done, bf16[4,32,5248]{2,1,0:T(8,128)(2,1)} %collective-permute-done.4.refs_1_, bf16[4,32,5248]{2,1,0:T(8,128)(2,1)} %copy-done.2, bf16[2,32,5248]{2,1,0:T(8,128)(2,1)} %copy-done.7, ...), custom_call_target="tpu_custom_call" | custom-call | flops 1000000000 | bytes 8000000 | tf_op jit(solution)/shard_map/place_rows/pallas_call | solution.py:41
  177.3 7.3 %cross_forward.6 = bf16[1072,256]{1,0:T(8,128)(2,1)} custom-call(s32[4,5]{1,0:T(4,128)} %pad_add_fusion.info_ref, bf16[1024,256]{1,0:T(8,128)(2,1)} %collective-permute-done.14.query_ref, bf16[8,512,1024]{2,1,0:T(8,128)(2,1)} %bitcast.96), custom_call_target="tpu_custom_call" | custom-call | flops 6000000000 | bytes 4000000 | tf_op jit(solution)/shard_map/cross_forward/pallas_call | solution.py:428
  184.6 3.5 collective-permute-start.15
  190.0 2.3 copy.99
  192.2 2.3 copy.101
  199.3 7.5 %cross_forward.7 = bf16[1072,256]{1,0:T(8,128)(2,1)} custom-call(s32[4,5]{1,0:T(4,128)} %pad_add_fusion.info_ref, bf16[1024,256]{1,0:T(8,128)(2,1)} %broadcast_select_fusion.2.query_ref, bf16[8,512,1024]{2,1,0:T(8,128)(2,1)} %bitcast.97), custom_call_target="tpu_custom_call" | custom-call | flops 6000000000 | bytes 4000000 | tf_op jit(solution)/shard_map/cross_forward/pallas_call | solution.py:428
  206.8 2.5 collective-permute-start.22
  209.9 18.3 %collective-permute-done.16.refs_2_ = bf16[1072,256]{1,0:T(8,128)(2,1)} collective-permute-done((bf16[1072,256]{1,0:T(8,128)(2,1)}, bf16[1072,256]{1,0:T(8,128)(2,1)}, u32[]{:S(2)}, u32[]{:S(2)}) %collective-permute-start.16) | collective-permute-done | bytes 548896 | tf_op jit(solution)/shard_map/ppermute | solution.py:563
  229.0 5.0 cross_join.1
  234.0 12.2 %collective-permute-start.23 = (bf16[256,1024]{1,0:T(8,128)(2,1)}, bf16[256,1024]{1,0:T(8,128)(2,1)S(1)}, u32[]{:S(2)}, u32[]{:S(2)}) collective-permute-start(bf16[256,1024]{1,0:T(8,128)(2,1)} %get-tuple-element.219.row_ref), channel_id=1, source_target_pairs={{0,4},{1,5},{2,6},{3,7},{4,0},{5,1},{6,2},{7,3},{8,12},{9,13},{10,... | collective-permute-start | bytes 1572872 | tf_op jit(solution)/shard_map/ppermute | solution.py:563
  246.9 7.3 %ffn_chunk.4 = (bf16[256,1024]{1,0:T(8,128)(2,1)}, bf16[4,256,1024]{2,1,0:T(8,128)(2,1)}, bf16[4,256,1024]{2,1,0:T(8,128)(2,1)}, bf16[4,256,1024]{2,1,0:T(8,128)...) custom-call(s32[3]{0:T(128)} %pad_add_fusion.1.me_ref, ...), custom_call_target="tpu_custom_call" | custom-call | flops 3000000000 | bytes 8000000 | tf_op jit(solution)/shard_map/ffn_chunk/pallas_call | solution.py:542
  254.2 16.2 %collective-permute-done.23.row_ref = bf16[256,1024]{1,0:T(8,128)(2,1)S(1)} collective-permute-done((bf16[256,1024]{1,0:T(8,128)(2,1)}, bf16[256,1024]{1,0:T(8,128)(2,1)S(1)}, u32[]{:S(2)}, u32[]{:S(2)}) %collective-permute-start.23) | collective-permute-done | bytes 524320 | tf_op jit(solution)/shard_map/ppermute | solution.py:563
  270.4 10.0 %collective-permute-start.24 = (bf16[256,1024]{1,0:T(8,128)(2,1)S(1)}, bf16[256,1024]{1,0:T(8,128)(2,1)S(1)}, u32[]{:S(2)}, u32[]{:S(2)}) collective-permute-start(bf16[256,1024]{1,0:T(8,128)(2,1)S(1)} %collective-permute-done.23.row_ref), channel_id=1, source_target_pairs={{4,6},{5,7},{2,0},{3,1},{12,14},{13,15},{10,8},{11,9},{20,22},{21,... | collective-permute-start | bytes 1572872 | tf_op jit(solution)/shard_map/ppermute | solution.py:571
  281.2 7.4 %ffn_chunk.5 = (bf16[256,1024]{1,0:T(8,128)(2,1)}, bf16[4,256,1024]{2,1,0:T(8,128)(2,1)}, bf16[4,256,1024]{2,1,0:T(8,128)(2,1)}, bf16[4,256,1024]{2,1,0:T(8,128)...) custom-call(s32[3]{0:T(128)} %pad_add_fusion.1.me_ref, ...), custom_call_target="tpu_custom_call", output_to_operand_aliasing={{1}: (6, {}), {2}: (7, {}), {3}: (8, {}), {4}: (9, {}), {5}... | custom-call | flops 3000000000 | bytes 8000000 | tf_op jit(solution)/shard_map/ffn_chunk/pallas_call | solution.py:542
  288.6 2.8 collective-permute-start.27
  291.4 7.4 %ffn_chunk.6 = (bf16[256,1024]{1,0:T(8,128)(2,1)}, bf16[4,256,1024]{2,1,0:T(8,128)(2,1)}, bf16[4,256,1024]{2,1,0:T(8,128)(2,1)}, bf16[4,256,1024]{2,1,0:T(8,128)...) custom-call(s32[3]{0:T(128)} %pad_add_fusion.1.me_ref, ...), custom_call_target="tpu_custom_call", output_to_operand_aliasing={{1}: (6, {}), {2}: (7, {}), {3}: (8, {}), {4}: (9, {}), {5}... | custom-call | flops 3000000000 | bytes 8000000 | tf_op jit(solution)/shard_map/ffn_chunk/pallas_call | solution.py:542
  299.6 7.4 %ffn_chunk.7 = (bf16[256,1024]{1,0:T(8,128)(2,1)}, bf16[4,256,1024]{2,1,0:T(8,128)(2,1)}, bf16[4,256,1024]{2,1,0:T(8,128)(2,1)}, bf16[4,256,1024]{2,1,0:T(8,128)...) custom-call(s32[3]{0:T(128)} %pad_add_fusion.1.me_ref, ...), custom_call_target="tpu_custom_call", output_to_operand_aliasing={{1}: (6, {}), {2}: (7, {}), {3}: (8, {}), {4}: (9, {}), {5}... | custom-call | flops 3000000000 | bytes 8000000 | tf_op jit(solution)/shard_map/ffn_chunk/pallas_call | solution.py:542
  307.0 4.0 convolution_bitcast_fusion.2
  321.7 31.5 %collective-permute-done.28.refs_2_ = bf16[256,1024]{1,0:T(8,128)(2,1)S(1)} collective-permute-done((bf16[256,1024]{1,0:T(8,128)(2,1)S(1)}, bf16[256,1024]{1,0:T(8,128)(2,1)S(1)}, u32[]{:S(2)}, u32[]{:S(2)}) %collective-permute-start.28) | collective-permute-done | bytes 524320 | tf_op jit(solution)/shard_map/ppermute | solution.py:563
  354.2 5.1 ffn_join.1
  360.0 14.3 %collective-permute-start.34 = (bf16[1120,256]{1,0:T(8,128)(2,1)}, bf16[1120,256]{1,0:T(8,128)(2,1)S(1)}, u32[]{:S(2)}, u32[]{:S(2)}) collective-permute-start(bf16[1120,256]{1,0:T(8,128)(2,1)} %get-tuple-element.261.grad_ref), channel_id=1, source_target_pairs={{0,4},{1,5},{2,6},{3,7},{4,0},{5,1},{6,2},{7,3},{8,12},{9,13},{10,... | collective-permute-start | bytes 1720328 | tf_op jit(solution)/shard_map/ppermute | solution.py:563
  374.3 8.6 %cross_backward.4 = (bf16[1024,256]{1,0:T(8,128)(2,1)}, bf16[8,512,1024]{2,1,0:T(8,128)(2,1)}) custom-call(s32[4,5]{1,0:T(4,128)} %pad_add_fusion.info_ref, bf16[1024,256]{1,0:T(8,128)(2,1)} %get-tuple-element.185.query_ref, bf16[1120,256]{1,0:T(8,128)(2,1)} %get-tuple-element.261.grad_ref, bf16[8,512,1024]{2,1,0:T(8,128)(2,1)} %bitcast.98), custom_call_target="tpu_custom_call" | custom-call | flops 10000000000 | bytes 8000000 | tf_op jit(solution)/shard_map/cross_backward/pallas_call | solution.py:481
  382.9 29.0 %collective-permute-done.34.grad_ref = bf16[1120,256]{1,0:T(8,128)(2,1)S(1)} collective-permute-done((bf16[1120,256]{1,0:T(8,128)(2,1)}, bf16[1120,256]{1,0:T(8,128)(2,1)S(1)}, u32[]{:S(2)}, u32[]{:S(2)}) %collective-permute-start.34) | collective-permute-done | bytes 573472 | tf_op jit(solution)/shard_map/ppermute | solution.py:563
  414.5 8.6 %cross_backward.5 = (bf16[1024,256]{1,0:T(8,128)(2,1)}, bf16[8,512,1024]{2,1,0:T(8,128)(2,1)}) custom-call(s32[4,5]{1,0:T(4,128)} %pad_add_fusion.info_ref, bf16[1024,256]{1,0:T(8,128)(2,1)} %copy-done.55, bf16[1120,256]{1,0:T(8,128)(2,1)} %copy-done.54, bf16[8,512,1024]{2,1,0:T(8,128)(2,1)} %bitcast.99, ...), custom_call_target="tpu_custom_call", output_to_operand_aliasing={{1}: (4, {})} | custom-call | flops 10000000000 | bytes 8000000 | tf_op jit(solution)/shard_map/cross_backward/pallas_call | solution.py:481
  423.0 2.7 collective-permute-start.35
  425.8 8.7 %cross_backward.6 = (bf16[1024,256]{1,0:T(8,128)(2,1)}, bf16[8,512,1024]{2,1,0:T(8,128)(2,1)}) custom-call(s32[4,5]{1,0:T(4,128)} %pad_add_fusion.info_ref, bf16[1024,256]{1,0:T(8,128)(2,1)} %collective-permute-done.14.query_ref, bf16[1120,256]{1,0:T(8,128)(2,1)} %copy-done.53, bf16[8,512,1024]{2,1,0:T(8,128)(2,1)} %bitcast.100, ...), custom_call_target="tpu_custom_call", output_to_operand_aliasing={{1}: (4, {})} | custom-call | flops 10000000000 | bytes 8000000 | tf_op jit(solution)/shard_map/cross_backward/pallas_call | solution.py:481
  436.0 8.6 %cross_backward.7 = (bf16[1024,256]{1,0:T(8,128)(2,1)}, bf16[8,512,1024]{2,1,0:T(8,128)(2,1)}) custom-call(s32[4,5]{1,0:T(4,128)} %pad_add_fusion.info_ref, bf16[1024,256]{1,0:T(8,128)(2,1)} %broadcast_select_fusion.2.query_ref, bf16[1120,256]{1,0:T(8,128)(2,1)} %broadcast_select_fusion.grad_ref, ...), custom_call_target="tpu_custom_call", output_to_operand_aliasing={{1}: (4, {})} | custom-call | flops 10000000000 | bytes 8000000 | tf_op jit(solution)/shard_map/cross_backward/pallas_call | solution.py:481
  446.4 26.4 %memory_backward.1 = (bf16[4,2,2,256,1024]{4,3,2,1,0:T(8,128)(2,1)}, bf16[8,256,1024]{2,1,0:T(8,128)(2,1)}, bf16[16,32,2048]{2,1,0:T(8,128)(2,1)}, bf16[16,32,2048]{2,1,0:T(8,128)(2,1)}) custom-call(s32[3]{0:T(128)} %pad_add_fusion.1.me_ref, bf16[4,2,2,256,1024]{4,3,2,1,0:T(8,128)(2,1)} %bitcast.79, bf16[8,256,1024]{2,1,0:T(8,128)(2,1)} %collective-permute-done.3.other_ref, ...), custom_call_target="tpu_custom_call" | custom-call | flops 17200001024 | bytes 28000000 | tf_op jit(solution)/shard_map/memory_backward/pallas_call | solution.py:702
  473.8 6.0 query_join.1
  479.9 4.9 grad_blocks.2
  491.0 3.0 add_convert_fusion.11
  495.1 12.2 %self_backward.1 = (bf16[256,2048]{1,0:T(8,128)(2,1)}, f32[16,128]{1,0:T(8,128)}) custom-call(s32[2]{0:T(128)} %length_ref.3, bf16[256,1024]{1,0:T(8,128)(2,1)} %get-tuple-element.289.mix_grad_ref, bf16[256,2048]{1,0:T(8,128)(2,1)} %get-tuple-element.290.wide_ref, f32[32,128]{1,0:T(8,128)} %get-tuple-element.291.stat_ref, ...), custom_call_target="tpu_custom_call" | custom-call | flops 8000000000 | bytes 8000000 | tf_op jit(solution)/shard_map/self_backward/pallas_call | solution.py:41
  510.3 3.1 add_convert_fusion.7
  520.0 5.4 input_grads.1
  526.7 4.8 grad_blocks.3
  537.6 2.1 collective-permute-start.64
  539.7 8.7 %collective-permute-start.63 = (bf16[32,2048]{1,0:T(8,128)(2,1)}, bf16[32,2048]{1,0:T(8,128)(2,1)S(1)}, u32[]{:S(2)}, u32[]{:S(2)}) collective-permute-start(bf16[32,2048]{1,0:T(8,128)(2,1)} %get-tuple-element.380), channel_id=1, source_target_pairs={{0,4},{1,5},{2,6},{3,7},{4,0},{5,1},{6,2},{7,3},{8,12},{9,13},{10,... | collective-permute-start | bytes 393224 | tf_op jit(solution)/shard_map/ppermute | solution.py:563
  548.4 5.5 place_pairs.1
  554.6 2.5 collective-permute-done.63
  557.1 2.5 collective-permute-done.62
  562.3 5.9 collective-permute-done.47
  570.7 2.1 collective-permute-start.59
  572.8 2.4 collective-permute-start.57
  575.8 5.5 collective-permute-done.52
  582.6 2.0 multiply_reduce_fusion
  585.3 2.0 collective-permute-start.56
  587.4 2.4 collective-permute-start.54
  590.5 3.2 collective-permute-done.56
  593.7 4.3 collective-permute-done.55
  (336 shorter events, 91.5 us)
Async XLA Ops:
  7.2 131.3 %all-gather.6.cloned.1.call-start = ((), (), s32[]{:S(2)}) async-start(), calls=%async_computation.3 | async-start | bytes 2621440 | tf_op jit(solution)/shard_map/all_gather | solution.py:984
  12.1 34.8 %collective-permute-start.3 = (bf16[8,256,1024]{2,1,0:T(8,128)(2,1)}, bf16[8,256,1024]{2,1,0:T(8,128)(2,1)}, u32[]{:S(2)}, u32[]{:S(2)}) collective-permute-start(bf16[8,256,1024]{2,1,0:T(8,128)(2,1)} %bitcast.11), channel_id=1, source_target_pairs={{0,1},{1,0},{2,3},{3,2},{4,5},{5,4},{6,7},{7,6},{8,9},{9,8},{10,11... | collective-permute-start | bytes 12582920 | tf_op jit(solution)/shard_map/ppermute | solution.py:563
  13.0 13.6 %collective-permute-start.2 = (bf16[32,5248]{1,0:T(8,128)(2,1)S(1)}, bf16[32,5248]{1,0:T(8,128)(2,1)S(1)}, u32[]{:S(2)}, u32[]{:S(2)}) collective-permute-start(bf16[32,5248]{1,0:T(8,128)(2,1)S(1)} %constant_dynamic-update-slice_fusion), channel_id=1, source_target_pairs={{0,6},{1,7},{2,4},{3,5},{4,2},{5,3},{6,0},{7,1},{8,14},{9,15},{10,... | collective-permute-start | bytes 1007624 | tf_op jit(solution)/shard_map/ppermute | solution.py:563
  17.6 29.3 %collective-permute-start.1 = (bf16[32,5248]{1,0:T(8,128)(2,1)S(1)}, bf16[32,5248]{1,0:T(8,128)(2,1)S(1)}, u32[]{:S(2)}, u32[]{:S(2)}) collective-permute-start(bf16[32,5248]{1,0:T(8,128)(2,1)S(1)} %constant_dynamic-update-slice_fusion), channel_id=1, source_target_pairs={{0,4},{1,5},{2,6},{3,7},{4,0},{5,1},{6,2},{7,3},{8,12},{9,13},{10,... | collective-permute-start | bytes 1007624 | tf_op jit(solution)/shard_map/ppermute | solution.py:563
  17.6 29.3 %collective-permute-start = (bf16[32,5248]{1,0:T(8,128)(2,1)S(1)}, bf16[32,5248]{1,0:T(8,128)(2,1)S(1)}, u32[]{:S(2)}, u32[]{:S(2)}) collective-permute-start(bf16[32,5248]{1,0:T(8,128)(2,1)S(1)} %constant_dynamic-update-slice_fusion), channel_id=1, source_target_pairs={{0,2},{1,3},{2,0},{3,1},{4,6},{5,7},{6,4},{7,5},{8,10},{9,11},{10,... | collective-permute-start | bytes 1007624 | tf_op jit(solution)/shard_map/ppermute | solution.py:563
  47.2 31.2 %collective-permute-start.5 = (bf16[4,32,5248]{2,1,0:T(8,128)(2,1)S(1)}, bf16[4,32,5248]{2,1,0:T(8,128)(2,1)S(1)}, u32[]{:S(2)}, u32[]{:S(2)}) collective-permute-start(bf16[4,32,5248]{2,1,0:T(8,128)(2,1)S(1)} %pad_maximum_fusion.2.refs_0_), channel_id=1, source_target_pairs={{0,16},{8,24},{16,0},{24,8},{1,17},{9,25},{17,1},{25,9},{2,18},{10... | collective-permute-start | bytes 4030472 | tf_op jit(solution)/shard_map/ppermute | solution.py:563
  48.8 32.0 %collective-permute-start.4 = (bf16[4,32,5248]{2,1,0:T(8,128)(2,1)S(1)}, bf16[4,32,5248]{2,1,0:T(8,128)(2,1)}, u32[]{:S(2)}, u32[]{:S(2)}) collective-permute-start(bf16[4,32,5248]{2,1,0:T(8,128)(2,1)S(1)} %pad_maximum_fusion.2.refs_0_), channel_id=1, source_target_pairs={{0,8},{8,0},{16,24},{24,16},{1,9},{9,1},{17,25},{25,17},{2,10},{10... | collective-permute-start | bytes 4030472 | tf_op jit(solution)/shard_map/ppermute | solution.py:563
  50.3 177.9 %all-gather.4.cloned.1.call-start = ((), (), s32[]{:S(2)}) async-start(), calls=%async_computation.1 | async-start | bytes 2162688 | tf_op jit(solution)/shard_map/all_gather | solution.py:1027
  79.3 16.1 %collective-permute-start.6 = (bf16[2,32,5248]{2,1,0:T(8,128)(2,1)}, bf16[2,32,5248]{2,1,0:T(8,128)(2,1)S(1)}, u32[]{:S(2)}, u32[]{:S(2)}) collective-permute-start(bf16[2,32,5248]{2,1,0:T(8,128)(2,1)} %slice.326), channel_id=1, source_target_pairs={{0,8},{8,0},{16,24},{24,16},{1,9},{9,1},{17,25},{25,17},{2,10},{10... | collective-permute-start | bytes 2015240 | tf_op jit(solution)/shard_map/ppermute | solution.py:563
  82.8 16.0 %collective-permute-start.7 = (bf16[2,32,5248]{2,1,0:T(8,128)(2,1)}, bf16[2,32,5248]{2,1,0:T(8,128)(2,1)}, u32[]{:S(2)}, u32[]{:S(2)}) collective-permute-start(bf16[2,32,5248]{2,1,0:T(8,128)(2,1)} %slice.327), channel_id=1, source_target_pairs={{0,16},{8,24},{16,0},{24,8},{1,17},{9,25},{17,1},{25,9},{2,18},{10... | collective-permute-start | bytes 2015240 | tf_op jit(solution)/shard_map/ppermute | solution.py:563
  84.3 15.8 %collective-permute-start.8 = (bf16[4,32,5248]{2,1,0:T(8,128)(2,1)S(1)}, bf16[4,32,5248]{2,1,0:T(8,128)(2,1)}, u32[]{:S(2)}, u32[]{:S(2)}) collective-permute-start(bf16[4,32,5248]{2,1,0:T(8,128)(2,1)S(1)} %pad_maximum_fusion.2.refs_0_), channel_id=1, source_target_pairs={{0,1},{1,0},{2,3},{3,2},{4,5},{5,4},{6,7},{7,6},{8,9},{9,8},{10,11... | collective-permute-start | bytes 4030472 | tf_op jit(solution)/shard_map/ppermute | solution.py:563
  84.3 15.8 %collective-permute-start.10 = (bf16[4,32,5248]{2,1,0:T(8,128)(2,1)S(1)}, bf16[4,32,5248]{2,1,0:T(8,128)(2,1)}, u32[]{:S(2)}, u32[]{:S(2)}) collective-permute-start(bf16[4,32,5248]{2,1,0:T(8,128)(2,1)S(1)} %collective-permute-done.5.refs_2_), channel_id=1, source_target_pairs={{0,1},{1,0},{2,3},{3,2},{4,5},{5,4},{6,7},{7,6},{8,9},{9,8},{10,11... | collective-permute-start | bytes 4030472 | tf_op jit(solution)/shard_map/ppermute | solution.py:563
  84.8 16.3 %collective-permute-start.9 = (bf16[4,32,5248]{2,1,0:T(8,128)(2,1)}, bf16[4,32,5248]{2,1,0:T(8,128)(2,1)}, u32[]{:S(2)}, u32[]{:S(2)}) collective-permute-start(bf16[4,32,5248]{2,1,0:T(8,128)(2,1)} %collective-permute-done.4.refs_1_), channel_id=1, source_target_pairs={{0,1},{1,0},{2,3},{3,2},{4,5},{5,4},{6,7},{7,6},{8,9},{9,8},{10,11... | collective-permute-start | bytes 4030472 | tf_op jit(solution)/shard_map/ppermute | solution.py:563
  115.5 69.1 %collective-permute-start.18 = (bf16[1024,256]{1,0:T(8,128)(2,1)}, bf16[1024,256]{1,0:T(8,128)(2,1)S(1)}, u32[]{:S(2)}, u32[]{:S(2)}) collective-permute-start(bf16[1024,256]{1,0:T(8,128)(2,1)} %get-tuple-element.185.query_ref), channel_id=1, source_target_pairs={{2,4},{3,5},{4,2},{5,3},{10,12},{11,13},{12,10},{13,11},{18,20},{1... | collective-permute-start | bytes 1572872 | tf_op jit(solution)/shard_map/ppermute | solution.py:571
  116.2 37.9 %collective-permute-start.14 = (bf16[1024,256]{1,0:T(8,128)(2,1)}, bf16[1024,256]{1,0:T(8,128)(2,1)}, u32[]{:S(2)}, u32[]{:S(2)}) collective-permute-start(bf16[1024,256]{1,0:T(8,128)(2,1)} %get-tuple-element.185.query_ref), channel_id=1, source_target_pairs={{0,4},{1,5},{2,6},{3,7},{4,0},{5,1},{6,2},{7,3},{8,12},{9,13},{10,... | collective-permute-start | bytes 1572872 | tf_op jit(solution)/shard_map/ppermute | solution.py:563
  118.6 37.1 %collective-permute-start.13 = (bf16[1024,256]{1,0:T(8,128)(2,1)}, bf16[1024,256]{1,0:T(8,128)(2,1)S(1)}, u32[]{:S(2)}, u32[]{:S(2)}) collective-permute-start(bf16[1024,256]{1,0:T(8,128)(2,1)} %get-tuple-element.185.query_ref), channel_id=1, source_target_pairs={{0,2},{1,3},{2,0},{3,1},{4,6},{5,7},{6,4},{7,5},{8,10},{9,11},{10,... | collective-permute-start | bytes 1572872 | tf_op jit(solution)/shard_map/ppermute | solution.py:563
  138.5 334.3 %all-reduce.8.cloned.1.call-start = ((), (), s32[]{:S(2)}) async-start(), calls=%async_computation.4 | async-start | bytes 4325376 | tf_op jit(solution)/shard_map/psum | solution.py:1081
  154.1 33.9 %collective-permute-start.17 = (bf16[1024,256]{1,0:T(8,128)(2,1)}, bf16[1024,256]{1,0:T(8,128)(2,1)}, u32[]{:S(2)}, u32[]{:S(2)}) collective-permute-start(bf16[1024,256]{1,0:T(8,128)(2,1)} %collective-permute-done.14.query_ref), channel_id=1, source_target_pairs={{4,6},{5,7},{2,0},{3,1},{12,14},{13,15},{10,8},{11,9},{20,22},{21,... | collective-permute-start | bytes 1572872 | tf_op jit(solution)/shard_map/ppermute | solution.py:571
  163.8 26.2 %collective-permute-start.19 = (bf16[1024,352]{0,1:T(8,128)(2,1)}, bf16[1024,352]{0,1:T(8,128)(2,1)}, u32[]{:S(2)}, u32[]{:S(2)}) collective-permute-start(bf16[1024,352]{0,1:T(8,128)(2,1)} %param.39), channel_id=1, source_target_pairs={{0,1},{1,0},{2,3},{3,2},{4,5},{5,4},{6,7},{7,6},{8,9},{9,8},{10,11... | collective-permute-start | bytes 2162696 | tf_op jit(solution)/shard_map/ppermute | solution.py:563
  165.3 27.0 %collective-permute-start.20 = (bf16[1024,352]{0,1:T(8,128)(2,1)}, bf16[1024,352]{0,1:T(8,128)(2,1)}, u32[]{:S(2)}, u32[]{:S(2)}) collective-permute-start(bf16[1024,352]{0,1:T(8,128)(2,1)} %param.40), channel_id=1, source_target_pairs={{0,1},{1,0},{2,3},{3,2},{4,5},{5,4},{6,7},{7,6},{8,9},{9,8},{10,11... | collective-permute-start | bytes 2162696 | tf_op jit(solution)/shard_map/ppermute | solution.py:563
  167.3 27.2 %collective-permute-start.21 = (bf16[352,1024]{1,0:T(8,128)(2,1)}, bf16[352,1024]{1,0:T(8,128)(2,1)}, u32[]{:S(2)}, u32[]{:S(2)}) collective-permute-start(bf16[352,1024]{1,0:T(8,128)(2,1)} %param.41), channel_id=1, source_target_pairs={{0,1},{1,0},{2,3},{3,2},{4,5},{5,4},{6,7},{7,6},{8,9},{9,8},{10,11... | collective-permute-start | bytes 2162696 | tf_op jit(solution)/shard_map/ppermute | solution.py:563
  184.6 43.6 %collective-permute-start.15 = (bf16[1072,256]{1,0:T(8,128)(2,1)}, bf16[1072,256]{1,0:T(8,128)(2,1)}, u32[]{:S(2)}, u32[]{:S(2)}) collective-permute-start(bf16[1072,256]{1,0:T(8,128)(2,1)} %cross_forward.5), channel_id=1, source_target_pairs={{0,2},{1,3},{2,0},{3,1},{4,6},{5,7},{6,4},{7,5},{8,10},{9,11},{10,... | collective-permute-start | bytes 1646600 | tf_op jit(solution)/shard_map/ppermute | solution.py:563
  188.1 40.1 %collective-permute-start.16 = (bf16[1072,256]{1,0:T(8,128)(2,1)}, bf16[1072,256]{1,0:T(8,128)(2,1)}, u32[]{:S(2)}, u32[]{:S(2)}) collective-permute-start(bf16[1072,256]{1,0:T(8,128)(2,1)} %cross_forward.6), channel_id=1, source_target_pairs={{0,4},{1,5},{2,6},{3,7},{4,0},{5,1},{6,2},{7,3},{8,12},{9,13},{10,... | collective-permute-start | bytes 1646600 | tf_op jit(solution)/shard_map/ppermute | solution.py:563
  206.8 21.4 %collective-permute-start.22 = (bf16[1072,256]{1,0:T(8,128)(2,1)}, bf16[1072,256]{1,0:T(8,128)(2,1)S(1)}, u32[]{:S(2)}, u32[]{:S(2)}) collective-permute-start(bf16[1072,256]{1,0:T(8,128)(2,1)} %cross_forward.7), channel_id=1, source_target_pairs={{0,6},{1,7},{2,4},{3,5},{4,2},{5,3},{6,0},{7,1},{8,14},{9,15},{10,... | collective-permute-start | bytes 1646600 | tf_op jit(solution)/shard_map/ppermute | solution.py:563
  234.0 36.4 %collective-permute-start.23 = (bf16[256,1024]{1,0:T(8,128)(2,1)}, bf16[256,1024]{1,0:T(8,128)(2,1)S(1)}, u32[]{:S(2)}, u32[]{:S(2)}) collective-permute-start(bf16[256,1024]{1,0:T(8,128)(2,1)} %get-tuple-element.219.row_ref), channel_id=1, source_target_pairs={{0,4},{1,5},{2,6},{3,7},{4,0},{5,1},{6,2},{7,3},{8,12},{9,13},{10,... | collective-permute-start | bytes 1572872 | tf_op jit(solution)/shard_map/ppermute | solution.py:563
  246.2 34.2 %collective-permute-start.26 = (bf16[256,1024]{1,0:T(8,128)(2,1)}, bf16[256,1024]{1,0:T(8,128)(2,1)S(1)}, u32[]{:S(2)}, u32[]{:S(2)}) collective-permute-start(bf16[256,1024]{1,0:T(8,128)(2,1)} %get-tuple-element.219.row_ref), channel_id=1, source_target_pairs={{0,2},{1,3},{2,0},{3,1},{4,6},{5,7},{6,4},{7,5},{8,10},{9,11},{10,... | collective-permute-start | bytes 1572872 | tf_op jit(solution)/shard_map/ppermute | solution.py:563
  246.2 52.5 %collective-permute-start.25 = (bf16[256,1024]{1,0:T(8,128)(2,1)}, bf16[256,1024]{1,0:T(8,128)(2,1)S(1)}, u32[]{:S(2)}, u32[]{:S(2)}) collective-permute-start(bf16[256,1024]{1,0:T(8,128)(2,1)} %get-tuple-element.219.row_ref), channel_id=1, source_target_pairs={{2,4},{3,5},{4,2},{5,3},{10,12},{11,13},{12,10},{13,11},{18,20},{1... | collective-permute-start | bytes 1572872 | tf_op jit(solution)/shard_map/ppermute | solution.py:571
  270.4 28.3 %collective-permute-start.24 = (bf16[256,1024]{1,0:T(8,128)(2,1)S(1)}, bf16[256,1024]{1,0:T(8,128)(2,1)S(1)}, u32[]{:S(2)}, u32[]{:S(2)}) collective-permute-start(bf16[256,1024]{1,0:T(8,128)(2,1)S(1)} %collective-permute-done.23.row_ref), channel_id=1, source_target_pairs={{4,6},{5,7},{2,0},{3,1},{12,14},{13,15},{10,8},{11,9},{20,22},{21,... | collective-permute-start | bytes 1572872 | tf_op jit(solution)/shard_map/ppermute | solution.py:571
  288.6 18.4 %collective-permute-start.27 = (bf16[256,1024]{1,0:T(8,128)(2,1)}, bf16[256,1024]{1,0:T(8,128)(2,1)S(1)}, u32[]{:S(2)}, u32[]{:S(2)}) collective-permute-start(bf16[256,1024]{1,0:T(8,128)(2,1)} %get-tuple-element.247), channel_id=1, source_target_pairs={{0,2},{1,3},{2,0},{3,1},{4,6},{5,7},{6,4},{7,5},{8,10},{9,11},{10,... | collective-permute-start | bytes 1572872 | tf_op jit(solution)/shard_map/ppermute | solution.py:563
  311.1 7.1 %collective-permute-start.30 = (bf16[1024,352]{0,1:T(8,128)(2,1)S(1)}, bf16[1024,352]{0,1:T(8,128)(2,1)S(1)}, u32[]{:S(2)}, u32[]{:S(2)}) collective-permute-start(bf16[1024,352]{0,1:T(8,128)(2,1)S(1)} %slice.440), channel_id=1, source_target_pairs={{0,1},{1,0},{2,3},{3,2},{4,5},{5,4},{6,7},{7,6},{8,9},{9,8},{10,11... | collective-permute-start | bytes 2162696 | tf_op jit(solution)/shard_map/ppermute | solution.py:563
  315.8 37.3 %collective-permute-start.28 = (bf16[256,1024]{1,0:T(8,128)(2,1)S(1)}, bf16[256,1024]{1,0:T(8,128)(2,1)S(1)}, u32[]{:S(2)}, u32[]{:S(2)}) collective-permute-start(bf16[256,1024]{1,0:T(8,128)(2,1)S(1)} %copy-done.56), channel_id=1, source_target_pairs={{0,4},{1,5},{2,6},{3,7},{4,0},{5,1},{6,2},{7,3},{8,12},{9,13},{10,... | collective-permute-start | bytes 1572872 | tf_op jit(solution)/shard_map/ppermute | solution.py:563
  316.8 36.4 %collective-permute-start.29 = (bf16[256,1024]{1,0:T(8,128)(2,1)S(1)}, bf16[256,1024]{1,0:T(8,128)(2,1)S(1)}, u32[]{:S(2)}, u32[]{:S(2)}) collective-permute-start(bf16[256,1024]{1,0:T(8,128)(2,1)S(1)} %copy-done.57), channel_id=1, source_target_pairs={{0,6},{1,7},{2,4},{3,5},{4,2},{5,3},{6,0},{7,1},{8,14},{9,15},{10,... | collective-permute-start | bytes 1572872 | tf_op jit(solution)/shard_map/ppermute | solution.py:563
  353.2 229.1 %reduce-scatter.2.cloned.1.call-start = ((), (), s32[]{:S(2)}) async-start(), calls=%async_computation.2 | async-start | bytes 2621440 | tf_op jit(solution)/shard_map/reduce_scatter | solution.py:1131
  359.3 75.8 %collective-permute-start.38 = (bf16[1120,256]{1,0:T(8,128)(2,1)}, bf16[1120,256]{1,0:T(8,128)(2,1)S(1)}, u32[]{:S(2)}, u32[]{:S(2)}) collective-permute-start(bf16[1120,256]{1,0:T(8,128)(2,1)} %get-tuple-element.261.grad_ref), channel_id=1, source_target_pairs={{2,4},{3,5},{4,2},{5,3},{10,12},{11,13},{12,10},{13,11},{18,20},{1... | collective-permute-start | bytes 1720328 | tf_op jit(solution)/shard_map/ppermute | solution.py:571
  360.0 51.9 %collective-permute-start.34 = (bf16[1120,256]{1,0:T(8,128)(2,1)}, bf16[1120,256]{1,0:T(8,128)(2,1)S(1)}, u32[]{:S(2)}, u32[]{:S(2)}) collective-permute-start(bf16[1120,256]{1,0:T(8,128)(2,1)} %get-tuple-element.261.grad_ref), channel_id=1, source_target_pairs={{0,4},{1,5},{2,6},{3,7},{4,0},{5,1},{6,2},{7,3},{8,12},{9,13},{10,... | collective-permute-start | bytes 1720328 | tf_op jit(solution)/shard_map/ppermute | solution.py:563
  374.3 39.3 %collective-permute-start.33 = (bf16[1120,256]{1,0:T(8,128)(2,1)}, bf16[1120,256]{1,0:T(8,128)(2,1)S(1)}, u32[]{:S(2)}, u32[]{:S(2)}) collective-permute-start(bf16[1120,256]{1,0:T(8,128)(2,1)} %get-tuple-element.261.grad_ref), channel_id=1, source_target_pairs={{0,2},{1,3},{2,0},{3,1},{4,6},{5,7},{6,4},{7,5},{8,10},{9,11},{10,... | collective-permute-start | bytes 1720328 | tf_op jit(solution)/shard_map/ppermute | solution.py:563
  411.9 23.1 %collective-permute-start.37 = (bf16[1120,256]{1,0:T(8,128)(2,1)S(1)}, bf16[1120,256]{1,0:T(8,128)(2,1)S(1)}, u32[]{:S(2)}, u32[]{:S(2)}) collective-permute-start(bf16[1120,256]{1,0:T(8,128)(2,1)S(1)} %collective-permute-done.34.grad_ref), channel_id=1, source_target_pairs={{4,6},{5,7},{2,0},{3,1},{12,14},{13,15},{10,8},{11,9},{20,22},{21,... | collective-permute-start | bytes 1720328 | tf_op jit(solution)/shard_map/ppermute | solution.py:571
  423.0 21.6 %collective-permute-start.35 = (bf16[1024,256]{1,0:T(8,128)(2,1)}, bf16[1024,256]{1,0:T(8,128)(2,1)S(1)}, u32[]{:S(2)}, u32[]{:S(2)}) collective-permute-start(bf16[1024,256]{1,0:T(8,128)(2,1)} %get-tuple-element.266), channel_id=1, source_target_pairs={{0,2},{1,3},{2,0},{3,1},{4,6},{5,7},{6,4},{7,5},{8,10},{9,11},{10,... | collective-permute-start | bytes 1572872 | tf_op jit(solution)/shard_map/ppermute | solution.py:563
  434.4 38.4 %collective-permute-start.36 = (bf16[1024,256]{1,0:T(8,128)(2,1)}, bf16[1024,256]{1,0:T(8,128)(2,1)S(1)}, u32[]{:S(2)}, u32[]{:S(2)}) collective-permute-start(bf16[1024,256]{1,0:T(8,128)(2,1)} %get-tuple-element.268), channel_id=1, source_target_pairs={{0,4},{1,5},{2,6},{3,7},{4,0},{5,1},{6,2},{7,3},{8,12},{9,13},{10,... | collective-permute-start | bytes 1572872 | tf_op jit(solution)/shard_map/ppermute | solution.py:563
  444.6 28.2 %collective-permute-start.39 = (bf16[1024,256]{1,0:T(8,128)(2,1)}, bf16[1024,256]{1,0:T(8,128)(2,1)S(1)}, u32[]{:S(2)}, u32[]{:S(2)}) collective-permute-start(bf16[1024,256]{1,0:T(8,128)(2,1)} %get-tuple-element.270), channel_id=1, source_target_pairs={{0,6},{1,7},{2,4},{3,5},{4,2},{5,3},{6,0},{7,1},{8,14},{9,15},{10,... | collective-permute-start | bytes 1572872 | tf_op jit(solution)/shard_map/ppermute | solution.py:563
  479.8 9.7 %collective-permute-start.40 = (bf16[16,32,2048]{2,1,0:T(8,128)(2,1)}, bf16[16,32,2048]{2,1,0:T(8,128)(2,1)}, u32[]{:S(2)}, u32[]{:S(2)}) collective-permute-start(bf16[16,32,2048]{2,1,0:T(8,128)(2,1)} %get-tuple-element.287), channel_id=1, source_target_pairs={{0,1},{1,0},{2,3},{3,2},{4,5},{5,4},{6,7},{7,6},{8,9},{9,8},{10,11... | collective-permute-start | bytes 6291464 | tf_op jit(solution)/shard_map/ppermute | solution.py:563
  484.8 25.6 %collective-permute-start.43 = (bf16[16,32,2048]{2,1,0:T(8,128)(2,1)}, bf16[16,32,2048]{2,1,0:T(8,128)(2,1)}, u32[]{:S(2)}, u32[]{:S(2)}) collective-permute-start(bf16[16,32,2048]{2,1,0:T(8,128)(2,1)} %get-tuple-element.285), channel_id=1, source_target_pairs={{0,1},{1,0},{2,3},{3,2},{4,5},{5,4},{6,7},{7,6},{8,9},{9,8},{10,11... | collective-permute-start | bytes 6291464 | tf_op jit(solution)/shard_map/ppermute | solution.py:563
  485.4 54.3 %collective-permute-start.45 = (bf16[8,256,1024]{2,1,0:T(8,128)(2,1)}, bf16[8,256,1024]{2,1,0:T(8,128)(2,1)}, u32[]{:S(2)}, u32[]{:S(2)}) collective-permute-start(bf16[8,256,1024]{2,1,0:T(8,128)(2,1)} %get-tuple-element.304), channel_id=1, source_target_pairs={{0,1},{1,0},{2,3},{3,2},{4,5},{5,4},{6,7},{7,6},{8,9},{9,8},{10,11... | collective-permute-start | bytes 12582920 | tf_op jit(solution)/shard_map/ppermute | solution.py:563
  508.2 8.7 %collective-permute-start.42 = (bf16[2,32,2048]{2,1,0:T(8,128)(2,1)S(1)}, bf16[2,32,2048]{2,1,0:T(8,128)(2,1)S(1)}, u32[]{:S(2)}, u32[]{:S(2)}) collective-permute-start(bf16[2,32,2048]{2,1,0:T(8,128)(2,1)S(1)} %get-tuple-element.389), channel_id=1, source_target_pairs={{0,16},{8,24},{16,0},{24,8},{1,17},{9,25},{17,1},{25,9},{2,18},{10... | collective-permute-start | bytes 786440 | tf_op jit(solution)/shard_map/ppermute | solution.py:563
  509.8 8.8 %collective-permute-start.41 = (bf16[2,32,2048]{2,1,0:T(8,128)(2,1)S(1)}, bf16[2,32,2048]{2,1,0:T(8,128)(2,1)S(1)}, u32[]{:S(2)}, u32[]{:S(2)}) collective-permute-start(bf16[2,32,2048]{2,1,0:T(8,128)(2,1)S(1)} %get-tuple-element.390), channel_id=1, source_target_pairs={{0,8},{8,0},{16,24},{24,16},{1,9},{9,1},{17,25},{25,17},{2,10},{10... | collective-permute-start | bytes 786440 | tf_op jit(solution)/shard_map/ppermute | solution.py:563
  514.3 17.1 %collective-permute-start.49 = (bf16[2,32,2048]{2,1,0:T(8,128)(2,1)}, bf16[2,32,2048]{2,1,0:T(8,128)(2,1)S(1)}, u32[]{:S(2)}, u32[]{:S(2)}) collective-permute-start(bf16[2,32,2048]{2,1,0:T(8,128)(2,1)} %get-tuple-element.387), channel_id=1, source_target_pairs={{0,16},{8,24},{16,0},{24,8},{1,17},{9,25},{17,1},{25,9},{2,18},{10... | collective-permute-start | bytes 786440 | tf_op jit(solution)/shard_map/ppermute | solution.py:563
  515.2 16.2 %collective-permute-start.48 = (bf16[2,32,2048]{2,1,0:T(8,128)(2,1)}, bf16[2,32,2048]{2,1,0:T(8,128)(2,1)S(1)}, u32[]{:S(2)}, u32[]{:S(2)}) collective-permute-start(bf16[2,32,2048]{2,1,0:T(8,128)(2,1)} %get-tuple-element.388), channel_id=1, source_target_pairs={{0,8},{8,0},{16,24},{24,16},{1,9},{9,1},{17,25},{25,17},{2,10},{10... | collective-permute-start | bytes 786440 | tf_op jit(solution)/shard_map/ppermute | solution.py:563
  518.7 15.2 %collective-permute-start.61 = (bf16[4,32,2048]{2,1,0:T(8,128)(2,1)S(1)}, bf16[4,32,2048]{2,1,0:T(8,128)(2,1)}, u32[]{:S(2)}, u32[]{:S(2)}) collective-permute-start(bf16[4,32,2048]{2,1,0:T(8,128)(2,1)S(1)} %pad_maximum_fusion.6), channel_id=1, source_target_pairs={{0,16},{8,24},{16,0},{24,8},{1,17},{9,25},{17,1},{25,9},{2,18},{10... | collective-permute-start | bytes 1572872 | tf_op jit(solution)/shard_map/ppermute | solution.py:563
  519.2 16.2 %collective-permute-start.60 = (bf16[4,32,2048]{2,1,0:T(8,128)(2,1)S(1)}, bf16[4,32,2048]{2,1,0:T(8,128)(2,1)}, u32[]{:S(2)}, u32[]{:S(2)}) collective-permute-start(bf16[4,32,2048]{2,1,0:T(8,128)(2,1)S(1)} %pad_maximum_fusion.5), channel_id=1, source_target_pairs={{0,8},{8,0},{16,24},{24,16},{1,9},{9,1},{17,25},{25,17},{2,10},{10... | collective-permute-start | bytes 1572872 | tf_op jit(solution)/shard_map/ppermute | solution.py:563
  531.4 22.5 %collective-permute-start.44 = (bf16[16,32,2176]{2,1,0:T(8,128)(2,1)}, bf16[16,32,2176]{2,1,0:T(8,128)(2,1)S(1)}, u32[]{:S(2)}, u32[]{:S(2)}) collective-permute-start(bf16[16,32,2176]{2,1,0:T(8,128)(2,1)} %get-tuple-element.303), channel_id=1, source_target_pairs={{0,1},{1,0},{2,3},{3,2},{4,5},{5,4},{6,7},{7,6},{8,9},{9,8},{10,11... | collective-permute-start | bytes 6684680 | tf_op jit(solution)/shard_map/ppermute | solution.py:563
  531.6 23.0 %collective-permute-start.51 = (bf16[4,32,2048]{2,1,0:T(8,128)(2,1)S(1)}, bf16[4,32,2048]{2,1,0:T(8,128)(2,1)S(1)}, u32[]{:S(2)}, u32[]{:S(2)}) collective-permute-start(bf16[4,32,2048]{2,1,0:T(8,128)(2,1)S(1)} %pad_maximum_fusion.8), channel_id=1, source_target_pairs={{0,16},{8,24},{16,0},{24,8},{1,17},{9,25},{17,1},{25,9},{2,18},{10... | collective-permute-start | bytes 1572872 | tf_op jit(solution)/shard_map/ppermute | solution.py:563
  533.9 20.7 %collective-permute-start.50 = (bf16[4,32,2048]{2,1,0:T(8,128)(2,1)S(1)}, bf16[4,32,2048]{2,1,0:T(8,128)(2,1)S(1)}, u32[]{:S(2)}, u32[]{:S(2)}) collective-permute-start(bf16[4,32,2048]{2,1,0:T(8,128)(2,1)S(1)} %pad_maximum_fusion.7), channel_id=1, source_target_pairs={{0,8},{8,0},{16,24},{24,16},{1,9},{9,1},{17,25},{25,17},{2,10},{10... | collective-permute-start | bytes 1572872 | tf_op jit(solution)/shard_map/ppermute | solution.py:563
  537.6 17.0 %collective-permute-start.64 = (bf16[32,2048]{1,0:T(8,128)(2,1)}, bf16[32,2048]{1,0:T(8,128)(2,1)S(1)}, u32[]{:S(2)}, u32[]{:S(2)}) collective-permute-start(bf16[32,2048]{1,0:T(8,128)(2,1)} %get-tuple-element.379), channel_id=1, source_target_pairs={{0,6},{1,7},{2,4},{3,5},{4,2},{5,3},{6,0},{7,1},{8,14},{9,15},{10,... | collective-permute-start | bytes 393224 | tf_op jit(solution)/shard_map/ppermute | solution.py:563
  539.7 17.4 %collective-permute-start.63 = (bf16[32,2048]{1,0:T(8,128)(2,1)}, bf16[32,2048]{1,0:T(8,128)(2,1)S(1)}, u32[]{:S(2)}, u32[]{:S(2)}) collective-permute-start(bf16[32,2048]{1,0:T(8,128)(2,1)} %get-tuple-element.380), channel_id=1, source_target_pairs={{0,4},{1,5},{2,6},{3,7},{4,0},{5,1},{6,2},{7,3},{8,12},{9,13},{10,... | collective-permute-start | bytes 393224 | tf_op jit(solution)/shard_map/ppermute | solution.py:563
  560.3 7.9 %collective-permute-start.47 = (bf16[2,32,2176]{2,1,0:T(8,128)(2,1)S(1)}, bf16[2,32,2176]{2,1,0:T(8,128)(2,1)S(1)}, u32[]{:S(2)}, u32[]{:S(2)}) collective-permute-start(bf16[2,32,2176]{2,1,0:T(8,128)(2,1)S(1)} %get-tuple-element.377), channel_id=1, source_target_pairs={{0,16},{8,24},{16,0},{24,8},{1,17},{9,25},{17,1},{25,9},{2,18},{10... | collective-permute-start | bytes 835592 | tf_op jit(solution)/shard_map/ppermute | solution.py:563
  560.6 7.6 %collective-permute-start.46 = (bf16[2,32,2176]{2,1,0:T(8,128)(2,1)S(1)}, bf16[2,32,2176]{2,1,0:T(8,128)(2,1)S(1)}, u32[]{:S(2)}, u32[]{:S(2)}) collective-permute-start(bf16[2,32,2176]{2,1,0:T(8,128)(2,1)S(1)} %get-tuple-element.378), channel_id=1, source_target_pairs={{0,8},{8,0},{16,24},{24,16},{1,9},{9,1},{17,25},{25,17},{2,10},{10... | collective-permute-start | bytes 835592 | tf_op jit(solution)/shard_map/ppermute | solution.py:563
  568.4 13.0 %collective-permute-start.52 = (bf16[4,32,2176]{2,1,0:T(8,128)(2,1)S(1)}, bf16[4,32,2176]{2,1,0:T(8,128)(2,1)S(1)}, u32[]{:S(2)}, u32[]{:S(2)}) collective-permute-start(bf16[4,32,2176]{2,1,0:T(8,128)(2,1)S(1)} %pad_maximum_fusion.3), channel_id=1, source_target_pairs={{0,8},{8,0},{16,24},{24,16},{1,9},{9,1},{17,25},{25,17},{2,10},{10... | collective-permute-start | bytes 1671176 | tf_op jit(solution)/shard_map/ppermute | solution.py:563
  569.8 12.2 %collective-permute-start.53 = (bf16[4,32,2176]{2,1,0:T(8,128)(2,1)S(1)}, bf16[4,32,2176]{2,1,0:T(8,128)(2,1)S(1)}, u32[]{:S(2)}, u32[]{:S(2)}) collective-permute-start(bf16[4,32,2176]{2,1,0:T(8,128)(2,1)S(1)} %pad_maximum_fusion.4), channel_id=1, source_target_pairs={{0,16},{8,24},{16,0},{24,8},{1,17},{9,25},{17,1},{25,9},{2,18},{10... | collective-permute-start | bytes 1671176 | tf_op jit(solution)/shard_map/ppermute | solution.py:563
  570.7 11.6 %collective-permute-start.59 = (bf16[32,2048]{1,0:T(8,128)(2,1)S(1)}, bf16[32,2048]{1,0:T(8,128)(2,1)S(1)}, u32[]{:S(2)}, u32[]{:S(2)}) collective-permute-start(bf16[32,2048]{1,0:T(8,128)(2,1)S(1)} %get-tuple-element.383), channel_id=1, source_target_pairs={{0,6},{1,7},{2,4},{3,5},{4,2},{5,3},{6,0},{7,1},{8,14},{9,15},{10,... | collective-permute-start | bytes 393224 | tf_op jit(solution)/shard_map/ppermute | solution.py:563
  572.8 9.8 %collective-permute-start.58 = (bf16[32,2048]{1,0:T(8,128)(2,1)S(1)}, bf16[32,2048]{1,0:T(8,128)(2,1)S(1)}, u32[]{:S(2)}, u32[]{:S(2)}) collective-permute-start(bf16[32,2048]{1,0:T(8,128)(2,1)S(1)} %get-tuple-element.384), channel_id=1, source_target_pairs={{0,4},{1,5},{2,6},{3,7},{4,0},{5,1},{6,2},{7,3},{8,12},{9,13},{10,... | collective-permute-start | bytes 393224 | tf_op jit(solution)/shard_map/ppermute | solution.py:563
  572.8 9.8 %collective-permute-start.57 = (bf16[32,2048]{1,0:T(8,128)(2,1)S(1)}, bf16[32,2048]{1,0:T(8,128)(2,1)S(1)}, u32[]{:S(2)}, u32[]{:S(2)}) collective-permute-start(bf16[32,2048]{1,0:T(8,128)(2,1)S(1)} %get-tuple-element.385), channel_id=1, source_target_pairs={{0,2},{1,3},{2,0},{3,1},{4,6},{5,7},{6,4},{7,5},{8,10},{9,11},{10,... | collective-permute-start | bytes 393224 | tf_op jit(solution)/shard_map/ppermute | solution.py:563
  585.3 8.4 %collective-permute-start.56 = (bf16[32,2176]{1,0:T(8,128)(2,1)S(1)}, bf16[32,2176]{1,0:T(8,128)(2,1)S(1)}, u32[]{:S(2)}, u32[]{:S(2)}) collective-permute-start(bf16[32,2176]{1,0:T(8,128)(2,1)S(1)} %get-tuple-element.373), channel_id=1, source_target_pairs={{0,6},{1,7},{2,4},{3,5},{4,2},{5,3},{6,0},{7,1},{8,14},{9,15},{10,... | collective-permute-start | bytes 417800 | tf_op jit(solution)/shard_map/ppermute | solution.py:563
  587.4 10.7 %collective-permute-start.55 = (bf16[32,2176]{1,0:T(8,128)(2,1)S(1)}, bf16[32,2176]{1,0:T(8,128)(2,1)S(1)}, u32[]{:S(2)}, u32[]{:S(2)}) collective-permute-start(bf16[32,2176]{1,0:T(8,128)(2,1)S(1)} %get-tuple-element.374), channel_id=1, source_target_pairs={{0,4},{1,5},{2,6},{3,7},{4,0},{5,1},{6,2},{7,3},{8,12},{9,13},{10,... | collective-permute-start | bytes 417800 | tf_op jit(solution)/shard_map/ppermute | solution.py:563
  587.4 10.7 %collective-permute-start.54 = (bf16[32,2176]{1,0:T(8,128)(2,1)S(1)}, bf16[32,2176]{1,0:T(8,128)(2,1)S(1)}, u32[]{:S(2)}, u32[]{:S(2)}) collective-permute-start(bf16[32,2176]{1,0:T(8,128)(2,1)S(1)} %get-tuple-element.375), channel_id=1, source_target_pairs={{0,2},{1,3},{2,0},{3,1},{4,6},{5,7},{6,4},{7,5},{8,10},{9,11},{10,... | collective-permute-start | bytes 417800 | tf_op jit(solution)/shard_map/ppermute | solution.py:563
  (65 other events, 416.4 us)
Sparse Core Ops, SparseCore 0:
  50.4 44.1 all-gather.5
  138.6 67.8 all-gather.3
  353.3 80.3 all-reduce.7
  489.6 50.1 reduce-scatter.1

commit v4 on v3

--- a/solution.py
+++ b/solution.py
@@ -563,7 +563,7 @@
     return lax.ppermute(value, axis, [(place, place ^ mask) for place in range(size)])
 
 
-def visit_chunks(value, size, work):
+def visit_chunks(value, size, work, settle=False):
     lines = size // 2
 
     def by_lines(array, pairs):
@@ -575,14 +575,18 @@
         return [work(chunk, one) for chunk, one in enumerate(chunks)]
     across = exchange(value, "ffn", size, 4)
     beside = exchange(value, "ffn", size, 2)
-    middle = by_lines(value, [(1, 2), (2, 1)])
     results = [work(0, value)]
     across = after(across, results[0])
+    middle = by_lines(after(value, across), [(1, 2), (2, 1)])
     onward = by_lines(across, [(2, 3), (1, 0)])
     results.append(work(1, after(beside, across)))
+    line = lax.axis_index("ffn") // 2
+    last = [middle, onward]
+    if settle:
+        last = after(last, results[1])
+        across = after(across, last)
     results.append(work(2, across))
-    line = lax.axis_index("ffn") // 2
-    results.append(work(3, jnp.where((line == 0) | (line == 3), onward, middle)))
+    results.append(work(3, jnp.where((line == 0) | (line == 3), last[1], last[0])))
     return results
 
 
@@ -633,8 +637,8 @@
 
 
 def memory_forward_kernel(me_ref, own_ref, other_ref, weight_ref, out_ref):
-    pairs, held, width = other_ref.shape
-    for place, rows in enumerate((own_ref[0, 0], other_ref[...])):
+    pairs, held, width = other_ref.shape[2:]
+    for place, rows in enumerate((own_ref[0, 0], other_ref[0, 0])):
         part = matmul(rows.reshape(pairs * held, width), weight_ref[...]).astype(bf16)
         out_ref[:, place] = part.reshape(pairs, held, part.shape[1])
 
@@ -653,7 +657,7 @@
             grid=(lines,),
             in_specs=[
                 own_pairs(memory),
-                pl.BlockSpec((step, held, width), lambda line, me: (line, 0, 0)),
+                own_pairs(memory),
                 pl.BlockSpec((width, 2 * KEYS), lambda line, me: (0, 0)),
             ],
             out_specs=pl.BlockSpec((step, 2, held, 2 * KEYS), lambda line, me: (line, 0, 0, 0)),
@@ -670,9 +674,9 @@
 ):
     own_grad_ref, other_grad_ref, kept_ref, sent_ref, total = rest
     step = pl.program_id(0)
-    pairs, held, width = other_ref.shape
+    pairs, held, width = other_ref.shape[2:]
     for place, (rows, out_ref) in enumerate(
-        ((own_ref[0, 0], own_grad_ref), (other_ref[...], other_grad_ref))
+        ((own_ref[0, 0], own_grad_ref), (other_ref[0, 0], other_grad_ref))
     ):
         grads = grad_ref[:, place].reshape(pairs * held, grad_ref.shape[3])
         out = contract(grads, weight_ref[...], 1, 1).astype(bf16)
@@ -706,7 +710,7 @@
             grid=(lines,),
             in_specs=[
                 own_pairs(memory),
-                block,
+                own_pairs(memory),
                 pl.BlockSpec((step, 2, held, 2 * KEYS), lambda line, me: (line, 0, 0, 0)),
                 pl.BlockSpec((width, 2 * KEYS), lambda line, me: (0, 0)),
                 pl.BlockSpec(mixed.shape, lambda line, me: (0, 0)),
@@ -721,7 +725,7 @@
         ),
         out_shape=[
             jax.ShapeDtypeStruct(memory.shape, bf16),
-            jax.ShapeDtypeStruct(other.shape, bf16),
+            jax.ShapeDtypeStruct((lines * step, held, width), bf16),
             jax.ShapeDtypeStruct(shape, bf16),
             jax.ShapeDtypeStruct(shape, bf16),
         ],
@@ -903,12 +907,11 @@
     return lax.optimization_barrier((values, earlier))[0]
 
 
-def gather_pieces(sizes, pack, beside):
+def gather_pieces(sizes, pack):
     tok_size, ffn_size = sizes
     lines = ffn_size // 2
     half = lines // 2
     line = [pack] + [exchange(pack, "ffn", ffn_size, 2 * step) for step in range(1, lines)]
-    line, extra = lax.optimization_barrier((line, beside(())))
     begun = line
     line = jnp.stack(line)
     by_x = exchange(line, "tok", tok_size, 1)
@@ -916,7 +919,7 @@
     top = exchange(by_y[:half], "tok", tok_size, 1)
     bottom = exchange(by_x[half:], "tok", tok_size, 2)
     held = [line, by_x, by_y, top, bottom]
-    return held + [exchange(one, "ffn", ffn_size, 1) for one in held], extra, begun
+    return held + [exchange(one, "ffn", ffn_size, 1) for one in held], begun
 
 
 def on_device(
@@ -971,15 +974,12 @@
     same_core = [[2 * line + one for line in range(lines)] for one in range(2)]
     memory_lines = memory.reshape(lines, 2, pair_count, held, D)
 
-    def swap_memory(begun):
-        sent = lax.dynamic_index_in_dim(after(memory_lines, begun), 1 - core, 1, keepdims=False)
-        return exchange(sent.reshape(lines * pair_count, held, D), "ffn", ffn_size, 1)
+    memory_other = exchange(memory_lines, "ffn", ffn_size, 1)
 
     if direct:
-        pieces, memory_other, begun = gather_pieces(sizes, pack, swap_memory)
+        pieces, begun = gather_pieces(sizes, pack)
     else:
         pieces = [lax.all_gather(pack, both, axis=0, tiled=True)]
-        memory_other = swap_memory(pieces)
         begun = pieces
     cotangents = lax.all_gather(
         after(out_grad, begun),
@@ -1032,26 +1032,23 @@
         query_chunks.append(chunk_queries)
         if chunk:
             chunk_queries = after(chunk_queries, mixed_parts[-1])
-        if chunk == lines - 1:
-            chunk_queries = after(chunk_queries, (kept["placed"], kept["units"]))
         mixed_parts.append(cross_forward(chunk, info, chunk_queries, memory_parts))
-        if chunk == 1:
-            held_pieces, units = after((pieces, (ffn_gate, ffn_up, ffn_down)), mixed_parts[1])
-            kept["placed"] = place_rows(
-                sizes, share, me, held_pieces, (0, D + 2 * KEYS + SMALL), 2 * D
-            )
-            kept["units"] = [
-                jnp.concatenate([array, exchange(array, "ffn", ffn_size, 1)], axis=dim)
-                for array, dim in zip(units, (1, 1, 0), strict=True)
-            ]
         return mixed_parts[-1]
 
     visit_chunks(cross_queries, ffn_size, visit_forward)
     output_weights = kept["output"]
-    full_first, full_second = kept["placed"]
-    both_gate, both_up, both_down = kept["units"]
+    held_pieces, units = after((pieces, (ffn_gate, ffn_up, ffn_down)), mixed_parts[-1])
+    placed = place_rows(sizes, share, me, held_pieces, (0, D + 2 * KEYS + SMALL), 2 * D)
+    units = [
+        jnp.concatenate([array, exchange(array, "ffn", ffn_size, 1)], axis=dim)
+        for array, dim in zip(units, (1, 1, 0), strict=True)
+    ]
+    full_first, full_second = placed
+    both_gate, both_up, both_down = units
+    mixed_parts = return_chunks(mixed_parts, ffn_size)
+    mixed_parts = mixed_parts[:1] + after(mixed_parts[1:], (placed, units))
     cross_mixed, cross_stats, hidden_two, normed_three, cross_squares = cross_join(
-        hidden_one, gains, output_weights, return_chunks(mixed_parts, ffn_size)
+        hidden_one, gains, output_weights, mixed_parts
     )
 
     earlier, row_parts = [], []
@@ -1094,7 +1091,7 @@
         query_parts.append(part)
         return part
 
-    visit_chunks(grad_pack, ffn_size, visit_backward)
+    visit_chunks(grad_pack, ffn_size, visit_backward, settle=True)
     memory_grads = earlier[0]
     query_parts = return_chunks(query_parts, ffn_size)
     memory_grad, other_grad, *memory_sum = memory_backward(

time: 613 us -> 598 us (0.976)
  waiting for transfers between devices: 202 us -> 180 us
  starting transfers between devices: 107 us -> 114 us
    ppermute x59, waiting for transfers between devices: 202 us -> 180 us  [exchange(): lax.ppermute(value, axis, [(place, place ^ mask) for place in range(size)])]
    ppermute x59, starting transfers between devices: 91.7 us -> 98 us  [exchange(): lax.ppermute(value, axis, [(place, place ^ mask) for place in range(size)])]
    unnamed x131 -> x119, local copies, waits for them, and re-layouts: 10 us -> 13.5 us
  transfers between devices with their start and end apart: 69 -> 69, of which waited for: 22 -> 23; matrix products, arithmetic and copies ran while one was open for 9% -> 10% of each run, Pallas kernels for 32% -> 33%
where the time goes in v4:
time: 598 us; the launch traced here: 592 us
  Pallas kernels  209 us (35%)
  waiting for transfers between devices  180 us (30%)
  starting transfers between devices  114 us (19%)
  local copies, waits for them, and re-layouts  37.7 us (6%)
  other arithmetic  29.2 us (5%)
  between operations  15 us (3%)
  matrix products  7.64 us (1%)
    ppermute x59, waiting for transfers between devices, exchange(): lax.ppermute(value, axis, [(place, place ^ mask) for place in range(size)])  180 us
    ppermute x59, starting transfers between devices, exchange(): lax.ppermute(value, axis, [(place, place ^ mask) for place in range(size)])  98 us
    pallas_call x9, Pallas kernels, vmem_call(): pl.pallas_call(body, in_specs=[pl.BlockSpec(memory_space=pltpu.SMEM)] * l...  59.9 us
    pallas_call x4, Pallas kernels, cross_backward(): pl.pallas_call(functools.partial(cross_backward_kernel, chunk), grid_spec...  34.4 us
    pallas_call x4, Pallas kernels, cross_forward(): pl.pallas_call(functools.partial(cross_forward_kernel, chunk), grid_spec=...  29.7 us
    pallas_call x4, Pallas kernels, ffn_chunk(): pl.pallas_call(ffn_kernel, grid_spec=pltpu.PrefetchScalarGridSpec(num_sca...  29.3 us
    pallas_call x1, Pallas kernels, memory_backward(): pl.pallas_call(functools.partial(memory_backward_kernel, sizes), grid_spe...  26.5 us
    ppermute x6, starting transfers between devices, by_lines(): return lax.ppermute(array, 'ffn', pairs)  15.3 us
  transfers between devices with their start and end apart: 69, of which 23 were waited for; matrix products, arithmetic and copies ran while one was open for 10% of the time, Pallas kernels for 33%

profile of v4, /device:TPU:0, one launch (start us, length us, event | category | flops | bytes accessed | tf_op | source)
XLA Modules:
  0.0 592.1 jit_solution(16515503110957351516)
XLA Ops:
  15.5 4.6 collective-permute-start.2
  20.7 8.3 %collective-permute-done.2 = bf16[32,5248]{1,0:T(8,128)(2,1)S(1)} collective-permute-done((bf16[32,5248]{1,0:T(8,128)(2,1)S(1)}, bf16[32,5248]{1,0:T(8,128)(2,1)S(1)}, u32[]{:S(2)}, u32[]{:S(2)}) %collective-permute-start.2) | collective-permute-done | bytes 335904 | tf_op jit(solution)/shard_map/ppermute | solution.py:563
  29.0 20.4 %collective-permute-done.1 = bf16[32,5248]{1,0:T(8,128)(2,1)S(1)} collective-permute-done((bf16[32,5248]{1,0:T(8,128)(2,1)S(1)}, bf16[32,5248]{1,0:T(8,128)(2,1)S(1)}, u32[]{:S(2)}, u32[]{:S(2)}) %collective-permute-start.1) | collective-permute-done | bytes 335904 | tf_op jit(solution)/shard_map/ppermute | solution.py:563
  52.8 28.0 %collective-permute-done.4.refs_2_ = bf16[4,32,5248]{2,1,0:T(8,128)(2,1)S(1)} collective-permute-done((bf16[4,32,5248]{2,1,0:T(8,128)(2,1)S(1)}, bf16[4,32,5248]{2,1,0:T(8,128)(2,1)S(1)}, u32[]{:S(2)}, u32[]{:S(2)}) %collective-permute-start.4) | collective-permute-done | bytes 1343520 | tf_op jit(solution)/shard_map/ppermute | solution.py:563
  83.2 2.0 slice.327
  87.6 10.2 %collective-permute-done.5.refs_3_ = bf16[2,32,5248]{2,1,0:T(8,128)(2,1)S(1)} collective-permute-done((bf16[2,32,5248]{2,1,0:T(8,128)(2,1)}, bf16[2,32,5248]{2,1,0:T(8,128)(2,1)S(1)}, u32[]{:S(2)}, u32[]{:S(2)}) %collective-permute-start.5) | collective-permute-done | bytes 671776 | tf_op jit(solution)/shard_map/ppermute | solution.py:563
  97.9 3.3 collective-permute-done.6.refs_4_
  105.4 7.4 %self_forward.1 = (bf16[256,1024]{1,0:T(8,128)(2,1)}, bf16[256,2048]{1,0:T(8,128)(2,1)}, bf16[256,1024]{1,0:T(8,128)(2,1)}, f32[32,128]{1,0:T(8,128)}, f32[8,1024]{1,0:T(8,128)}) custom-call(s32[3]{0:T(128)} %pad_add_fusion.1.me_ref, s32[2]{0:T(128)} %length_ref.3, bf16[256,1024]{1,0:T(8,128)(2,1)} %row_ref.5, s32[128,128]{1,0:T(8,128)} %fusion.6.lane_ref, ...), custom_call_target="tpu_custom_call" | custom-call | flops 1000000000 | bytes 8000000 | tf_op jit(solution)/shard_map/self_forward/pallas_call | solution.py:41
  112.8 6.1 %self_output.1 = (f32[256,1024]{1,0:T(8,128)}, bf16[256,1024]{1,0:T(8,128)(2,1)}, bf16[1024,256]{1,0:T(8,128)(2,1)}, f32[256,1]{1,0:T(8,128)}) custom-call(s32[3]{0:T(128)} %pad_add_fusion.1.me_ref, bf16[256,1024]{1,0:T(8,128)(2,1)} %row_ref.5, bf16[256,1024]{1,0:T(8,128)(2,1)} %get-tuple-element.179.mix_ref.refs_2_, ...), custom_call_target="tpu_custom_call" | custom-call | flops 1000000000 | bytes 8000000 | tf_op jit(solution)/shard_map/self_output/pallas_call | solution.py:41
  119.1 3.0 collective-permute-start.13
  122.9 3.9 place_rows.2.weight_ref
  127.6 13.7 %memory_forward.1 = bf16[8,2,256,1024]{3,2,1,0:T(8,128)(2,1)} custom-call(s32[3]{0:T(128)} %pad_add_fusion.1.me_ref, bf16[4,2,2,256,1024]{4,3,2,1,0:T(8,128)(2,1)} %bitcast.91, bf16[4,2,2,256,1024]{4,3,2,1,0:T(8,128)(2,1)} %collective-permute-done.12.other_ref, bf16[1024,1024]{1,0:T(8,128)(2,1)} %place_rows.2.weight_ref), custom_call_target="tpu_custom_call" | custom-call | flops 8600000512 | bytes 18000000 | tf_op jit(solution)/shard_map/memory_forward/pallas_call | solution.py:653
  141.3 7.5 %cross_forward.4.refs_0_ = bf16[1072,256]{1,0:T(8,128)(2,1)} custom-call(s32[4,5]{1,0:T(4,128)} %pad_add_fusion.info_ref, bf16[1024,256]{1,0:T(8,128)(2,1)} %get-tuple-element.199.query_ref, bf16[8,512,1024]{2,1,0:T(8,128)(2,1)} %bitcast.93), custom_call_target="tpu_custom_call" | custom-call | flops 6000000000 | bytes 4000000 | tf_op jit(solution)/shard_map/cross_forward/pallas_call | solution.py:428
  151.1 7.3 %cross_forward.5 = bf16[1072,256]{1,0:T(8,128)(2,1)} custom-call(s32[4,5]{1,0:T(4,128)} %pad_add_fusion.info_ref, bf16[1024,256]{1,0:T(8,128)(2,1)} %copy-done.49, bf16[8,512,1024]{2,1,0:T(8,128)(2,1)} %bitcast.94), custom_call_target="tpu_custom_call" | custom-call | flops 6000000000 | bytes 4000000 | tf_op jit(solution)/shard_map/cross_forward/pallas_call | solution.py:428
  158.5 7.4 %cross_forward.6 = bf16[1072,256]{1,0:T(8,128)(2,1)} custom-call(s32[4,5]{1,0:T(4,128)} %pad_add_fusion.info_ref, bf16[1024,256]{1,0:T(8,128)(2,1)} %copy-done.48, bf16[8,512,1024]{2,1,0:T(8,128)(2,1)} %bitcast.95), custom_call_target="tpu_custom_call" | custom-call | flops 6000000000 | bytes 4000000 | tf_op jit(solution)/shard_map/cross_forward/pallas_call | solution.py:428
  166.9 7.5 %cross_forward.7 = bf16[1072,256]{1,0:T(8,128)(2,1)} custom-call(s32[4,5]{1,0:T(4,128)} %pad_add_fusion.info_ref, bf16[1024,256]{1,0:T(8,128)(2,1)} %broadcast_select_fusion.2.query_ref, bf16[8,512,1024]{2,1,0:T(8,128)(2,1)} %bitcast.96), custom_call_target="tpu_custom_call" | custom-call | flops 6000000000 | bytes 4000000 | tf_op jit(solution)/shard_map/cross_forward/pallas_call | solution.py:428
  175.6 5.1 collective-permute-start.16
  182.5 8.8 %place_rows.3 = (bf16[1024,2048]{1,0:T(8,128)(2,1)}, bf16[1024,2048]{1,0:T(8,128)(2,1)}) custom-call(s32[3]{0:T(128)} %pad_add_fusion.1.me_ref, bf16[4,32,5248]{2,1,0:T(8,128)(2,1)} %copy-done, bf16[4,32,5248]{2,1,0:T(8,128)(2,1)} %collective-permute-done.3.refs_1_, bf16[4,32,5248]{2,1,0:T(8,128)(2,1)} %copy-done.2, bf16[2,32,5248]{2,1,0:T(8,128)(2,1)} %copy-done.8, ...), custom_call_target="tpu_custom_call" | custom-call | flops 1000000000 | bytes 8000000 | tf_op jit(solution)/shard_map/place_rows/pallas_call | solution.py:41
  195.2 2.3 copy.99
  197.4 2.3 copy.101
  204.6 4.1 collective-permute-done.16.refs_2_
  208.7 12.6 %collective-permute-done.19.refs_3_ = bf16[1072,256]{1,0:T(8,128)(2,1)} collective-permute-done((bf16[1072,256]{1,0:T(8,128)(2,1)}, bf16[1072,256]{1,0:T(8,128)(2,1)}, u32[]{:S(2)}, u32[]{:S(2)}) %collective-permute-start.19) | collective-permute-done | bytes 548896 | tf_op jit(solution)/shard_map/ppermute | solution.py:563
  221.4 5.0 cross_join.1
  226.3 11.1 %collective-permute-start.23 = (bf16[256,1024]{1,0:T(8,128)(2,1)}, bf16[256,1024]{1,0:T(8,128)(2,1)S(1)}, u32[]{:S(2)}, u32[]{:S(2)}) collective-permute-start(bf16[256,1024]{1,0:T(8,128)(2,1)} %get-tuple-element.223.row_ref), channel_id=1, source_target_pairs={{0,4},{1,5},{2,6},{3,7},{4,0},{5,1},{6,2},{7,3},{8,12},{9,13},{10,... | collective-permute-start | bytes 1572872 | tf_op jit(solution)/shard_map/ppermute | solution.py:563
  237.8 7.3 %ffn_chunk.4 = (bf16[256,1024]{1,0:T(8,128)(2,1)}, bf16[4,256,1024]{2,1,0:T(8,128)(2,1)}, bf16[4,256,1024]{2,1,0:T(8,128)(2,1)}, bf16[4,256,1024]{2,1,0:T(8,128)...) custom-call(s32[3]{0:T(128)} %pad_add_fusion.1.me_ref, ...), custom_call_target="tpu_custom_call" | custom-call | flops 3000000000 | bytes 8000000 | tf_op jit(solution)/shard_map/ffn_chunk/pallas_call | solution.py:542
  245.1 15.9 %collective-permute-done.23.row_ref = bf16[256,1024]{1,0:T(8,128)(2,1)S(1)} collective-permute-done((bf16[256,1024]{1,0:T(8,128)(2,1)}, bf16[256,1024]{1,0:T(8,128)(2,1)S(1)}, u32[]{:S(2)}, u32[]{:S(2)}) %collective-permute-start.23) | collective-permute-done | bytes 524320 | tf_op jit(solution)/shard_map/ppermute | solution.py:563
  262.3 9.4 %collective-permute-start.25 = (bf16[256,1024]{1,0:T(8,128)(2,1)S(1)}, bf16[256,1024]{1,0:T(8,128)(2,1)S(1)}, u32[]{:S(2)}, u32[]{:S(2)}) collective-permute-start(bf16[256,1024]{1,0:T(8,128)(2,1)S(1)} %copy-done.53), channel_id=1, source_target_pairs={{2,4},{3,5},{4,2},{5,3},{10,12},{11,13},{12,10},{13,11},{18,20},{1... | collective-permute-start | bytes 1572872 | tf_op jit(solution)/shard_map/ppermute | solution.py:571
  271.8 7.4 %ffn_chunk.5 = (bf16[256,1024]{1,0:T(8,128)(2,1)}, bf16[4,256,1024]{2,1,0:T(8,128)(2,1)}, bf16[4,256,1024]{2,1,0:T(8,128)(2,1)}, bf16[4,256,1024]{2,1,0:T(8,128)...) custom-call(s32[3]{0:T(128)} %pad_add_fusion.1.me_ref, ...), custom_call_target="tpu_custom_call", output_to_operand_aliasing={{1}: (6, {}), {2}: (7, {}), {3}: (8, {}), {4}: (9, {}), {5}... | custom-call | flops 3000000000 | bytes 8000000 | tf_op jit(solution)/shard_map/ffn_chunk/pallas_call | solution.py:542
  279.2 5.9 %collective-permute-start.27 = (bf16[256,1024]{1,0:T(8,128)(2,1)}, bf16[256,1024]{1,0:T(8,128)(2,1)S(1)}, u32[]{:S(2)}, u32[]{:S(2)}) collective-permute-start(bf16[256,1024]{1,0:T(8,128)(2,1)} %get-tuple-element.249), channel_id=1, source_target_pairs={{0,2},{1,3},{2,0},{3,1},{4,6},{5,7},{6,4},{7,5},{8,10},{9,11},{10,... | collective-permute-start | bytes 1572872 | tf_op jit(solution)/shard_map/ppermute | solution.py:563
  285.1 7.3 %ffn_chunk.6 = (bf16[256,1024]{1,0:T(8,128)(2,1)}, bf16[4,256,1024]{2,1,0:T(8,128)(2,1)}, bf16[4,256,1024]{2,1,0:T(8,128)(2,1)}, bf16[4,256,1024]{2,1,0:T(8,128)...) custom-call(s32[3]{0:T(128)} %pad_add_fusion.1.me_ref, ...), custom_call_target="tpu_custom_call", output_to_operand_aliasing={{1}: (6, {}), {2}: (7, {}), {3}: (8, {}), {4}: (9, {}), {5}... | custom-call | flops 3000000000 | bytes 8000000 | tf_op jit(solution)/shard_map/ffn_chunk/pallas_call | solution.py:542
  293.3 7.3 %ffn_chunk.7 = (bf16[256,1024]{1,0:T(8,128)(2,1)}, bf16[4,256,1024]{2,1,0:T(8,128)(2,1)}, bf16[4,256,1024]{2,1,0:T(8,128)(2,1)}, bf16[4,256,1024]{2,1,0:T(8,128)...) custom-call(s32[3]{0:T(128)} %pad_add_fusion.1.me_ref, ...), custom_call_target="tpu_custom_call", output_to_operand_aliasing={{1}: (6, {}), {2}: (7, {}), {3}: (8, {}), {4}: (9, {}), {5}... | custom-call | flops 3000000000 | bytes 8000000 | tf_op jit(solution)/shard_map/ffn_chunk/pallas_call | solution.py:542
  300.7 4.0 convolution_bitcast_fusion.2
  309.5 2.3 collective-permute-start.29
  315.3 31.3 %collective-permute-done.28.refs_2_ = bf16[256,1024]{1,0:T(8,128)(2,1)S(1)} collective-permute-done((bf16[256,1024]{1,0:T(8,128)(2,1)S(1)}, bf16[256,1024]{1,0:T(8,128)(2,1)S(1)}, u32[]{:S(2)}, u32[]{:S(2)}) %collective-permute-start.28) | collective-permute-done | bytes 524320 | tf_op jit(solution)/shard_map/ppermute | solution.py:563
  347.6 5.2 ffn_join.1
  352.7 11.6 %collective-permute-start.34 = (bf16[1120,256]{1,0:T(8,128)(2,1)}, bf16[1120,256]{1,0:T(8,128)(2,1)S(1)}, u32[]{:S(2)}, u32[]{:S(2)}) collective-permute-start(bf16[1120,256]{1,0:T(8,128)(2,1)} %get-tuple-element.269.grad_ref), channel_id=1, source_target_pairs={{0,4},{1,5},{2,6},{3,7},{4,0},{5,1},{6,2},{7,3},{8,12},{9,13},{10,... | collective-permute-start | bytes 1720328 | tf_op jit(solution)/shard_map/ppermute | solution.py:563
  364.4 8.6 %cross_backward.4 = (bf16[1024,256]{1,0:T(8,128)(2,1)}, bf16[8,512,1024]{2,1,0:T(8,128)(2,1)}) custom-call(s32[4,5]{1,0:T(4,128)} %pad_add_fusion.info_ref, bf16[1024,256]{1,0:T(8,128)(2,1)} %get-tuple-element.199.query_ref, bf16[1120,256]{1,0:T(8,128)(2,1)} %get-tuple-element.269.grad_ref, bf16[8,512,1024]{2,1,0:T(8,128)(2,1)} %bitcast.97), custom_call_target="tpu_custom_call" | custom-call | flops 10000000000 | bytes 8000000 | tf_op jit(solution)/shard_map/cross_backward/pallas_call | solution.py:481
  373.0 16.9 %collective-permute-done.34.grad_ref = bf16[1120,256]{1,0:T(8,128)(2,1)S(1)} collective-permute-done((bf16[1120,256]{1,0:T(8,128)(2,1)}, bf16[1120,256]{1,0:T(8,128)(2,1)S(1)}, u32[]{:S(2)}, u32[]{:S(2)}) %collective-permute-start.34) | collective-permute-done | bytes 573472 | tf_op jit(solution)/shard_map/ppermute | solution.py:563
  392.3 8.6 %cross_backward.5 = (bf16[1024,256]{1,0:T(8,128)(2,1)}, bf16[8,512,1024]{2,1,0:T(8,128)(2,1)}) custom-call(s32[4,5]{1,0:T(4,128)} %pad_add_fusion.info_ref, bf16[1024,256]{1,0:T(8,128)(2,1)} %copy-done.49, bf16[1120,256]{1,0:T(8,128)(2,1)} %copy-done.47, bf16[8,512,1024]{2,1,0:T(8,128)(2,1)} %bitcast.98, ...), custom_call_target="tpu_custom_call", output_to_operand_aliasing={{1}: (4, {})} | custom-call | flops 10000000000 | bytes 8000000 | tf_op jit(solution)/shard_map/cross_backward/pallas_call | solution.py:481
  400.9 5.7 collective-permute-start.35
  407.6 8.6 %cross_backward.6 = (bf16[1024,256]{1,0:T(8,128)(2,1)}, bf16[8,512,1024]{2,1,0:T(8,128)(2,1)}) custom-call(s32[4,5]{1,0:T(4,128)} %pad_add_fusion.info_ref, bf16[1024,256]{1,0:T(8,128)(2,1)} %copy-done.48, bf16[1120,256]{1,0:T(8,128)(2,1)} %copy-done.45, bf16[8,512,1024]{2,1,0:T(8,128)(2,1)} %bitcast.99, ...), custom_call_target="tpu_custom_call", output_to_operand_aliasing={{1}: (4, {})} | custom-call | flops 10000000000 | bytes 8000000 | tf_op jit(solution)/shard_map/cross_backward/pallas_call | solution.py:481
  416.2 4.4 collective-permute-start.38
  420.6 8.6 %cross_backward.7 = (bf16[1024,256]{1,0:T(8,128)(2,1)}, bf16[8,512,1024]{2,1,0:T(8,128)(2,1)}) custom-call(s32[4,5]{1,0:T(4,128)} %pad_add_fusion.info_ref, bf16[1024,256]{1,0:T(8,128)(2,1)} %broadcast_select_fusion.2.query_ref, bf16[1120,256]{1,0:T(8,128)(2,1)} %broadcast_select_fusion.grad_ref, ...), custom_call_target="tpu_custom_call", output_to_operand_aliasing={{1}: (4, {})} | custom-call | flops 10000000000 | bytes 8000000 | tf_op jit(solution)/shard_map/cross_backward/pallas_call | solution.py:481
  430.5 26.5 %memory_backward.1 = (bf16[4,2,2,256,1024]{4,3,2,1,0:T(8,128)(2,1)}, bf16[8,256,1024]{2,1,0:T(8,128)(2,1)}, bf16[16,32,2048]{2,1,0:T(8,128)(2,1)}, bf16[16,32,2048]{2,1,0:T(8,128)(2,1)}) custom-call(s32[3]{0:T(128)} %pad_add_fusion.1.me_ref, bf16[4,2,2,256,1024]{4,3,2,1,0:T(8,128)(2,1)} %bitcast.92, ...), custom_call_target="tpu_custom_call" | custom-call | flops 17200001024 | bytes 28000000 | tf_op jit(solution)/shard_map/memory_backward/pallas_call | solution.py:706
  458.1 6.0 %query_join.1 = (bf16[1024,256]{1,0:T(8,128)(2,1)}, f32[256,1024]{1,0:T(8,128)}, bf16[256,1024]{1,0:T(8,128)(2,1)}, bf16[256,1024]{1,0:T(8,128)(2,1)}, f32[1,1024]{1,0:T(1,128)}) custom-call(f32[256,1024]{1,0:T(8,128)} %get-tuple-element.262.grad_ref, f32[256,1024]{1,0:T(8,128)} %get-tuple-element.181.hidden_ref, f32[3,1024]{1,0:T(4,128)} %slice.247.gain_ref, ...), custom_call_target="tpu_custom_call" | custom-call | flops 1000000000 | bytes 8000000 | tf_op jit(solution)/shard_map/query_join/pallas_call | solution.py:41
  464.1 5.0 grad_blocks.2
  475.4 3.0 add_convert_fusion.11
  479.5 12.2 %self_backward.1 = (bf16[256,2048]{1,0:T(8,128)(2,1)}, f32[16,128]{1,0:T(8,128)}) custom-call(s32[2]{0:T(128)} %length_ref.3, bf16[256,1024]{1,0:T(8,128)(2,1)} %get-tuple-element.295.mix_grad_ref, bf16[256,2048]{1,0:T(8,128)(2,1)} %get-tuple-element.296.wide_ref, f32[32,128]{1,0:T(8,128)} %get-tuple-element.297.stat_ref, ...), custom_call_target="tpu_custom_call" | custom-call | flops 8000000000 | bytes 8000000 | tf_op jit(solution)/shard_map/self_backward/pallas_call | solution.py:41
  495.3 3.1 add_convert_fusion.7
  504.7 5.4 input_grads.1
  511.5 4.8 grad_blocks.3
  522.1 2.6 collective-permute-start.64
  524.6 7.1 %collective-permute-start.63 = (bf16[32,2048]{1,0:T(8,128)(2,1)}, bf16[32,2048]{1,0:T(8,128)(2,1)S(1)}, u32[]{:S(2)}, u32[]{:S(2)}) collective-permute-start(bf16[32,2048]{1,0:T(8,128)(2,1)} %get-tuple-element.386), channel_id=1, source_target_pairs={{0,4},{1,5},{2,6},{3,7},{4,0},{5,1},{6,2},{7,3},{8,12},{9,13},{10,... | collective-permute-start | bytes 393224 | tf_op jit(solution)/shard_map/ppermute | solution.py:563
  531.7 5.5 place_pairs.1
  537.9 2.7 collective-permute-done.63
  540.6 2.7 collective-permute-done.62
  547.0 5.4 collective-permute-done.47
  554.9 2.1 collective-permute-start.59
  557.0 2.4 collective-permute-start.57
  560.0 6.1 %collective-permute-done.52 = bf16[4,32,2176]{2,1,0:T(8,128)(2,1)S(1)} collective-permute-done((bf16[4,32,2176]{2,1,0:T(8,128)(2,1)S(1)}, bf16[4,32,2176]{2,1,0:T(8,128)(2,1)S(1)}, u32[]{:S(2)}, u32[]{:S(2)}) %collective-permute-start.52) | collective-permute-done | bytes 557088 | tf_op jit(solution)/shard_map/ppermute | solution.py:563
  567.4 2.0 multiply_reduce_fusion
  571.9 2.6 collective-permute-start.54
  575.3 3.3 collective-permute-done.56
  578.6 3.9 collective-permute-done.55
  (323 shorter events, 94.4 us)
Async XLA Ops:
  7.2 120.4 %all-gather.6.cloned.1.call-start = ((), (), s32[]{:S(2)}) async-start(), calls=%async_computation.3 | async-start | bytes 2621440 | tf_op jit(solution)/shard_map/all_gather | solution.py:984
  7.2 120.4 %collective-permute-start.12 = (bf16[4,2,2,256,1024]{4,3,2,1,0:T(8,128)(2,1)}, bf16[4,2,2,256,1024]{4,3,2,1,0:T(8,128)(2,1)}, u32[]{:S(2)}, u32[]{:S(2)}) collective-permute-start(bf16[4,2,2,256,1024]{4,3,2,1,0:T(8,128)(2,1)} %bitcast.90), channel_id=1, source_target_pairs={{0,1},{1,0},{2,3},{3,2},{4,5},{5,4},{6,7},{7,6},{8,9},{9,8},{10,11... | collective-permute-start | bytes 25165832 | tf_op jit(solution)/shard_map/ppermute | solution.py:563
  15.5 13.5 %collective-permute-start.2 = (bf16[32,5248]{1,0:T(8,128)(2,1)S(1)}, bf16[32,5248]{1,0:T(8,128)(2,1)S(1)}, u32[]{:S(2)}, u32[]{:S(2)}) collective-permute-start(bf16[32,5248]{1,0:T(8,128)(2,1)S(1)} %constant_dynamic-update-slice_fusion), channel_id=1, source_target_pairs={{0,6},{1,7},{2,4},{3,5},{4,2},{5,3},{6,0},{7,1},{8,14},{9,15},{10,... | collective-permute-start | bytes 1007624 | tf_op jit(solution)/shard_map/ppermute | solution.py:563
  20.1 29.3 %collective-permute-start.1 = (bf16[32,5248]{1,0:T(8,128)(2,1)S(1)}, bf16[32,5248]{1,0:T(8,128)(2,1)S(1)}, u32[]{:S(2)}, u32[]{:S(2)}) collective-permute-start(bf16[32,5248]{1,0:T(8,128)(2,1)S(1)} %constant_dynamic-update-slice_fusion), channel_id=1, source_target_pairs={{0,4},{1,5},{2,6},{3,7},{4,0},{5,1},{6,2},{7,3},{8,12},{9,13},{10,... | collective-permute-start | bytes 1007624 | tf_op jit(solution)/shard_map/ppermute | solution.py:563
  20.1 29.3 %collective-permute-start = (bf16[32,5248]{1,0:T(8,128)(2,1)S(1)}, bf16[32,5248]{1,0:T(8,128)(2,1)S(1)}, u32[]{:S(2)}, u32[]{:S(2)}) collective-permute-start(bf16[32,5248]{1,0:T(8,128)(2,1)S(1)} %constant_dynamic-update-slice_fusion), channel_id=1, source_target_pairs={{0,2},{1,3},{2,0},{3,1},{4,6},{5,7},{6,4},{7,5},{8,10},{9,11},{10,... | collective-permute-start | bytes 1007624 | tf_op jit(solution)/shard_map/ppermute | solution.py:563
  49.6 31.2 %collective-permute-start.4 = (bf16[4,32,5248]{2,1,0:T(8,128)(2,1)S(1)}, bf16[4,32,5248]{2,1,0:T(8,128)(2,1)S(1)}, u32[]{:S(2)}, u32[]{:S(2)}) collective-permute-start(bf16[4,32,5248]{2,1,0:T(8,128)(2,1)S(1)} %pad_maximum_fusion.2.refs_0_), channel_id=1, source_target_pairs={{0,16},{8,24},{16,0},{24,8},{1,17},{9,25},{17,1},{25,9},{2,18},{10... | collective-permute-start | bytes 4030472 | tf_op jit(solution)/shard_map/ppermute | solution.py:563
  51.2 32.0 %collective-permute-start.3 = (bf16[4,32,5248]{2,1,0:T(8,128)(2,1)S(1)}, bf16[4,32,5248]{2,1,0:T(8,128)(2,1)}, u32[]{:S(2)}, u32[]{:S(2)}) collective-permute-start(bf16[4,32,5248]{2,1,0:T(8,128)(2,1)S(1)} %pad_maximum_fusion.2.refs_0_), channel_id=1, source_target_pairs={{0,8},{8,0},{16,24},{24,16},{1,9},{9,1},{17,25},{25,17},{2,10},{10... | collective-permute-start | bytes 4030472 | tf_op jit(solution)/shard_map/ppermute | solution.py:563
  52.7 34.0 %collective-permute-start.7 = (bf16[4,32,5248]{2,1,0:T(8,128)(2,1)S(1)}, bf16[4,32,5248]{2,1,0:T(8,128)(2,1)}, u32[]{:S(2)}, u32[]{:S(2)}) collective-permute-start(bf16[4,32,5248]{2,1,0:T(8,128)(2,1)S(1)} %pad_maximum_fusion.2.refs_0_), channel_id=1, source_target_pairs={{0,1},{1,0},{2,3},{3,2},{4,5},{5,4},{6,7},{7,6},{8,9},{9,8},{10,11... | collective-permute-start | bytes 4030472 | tf_op jit(solution)/shard_map/ppermute | solution.py:563
  52.7 168.6 %all-gather.4.cloned.1.call-start = ((), (), s32[]{:S(2)}) async-start(), calls=%async_computation.1 | async-start | bytes 2162688 | tf_op jit(solution)/shard_map/all_gather | solution.py:1027
  81.7 16.1 %collective-permute-start.5 = (bf16[2,32,5248]{2,1,0:T(8,128)(2,1)}, bf16[2,32,5248]{2,1,0:T(8,128)(2,1)S(1)}, u32[]{:S(2)}, u32[]{:S(2)}) collective-permute-start(bf16[2,32,5248]{2,1,0:T(8,128)(2,1)} %slice.326), channel_id=1, source_target_pairs={{0,8},{8,0},{16,24},{24,16},{1,9},{9,1},{17,25},{25,17},{2,10},{10... | collective-permute-start | bytes 2015240 | tf_op jit(solution)/shard_map/ppermute | solution.py:563
  85.2 16.0 %collective-permute-start.6 = (bf16[2,32,5248]{2,1,0:T(8,128)(2,1)}, bf16[2,32,5248]{2,1,0:T(8,128)(2,1)}, u32[]{:S(2)}, u32[]{:S(2)}) collective-permute-start(bf16[2,32,5248]{2,1,0:T(8,128)(2,1)} %slice.327), channel_id=1, source_target_pairs={{0,16},{8,24},{16,0},{24,8},{1,17},{9,25},{17,1},{25,9},{2,18},{10... | collective-permute-start | bytes 2015240 | tf_op jit(solution)/shard_map/ppermute | solution.py:563
  86.7 15.8 %collective-permute-start.9 = (bf16[4,32,5248]{2,1,0:T(8,128)(2,1)S(1)}, bf16[4,32,5248]{2,1,0:T(8,128)(2,1)}, u32[]{:S(2)}, u32[]{:S(2)}) collective-permute-start(bf16[4,32,5248]{2,1,0:T(8,128)(2,1)S(1)} %collective-permute-done.4.refs_2_), channel_id=1, source_target_pairs={{0,1},{1,0},{2,3},{3,2},{4,5},{5,4},{6,7},{7,6},{8,9},{9,8},{10,11... | collective-permute-start | bytes 4030472 | tf_op jit(solution)/shard_map/ppermute | solution.py:563
  86.7 16.8 %collective-permute-start.8 = (bf16[4,32,5248]{2,1,0:T(8,128)(2,1)}, bf16[4,32,5248]{2,1,0:T(8,128)(2,1)S(1)}, u32[]{:S(2)}, u32[]{:S(2)}) collective-permute-start(bf16[4,32,5248]{2,1,0:T(8,128)(2,1)} %collective-permute-done.3.refs_1_), channel_id=1, source_target_pairs={{0,1},{1,0},{2,3},{3,2},{4,5},{5,4},{6,7},{7,6},{8,9},{9,8},{10,11... | collective-permute-start | bytes 4030472 | tf_op jit(solution)/shard_map/ppermute | solution.py:563
  119.0 29.9 %collective-permute-start.14 = (bf16[1024,256]{1,0:T(8,128)(2,1)}, bf16[1024,256]{1,0:T(8,128)(2,1)S(1)}, u32[]{:S(2)}, u32[]{:S(2)}) collective-permute-start(bf16[1024,256]{1,0:T(8,128)(2,1)} %get-tuple-element.199.query_ref), channel_id=1, source_target_pairs={{0,4},{1,5},{2,6},{3,7},{4,0},{5,1},{6,2},{7,3},{8,12},{9,13},{10,... | collective-permute-start | bytes 1572872 | tf_op jit(solution)/shard_map/ppermute | solution.py:563
  119.1 31.1 %collective-permute-start.13 = (bf16[1024,256]{1,0:T(8,128)(2,1)}, bf16[1024,256]{1,0:T(8,128)(2,1)S(1)}, u32[]{:S(2)}, u32[]{:S(2)}) collective-permute-start(bf16[1024,256]{1,0:T(8,128)(2,1)} %get-tuple-element.199.query_ref), channel_id=1, source_target_pairs={{0,2},{1,3},{2,0},{3,1},{4,6},{5,7},{6,4},{7,5},{8,10},{9,11},{10,... | collective-permute-start | bytes 1572872 | tf_op jit(solution)/shard_map/ppermute | solution.py:563
  127.6 329.5 %all-reduce.8.cloned.1.call-start = ((), (), s32[]{:S(2)}) async-start(), calls=%async_computation.4 | async-start | bytes 4325376 | tf_op jit(solution)/shard_map/psum | solution.py:1078
  148.8 17.3 %collective-permute-start.17 = (bf16[1024,256]{1,0:T(8,128)(2,1)S(1)}, bf16[1024,256]{1,0:T(8,128)(2,1)S(1)}, u32[]{:S(2)}, u32[]{:S(2)}) collective-permute-start(bf16[1024,256]{1,0:T(8,128)(2,1)S(1)} %collective-permute-done.14.query_ref), channel_id=1, source_target_pairs={{4,6},{5,7},{2,0},{3,1},{12,14},{13,15},{10,8},{11,9},{20,22},{21,... | collective-permute-start | bytes 1572872 | tf_op jit(solution)/shard_map/ppermute | solution.py:571
  150.2 15.7 %collective-permute-start.18 = (bf16[1024,256]{1,0:T(8,128)(2,1)S(1)}, bf16[1024,256]{1,0:T(8,128)(2,1)S(1)}, u32[]{:S(2)}, u32[]{:S(2)}) collective-permute-start(bf16[1024,256]{1,0:T(8,128)(2,1)S(1)} %copy-done.50), channel_id=1, source_target_pairs={{2,4},{3,5},{4,2},{5,3},{10,12},{11,13},{12,10},{13,11},{18,20},{1... | collective-permute-start | bytes 1572872 | tf_op jit(solution)/shard_map/ppermute | solution.py:571
  174.4 16.9 %collective-permute-start.20 = (bf16[1024,352]{0,1:T(8,128)(2,1)S(1)}, bf16[1024,352]{0,1:T(8,128)(2,1)S(1)}, u32[]{:S(2)}, u32[]{:S(2)}) collective-permute-start(bf16[1024,352]{0,1:T(8,128)(2,1)S(1)} %copy-done.24), channel_id=1, source_target_pairs={{0,1},{1,0},{2,3},{3,2},{4,5},{5,4},{6,7},{7,6},{8,9},{9,8},{10,11... | collective-permute-start | bytes 2162696 | tf_op jit(solution)/shard_map/ppermute | solution.py:563
  174.5 23.0 %collective-permute-start.21 = (bf16[1024,352]{0,1:T(8,128)(2,1)}, bf16[1024,352]{0,1:T(8,128)(2,1)}, u32[]{:S(2)}, u32[]{:S(2)}) collective-permute-start(bf16[1024,352]{0,1:T(8,128)(2,1)} %param.40), channel_id=1, source_target_pairs={{0,1},{1,0},{2,3},{3,2},{4,5},{5,4},{6,7},{7,6},{8,9},{9,8},{10,11... | collective-permute-start | bytes 2162696 | tf_op jit(solution)/shard_map/ppermute | solution.py:563
  175.0 24.7 %collective-permute-start.22 = (bf16[352,1024]{1,0:T(8,128)(2,1)}, bf16[352,1024]{1,0:T(8,128)(2,1)}, u32[]{:S(2)}, u32[]{:S(2)}) collective-permute-start(bf16[352,1024]{1,0:T(8,128)(2,1)} %param.41), channel_id=1, source_target_pairs={{0,1},{1,0},{2,3},{3,2},{4,5},{5,4},{6,7},{7,6},{8,9},{9,8},{10,11... | collective-permute-start | bytes 2162696 | tf_op jit(solution)/shard_map/ppermute | solution.py:563
  175.6 33.1 %collective-permute-start.16 = (bf16[1072,256]{1,0:T(8,128)(2,1)}, bf16[1072,256]{1,0:T(8,128)(2,1)}, u32[]{:S(2)}, u32[]{:S(2)}) collective-permute-start(bf16[1072,256]{1,0:T(8,128)(2,1)} %cross_forward.6), channel_id=1, source_target_pairs={{0,4},{1,5},{2,6},{3,7},{4,0},{5,1},{6,2},{7,3},{8,12},{9,13},{10,... | collective-permute-start | bytes 1646600 | tf_op jit(solution)/shard_map/ppermute | solution.py:563
  180.7 28.0 %collective-permute-start.15 = (bf16[1072,256]{1,0:T(8,128)(2,1)}, bf16[1072,256]{1,0:T(8,128)(2,1)}, u32[]{:S(2)}, u32[]{:S(2)}) collective-permute-start(bf16[1072,256]{1,0:T(8,128)(2,1)} %cross_forward.5), channel_id=1, source_target_pairs={{0,2},{1,3},{2,0},{3,1},{4,6},{5,7},{6,4},{7,5},{8,10},{9,11},{10,... | collective-permute-start | bytes 1646600 | tf_op jit(solution)/shard_map/ppermute | solution.py:563
  192.2 29.1 %collective-permute-start.19 = (bf16[1072,256]{1,0:T(8,128)(2,1)}, bf16[1072,256]{1,0:T(8,128)(2,1)}, u32[]{:S(2)}, u32[]{:S(2)}) collective-permute-start(bf16[1072,256]{1,0:T(8,128)(2,1)} %cross_forward.7), channel_id=1, source_target_pairs={{0,6},{1,7},{2,4},{3,5},{4,2},{5,3},{6,0},{7,1},{8,14},{9,15},{10,... | collective-permute-start | bytes 1646600 | tf_op jit(solution)/shard_map/ppermute | solution.py:563
  226.3 34.7 %collective-permute-start.23 = (bf16[256,1024]{1,0:T(8,128)(2,1)}, bf16[256,1024]{1,0:T(8,128)(2,1)S(1)}, u32[]{:S(2)}, u32[]{:S(2)}) collective-permute-start(bf16[256,1024]{1,0:T(8,128)(2,1)} %get-tuple-element.223.row_ref), channel_id=1, source_target_pairs={{0,4},{1,5},{2,6},{3,7},{4,0},{5,1},{6,2},{7,3},{8,12},{9,13},{10,... | collective-permute-start | bytes 1572872 | tf_op jit(solution)/shard_map/ppermute | solution.py:563
  237.5 24.9 %collective-permute-start.26 = (bf16[256,1024]{1,0:T(8,128)(2,1)}, bf16[256,1024]{1,0:T(8,128)(2,1)S(1)}, u32[]{:S(2)}, u32[]{:S(2)}) collective-permute-start(bf16[256,1024]{1,0:T(8,128)(2,1)} %get-tuple-element.223.row_ref), channel_id=1, source_target_pairs={{0,2},{1,3},{2,0},{3,1},{4,6},{5,7},{6,4},{7,5},{8,10},{9,11},{10,... | collective-permute-start | bytes 1572872 | tf_op jit(solution)/shard_map/ppermute | solution.py:563
  261.0 31.4 %collective-permute-start.24 = (bf16[256,1024]{1,0:T(8,128)(2,1)S(1)}, bf16[256,1024]{1,0:T(8,128)(2,1)S(1)}, u32[]{:S(2)}, u32[]{:S(2)}) collective-permute-start(bf16[256,1024]{1,0:T(8,128)(2,1)S(1)} %collective-permute-done.23.row_ref), channel_id=1, source_target_pairs={{4,6},{5,7},{2,0},{3,1},{12,14},{13,15},{10,8},{11,9},{20,22},{21,... | collective-permute-start | bytes 1572872 | tf_op jit(solution)/shard_map/ppermute | solution.py:571
  262.3 30.1 %collective-permute-start.25 = (bf16[256,1024]{1,0:T(8,128)(2,1)S(1)}, bf16[256,1024]{1,0:T(8,128)(2,1)S(1)}, u32[]{:S(2)}, u32[]{:S(2)}) collective-permute-start(bf16[256,1024]{1,0:T(8,128)(2,1)S(1)} %copy-done.53), channel_id=1, source_target_pairs={{2,4},{3,5},{4,2},{5,3},{10,12},{11,13},{12,10},{13,11},{18,20},{1... | collective-permute-start | bytes 1572872 | tf_op jit(solution)/shard_map/ppermute | solution.py:571
  279.2 21.4 %collective-permute-start.27 = (bf16[256,1024]{1,0:T(8,128)(2,1)}, bf16[256,1024]{1,0:T(8,128)(2,1)S(1)}, u32[]{:S(2)}, u32[]{:S(2)}) collective-permute-start(bf16[256,1024]{1,0:T(8,128)(2,1)} %get-tuple-element.249), channel_id=1, source_target_pairs={{0,2},{1,3},{2,0},{3,1},{4,6},{5,7},{6,4},{7,5},{8,10},{9,11},{10,... | collective-permute-start | bytes 1572872 | tf_op jit(solution)/shard_map/ppermute | solution.py:563
  304.7 7.1 %collective-permute-start.30 = (bf16[1024,352]{0,1:T(8,128)(2,1)S(1)}, bf16[1024,352]{0,1:T(8,128)(2,1)S(1)}, u32[]{:S(2)}, u32[]{:S(2)}) collective-permute-start(bf16[1024,352]{0,1:T(8,128)(2,1)S(1)} %slice.440), channel_id=1, source_target_pairs={{0,1},{1,0},{2,3},{3,2},{4,5},{5,4},{6,7},{7,6},{8,9},{9,8},{10,11... | collective-permute-start | bytes 2162696 | tf_op jit(solution)/shard_map/ppermute | solution.py:563
  309.5 37.1 %collective-permute-start.28 = (bf16[256,1024]{1,0:T(8,128)(2,1)S(1)}, bf16[256,1024]{1,0:T(8,128)(2,1)S(1)}, u32[]{:S(2)}, u32[]{:S(2)}) collective-permute-start(bf16[256,1024]{1,0:T(8,128)(2,1)S(1)} %copy-done.51), channel_id=1, source_target_pairs={{0,4},{1,5},{2,6},{3,7},{4,0},{5,1},{6,2},{7,3},{8,12},{9,13},{10,... | collective-permute-start | bytes 1572872 | tf_op jit(solution)/shard_map/ppermute | solution.py:563
  309.5 37.1 %collective-permute-start.29 = (bf16[256,1024]{1,0:T(8,128)(2,1)S(1)}, bf16[256,1024]{1,0:T(8,128)(2,1)S(1)}, u32[]{:S(2)}, u32[]{:S(2)}) collective-permute-start(bf16[256,1024]{1,0:T(8,128)(2,1)S(1)} %copy-done.52), channel_id=1, source_target_pairs={{0,6},{1,7},{2,4},{3,5},{4,2},{5,3},{6,0},{7,1},{8,14},{9,15},{10,... | collective-permute-start | bytes 1572872 | tf_op jit(solution)/shard_map/ppermute | solution.py:563
  346.6 220.0 %reduce-scatter.2.cloned.1.call-start = ((), (), s32[]{:S(2)}) async-start(), calls=%async_computation.2 | async-start | bytes 2621440 | tf_op jit(solution)/shard_map/reduce_scatter | solution.py:1128
  352.7 37.1 %collective-permute-start.34 = (bf16[1120,256]{1,0:T(8,128)(2,1)}, bf16[1120,256]{1,0:T(8,128)(2,1)S(1)}, u32[]{:S(2)}, u32[]{:S(2)}) collective-permute-start(bf16[1120,256]{1,0:T(8,128)(2,1)} %get-tuple-element.269.grad_ref), channel_id=1, source_target_pairs={{0,4},{1,5},{2,6},{3,7},{4,0},{5,1},{6,2},{7,3},{8,12},{9,13},{10,... | collective-permute-start | bytes 1720328 | tf_op jit(solution)/shard_map/ppermute | solution.py:563
  364.4 26.8 %collective-permute-start.33 = (bf16[1120,256]{1,0:T(8,128)(2,1)}, bf16[1120,256]{1,0:T(8,128)(2,1)S(1)}, u32[]{:S(2)}, u32[]{:S(2)}) collective-permute-start(bf16[1120,256]{1,0:T(8,128)(2,1)} %get-tuple-element.269.grad_ref), channel_id=1, source_target_pairs={{0,2},{1,3},{2,0},{3,1},{4,6},{5,7},{6,4},{7,5},{8,10},{9,11},{10,... | collective-permute-start | bytes 1720328 | tf_op jit(solution)/shard_map/ppermute | solution.py:563
  389.9 16.8 %collective-permute-start.37 = (bf16[1120,256]{1,0:T(8,128)(2,1)S(1)}, bf16[1120,256]{1,0:T(8,128)(2,1)S(1)}, u32[]{:S(2)}, u32[]{:S(2)}) collective-permute-start(bf16[1120,256]{1,0:T(8,128)(2,1)S(1)} %collective-permute-done.34.grad_ref), channel_id=1, source_target_pairs={{4,6},{5,7},{2,0},{3,1},{12,14},{13,15},{10,8},{11,9},{20,22},{21,... | collective-permute-start | bytes 1720328 | tf_op jit(solution)/shard_map/ppermute | solution.py:571
  391.2 15.4 %collective-permute-start.36 = (bf16[1120,256]{1,0:T(8,128)(2,1)S(1)}, bf16[1120,256]{1,0:T(8,128)(2,1)S(1)}, u32[]{:S(2)}, u32[]{:S(2)}) collective-permute-start(bf16[1120,256]{1,0:T(8,128)(2,1)S(1)} %copy-done.46), channel_id=1, source_target_pairs={{2,4},{3,5},{4,2},{5,3},{10,12},{11,13},{12,10},{13,11},{18,20},{1... | collective-permute-start | bytes 1720328 | tf_op jit(solution)/shard_map/ppermute | solution.py:571
  400.9 28.4 %collective-permute-start.35 = (bf16[1024,256]{1,0:T(8,128)(2,1)}, bf16[1024,256]{1,0:T(8,128)(2,1)S(1)}, u32[]{:S(2)}, u32[]{:S(2)}) collective-permute-start(bf16[1024,256]{1,0:T(8,128)(2,1)} %get-tuple-element.268), channel_id=1, source_target_pairs={{0,2},{1,3},{2,0},{3,1},{4,6},{5,7},{6,4},{7,5},{8,10},{9,11},{10,... | collective-permute-start | bytes 1572872 | tf_op jit(solution)/shard_map/ppermute | solution.py:563
  416.2 40.9 %collective-permute-start.38 = (bf16[1024,256]{1,0:T(8,128)(2,1)}, bf16[1024,256]{1,0:T(8,128)(2,1)S(1)}, u32[]{:S(2)}, u32[]{:S(2)}) collective-permute-start(bf16[1024,256]{1,0:T(8,128)(2,1)} %get-tuple-element.274), channel_id=1, source_target_pairs={{0,4},{1,5},{2,6},{3,7},{4,0},{5,1},{6,2},{7,3},{8,12},{9,13},{10,... | collective-permute-start | bytes 1572872 | tf_op jit(solution)/shard_map/ppermute | solution.py:563
  429.3 27.8 %collective-permute-start.39 = (bf16[1024,256]{1,0:T(8,128)(2,1)}, bf16[1024,256]{1,0:T(8,128)(2,1)S(1)}, u32[]{:S(2)}, u32[]{:S(2)}) collective-permute-start(bf16[1024,256]{1,0:T(8,128)(2,1)} %get-tuple-element.276), channel_id=1, source_target_pairs={{0,6},{1,7},{2,4},{3,5},{4,2},{5,3},{6,0},{7,1},{8,14},{9,15},{10,... | collective-permute-start | bytes 1572872 | tf_op jit(solution)/shard_map/ppermute | solution.py:563
  464.1 9.8 %collective-permute-start.40 = (bf16[16,32,2048]{2,1,0:T(8,128)(2,1)}, bf16[16,32,2048]{2,1,0:T(8,128)(2,1)}, u32[]{:S(2)}, u32[]{:S(2)}) collective-permute-start(bf16[16,32,2048]{2,1,0:T(8,128)(2,1)} %get-tuple-element.293), channel_id=1, source_target_pairs={{0,1},{1,0},{2,3},{3,2},{4,5},{5,4},{6,7},{7,6},{8,9},{9,8},{10,11... | collective-permute-start | bytes 6291464 | tf_op jit(solution)/shard_map/ppermute | solution.py:563
  469.1 26.2 %collective-permute-start.43 = (bf16[16,32,2048]{2,1,0:T(8,128)(2,1)}, bf16[16,32,2048]{2,1,0:T(8,128)(2,1)}, u32[]{:S(2)}, u32[]{:S(2)}) collective-permute-start(bf16[16,32,2048]{2,1,0:T(8,128)(2,1)} %get-tuple-element.291), channel_id=1, source_target_pairs={{0,1},{1,0},{2,3},{3,2},{4,5},{5,4},{6,7},{7,6},{8,9},{9,8},{10,11... | collective-permute-start | bytes 6291464 | tf_op jit(solution)/shard_map/ppermute | solution.py:563
  469.8 54.8 %collective-permute-start.45 = (bf16[8,256,1024]{2,1,0:T(8,128)(2,1)}, bf16[8,256,1024]{2,1,0:T(8,128)(2,1)}, u32[]{:S(2)}, u32[]{:S(2)}) collective-permute-start(bf16[8,256,1024]{2,1,0:T(8,128)(2,1)} %get-tuple-element.310), channel_id=1, source_target_pairs={{0,1},{1,0},{2,3},{3,2},{4,5},{5,4},{6,7},{7,6},{8,9},{9,8},{10,11... | collective-permute-start | bytes 12582920 | tf_op jit(solution)/shard_map/ppermute | solution.py:563
  492.6 8.7 %collective-permute-start.42 = (bf16[2,32,2048]{2,1,0:T(8,128)(2,1)S(1)}, bf16[2,32,2048]{2,1,0:T(8,128)(2,1)S(1)}, u32[]{:S(2)}, u32[]{:S(2)}) collective-permute-start(bf16[2,32,2048]{2,1,0:T(8,128)(2,1)S(1)} %get-tuple-element.395), channel_id=1, source_target_pairs={{0,16},{8,24},{16,0},{24,8},{1,17},{9,25},{17,1},{25,9},{2,18},{10... | collective-permute-start | bytes 786440 | tf_op jit(solution)/shard_map/ppermute | solution.py:563
  494.3 8.5 %collective-permute-start.41 = (bf16[2,32,2048]{2,1,0:T(8,128)(2,1)S(1)}, bf16[2,32,2048]{2,1,0:T(8,128)(2,1)S(1)}, u32[]{:S(2)}, u32[]{:S(2)}) collective-permute-start(bf16[2,32,2048]{2,1,0:T(8,128)(2,1)S(1)} %get-tuple-element.396), channel_id=1, source_target_pairs={{0,8},{8,0},{16,24},{24,16},{1,9},{9,1},{17,25},{25,17},{2,10},{10... | collective-permute-start | bytes 786440 | tf_op jit(solution)/shard_map/ppermute | solution.py:563
  499.3 17.0 %collective-permute-start.49 = (bf16[2,32,2048]{2,1,0:T(8,128)(2,1)}, bf16[2,32,2048]{2,1,0:T(8,128)(2,1)S(1)}, u32[]{:S(2)}, u32[]{:S(2)}) collective-permute-start(bf16[2,32,2048]{2,1,0:T(8,128)(2,1)} %get-tuple-element.393), channel_id=1, source_target_pairs={{0,16},{8,24},{16,0},{24,8},{1,17},{9,25},{17,1},{25,9},{2,18},{10... | collective-permute-start | bytes 786440 | tf_op jit(solution)/shard_map/ppermute | solution.py:563
  500.0 16.3 %collective-permute-start.48 = (bf16[2,32,2048]{2,1,0:T(8,128)(2,1)}, bf16[2,32,2048]{2,1,0:T(8,128)(2,1)S(1)}, u32[]{:S(2)}, u32[]{:S(2)}) collective-permute-start(bf16[2,32,2048]{2,1,0:T(8,128)(2,1)} %get-tuple-element.394), channel_id=1, source_target_pairs={{0,8},{8,0},{16,24},{24,16},{1,9},{9,1},{17,25},{25,17},{2,10},{10... | collective-permute-start | bytes 786440 | tf_op jit(solution)/shard_map/ppermute | solution.py:563
  502.9 15.9 %collective-permute-start.61 = (bf16[4,32,2048]{2,1,0:T(8,128)(2,1)S(1)}, bf16[4,32,2048]{2,1,0:T(8,128)(2,1)}, u32[]{:S(2)}, u32[]{:S(2)}) collective-permute-start(bf16[4,32,2048]{2,1,0:T(8,128)(2,1)S(1)} %pad_maximum_fusion.6), channel_id=1, source_target_pairs={{0,16},{8,24},{16,0},{24,8},{1,17},{9,25},{17,1},{25,9},{2,18},{10... | collective-permute-start | bytes 1572872 | tf_op jit(solution)/shard_map/ppermute | solution.py:563
  503.4 16.5 %collective-permute-start.60 = (bf16[4,32,2048]{2,1,0:T(8,128)(2,1)S(1)}, bf16[4,32,2048]{2,1,0:T(8,128)(2,1)}, u32[]{:S(2)}, u32[]{:S(2)}) collective-permute-start(bf16[4,32,2048]{2,1,0:T(8,128)(2,1)S(1)} %pad_maximum_fusion.5), channel_id=1, source_target_pairs={{0,8},{8,0},{16,24},{24,16},{1,9},{9,1},{17,25},{25,17},{2,10},{10... | collective-permute-start | bytes 1572872 | tf_op jit(solution)/shard_map/ppermute | solution.py:563
  516.3 21.0 %collective-permute-start.44 = (bf16[16,32,2176]{2,1,0:T(8,128)(2,1)}, bf16[16,32,2176]{2,1,0:T(8,128)(2,1)S(1)}, u32[]{:S(2)}, u32[]{:S(2)}) collective-permute-start(bf16[16,32,2176]{2,1,0:T(8,128)(2,1)} %get-tuple-element.309), channel_id=1, source_target_pairs={{0,1},{1,0},{2,3},{3,2},{4,5},{5,4},{6,7},{7,6},{8,9},{9,8},{10,11... | collective-permute-start | bytes 6684680 | tf_op jit(solution)/shard_map/ppermute | solution.py:563
  516.4 21.5 %collective-permute-start.51 = (bf16[4,32,2048]{2,1,0:T(8,128)(2,1)S(1)}, bf16[4,32,2048]{2,1,0:T(8,128)(2,1)}, u32[]{:S(2)}, u32[]{:S(2)}) collective-permute-start(bf16[4,32,2048]{2,1,0:T(8,128)(2,1)S(1)} %pad_maximum_fusion.8), channel_id=1, source_target_pairs={{0,16},{8,24},{16,0},{24,8},{1,17},{9,25},{17,1},{25,9},{2,18},{10... | collective-permute-start | bytes 1572872 | tf_op jit(solution)/shard_map/ppermute | solution.py:563
  518.8 19.1 %collective-permute-start.50 = (bf16[4,32,2048]{2,1,0:T(8,128)(2,1)S(1)}, bf16[4,32,2048]{2,1,0:T(8,128)(2,1)S(1)}, u32[]{:S(2)}, u32[]{:S(2)}) collective-permute-start(bf16[4,32,2048]{2,1,0:T(8,128)(2,1)S(1)} %pad_maximum_fusion.7), channel_id=1, source_target_pairs={{0,8},{8,0},{16,24},{24,16},{1,9},{9,1},{17,25},{25,17},{2,10},{10... | collective-permute-start | bytes 1572872 | tf_op jit(solution)/shard_map/ppermute | solution.py:563
  522.1 15.9 %collective-permute-start.64 = (bf16[32,2048]{1,0:T(8,128)(2,1)}, bf16[32,2048]{1,0:T(8,128)(2,1)S(1)}, u32[]{:S(2)}, u32[]{:S(2)}) collective-permute-start(bf16[32,2048]{1,0:T(8,128)(2,1)} %get-tuple-element.385), channel_id=1, source_target_pairs={{0,6},{1,7},{2,4},{3,5},{4,2},{5,3},{6,0},{7,1},{8,14},{9,15},{10,... | collective-permute-start | bytes 393224 | tf_op jit(solution)/shard_map/ppermute | solution.py:563
  524.6 16.0 %collective-permute-start.63 = (bf16[32,2048]{1,0:T(8,128)(2,1)}, bf16[32,2048]{1,0:T(8,128)(2,1)S(1)}, u32[]{:S(2)}, u32[]{:S(2)}) collective-permute-start(bf16[32,2048]{1,0:T(8,128)(2,1)} %get-tuple-element.386), channel_id=1, source_target_pairs={{0,4},{1,5},{2,6},{3,7},{4,0},{5,1},{6,2},{7,3},{8,12},{9,13},{10,... | collective-permute-start | bytes 393224 | tf_op jit(solution)/shard_map/ppermute | solution.py:563
  544.0 8.4 %collective-permute-start.47 = (bf16[2,32,2176]{2,1,0:T(8,128)(2,1)S(1)}, bf16[2,32,2176]{2,1,0:T(8,128)(2,1)S(1)}, u32[]{:S(2)}, u32[]{:S(2)}) collective-permute-start(bf16[2,32,2176]{2,1,0:T(8,128)(2,1)S(1)} %get-tuple-element.383), channel_id=1, source_target_pairs={{0,16},{8,24},{16,0},{24,8},{1,17},{9,25},{17,1},{25,9},{2,18},{10... | collective-permute-start | bytes 835592 | tf_op jit(solution)/shard_map/ppermute | solution.py:563
  544.1 8.3 %collective-permute-start.46 = (bf16[2,32,2176]{2,1,0:T(8,128)(2,1)S(1)}, bf16[2,32,2176]{2,1,0:T(8,128)(2,1)S(1)}, u32[]{:S(2)}, u32[]{:S(2)}) collective-permute-start(bf16[2,32,2176]{2,1,0:T(8,128)(2,1)S(1)} %get-tuple-element.384), channel_id=1, source_target_pairs={{0,8},{8,0},{16,24},{24,16},{1,9},{9,1},{17,25},{25,17},{2,10},{10... | collective-permute-start | bytes 835592 | tf_op jit(solution)/shard_map/ppermute | solution.py:563
  552.6 13.5 %collective-permute-start.52 = (bf16[4,32,2176]{2,1,0:T(8,128)(2,1)S(1)}, bf16[4,32,2176]{2,1,0:T(8,128)(2,1)S(1)}, u32[]{:S(2)}, u32[]{:S(2)}) collective-permute-start(bf16[4,32,2176]{2,1,0:T(8,128)(2,1)S(1)} %pad_maximum_fusion.3), channel_id=1, source_target_pairs={{0,8},{8,0},{16,24},{24,16},{1,9},{9,1},{17,25},{25,17},{2,10},{10... | collective-permute-start | bytes 1671176 | tf_op jit(solution)/shard_map/ppermute | solution.py:563
  553.8 12.6 %collective-permute-start.53 = (bf16[4,32,2176]{2,1,0:T(8,128)(2,1)S(1)}, bf16[4,32,2176]{2,1,0:T(8,128)(2,1)S(1)}, u32[]{:S(2)}, u32[]{:S(2)}) collective-permute-start(bf16[4,32,2176]{2,1,0:T(8,128)(2,1)S(1)} %pad_maximum_fusion.4), channel_id=1, source_target_pairs={{0,16},{8,24},{16,0},{24,8},{1,17},{9,25},{17,1},{25,9},{2,18},{10... | collective-permute-start | bytes 1671176 | tf_op jit(solution)/shard_map/ppermute | solution.py:563
  554.9 11.7 %collective-permute-start.59 = (bf16[32,2048]{1,0:T(8,128)(2,1)S(1)}, bf16[32,2048]{1,0:T(8,128)(2,1)S(1)}, u32[]{:S(2)}, u32[]{:S(2)}) collective-permute-start(bf16[32,2048]{1,0:T(8,128)(2,1)S(1)} %get-tuple-element.389), channel_id=1, source_target_pairs={{0,6},{1,7},{2,4},{3,5},{4,2},{5,3},{6,0},{7,1},{8,14},{9,15},{10,... | collective-permute-start | bytes 393224 | tf_op jit(solution)/shard_map/ppermute | solution.py:563
  557.0 10.3 %collective-permute-start.58 = (bf16[32,2048]{1,0:T(8,128)(2,1)S(1)}, bf16[32,2048]{1,0:T(8,128)(2,1)S(1)}, u32[]{:S(2)}, u32[]{:S(2)}) collective-permute-start(bf16[32,2048]{1,0:T(8,128)(2,1)S(1)} %get-tuple-element.390), channel_id=1, source_target_pairs={{0,4},{1,5},{2,6},{3,7},{4,0},{5,1},{6,2},{7,3},{8,12},{9,13},{10,... | collective-permute-start | bytes 393224 | tf_op jit(solution)/shard_map/ppermute | solution.py:563
  557.0 10.3 %collective-permute-start.57 = (bf16[32,2048]{1,0:T(8,128)(2,1)S(1)}, bf16[32,2048]{1,0:T(8,128)(2,1)S(1)}, u32[]{:S(2)}, u32[]{:S(2)}) collective-permute-start(bf16[32,2048]{1,0:T(8,128)(2,1)S(1)} %get-tuple-element.391), channel_id=1, source_target_pairs={{0,2},{1,3},{2,0},{3,1},{4,6},{5,7},{6,4},{7,5},{8,10},{9,11},{10,... | collective-permute-start | bytes 393224 | tf_op jit(solution)/shard_map/ppermute | solution.py:563
  570.1 8.5 %collective-permute-start.56 = (bf16[32,2176]{1,0:T(8,128)(2,1)S(1)}, bf16[32,2176]{1,0:T(8,128)(2,1)S(1)}, u32[]{:S(2)}, u32[]{:S(2)}) collective-permute-start(bf16[32,2176]{1,0:T(8,128)(2,1)S(1)} %get-tuple-element.379), channel_id=1, source_target_pairs={{0,6},{1,7},{2,4},{3,5},{4,2},{5,3},{6,0},{7,1},{8,14},{9,15},{10,... | collective-permute-start | bytes 417800 | tf_op jit(solution)/shard_map/ppermute | solution.py:563
  571.9 10.6 %collective-permute-start.55 = (bf16[32,2176]{1,0:T(8,128)(2,1)S(1)}, bf16[32,2176]{1,0:T(8,128)(2,1)S(1)}, u32[]{:S(2)}, u32[]{:S(2)}) collective-permute-start(bf16[32,2176]{1,0:T(8,128)(2,1)S(1)} %get-tuple-element.380), channel_id=1, source_target_pairs={{0,4},{1,5},{2,6},{3,7},{4,0},{5,1},{6,2},{7,3},{8,12},{9,13},{10,... | collective-permute-start | bytes 417800 | tf_op jit(solution)/shard_map/ppermute | solution.py:563
  571.9 10.6 %collective-permute-start.54 = (bf16[32,2176]{1,0:T(8,128)(2,1)S(1)}, bf16[32,2176]{1,0:T(8,128)(2,1)S(1)}, u32[]{:S(2)}, u32[]{:S(2)}) collective-permute-start(bf16[32,2176]{1,0:T(8,128)(2,1)S(1)} %get-tuple-element.381), channel_id=1, source_target_pairs={{0,2},{1,3},{2,0},{3,1},{4,6},{5,7},{6,4},{7,5},{8,10},{9,11},{10,... | collective-permute-start | bytes 417800 | tf_op jit(solution)/shard_map/ppermute | solution.py:563
  (59 other events, 458.5 us)
Sparse Core Ops, SparseCore 0:
  52.9 44.3 all-gather.5
  127.7 72.4 all-gather.3
  346.8 79.9 all-reduce.7
  474.0 49.1 reduce-scatter.1

commit v5 on v4

--- a/solution.py
+++ b/solution.py
@@ -1115,7 +1115,7 @@
     if direct:
         middle = grad_blocks(sizes, me, products)
         outer = reduce_core(sizes, after(memory_sum, query_grads), middle)
-        mix_grad = after(mix_grad, (middle, outer))
+        mix_grad = after(mix_grad, middle)
     wide_grad, table_grad = self_backward(
         target_lengths, mix_grad, self_wide, self_stats, small_rows, lanes_of, buckets
     )
@@ -1148,7 +1148,7 @@
         middle = reduce_sides(sizes, middle, first)
         first = reduce_corner(sizes, first, middle)
         first = reduce_sides(sizes, first)
-        middle_sum = reduce_line(sizes, middle, (first, branch_sum))
+        middle_sum = reduce_line(sizes, middle, first)
         first_sum = reduce_line(sizes, first)
         branch_sum = after(branch_sum, first)
     else:

time: 598 us -> 598 us (level)
    unnamed x119 -> x105, local copies, waits for them, and re-layouts: 13.5 us -> 11.7 us
where the time goes in v5:
time: 598 us; the launch traced here: 592 us
  Pallas kernels  209 us (35%)
  waiting for transfers between devices  182 us (30%)
  starting transfers between devices  113 us (19%)
  local copies, waits for them, and re-layouts  35.1 us (6%)
  other arithmetic  30.3 us (5%)
  between operations  15 us (3%)
  matrix products  7.66 us (1%)
    ppermute x59, waiting for transfers between devices, exchange(): lax.ppermute(value, axis, [(place, place ^ mask) for place in range(size)])  182 us
    ppermute x59, starting transfers between devices, exchange(): lax.ppermute(value, axis, [(place, place ^ mask) for place in range(size)])  97.8 us
    pallas_call x9, Pallas kernels, vmem_call(): pl.pallas_call(body, in_specs=[pl.BlockSpec(memory_space=pltpu.SMEM)] * l...  60 us
    pallas_call x4, Pallas kernels, cross_backward(): pl.pallas_call(functools.partial(cross_backward_kernel, chunk), grid_spec...  34.4 us
    pallas_call x4, Pallas kernels, cross_forward(): pl.pallas_call(functools.partial(cross_forward_kernel, chunk), grid_spec=...  29.7 us
    pallas_call x4, Pallas kernels, ffn_chunk(): pl.pallas_call(ffn_kernel, grid_spec=pltpu.PrefetchScalarGridSpec(num_sca...  29.4 us
    pallas_call x1, Pallas kernels, memory_backward(): pl.pallas_call(functools.partial(memory_backward_kernel, sizes), grid_spe...  26.4 us
    ppermute x6, starting transfers between devices, by_lines(): return lax.ppermute(array, 'ffn', pairs)  15.3 us
  transfers between devices with their start and end apart: 69, of which 23 were waited for; matrix products, arithmetic and copies ran while one was open for 10% of the time, Pallas kernels for 33%

profile of v5, /device:TPU:0, one launch (start us, length us, event | category | flops | bytes accessed | tf_op | source)
XLA Modules:
  0.0 592.3 jit_solution(8107485414882052494)
XLA Ops:
  15.5 4.6 collective-permute-start.2
  20.7 8.3 %collective-permute-done.2 = bf16[32,5248]{1,0:T(8,128)(2,1)S(1)} collective-permute-done((bf16[32,5248]{1,0:T(8,128)(2,1)S(1)}, bf16[32,5248]{1,0:T(8,128)(2,1)S(1)}, u32[]{:S(2)}, u32[]{:S(2)}) %collective-permute-start.2) | collective-permute-done | bytes 335904 | tf_op jit(solution)/shard_map/ppermute | solution.py:563
  29.0 20.4 %collective-permute-done.1 = bf16[32,5248]{1,0:T(8,128)(2,1)S(1)} collective-permute-done((bf16[32,5248]{1,0:T(8,128)(2,1)S(1)}, bf16[32,5248]{1,0:T(8,128)(2,1)S(1)}, u32[]{:S(2)}, u32[]{:S(2)}) %collective-permute-start.1) | collective-permute-done | bytes 335904 | tf_op jit(solution)/shard_map/ppermute | solution.py:563
  52.8 28.0 %collective-permute-done.4.refs_2_ = bf16[4,32,5248]{2,1,0:T(8,128)(2,1)S(1)} collective-permute-done((bf16[4,32,5248]{2,1,0:T(8,128)(2,1)S(1)}, bf16[4,32,5248]{2,1,0:T(8,128)(2,1)S(1)}, u32[]{:S(2)}, u32[]{:S(2)}) %collective-permute-start.4) | collective-permute-done | bytes 1343520 | tf_op jit(solution)/shard_map/ppermute | solution.py:563
  83.2 2.0 slice.327
  87.6 10.2 %collective-permute-done.5.refs_3_ = bf16[2,32,5248]{2,1,0:T(8,128)(2,1)S(1)} collective-permute-done((bf16[2,32,5248]{2,1,0:T(8,128)(2,1)}, bf16[2,32,5248]{2,1,0:T(8,128)(2,1)S(1)}, u32[]{:S(2)}, u32[]{:S(2)}) %collective-permute-start.5) | collective-permute-done | bytes 671776 | tf_op jit(solution)/shard_map/ppermute | solution.py:563
  97.9 3.3 collective-permute-done.6.refs_4_
  105.5 7.4 %self_forward.1 = (bf16[256,1024]{1,0:T(8,128)(2,1)}, bf16[256,2048]{1,0:T(8,128)(2,1)}, bf16[256,1024]{1,0:T(8,128)(2,1)}, f32[32,128]{1,0:T(8,128)}, f32[8,1024]{1,0:T(8,128)}) custom-call(s32[3]{0:T(128)} %pad_add_fusion.1.me_ref, s32[2]{0:T(128)} %length_ref.3, bf16[256,1024]{1,0:T(8,128)(2,1)} %row_ref.5, s32[128,128]{1,0:T(8,128)} %fusion.6.lane_ref, ...), custom_call_target="tpu_custom_call" | custom-call | flops 1000000000 | bytes 8000000 | tf_op jit(solution)/shard_map/self_forward/pallas_call | solution.py:41
  112.9 6.1 %self_output.1 = (f32[256,1024]{1,0:T(8,128)}, bf16[256,1024]{1,0:T(8,128)(2,1)}, bf16[1024,256]{1,0:T(8,128)(2,1)}, f32[256,1]{1,0:T(8,128)}) custom-call(s32[3]{0:T(128)} %pad_add_fusion.1.me_ref, bf16[256,1024]{1,0:T(8,128)(2,1)} %row_ref.5, bf16[256,1024]{1,0:T(8,128)(2,1)} %get-tuple-element.179.mix_ref.refs_2_, ...), custom_call_target="tpu_custom_call" | custom-call | flops 1000000000 | bytes 8000000 | tf_op jit(solution)/shard_map/self_output/pallas_call | solution.py:41
  119.1 3.0 collective-permute-start.13
  123.0 3.9 place_rows.2.weight_ref
  127.7 13.7 %memory_forward.1 = bf16[8,2,256,1024]{3,2,1,0:T(8,128)(2,1)} custom-call(s32[3]{0:T(128)} %pad_add_fusion.1.me_ref, bf16[4,2,2,256,1024]{4,3,2,1,0:T(8,128)(2,1)} %bitcast.91, bf16[4,2,2,256,1024]{4,3,2,1,0:T(8,128)(2,1)} %collective-permute-done.12.other_ref, bf16[1024,1024]{1,0:T(8,128)(2,1)} %place_rows.2.weight_ref), custom_call_target="tpu_custom_call" | custom-call | flops 8600000512 | bytes 18000000 | tf_op jit(solution)/shard_map/memory_forward/pallas_call | solution.py:653
  141.4 7.5 %cross_forward.4.refs_0_ = bf16[1072,256]{1,0:T(8,128)(2,1)} custom-call(s32[4,5]{1,0:T(4,128)} %pad_add_fusion.info_ref, bf16[1024,256]{1,0:T(8,128)(2,1)} %get-tuple-element.199.query_ref, bf16[8,512,1024]{2,1,0:T(8,128)(2,1)} %bitcast.93), custom_call_target="tpu_custom_call" | custom-call | flops 6000000000 | bytes 4000000 | tf_op jit(solution)/shard_map/cross_forward/pallas_call | solution.py:428
  151.2 7.3 %cross_forward.5 = bf16[1072,256]{1,0:T(8,128)(2,1)} custom-call(s32[4,5]{1,0:T(4,128)} %pad_add_fusion.info_ref, bf16[1024,256]{1,0:T(8,128)(2,1)} %copy-done.42, bf16[8,512,1024]{2,1,0:T(8,128)(2,1)} %bitcast.94), custom_call_target="tpu_custom_call" | custom-call | flops 6000000000 | bytes 4000000 | tf_op jit(solution)/shard_map/cross_forward/pallas_call | solution.py:428
  158.6 7.4 %cross_forward.6 = bf16[1072,256]{1,0:T(8,128)(2,1)} custom-call(s32[4,5]{1,0:T(4,128)} %pad_add_fusion.info_ref, bf16[1024,256]{1,0:T(8,128)(2,1)} %copy-done.41, bf16[8,512,1024]{2,1,0:T(8,128)(2,1)} %bitcast.95), custom_call_target="tpu_custom_call" | custom-call | flops 6000000000 | bytes 4000000 | tf_op jit(solution)/shard_map/cross_forward/pallas_call | solution.py:428
  167.1 7.5 %cross_forward.7 = bf16[1072,256]{1,0:T(8,128)(2,1)} custom-call(s32[4,5]{1,0:T(4,128)} %pad_add_fusion.info_ref, bf16[1024,256]{1,0:T(8,128)(2,1)} %broadcast_select_fusion.2.query_ref, bf16[8,512,1024]{2,1,0:T(8,128)(2,1)} %bitcast.96), custom_call_target="tpu_custom_call" | custom-call | flops 6000000000 | bytes 4000000 | tf_op jit(solution)/shard_map/cross_forward/pallas_call | solution.py:428
  175.8 5.1 collective-permute-start.16
  182.7 8.8 %place_rows.3 = (bf16[1024,2048]{1,0:T(8,128)(2,1)}, bf16[1024,2048]{1,0:T(8,128)(2,1)}) custom-call(s32[3]{0:T(128)} %pad_add_fusion.1.me_ref, bf16[4,32,5248]{2,1,0:T(8,128)(2,1)} %copy-done, bf16[4,32,5248]{2,1,0:T(8,128)(2,1)} %collective-permute-done.3.refs_1_, bf16[4,32,5248]{2,1,0:T(8,128)(2,1)} %copy-done.2, bf16[2,32,5248]{2,1,0:T(8,128)(2,1)} %copy-done.8, ...), custom_call_target="tpu_custom_call" | custom-call | flops 1000000000 | bytes 8000000 | tf_op jit(solution)/shard_map/place_rows/pallas_call | solution.py:41
  195.4 2.3 copy.99
  197.7 2.3 copy.101
  204.8 3.9 collective-permute-done.16.refs_2_
  208.7 12.8 %collective-permute-done.19.refs_3_ = bf16[1072,256]{1,0:T(8,128)(2,1)} collective-permute-done((bf16[1072,256]{1,0:T(8,128)(2,1)}, bf16[1072,256]{1,0:T(8,128)(2,1)}, u32[]{:S(2)}, u32[]{:S(2)}) %collective-permute-start.19) | collective-permute-done | bytes 548896 | tf_op jit(solution)/shard_map/ppermute | solution.py:563
  221.5 5.0 cross_join.1
  226.5 11.0 %collective-permute-start.23 = (bf16[256,1024]{1,0:T(8,128)(2,1)}, bf16[256,1024]{1,0:T(8,128)(2,1)S(1)}, u32[]{:S(2)}, u32[]{:S(2)}) collective-permute-start(bf16[256,1024]{1,0:T(8,128)(2,1)} %get-tuple-element.223.row_ref), channel_id=1, source_target_pairs={{0,4},{1,5},{2,6},{3,7},{4,0},{5,1},{6,2},{7,3},{8,12},{9,13},{10,... | collective-permute-start | bytes 1572872 | tf_op jit(solution)/shard_map/ppermute | solution.py:563
  237.9 7.3 %ffn_chunk.4 = (bf16[256,1024]{1,0:T(8,128)(2,1)}, bf16[4,256,1024]{2,1,0:T(8,128)(2,1)}, bf16[4,256,1024]{2,1,0:T(8,128)(2,1)}, bf16[4,256,1024]{2,1,0:T(8,128)...) custom-call(s32[3]{0:T(128)} %pad_add_fusion.1.me_ref, ...), custom_call_target="tpu_custom_call" | custom-call | flops 3000000000 | bytes 8000000 | tf_op jit(solution)/shard_map/ffn_chunk/pallas_call | solution.py:542
  245.2 15.8 %collective-permute-done.23.row_ref = bf16[256,1024]{1,0:T(8,128)(2,1)S(1)} collective-permute-done((bf16[256,1024]{1,0:T(8,128)(2,1)}, bf16[256,1024]{1,0:T(8,128)(2,1)S(1)}, u32[]{:S(2)}, u32[]{:S(2)}) %collective-permute-start.23) | collective-permute-done | bytes 524320 | tf_op jit(solution)/shard_map/ppermute | solution.py:563
  262.3 9.4 %collective-permute-start.25 = (bf16[256,1024]{1,0:T(8,128)(2,1)S(1)}, bf16[256,1024]{1,0:T(8,128)(2,1)S(1)}, u32[]{:S(2)}, u32[]{:S(2)}) collective-permute-start(bf16[256,1024]{1,0:T(8,128)(2,1)S(1)} %copy-done.46), channel_id=1, source_target_pairs={{2,4},{3,5},{4,2},{5,3},{10,12},{11,13},{12,10},{13,11},{18,20},{1... | collective-permute-start | bytes 1572872 | tf_op jit(solution)/shard_map/ppermute | solution.py:571
  271.8 7.4 %ffn_chunk.5 = (bf16[256,1024]{1,0:T(8,128)(2,1)}, bf16[4,256,1024]{2,1,0:T(8,128)(2,1)}, bf16[4,256,1024]{2,1,0:T(8,128)(2,1)}, bf16[4,256,1024]{2,1,0:T(8,128)...) custom-call(s32[3]{0:T(128)} %pad_add_fusion.1.me_ref, ...), custom_call_target="tpu_custom_call", output_to_operand_aliasing={{1}: (6, {}), {2}: (7, {}), {3}: (8, {}), {4}: (9, {}), {5}... | custom-call | flops 3000000000 | bytes 8000000 | tf_op jit(solution)/shard_map/ffn_chunk/pallas_call | solution.py:542
  279.1 6.1 %collective-permute-start.27 = (bf16[256,1024]{1,0:T(8,128)(2,1)}, bf16[256,1024]{1,0:T(8,128)(2,1)S(1)}, u32[]{:S(2)}, u32[]{:S(2)}) collective-permute-start(bf16[256,1024]{1,0:T(8,128)(2,1)} %get-tuple-element.249), channel_id=1, source_target_pairs={{0,2},{1,3},{2,0},{3,1},{4,6},{5,7},{6,4},{7,5},{8,10},{9,11},{10,... | collective-permute-start | bytes 1572872 | tf_op jit(solution)/shard_map/ppermute | solution.py:563
  285.2 7.3 %ffn_chunk.6 = (bf16[256,1024]{1,0:T(8,128)(2,1)}, bf16[4,256,1024]{2,1,0:T(8,128)(2,1)}, bf16[4,256,1024]{2,1,0:T(8,128)(2,1)}, bf16[4,256,1024]{2,1,0:T(8,128)...) custom-call(s32[3]{0:T(128)} %pad_add_fusion.1.me_ref, ...), custom_call_target="tpu_custom_call", output_to_operand_aliasing={{1}: (6, {}), {2}: (7, {}), {3}: (8, {}), {4}: (9, {}), {5}... | custom-call | flops 3000000000 | bytes 8000000 | tf_op jit(solution)/shard_map/ffn_chunk/pallas_call | solution.py:542
  293.4 7.3 %ffn_chunk.7 = (bf16[256,1024]{1,0:T(8,128)(2,1)}, bf16[4,256,1024]{2,1,0:T(8,128)(2,1)}, bf16[4,256,1024]{2,1,0:T(8,128)(2,1)}, bf16[4,256,1024]{2,1,0:T(8,128)...) custom-call(s32[3]{0:T(128)} %pad_add_fusion.1.me_ref, ...), custom_call_target="tpu_custom_call", output_to_operand_aliasing={{1}: (6, {}), {2}: (7, {}), {3}: (8, {}), {4}: (9, {}), {5}... | custom-call | flops 3000000000 | bytes 8000000 | tf_op jit(solution)/shard_map/ffn_chunk/pallas_call | solution.py:542
  300.8 4.0 convolution_bitcast_fusion.2
  307.4 1.9 convolution_bitcast_fusion
  309.6 2.4 collective-permute-start.29
  315.4 31.4 %collective-permute-done.28.refs_2_ = bf16[256,1024]{1,0:T(8,128)(2,1)S(1)} collective-permute-done((bf16[256,1024]{1,0:T(8,128)(2,1)S(1)}, bf16[256,1024]{1,0:T(8,128)(2,1)S(1)}, u32[]{:S(2)}, u32[]{:S(2)}) %collective-permute-start.28) | collective-permute-done | bytes 524320 | tf_op jit(solution)/shard_map/ppermute | solution.py:563
  347.7 5.2 ffn_join.1
  352.9 11.5 %collective-permute-start.34 = (bf16[1120,256]{1,0:T(8,128)(2,1)}, bf16[1120,256]{1,0:T(8,128)(2,1)S(1)}, u32[]{:S(2)}, u32[]{:S(2)}) collective-permute-start(bf16[1120,256]{1,0:T(8,128)(2,1)} %get-tuple-element.269.grad_ref), channel_id=1, source_target_pairs={{0,4},{1,5},{2,6},{3,7},{4,0},{5,1},{6,2},{7,3},{8,12},{9,13},{10,... | collective-permute-start | bytes 1720328 | tf_op jit(solution)/shard_map/ppermute | solution.py:563
  364.5 8.7 %cross_backward.4 = (bf16[1024,256]{1,0:T(8,128)(2,1)}, bf16[8,512,1024]{2,1,0:T(8,128)(2,1)}) custom-call(s32[4,5]{1,0:T(4,128)} %pad_add_fusion.info_ref, bf16[1024,256]{1,0:T(8,128)(2,1)} %get-tuple-element.199.query_ref, bf16[1120,256]{1,0:T(8,128)(2,1)} %get-tuple-element.269.grad_ref, bf16[8,512,1024]{2,1,0:T(8,128)(2,1)} %bitcast.97), custom_call_target="tpu_custom_call" | custom-call | flops 10000000000 | bytes 8000000 | tf_op jit(solution)/shard_map/cross_backward/pallas_call | solution.py:481
  373.2 16.7 %collective-permute-done.34.grad_ref = bf16[1120,256]{1,0:T(8,128)(2,1)S(1)} collective-permute-done((bf16[1120,256]{1,0:T(8,128)(2,1)}, bf16[1120,256]{1,0:T(8,128)(2,1)S(1)}, u32[]{:S(2)}, u32[]{:S(2)}) %collective-permute-start.34) | collective-permute-done | bytes 573472 | tf_op jit(solution)/shard_map/ppermute | solution.py:563
  392.3 8.6 %cross_backward.5 = (bf16[1024,256]{1,0:T(8,128)(2,1)}, bf16[8,512,1024]{2,1,0:T(8,128)(2,1)}) custom-call(s32[4,5]{1,0:T(4,128)} %pad_add_fusion.info_ref, bf16[1024,256]{1,0:T(8,128)(2,1)} %copy-done.42, bf16[1120,256]{1,0:T(8,128)(2,1)} %copy-done.40, bf16[8,512,1024]{2,1,0:T(8,128)(2,1)} %bitcast.98, ...), custom_call_target="tpu_custom_call", output_to_operand_aliasing={{1}: (4, {})} | custom-call | flops 10000000000 | bytes 8000000 | tf_op jit(solution)/shard_map/cross_backward/pallas_call | solution.py:481
  400.9 5.9 %collective-permute-start.35 = (bf16[1024,256]{1,0:T(8,128)(2,1)}, bf16[1024,256]{1,0:T(8,128)(2,1)S(1)}, u32[]{:S(2)}, u32[]{:S(2)}) collective-permute-start(bf16[1024,256]{1,0:T(8,128)(2,1)} %get-tuple-element.268), channel_id=1, source_target_pairs={{0,2},{1,3},{2,0},{3,1},{4,6},{5,7},{6,4},{7,5},{8,10},{9,11},{10,... | collective-permute-start | bytes 1572872 | tf_op jit(solution)/shard_map/ppermute | solution.py:563
  407.8 8.6 %cross_backward.6 = (bf16[1024,256]{1,0:T(8,128)(2,1)}, bf16[8,512,1024]{2,1,0:T(8,128)(2,1)}) custom-call(s32[4,5]{1,0:T(4,128)} %pad_add_fusion.info_ref, bf16[1024,256]{1,0:T(8,128)(2,1)} %copy-done.41, bf16[1120,256]{1,0:T(8,128)(2,1)} %copy-done.38, bf16[8,512,1024]{2,1,0:T(8,128)(2,1)} %bitcast.99, ...), custom_call_target="tpu_custom_call", output_to_operand_aliasing={{1}: (4, {})} | custom-call | flops 10000000000 | bytes 8000000 | tf_op jit(solution)/shard_map/cross_backward/pallas_call | solution.py:481
  416.4 4.5 collective-permute-start.38
  420.9 8.6 %cross_backward.7 = (bf16[1024,256]{1,0:T(8,128)(2,1)}, bf16[8,512,1024]{2,1,0:T(8,128)(2,1)}) custom-call(s32[4,5]{1,0:T(4,128)} %pad_add_fusion.info_ref, bf16[1024,256]{1,0:T(8,128)(2,1)} %broadcast_select_fusion.2.query_ref, bf16[1120,256]{1,0:T(8,128)(2,1)} %broadcast_select_fusion.grad_ref, ...), custom_call_target="tpu_custom_call", output_to_operand_aliasing={{1}: (4, {})} | custom-call | flops 10000000000 | bytes 8000000 | tf_op jit(solution)/shard_map/cross_backward/pallas_call | solution.py:481
  430.7 26.4 %memory_backward.1 = (bf16[4,2,2,256,1024]{4,3,2,1,0:T(8,128)(2,1)}, bf16[8,256,1024]{2,1,0:T(8,128)(2,1)}, bf16[16,32,2048]{2,1,0:T(8,128)(2,1)}, bf16[16,32,2048]{2,1,0:T(8,128)(2,1)}) custom-call(s32[3]{0:T(128)} %pad_add_fusion.1.me_ref, bf16[4,2,2,256,1024]{4,3,2,1,0:T(8,128)(2,1)} %bitcast.92, ...), custom_call_target="tpu_custom_call" | custom-call | flops 17200001024 | bytes 28000000 | tf_op jit(solution)/shard_map/memory_backward/pallas_call | solution.py:706
  458.1 6.0 %query_join.1 = (bf16[1024,256]{1,0:T(8,128)(2,1)}, f32[256,1024]{1,0:T(8,128)}, bf16[256,1024]{1,0:T(8,128)(2,1)}, bf16[256,1024]{1,0:T(8,128)(2,1)}, f32[1,1024]{1,0:T(1,128)}) custom-call(f32[256,1024]{1,0:T(8,128)} %get-tuple-element.262.grad_ref, f32[256,1024]{1,0:T(8,128)} %get-tuple-element.181.hidden_ref, f32[3,1024]{1,0:T(4,128)} %slice.247.gain_ref, ...), custom_call_target="tpu_custom_call" | custom-call | flops 1000000000 | bytes 8000000 | tf_op jit(solution)/shard_map/query_join/pallas_call | solution.py:41
  464.2 4.9 grad_blocks.2
  473.8 12.2 %self_backward.1 = (bf16[256,2048]{1,0:T(8,128)(2,1)}, f32[16,128]{1,0:T(8,128)}) custom-call(s32[2]{0:T(128)} %length_ref.3, bf16[256,1024]{1,0:T(8,128)(2,1)} %get-tuple-element.292.mix_grad_ref, bf16[256,2048]{1,0:T(8,128)(2,1)} %get-tuple-element.293.wide_ref, f32[32,128]{1,0:T(8,128)} %get-tuple-element.294.stat_ref, ...), custom_call_target="tpu_custom_call" | custom-call | flops 8000000000 | bytes 8000000 | tf_op jit(solution)/shard_map/self_backward/pallas_call | solution.py:41
  486.9 2.3 add_convert_fusion.11
  491.8 2.3 add_convert_fusion.7
  502.7 5.4 input_grads.1
  509.5 4.8 grad_blocks.3
  520.1 2.7 collective-permute-start.64
  522.8 7.1 %collective-permute-start.63 = (bf16[32,2048]{1,0:T(8,128)(2,1)}, bf16[32,2048]{1,0:T(8,128)(2,1)}, u32[]{:S(2)}, u32[]{:S(2)}) collective-permute-start(bf16[32,2048]{1,0:T(8,128)(2,1)} %get-tuple-element.386), channel_id=1, source_target_pairs={{0,4},{1,5},{2,6},{3,7},{4,0},{5,1},{6,2},{7,3},{8,12},{9,13},{10,... | collective-permute-start | bytes 393224 | tf_op jit(solution)/shard_map/ppermute | solution.py:563
  529.9 5.5 place_pairs.1
  536.1 3.1 collective-permute-done.63
  539.3 2.6 collective-permute-done.62
  545.7 6.3 %collective-permute-done.47 = bf16[2,32,2176]{2,1,0:T(8,128)(2,1)S(1)} collective-permute-done((bf16[2,32,2176]{2,1,0:T(8,128)(2,1)S(1)}, bf16[2,32,2176]{2,1,0:T(8,128)(2,1)S(1)}, u32[]{:S(2)}, u32[]{:S(2)}) %collective-permute-start.47) | collective-permute-done | bytes 278560 | tf_op jit(solution)/shard_map/ppermute | solution.py:563
  556.4 2.9 collective-permute-start.57
  560.0 5.8 collective-permute-done.52
  567.4 2.0 multiply_reduce_fusion
  571.7 2.9 collective-permute-start.54
  575.4 3.2 collective-permute-done.56
  578.6 4.2 collective-permute-done.55
  (309 shorter events, 94.4 us)
Async XLA Ops:
  7.2 120.5 %all-gather.6.cloned.1.call-start = ((), (), s32[]{:S(2)}) async-start(), calls=%async_computation.3 | async-start | bytes 2621440 | tf_op jit(solution)/shard_map/all_gather | solution.py:984
  7.2 120.5 %collective-permute-start.12 = (bf16[4,2,2,256,1024]{4,3,2,1,0:T(8,128)(2,1)}, bf16[4,2,2,256,1024]{4,3,2,1,0:T(8,128)(2,1)}, u32[]{:S(2)}, u32[]{:S(2)}) collective-permute-start(bf16[4,2,2,256,1024]{4,3,2,1,0:T(8,128)(2,1)} %bitcast.90), channel_id=1, source_target_pairs={{0,1},{1,0},{2,3},{3,2},{4,5},{5,4},{6,7},{7,6},{8,9},{9,8},{10,11... | collective-permute-start | bytes 25165832 | tf_op jit(solution)/shard_map/ppermute | solution.py:563
  15.5 13.5 %collective-permute-start.2 = (bf16[32,5248]{1,0:T(8,128)(2,1)S(1)}, bf16[32,5248]{1,0:T(8,128)(2,1)S(1)}, u32[]{:S(2)}, u32[]{:S(2)}) collective-permute-start(bf16[32,5248]{1,0:T(8,128)(2,1)S(1)} %constant_dynamic-update-slice_fusion), channel_id=1, source_target_pairs={{0,6},{1,7},{2,4},{3,5},{4,2},{5,3},{6,0},{7,1},{8,14},{9,15},{10,... | collective-permute-start | bytes 1007624 | tf_op jit(solution)/shard_map/ppermute | solution.py:563
  20.1 29.3 %collective-permute-start.1 = (bf16[32,5248]{1,0:T(8,128)(2,1)S(1)}, bf16[32,5248]{1,0:T(8,128)(2,1)S(1)}, u32[]{:S(2)}, u32[]{:S(2)}) collective-permute-start(bf16[32,5248]{1,0:T(8,128)(2,1)S(1)} %constant_dynamic-update-slice_fusion), channel_id=1, source_target_pairs={{0,4},{1,5},{2,6},{3,7},{4,0},{5,1},{6,2},{7,3},{8,12},{9,13},{10,... | collective-permute-start | bytes 1007624 | tf_op jit(solution)/shard_map/ppermute | solution.py:563
  20.1 29.3 %collective-permute-start = (bf16[32,5248]{1,0:T(8,128)(2,1)S(1)}, bf16[32,5248]{1,0:T(8,128)(2,1)S(1)}, u32[]{:S(2)}, u32[]{:S(2)}) collective-permute-start(bf16[32,5248]{1,0:T(8,128)(2,1)S(1)} %constant_dynamic-update-slice_fusion), channel_id=1, source_target_pairs={{0,2},{1,3},{2,0},{3,1},{4,6},{5,7},{6,4},{7,5},{8,10},{9,11},{10,... | collective-permute-start | bytes 1007624 | tf_op jit(solution)/shard_map/ppermute | solution.py:563
  49.6 31.2 %collective-permute-start.4 = (bf16[4,32,5248]{2,1,0:T(8,128)(2,1)S(1)}, bf16[4,32,5248]{2,1,0:T(8,128)(2,1)S(1)}, u32[]{:S(2)}, u32[]{:S(2)}) collective-permute-start(bf16[4,32,5248]{2,1,0:T(8,128)(2,1)S(1)} %pad_maximum_fusion.2.refs_0_), channel_id=1, source_target_pairs={{0,16},{8,24},{16,0},{24,8},{1,17},{9,25},{17,1},{25,9},{2,18},{10... | collective-permute-start | bytes 4030472 | tf_op jit(solution)/shard_map/ppermute | solution.py:563
  51.2 32.0 %collective-permute-start.3 = (bf16[4,32,5248]{2,1,0:T(8,128)(2,1)S(1)}, bf16[4,32,5248]{2,1,0:T(8,128)(2,1)}, u32[]{:S(2)}, u32[]{:S(2)}) collective-permute-start(bf16[4,32,5248]{2,1,0:T(8,128)(2,1)S(1)} %pad_maximum_fusion.2.refs_0_), channel_id=1, source_target_pairs={{0,8},{8,0},{16,24},{24,16},{1,9},{9,1},{17,25},{25,17},{2,10},{10... | collective-permute-start | bytes 4030472 | tf_op jit(solution)/shard_map/ppermute | solution.py:563
  52.7 34.0 %collective-permute-start.7 = (bf16[4,32,5248]{2,1,0:T(8,128)(2,1)S(1)}, bf16[4,32,5248]{2,1,0:T(8,128)(2,1)}, u32[]{:S(2)}, u32[]{:S(2)}) collective-permute-start(bf16[4,32,5248]{2,1,0:T(8,128)(2,1)S(1)} %pad_maximum_fusion.2.refs_0_), channel_id=1, source_target_pairs={{0,1},{1,0},{2,3},{3,2},{4,5},{5,4},{6,7},{7,6},{8,9},{9,8},{10,11... | collective-permute-start | bytes 4030472 | tf_op jit(solution)/shard_map/ppermute | solution.py:563
  52.7 168.8 %all-gather.4.cloned.1.call-start = ((), (), s32[]{:S(2)}) async-start(), calls=%async_computation.1 | async-start | bytes 2162688 | tf_op jit(solution)/shard_map/all_gather | solution.py:1027
  81.7 16.1 %collective-permute-start.5 = (bf16[2,32,5248]{2,1,0:T(8,128)(2,1)}, bf16[2,32,5248]{2,1,0:T(8,128)(2,1)S(1)}, u32[]{:S(2)}, u32[]{:S(2)}) collective-permute-start(bf16[2,32,5248]{2,1,0:T(8,128)(2,1)} %slice.326), channel_id=1, source_target_pairs={{0,8},{8,0},{16,24},{24,16},{1,9},{9,1},{17,25},{25,17},{2,10},{10... | collective-permute-start | bytes 2015240 | tf_op jit(solution)/shard_map/ppermute | solution.py:563
  85.2 16.0 %collective-permute-start.6 = (bf16[2,32,5248]{2,1,0:T(8,128)(2,1)}, bf16[2,32,5248]{2,1,0:T(8,128)(2,1)}, u32[]{:S(2)}, u32[]{:S(2)}) collective-permute-start(bf16[2,32,5248]{2,1,0:T(8,128)(2,1)} %slice.327), channel_id=1, source_target_pairs={{0,16},{8,24},{16,0},{24,8},{1,17},{9,25},{17,1},{25,9},{2,18},{10... | collective-permute-start | bytes 2015240 | tf_op jit(solution)/shard_map/ppermute | solution.py:563
  86.7 15.8 %collective-permute-start.9 = (bf16[4,32,5248]{2,1,0:T(8,128)(2,1)S(1)}, bf16[4,32,5248]{2,1,0:T(8,128)(2,1)}, u32[]{:S(2)}, u32[]{:S(2)}) collective-permute-start(bf16[4,32,5248]{2,1,0:T(8,128)(2,1)S(1)} %collective-permute-done.4.refs_2_), channel_id=1, source_target_pairs={{0,1},{1,0},{2,3},{3,2},{4,5},{5,4},{6,7},{7,6},{8,9},{9,8},{10,11... | collective-permute-start | bytes 4030472 | tf_op jit(solution)/shard_map/ppermute | solution.py:563
  86.7 16.8 %collective-permute-start.8 = (bf16[4,32,5248]{2,1,0:T(8,128)(2,1)}, bf16[4,32,5248]{2,1,0:T(8,128)(2,1)S(1)}, u32[]{:S(2)}, u32[]{:S(2)}) collective-permute-start(bf16[4,32,5248]{2,1,0:T(8,128)(2,1)} %collective-permute-done.3.refs_1_), channel_id=1, source_target_pairs={{0,1},{1,0},{2,3},{3,2},{4,5},{5,4},{6,7},{7,6},{8,9},{9,8},{10,11... | collective-permute-start | bytes 4030472 | tf_op jit(solution)/shard_map/ppermute | solution.py:563
  119.0 29.9 %collective-permute-start.14 = (bf16[1024,256]{1,0:T(8,128)(2,1)}, bf16[1024,256]{1,0:T(8,128)(2,1)S(1)}, u32[]{:S(2)}, u32[]{:S(2)}) collective-permute-start(bf16[1024,256]{1,0:T(8,128)(2,1)} %get-tuple-element.199.query_ref), channel_id=1, source_target_pairs={{0,4},{1,5},{2,6},{3,7},{4,0},{5,1},{6,2},{7,3},{8,12},{9,13},{10,... | collective-permute-start | bytes 1572872 | tf_op jit(solution)/shard_map/ppermute | solution.py:563
  119.1 31.2 %collective-permute-start.13 = (bf16[1024,256]{1,0:T(8,128)(2,1)}, bf16[1024,256]{1,0:T(8,128)(2,1)S(1)}, u32[]{:S(2)}, u32[]{:S(2)}) collective-permute-start(bf16[1024,256]{1,0:T(8,128)(2,1)} %get-tuple-element.199.query_ref), channel_id=1, source_target_pairs={{0,2},{1,3},{2,0},{3,1},{4,6},{5,7},{6,4},{7,5},{8,10},{9,11},{10,... | collective-permute-start | bytes 1572872 | tf_op jit(solution)/shard_map/ppermute | solution.py:563
  127.7 329.5 %all-reduce.8.cloned.1.call-start = ((), (), s32[]{:S(2)}) async-start(), calls=%async_computation.4 | async-start | bytes 4325376 | tf_op jit(solution)/shard_map/psum | solution.py:1078
  149.0 17.3 %collective-permute-start.17 = (bf16[1024,256]{1,0:T(8,128)(2,1)S(1)}, bf16[1024,256]{1,0:T(8,128)(2,1)S(1)}, u32[]{:S(2)}, u32[]{:S(2)}) collective-permute-start(bf16[1024,256]{1,0:T(8,128)(2,1)S(1)} %collective-permute-done.14.query_ref), channel_id=1, source_target_pairs={{4,6},{5,7},{2,0},{3,1},{12,14},{13,15},{10,8},{11,9},{20,22},{21,... | collective-permute-start | bytes 1572872 | tf_op jit(solution)/shard_map/ppermute | solution.py:571
  150.3 15.7 %collective-permute-start.18 = (bf16[1024,256]{1,0:T(8,128)(2,1)S(1)}, bf16[1024,256]{1,0:T(8,128)(2,1)S(1)}, u32[]{:S(2)}, u32[]{:S(2)}) collective-permute-start(bf16[1024,256]{1,0:T(8,128)(2,1)S(1)} %copy-done.43), channel_id=1, source_target_pairs={{2,4},{3,5},{4,2},{5,3},{10,12},{11,13},{12,10},{13,11},{18,20},{1... | collective-permute-start | bytes 1572872 | tf_op jit(solution)/shard_map/ppermute | solution.py:571
  174.6 16.9 %collective-permute-start.20 = (bf16[1024,352]{0,1:T(8,128)(2,1)S(1)}, bf16[1024,352]{0,1:T(8,128)(2,1)S(1)}, u32[]{:S(2)}, u32[]{:S(2)}) collective-permute-start(bf16[1024,352]{0,1:T(8,128)(2,1)S(1)} %copy-done.17), channel_id=1, source_target_pairs={{0,1},{1,0},{2,3},{3,2},{4,5},{5,4},{6,7},{7,6},{8,9},{9,8},{10,11... | collective-permute-start | bytes 2162696 | tf_op jit(solution)/shard_map/ppermute | solution.py:563
  174.6 23.1 %collective-permute-start.21 = (bf16[1024,352]{0,1:T(8,128)(2,1)}, bf16[1024,352]{0,1:T(8,128)(2,1)}, u32[]{:S(2)}, u32[]{:S(2)}) collective-permute-start(bf16[1024,352]{0,1:T(8,128)(2,1)} %param.40), channel_id=1, source_target_pairs={{0,1},{1,0},{2,3},{3,2},{4,5},{5,4},{6,7},{7,6},{8,9},{9,8},{10,11... | collective-permute-start | bytes 2162696 | tf_op jit(solution)/shard_map/ppermute | solution.py:563
  175.1 24.8 %collective-permute-start.22 = (bf16[352,1024]{1,0:T(8,128)(2,1)}, bf16[352,1024]{1,0:T(8,128)(2,1)}, u32[]{:S(2)}, u32[]{:S(2)}) collective-permute-start(bf16[352,1024]{1,0:T(8,128)(2,1)} %param.41), channel_id=1, source_target_pairs={{0,1},{1,0},{2,3},{3,2},{4,5},{5,4},{6,7},{7,6},{8,9},{9,8},{10,11... | collective-permute-start | bytes 2162696 | tf_op jit(solution)/shard_map/ppermute | solution.py:563
  175.8 32.9 %collective-permute-start.16 = (bf16[1072,256]{1,0:T(8,128)(2,1)}, bf16[1072,256]{1,0:T(8,128)(2,1)}, u32[]{:S(2)}, u32[]{:S(2)}) collective-permute-start(bf16[1072,256]{1,0:T(8,128)(2,1)} %cross_forward.6), channel_id=1, source_target_pairs={{0,4},{1,5},{2,6},{3,7},{4,0},{5,1},{6,2},{7,3},{8,12},{9,13},{10,... | collective-permute-start | bytes 1646600 | tf_op jit(solution)/shard_map/ppermute | solution.py:563
  180.9 27.9 %collective-permute-start.15 = (bf16[1072,256]{1,0:T(8,128)(2,1)}, bf16[1072,256]{1,0:T(8,128)(2,1)}, u32[]{:S(2)}, u32[]{:S(2)}) collective-permute-start(bf16[1072,256]{1,0:T(8,128)(2,1)} %cross_forward.5), channel_id=1, source_target_pairs={{0,2},{1,3},{2,0},{3,1},{4,6},{5,7},{6,4},{7,5},{8,10},{9,11},{10,... | collective-permute-start | bytes 1646600 | tf_op jit(solution)/shard_map/ppermute | solution.py:563
  192.4 29.1 %collective-permute-start.19 = (bf16[1072,256]{1,0:T(8,128)(2,1)}, bf16[1072,256]{1,0:T(8,128)(2,1)}, u32[]{:S(2)}, u32[]{:S(2)}) collective-permute-start(bf16[1072,256]{1,0:T(8,128)(2,1)} %cross_forward.7), channel_id=1, source_target_pairs={{0,6},{1,7},{2,4},{3,5},{4,2},{5,3},{6,0},{7,1},{8,14},{9,15},{10,... | collective-permute-start | bytes 1646600 | tf_op jit(solution)/shard_map/ppermute | solution.py:563
  226.5 34.5 %collective-permute-start.23 = (bf16[256,1024]{1,0:T(8,128)(2,1)}, bf16[256,1024]{1,0:T(8,128)(2,1)S(1)}, u32[]{:S(2)}, u32[]{:S(2)}) collective-permute-start(bf16[256,1024]{1,0:T(8,128)(2,1)} %get-tuple-element.223.row_ref), channel_id=1, source_target_pairs={{0,4},{1,5},{2,6},{3,7},{4,0},{5,1},{6,2},{7,3},{8,12},{9,13},{10,... | collective-permute-start | bytes 1572872 | tf_op jit(solution)/shard_map/ppermute | solution.py:563
  237.5 24.8 %collective-permute-start.26 = (bf16[256,1024]{1,0:T(8,128)(2,1)}, bf16[256,1024]{1,0:T(8,128)(2,1)S(1)}, u32[]{:S(2)}, u32[]{:S(2)}) collective-permute-start(bf16[256,1024]{1,0:T(8,128)(2,1)} %get-tuple-element.223.row_ref), channel_id=1, source_target_pairs={{0,2},{1,3},{2,0},{3,1},{4,6},{5,7},{6,4},{7,5},{8,10},{9,11},{10,... | collective-permute-start | bytes 1572872 | tf_op jit(solution)/shard_map/ppermute | solution.py:563
  261.0 31.6 %collective-permute-start.24 = (bf16[256,1024]{1,0:T(8,128)(2,1)S(1)}, bf16[256,1024]{1,0:T(8,128)(2,1)S(1)}, u32[]{:S(2)}, u32[]{:S(2)}) collective-permute-start(bf16[256,1024]{1,0:T(8,128)(2,1)S(1)} %collective-permute-done.23.row_ref), channel_id=1, source_target_pairs={{4,6},{5,7},{2,0},{3,1},{12,14},{13,15},{10,8},{11,9},{20,22},{21,... | collective-permute-start | bytes 1572872 | tf_op jit(solution)/shard_map/ppermute | solution.py:571
  262.3 30.2 %collective-permute-start.25 = (bf16[256,1024]{1,0:T(8,128)(2,1)S(1)}, bf16[256,1024]{1,0:T(8,128)(2,1)S(1)}, u32[]{:S(2)}, u32[]{:S(2)}) collective-permute-start(bf16[256,1024]{1,0:T(8,128)(2,1)S(1)} %copy-done.46), channel_id=1, source_target_pairs={{2,4},{3,5},{4,2},{5,3},{10,12},{11,13},{12,10},{13,11},{18,20},{1... | collective-permute-start | bytes 1572872 | tf_op jit(solution)/shard_map/ppermute | solution.py:571
  279.1 21.6 %collective-permute-start.27 = (bf16[256,1024]{1,0:T(8,128)(2,1)}, bf16[256,1024]{1,0:T(8,128)(2,1)S(1)}, u32[]{:S(2)}, u32[]{:S(2)}) collective-permute-start(bf16[256,1024]{1,0:T(8,128)(2,1)} %get-tuple-element.249), channel_id=1, source_target_pairs={{0,2},{1,3},{2,0},{3,1},{4,6},{5,7},{6,4},{7,5},{8,10},{9,11},{10,... | collective-permute-start | bytes 1572872 | tf_op jit(solution)/shard_map/ppermute | solution.py:563
  304.9 7.1 %collective-permute-start.30 = (bf16[1024,352]{0,1:T(8,128)(2,1)S(1)}, bf16[1024,352]{0,1:T(8,128)(2,1)S(1)}, u32[]{:S(2)}, u32[]{:S(2)}) collective-permute-start(bf16[1024,352]{0,1:T(8,128)(2,1)S(1)} %slice.440), channel_id=1, source_target_pairs={{0,1},{1,0},{2,3},{3,2},{4,5},{5,4},{6,7},{7,6},{8,9},{9,8},{10,11... | collective-permute-start | bytes 2162696 | tf_op jit(solution)/shard_map/ppermute | solution.py:563
  309.6 37.2 %collective-permute-start.28 = (bf16[256,1024]{1,0:T(8,128)(2,1)S(1)}, bf16[256,1024]{1,0:T(8,128)(2,1)S(1)}, u32[]{:S(2)}, u32[]{:S(2)}) collective-permute-start(bf16[256,1024]{1,0:T(8,128)(2,1)S(1)} %copy-done.44), channel_id=1, source_target_pairs={{0,4},{1,5},{2,6},{3,7},{4,0},{5,1},{6,2},{7,3},{8,12},{9,13},{10,... | collective-permute-start | bytes 1572872 | tf_op jit(solution)/shard_map/ppermute | solution.py:563
  309.6 37.1 %collective-permute-start.29 = (bf16[256,1024]{1,0:T(8,128)(2,1)S(1)}, bf16[256,1024]{1,0:T(8,128)(2,1)S(1)}, u32[]{:S(2)}, u32[]{:S(2)}) collective-permute-start(bf16[256,1024]{1,0:T(8,128)(2,1)S(1)} %copy-done.45), channel_id=1, source_target_pairs={{0,6},{1,7},{2,4},{3,5},{4,2},{5,3},{6,0},{7,1},{8,14},{9,15},{10,... | collective-permute-start | bytes 1572872 | tf_op jit(solution)/shard_map/ppermute | solution.py:563
  346.8 220.6 %reduce-scatter.2.cloned.1.call-start = ((), (), s32[]{:S(2)}) async-start(), calls=%async_computation.2 | async-start | bytes 2621440 | tf_op jit(solution)/shard_map/reduce_scatter | solution.py:1128
  352.9 37.0 %collective-permute-start.34 = (bf16[1120,256]{1,0:T(8,128)(2,1)}, bf16[1120,256]{1,0:T(8,128)(2,1)S(1)}, u32[]{:S(2)}, u32[]{:S(2)}) collective-permute-start(bf16[1120,256]{1,0:T(8,128)(2,1)} %get-tuple-element.269.grad_ref), channel_id=1, source_target_pairs={{0,4},{1,5},{2,6},{3,7},{4,0},{5,1},{6,2},{7,3},{8,12},{9,13},{10,... | collective-permute-start | bytes 1720328 | tf_op jit(solution)/shard_map/ppermute | solution.py:563
  364.4 26.8 %collective-permute-start.33 = (bf16[1120,256]{1,0:T(8,128)(2,1)}, bf16[1120,256]{1,0:T(8,128)(2,1)S(1)}, u32[]{:S(2)}, u32[]{:S(2)}) collective-permute-start(bf16[1120,256]{1,0:T(8,128)(2,1)} %get-tuple-element.269.grad_ref), channel_id=1, source_target_pairs={{0,2},{1,3},{2,0},{3,1},{4,6},{5,7},{6,4},{7,5},{8,10},{9,11},{10,... | collective-permute-start | bytes 1720328 | tf_op jit(solution)/shard_map/ppermute | solution.py:563
  389.9 17.0 %collective-permute-start.37 = (bf16[1120,256]{1,0:T(8,128)(2,1)S(1)}, bf16[1120,256]{1,0:T(8,128)(2,1)S(1)}, u32[]{:S(2)}, u32[]{:S(2)}) collective-permute-start(bf16[1120,256]{1,0:T(8,128)(2,1)S(1)} %collective-permute-done.34.grad_ref), channel_id=1, source_target_pairs={{4,6},{5,7},{2,0},{3,1},{12,14},{13,15},{10,8},{11,9},{20,22},{21,... | collective-permute-start | bytes 1720328 | tf_op jit(solution)/shard_map/ppermute | solution.py:571
  391.2 15.7 %collective-permute-start.36 = (bf16[1120,256]{1,0:T(8,128)(2,1)S(1)}, bf16[1120,256]{1,0:T(8,128)(2,1)S(1)}, u32[]{:S(2)}, u32[]{:S(2)}) collective-permute-start(bf16[1120,256]{1,0:T(8,128)(2,1)S(1)} %copy-done.39), channel_id=1, source_target_pairs={{2,4},{3,5},{4,2},{5,3},{10,12},{11,13},{12,10},{13,11},{18,20},{1... | collective-permute-start | bytes 1720328 | tf_op jit(solution)/shard_map/ppermute | solution.py:571
  400.9 28.5 %collective-permute-start.35 = (bf16[1024,256]{1,0:T(8,128)(2,1)}, bf16[1024,256]{1,0:T(8,128)(2,1)S(1)}, u32[]{:S(2)}, u32[]{:S(2)}) collective-permute-start(bf16[1024,256]{1,0:T(8,128)(2,1)} %get-tuple-element.268), channel_id=1, source_target_pairs={{0,2},{1,3},{2,0},{3,1},{4,6},{5,7},{6,4},{7,5},{8,10},{9,11},{10,... | collective-permute-start | bytes 1572872 | tf_op jit(solution)/shard_map/ppermute | solution.py:563
  416.4 40.8 %collective-permute-start.38 = (bf16[1024,256]{1,0:T(8,128)(2,1)}, bf16[1024,256]{1,0:T(8,128)(2,1)S(1)}, u32[]{:S(2)}, u32[]{:S(2)}) collective-permute-start(bf16[1024,256]{1,0:T(8,128)(2,1)} %get-tuple-element.274), channel_id=1, source_target_pairs={{0,4},{1,5},{2,6},{3,7},{4,0},{5,1},{6,2},{7,3},{8,12},{9,13},{10,... | collective-permute-start | bytes 1572872 | tf_op jit(solution)/shard_map/ppermute | solution.py:563
  429.4 27.7 %collective-permute-start.39 = (bf16[1024,256]{1,0:T(8,128)(2,1)}, bf16[1024,256]{1,0:T(8,128)(2,1)S(1)}, u32[]{:S(2)}, u32[]{:S(2)}) collective-permute-start(bf16[1024,256]{1,0:T(8,128)(2,1)} %get-tuple-element.276), channel_id=1, source_target_pairs={{0,6},{1,7},{2,4},{3,5},{4,2},{5,3},{6,0},{7,1},{8,14},{9,15},{10,... | collective-permute-start | bytes 1572872 | tf_op jit(solution)/shard_map/ppermute | solution.py:563
  464.2 22.7 %collective-permute-start.40 = (bf16[16,32,2048]{2,1,0:T(8,128)(2,1)}, bf16[16,32,2048]{2,1,0:T(8,128)(2,1)}, u32[]{:S(2)}, u32[]{:S(2)}) collective-permute-start(bf16[16,32,2048]{2,1,0:T(8,128)(2,1)} %get-tuple-element.297), channel_id=1, source_target_pairs={{0,1},{1,0},{2,3},{3,2},{4,5},{5,4},{6,7},{7,6},{8,9},{9,8},{10,11... | collective-permute-start | bytes 6291464 | tf_op jit(solution)/shard_map/ppermute | solution.py:563
  469.1 22.7 %collective-permute-start.43 = (bf16[16,32,2048]{2,1,0:T(8,128)(2,1)}, bf16[16,32,2048]{2,1,0:T(8,128)(2,1)}, u32[]{:S(2)}, u32[]{:S(2)}) collective-permute-start(bf16[16,32,2048]{2,1,0:T(8,128)(2,1)} %get-tuple-element.291), channel_id=1, source_target_pairs={{0,1},{1,0},{2,3},{3,2},{4,5},{5,4},{6,7},{7,6},{8,9},{9,8},{10,11... | collective-permute-start | bytes 6291464 | tf_op jit(solution)/shard_map/ppermute | solution.py:563
  469.8 53.0 %collective-permute-start.45 = (bf16[8,256,1024]{2,1,0:T(8,128)(2,1)}, bf16[8,256,1024]{2,1,0:T(8,128)(2,1)}, u32[]{:S(2)}, u32[]{:S(2)}) collective-permute-start(bf16[8,256,1024]{2,1,0:T(8,128)(2,1)} %get-tuple-element.310), channel_id=1, source_target_pairs={{0,1},{1,0},{2,3},{3,2},{4,5},{5,4},{6,7},{7,6},{8,9},{9,8},{10,11... | collective-permute-start | bytes 12582920 | tf_op jit(solution)/shard_map/ppermute | solution.py:563
  489.3 9.0 %collective-permute-start.42 = (bf16[2,32,2048]{2,1,0:T(8,128)(2,1)S(1)}, bf16[2,32,2048]{2,1,0:T(8,128)(2,1)S(1)}, u32[]{:S(2)}, u32[]{:S(2)}) collective-permute-start(bf16[2,32,2048]{2,1,0:T(8,128)(2,1)S(1)} %get-tuple-element.395), channel_id=1, source_target_pairs={{0,16},{8,24},{16,0},{24,8},{1,17},{9,25},{17,1},{25,9},{2,18},{10... | collective-permute-start | bytes 786440 | tf_op jit(solution)/shard_map/ppermute | solution.py:563
  490.8 9.0 %collective-permute-start.41 = (bf16[2,32,2048]{2,1,0:T(8,128)(2,1)S(1)}, bf16[2,32,2048]{2,1,0:T(8,128)(2,1)S(1)}, u32[]{:S(2)}, u32[]{:S(2)}) collective-permute-start(bf16[2,32,2048]{2,1,0:T(8,128)(2,1)S(1)} %get-tuple-element.396), channel_id=1, source_target_pairs={{0,8},{8,0},{16,24},{24,16},{1,9},{9,1},{17,25},{25,17},{2,10},{10... | collective-permute-start | bytes 786440 | tf_op jit(solution)/shard_map/ppermute | solution.py:563
  495.0 19.3 %collective-permute-start.49 = (bf16[2,32,2048]{2,1,0:T(8,128)(2,1)}, bf16[2,32,2048]{2,1,0:T(8,128)(2,1)S(1)}, u32[]{:S(2)}, u32[]{:S(2)}) collective-permute-start(bf16[2,32,2048]{2,1,0:T(8,128)(2,1)} %get-tuple-element.393), channel_id=1, source_target_pairs={{0,16},{8,24},{16,0},{24,8},{1,17},{9,25},{17,1},{25,9},{2,18},{10... | collective-permute-start | bytes 786440 | tf_op jit(solution)/shard_map/ppermute | solution.py:563
  496.0 18.3 %collective-permute-start.48 = (bf16[2,32,2048]{2,1,0:T(8,128)(2,1)}, bf16[2,32,2048]{2,1,0:T(8,128)(2,1)}, u32[]{:S(2)}, u32[]{:S(2)}) collective-permute-start(bf16[2,32,2048]{2,1,0:T(8,128)(2,1)} %get-tuple-element.394), channel_id=1, source_target_pairs={{0,8},{8,0},{16,24},{24,16},{1,9},{9,1},{17,25},{25,17},{2,10},{10... | collective-permute-start | bytes 786440 | tf_op jit(solution)/shard_map/ppermute | solution.py:563
  500.0 16.8 %collective-permute-start.61 = (bf16[4,32,2048]{2,1,0:T(8,128)(2,1)S(1)}, bf16[4,32,2048]{2,1,0:T(8,128)(2,1)}, u32[]{:S(2)}, u32[]{:S(2)}) collective-permute-start(bf16[4,32,2048]{2,1,0:T(8,128)(2,1)S(1)} %pad_maximum_fusion.6), channel_id=1, source_target_pairs={{0,16},{8,24},{16,0},{24,8},{1,17},{9,25},{17,1},{25,9},{2,18},{10... | collective-permute-start | bytes 1572872 | tf_op jit(solution)/shard_map/ppermute | solution.py:563
  501.1 16.8 %collective-permute-start.60 = (bf16[4,32,2048]{2,1,0:T(8,128)(2,1)}, bf16[4,32,2048]{2,1,0:T(8,128)(2,1)}, u32[]{:S(2)}, u32[]{:S(2)}) collective-permute-start(bf16[4,32,2048]{2,1,0:T(8,128)(2,1)} %pad_maximum_fusion.5), channel_id=1, source_target_pairs={{0,8},{8,0},{16,24},{24,16},{1,9},{9,1},{17,25},{25,17},{2,10},{10... | collective-permute-start | bytes 1572872 | tf_op jit(solution)/shard_map/ppermute | solution.py:563
  514.2 21.2 %collective-permute-start.44 = (bf16[16,32,2176]{2,1,0:T(8,128)(2,1)}, bf16[16,32,2176]{2,1,0:T(8,128)(2,1)S(1)}, u32[]{:S(2)}, u32[]{:S(2)}) collective-permute-start(bf16[16,32,2176]{2,1,0:T(8,128)(2,1)} %get-tuple-element.309), channel_id=1, source_target_pairs={{0,1},{1,0},{2,3},{3,2},{4,5},{5,4},{6,7},{7,6},{8,9},{9,8},{10,11... | collective-permute-start | bytes 6684680 | tf_op jit(solution)/shard_map/ppermute | solution.py:563
  515.3 20.8 %collective-permute-start.51 = (bf16[4,32,2048]{2,1,0:T(8,128)(2,1)S(1)}, bf16[4,32,2048]{2,1,0:T(8,128)(2,1)}, u32[]{:S(2)}, u32[]{:S(2)}) collective-permute-start(bf16[4,32,2048]{2,1,0:T(8,128)(2,1)S(1)} %pad_maximum_fusion.8), channel_id=1, source_target_pairs={{0,16},{8,24},{16,0},{24,8},{1,17},{9,25},{17,1},{25,9},{2,18},{10... | collective-permute-start | bytes 1572872 | tf_op jit(solution)/shard_map/ppermute | solution.py:563
  516.8 19.3 %collective-permute-start.50 = (bf16[4,32,2048]{2,1,0:T(8,128)(2,1)S(1)}, bf16[4,32,2048]{2,1,0:T(8,128)(2,1)S(1)}, u32[]{:S(2)}, u32[]{:S(2)}) collective-permute-start(bf16[4,32,2048]{2,1,0:T(8,128)(2,1)S(1)} %pad_maximum_fusion.7), channel_id=1, source_target_pairs={{0,8},{8,0},{16,24},{24,16},{1,9},{9,1},{17,25},{25,17},{2,10},{10... | collective-permute-start | bytes 1572872 | tf_op jit(solution)/shard_map/ppermute | solution.py:563
  520.1 16.0 %collective-permute-start.64 = (bf16[32,2048]{1,0:T(8,128)(2,1)}, bf16[32,2048]{1,0:T(8,128)(2,1)S(1)}, u32[]{:S(2)}, u32[]{:S(2)}) collective-permute-start(bf16[32,2048]{1,0:T(8,128)(2,1)} %get-tuple-element.385), channel_id=1, source_target_pairs={{0,6},{1,7},{2,4},{3,5},{4,2},{5,3},{6,0},{7,1},{8,14},{9,15},{10,... | collective-permute-start | bytes 393224 | tf_op jit(solution)/shard_map/ppermute | solution.py:563
  522.8 16.5 %collective-permute-start.63 = (bf16[32,2048]{1,0:T(8,128)(2,1)}, bf16[32,2048]{1,0:T(8,128)(2,1)}, u32[]{:S(2)}, u32[]{:S(2)}) collective-permute-start(bf16[32,2048]{1,0:T(8,128)(2,1)} %get-tuple-element.386), channel_id=1, source_target_pairs={{0,4},{1,5},{2,6},{3,7},{4,0},{5,1},{6,2},{7,3},{8,12},{9,13},{10,... | collective-permute-start | bytes 393224 | tf_op jit(solution)/shard_map/ppermute | solution.py:563
  543.5 8.5 %collective-permute-start.47 = (bf16[2,32,2176]{2,1,0:T(8,128)(2,1)S(1)}, bf16[2,32,2176]{2,1,0:T(8,128)(2,1)S(1)}, u32[]{:S(2)}, u32[]{:S(2)}) collective-permute-start(bf16[2,32,2176]{2,1,0:T(8,128)(2,1)S(1)} %get-tuple-element.383), channel_id=1, source_target_pairs={{0,16},{8,24},{16,0},{24,8},{1,17},{9,25},{17,1},{25,9},{2,18},{10... | collective-permute-start | bytes 835592 | tf_op jit(solution)/shard_map/ppermute | solution.py:563
  544.0 8.2 %collective-permute-start.46 = (bf16[2,32,2176]{2,1,0:T(8,128)(2,1)S(1)}, bf16[2,32,2176]{2,1,0:T(8,128)(2,1)S(1)}, u32[]{:S(2)}, u32[]{:S(2)}) collective-permute-start(bf16[2,32,2176]{2,1,0:T(8,128)(2,1)S(1)} %get-tuple-element.384), channel_id=1, source_target_pairs={{0,8},{8,0},{16,24},{24,16},{1,9},{9,1},{17,25},{25,17},{2,10},{10... | collective-permute-start | bytes 835592 | tf_op jit(solution)/shard_map/ppermute | solution.py:563
  552.3 13.4 %collective-permute-start.52 = (bf16[4,32,2176]{2,1,0:T(8,128)(2,1)S(1)}, bf16[4,32,2176]{2,1,0:T(8,128)(2,1)S(1)}, u32[]{:S(2)}, u32[]{:S(2)}) collective-permute-start(bf16[4,32,2176]{2,1,0:T(8,128)(2,1)S(1)} %pad_maximum_fusion.3), channel_id=1, source_target_pairs={{0,8},{8,0},{16,24},{24,16},{1,9},{9,1},{17,25},{25,17},{2,10},{10... | collective-permute-start | bytes 1671176 | tf_op jit(solution)/shard_map/ppermute | solution.py:563
  553.1 13.3 %collective-permute-start.53 = (bf16[4,32,2176]{2,1,0:T(8,128)(2,1)S(1)}, bf16[4,32,2176]{2,1,0:T(8,128)(2,1)S(1)}, u32[]{:S(2)}, u32[]{:S(2)}) collective-permute-start(bf16[4,32,2176]{2,1,0:T(8,128)(2,1)S(1)} %pad_maximum_fusion.4), channel_id=1, source_target_pairs={{0,16},{8,24},{16,0},{24,8},{1,17},{9,25},{17,1},{25,9},{2,18},{10... | collective-permute-start | bytes 1671176 | tf_op jit(solution)/shard_map/ppermute | solution.py:563
  554.8 11.8 %collective-permute-start.59 = (bf16[32,2048]{1,0:T(8,128)(2,1)S(1)}, bf16[32,2048]{1,0:T(8,128)(2,1)S(1)}, u32[]{:S(2)}, u32[]{:S(2)}) collective-permute-start(bf16[32,2048]{1,0:T(8,128)(2,1)S(1)} %get-tuple-element.389), channel_id=1, source_target_pairs={{0,6},{1,7},{2,4},{3,5},{4,2},{5,3},{6,0},{7,1},{8,14},{9,15},{10,... | collective-permute-start | bytes 393224 | tf_op jit(solution)/shard_map/ppermute | solution.py:563
  556.4 10.9 %collective-permute-start.58 = (bf16[32,2048]{1,0:T(8,128)(2,1)S(1)}, bf16[32,2048]{1,0:T(8,128)(2,1)S(1)}, u32[]{:S(2)}, u32[]{:S(2)}) collective-permute-start(bf16[32,2048]{1,0:T(8,128)(2,1)S(1)} %get-tuple-element.390), channel_id=1, source_target_pairs={{0,4},{1,5},{2,6},{3,7},{4,0},{5,1},{6,2},{7,3},{8,12},{9,13},{10,... | collective-permute-start | bytes 393224 | tf_op jit(solution)/shard_map/ppermute | solution.py:563
  556.4 10.9 %collective-permute-start.57 = (bf16[32,2048]{1,0:T(8,128)(2,1)S(1)}, bf16[32,2048]{1,0:T(8,128)(2,1)S(1)}, u32[]{:S(2)}, u32[]{:S(2)}) collective-permute-start(bf16[32,2048]{1,0:T(8,128)(2,1)S(1)} %get-tuple-element.391), channel_id=1, source_target_pairs={{0,2},{1,3},{2,0},{3,1},{4,6},{5,7},{6,4},{7,5},{8,10},{9,11},{10,... | collective-permute-start | bytes 393224 | tf_op jit(solution)/shard_map/ppermute | solution.py:563
  570.2 8.4 %collective-permute-start.56 = (bf16[32,2176]{1,0:T(8,128)(2,1)S(1)}, bf16[32,2176]{1,0:T(8,128)(2,1)S(1)}, u32[]{:S(2)}, u32[]{:S(2)}) collective-permute-start(bf16[32,2176]{1,0:T(8,128)(2,1)S(1)} %get-tuple-element.379), channel_id=1, source_target_pairs={{0,6},{1,7},{2,4},{3,5},{4,2},{5,3},{6,0},{7,1},{8,14},{9,15},{10,... | collective-permute-start | bytes 417800 | tf_op jit(solution)/shard_map/ppermute | solution.py:563
  571.7 11.1 %collective-permute-start.55 = (bf16[32,2176]{1,0:T(8,128)(2,1)S(1)}, bf16[32,2176]{1,0:T(8,128)(2,1)S(1)}, u32[]{:S(2)}, u32[]{:S(2)}) collective-permute-start(bf16[32,2176]{1,0:T(8,128)(2,1)S(1)} %get-tuple-element.380), channel_id=1, source_target_pairs={{0,4},{1,5},{2,6},{3,7},{4,0},{5,1},{6,2},{7,3},{8,12},{9,13},{10,... | collective-permute-start | bytes 417800 | tf_op jit(solution)/shard_map/ppermute | solution.py:563
  571.7 11.1 %collective-permute-start.54 = (bf16[32,2176]{1,0:T(8,128)(2,1)S(1)}, bf16[32,2176]{1,0:T(8,128)(2,1)S(1)}, u32[]{:S(2)}, u32[]{:S(2)}) collective-permute-start(bf16[32,2176]{1,0:T(8,128)(2,1)S(1)} %get-tuple-element.381), channel_id=1, source_target_pairs={{0,2},{1,3},{2,0},{3,1},{4,6},{5,7},{6,4},{7,5},{8,10},{9,11},{10,... | collective-permute-start | bytes 417800 | tf_op jit(solution)/shard_map/ppermute | solution.py:563
  (52 other events, 429.5 us)
Sparse Core Ops, SparseCore 0:
  52.9 44.3 all-gather.5
  127.8 72.1 all-gather.3
  346.9 79.7 all-reduce.7
  474.0 48.7 reduce-scatter.1
